TPU v7x, 512 devices: a whole 4x8x8 slice. The times are simulated.
512 devices in a mesh: replica: 32 (over y, x), tensor: 16 (over z, core).
Axes of the slice: x: 4, y: 8, z: 8, core: 2. Of those that a mesh axis runs over, the one named last changes fastest.
Arguments:
- inputs: bfloat16 [8192, 8192], P('replica', 'tensor'), may hold values from -6 to 6
- row_adapter_slot: int32 [8192], P('replica'), may hold values from 0 to 62
- transfer_plan: int32 [32, 31], replicated, may hold values from 0 to 1023, as said below
- key_value_weight: bfloat16 [8192, 2048], P('tensor'), may hold values from -0.0625 to 0.0625
- adapter_down: bfloat16 [1024, 64, 8192], P('replica', None, 'tensor'), may hold values from -0.0625 to 0.0625
- adapter_up: bfloat16 [1024, 64, 2048], P('replica', None, 'tensor'), may hold values from -0.75 to 0.75
Outputs:
- kv_out: bfloat16 [8192, 2048], P('replica', 'tensor')
Inputs may be any that keep to these rules, and one draw needn't show every extreme that they name: `transfer_plan`: row g holds 31 distinct adapters, none of whose home group (id // 32) is g, ordered by home group; at most 2 of them share a home, and in every draw each group has some home that supplies 2.
All inputs are finite; a program needn't handle non-finite values.
Results may differ from a plain program's by a relative error of at most 0.0025.
Values may be sent and summed in bfloat16 or wider, within the bound.
No kernel may reach another device: no remote copies, remote signals or barrier semaphores. Data moves between devices by JAX's collectives and lax.ppermute only.
A program may use at most 64 MiB of HBM per device.

v0:
```python
import jax
import jax.numpy as jnp
from jax import lax
from jax.sharding import PartitionSpec as P

IMPORT_LIMIT = 2


adapter_scale = 1.0


def shards(inputs, row_adapter_slot, transfer_plan, key_value_weight, adapter_down, adapter_up):
    row_count = inputs.shape[0]
    homed_adapters = adapter_down.shape[0]
    rank_extent = adapter_down.shape[1]
    group_count = lax.axis_size("replica")
    slot_count = transfer_plan.shape[1]
    my_group = lax.axis_index("replica")
    home_group = transfer_plan // homed_adapters
    offsets = transfer_plan % homed_adapters
    is_mine = (home_group == my_group).astype(jnp.int32)
    send_order = jnp.cumsum(is_mine, axis=1) - 1
    chosen = (is_mine[:, None, :] == 1) & (
        send_order[:, None, :] == jnp.arange(IMPORT_LIMIT, dtype=jnp.int32)[None, :, None]
    )
    outgoing_selection = jnp.sum(jnp.where(chosen, offsets[:, None, :], 0), axis=2).reshape(-1)
    down_outgoing = jnp.take(adapter_down, outgoing_selection, axis=0).reshape(
        group_count, IMPORT_LIMIT, rank_extent, -1
    )
    up_outgoing = jnp.take(adapter_up, outgoing_selection, axis=0).reshape(
        group_count, IMPORT_LIMIT, rank_extent, -1
    )
    down_received, up_received = (
        lax.all_to_all(down_outgoing, "replica", split_axis=0, concat_axis=0, tiled=True),
        lax.all_to_all(up_outgoing, "replica", split_axis=0, concat_axis=0, tiled=True),
    )
    own_plan = lax.dynamic_index_in_dim(transfer_plan, my_group, 0, keepdims=False)
    own_home = own_plan // homed_adapters
    slot_ids = jnp.arange(slot_count, dtype=jnp.int32)
    same_home = (own_home[:, None] == own_home[None, :]) & (slot_ids[None, :] < slot_ids[:, None])
    second_rank = jnp.sum(same_home.astype(jnp.int32), axis=1)
    source_group = own_home * IMPORT_LIMIT + second_rank
    down_table = jnp.concatenate(
        [
            adapter_down,
            jnp.take(
                down_received.reshape(group_count * IMPORT_LIMIT, rank_extent, -1),
                source_group,
                axis=0,
            ),
        ],
        axis=0,
    )
    local_count = down_table.shape[0]
    shrink_all = lax.dot_general(
        inputs,
        down_table.reshape(local_count * rank_extent, -1),
        (((1,), (1,)), ((), ())),
        preferred_element_type=jnp.float32,
    )
    selector = row_adapter_slot[:, None] == jnp.arange(local_count, dtype=jnp.int32)[None, :]
    shrink_part = jnp.sum(
        jnp.where(
            selector[:, :, None], shrink_all.reshape(row_count, local_count, rank_extent), 0.0
        ),
        axis=1,
    )
    base_part = jnp.dot(inputs, key_value_weight, preferred_element_type=jnp.float32)
    shrink = lax.psum(shrink_part, "tensor")
    base_output = lax.psum_scatter(base_part, "tensor", scatter_dimension=1, tiled=True)
    up_table = jnp.concatenate(
        [
            adapter_up,
            jnp.take(
                up_received.reshape(group_count * IMPORT_LIMIT, rank_extent, -1),
                source_group,
                axis=0,
            ),
        ],
        axis=0,
    )
    up_wide = up_table.reshape(local_count * rank_extent, -1).astype(jnp.float32)
    placed = jnp.where(selector[:, :, None], shrink[:, None, :], 0.0).reshape(
        row_count, local_count * rank_extent
    )
    adapter_update = jnp.dot(
        placed, up_wide, preferred_element_type=jnp.float32, precision=lax.Precision.HIGHEST
    )
    return (base_output + adapter_scale * adapter_update).astype(jnp.bfloat16)


def solution(mesh):
    placed = (
        P("replica", "tensor"),
        P("replica"),
        P(),
        P("tensor", None),
        P("replica", None, "tensor"),
        P("replica", None, "tensor"),
    )
    return jax.shard_map(
        shards, mesh=mesh, in_specs=placed, out_specs=P("replica", "tensor"), check_vma=False
    )
```

profile of v0, /device:TPU:1, one launch (start us, length us, event | category | flops | bytes accessed | tf_op | source)
XLA Modules:
  0.0 278.0 jit_solution(14623746664971491532)
XLA Ops:
  6.5 0.9 add_select_fusion
  7.4 0.7 broadcast_compare_fusion
  8.2 0.2 reduce_window_sum.11
  8.3 0.1 copy.8
  8.4 0.1 copy.7
  8.7 0.1 copy.11
  8.8 0.1 reshape.194
  8.9 0.1 copy.10
  9.0 1.8 gather_fusion.2
  10.8 1.2 broadcast_select_fusion.2
  12.1 10.5 %all-to-all-start.1 = ((bf16[32,2,64,128]{3,2,1,0:T(8,128)(2,1)}), bf16[32,2,64,128]{3,2,1,0:T(8,128)(2,1)S(1)}, u32[]{:S(2)}, u32[]{:S(2)}) async-start(bf16[32,2,64,128]{3,2,1,0:T(8,128)(2,1)} %broadcast_select_fusion.2), calls=%async_computation.2 | async-start | bytes 2097152 | tf_op jit(solution)/shard_map/all_to_all | solution.py:35
  22.6 4.4 %gather_fusion = bf16[64,64,512]{2,1,0:T(8,128)(2,1)} fusion(bf16[32,64,512]{2,1,0:T(8,128)(2,1)} %param.10, s32[1024]{0:T(1024)S(1)} %pad_clamp_fusion.1), kind=kCustom, calls=%fused_computation | custom fusion | bytes 8388864 | tf_op jit(solution)/shard_map/jit(_take)/gather | solution.py:27
  26.9 4.5 %broadcast_select_fusion = bf16[32,2,64,512]{3,2,1,0:T(8,128)(2,1)} fusion(bf16[32,2,64,512]{3,2,1,0:T(8,128)(2,1)} %bitcast.50, pred[32,2]{1,0:T(8,128)(4,1)S(1)} %copy.10), kind=kLoop, calls=%fused_computation.4 | loop fusion | flops 2097152 | bytes 8388672 | tf_op jit(solution)/shard_map/jit(_take)/select_n | solution.py:27
  31.5 17.3 %all-to-all-done.1 = bf16[32,2,64,128]{3,2,1,0:T(8,128)(2,1)S(1)} async-done(((bf16[32,2,64,128]{3,2,1,0:T(8,128)(2,1)}), bf16[32,2,64,128]{3,2,1,0:T(8,128)(2,1)S(1)}, u32[]{:S(2)}, u32[]{:S(2)}) %all-to-all-start.1) | async-done | bytes 1048608 | tf_op jit(solution)/shard_map/all_to_all | solution.py:35
  48.8 6.5 %all-to-all-start = ((bf16[32,2,64,512]{3,2,1,0:T(8,128)(2,1)}), bf16[32,2,64,512]{3,2,1,0:T(8,128)(2,1)}, u32[]{:S(2)}, u32[]{:S(2)}) async-start(bf16[32,2,64,512]{3,2,1,0:T(8,128)(2,1)} %broadcast_select_fusion), calls=%async_computation.1 | async-start | bytes 8388608 | tf_op jit(solution)/shard_map/all_to_all | solution.py:34
  55.3 2.1 fusion.29
  57.5 0.7 and_select_fusion.3
  58.2 0.7 fusion.25
  58.9 0.2 convert_reduce_fusion
  59.1 0.7 fusion.24
  59.8 0.7 compare_and_fusion.1
  60.6 1.4 gather_fusion.3
  62.0 85.9 %all-to-all-done = bf16[32,2,64,512]{3,2,1,0:T(8,128)(2,1)} async-done(((bf16[32,2,64,512]{3,2,1,0:T(8,128)(2,1)}), bf16[32,2,64,512]{3,2,1,0:T(8,128)(2,1)}, u32[]{:S(2)}, u32[]{:S(2)}) %all-to-all-start) | async-done | bytes 4194336 | tf_op jit(solution)/shard_map/all_to_all | solution.py:34
  147.9 4.2 %gather_fusion.1 = bf16[31,64,512]{2,1,0:T(8,128)(2,1)} fusion(bf16[64,64,512]{2,1,0:T(8,128)(2,1)} %bitcast.4, s32[1024]{0:T(1024)S(1)} %pad_clamp_fusion), kind=kCustom, calls=%fused_computation.1 | custom fusion | bytes 4063356 | tf_op jit(solution)/shard_map/jit(_take)/gather | solution.py:46
  152.0 2.0 broadcast_select_fusion.1
  154.0 0.2 copy-done.1
  154.2 0.4 pad_maximum_fusion
  154.6 1.3 fusion.30
  155.9 1.3 select_reduce_fusion
  157.2 0.9 broadcast_select_fusion.3
  158.1 107.9 %all-reduce.2.cloned.1.call-done = f32[256,64]{0,1:T(8,128)} async-done(((f32[256,64]{0,1:T(8,128)}), f32[256,64]{0,1:T(8,128)}) %all-reduce.2.cloned.1.call-update) | async-done | bytes 65552 | tf_op jit(solution)/shard_map/psum | solution.py:69
  266.0 5.2 %fusion.11 = bf16[256,128]{1,0:T(8,128)(2,1)} fusion(f32[256,128]{1,0:T(8,128)} %reduce-scatter.2.cloned.1.call-done, f32[256,64]{0,1:T(8,128)} %all-reduce.2.cloned.1.call-done, pred[256,63]{0,1:T(8,128)(4,1)S(1)} %iota_compare_fusion, bf16[31,64,128]{2,1,0:T(8,128)(2,1)} %broadcast_select_fusion.3, bf16[32,64,128]{2,1,0:T(8,128)(2,1)S(1)} %copy-done.2), kind=kOutput, calls=%fused_computation.15 | convolution fusion | flops 1587060736 | bytes 1310464 | tf_op jit(solution)/shard_map/dot_general | solution.py:86
  (24 shorter events, 0.3 us)
Async XLA Ops:
  6.5 48.8 %copy-start = (bf16[512,2048]{1,0:T(8,128)(2,1)S(1)}, bf16[512,2048]{1,0:T(8,128)(2,1)}, u32[]{:S(2)}) copy-start(bf16[512,2048]{1,0:T(8,128)(2,1)} %param.9) | copy-start | bytes 6291460
  12.1 36.7 %all-to-all-start.1 = ((bf16[32,2,64,128]{3,2,1,0:T(8,128)(2,1)}), bf16[32,2,64,128]{3,2,1,0:T(8,128)(2,1)S(1)}, u32[]{:S(2)}, u32[]{:S(2)}) async-start(bf16[32,2,64,128]{3,2,1,0:T(8,128)(2,1)} %broadcast_select_fusion.2), calls=%async_computation.2 | async-start | bytes 2097152 | tf_op jit(solution)/shard_map/all_to_all | solution.py:35
  31.5 23.8 %copy-start.4 = (bf16[256,512]{1,0:T(8,128)(2,1)S(1)}, bf16[256,512]{1,0:T(8,128)(2,1)}, u32[]{:S(2)}) copy-start(bf16[256,512]{1,0:T(8,128)(2,1)} %param.6) | copy-start | bytes 786436
  48.8 99.1 %all-to-all-start = ((bf16[32,2,64,512]{3,2,1,0:T(8,128)(2,1)}), bf16[32,2,64,512]{3,2,1,0:T(8,128)(2,1)}, u32[]{:S(2)}, u32[]{:S(2)}) async-start(bf16[32,2,64,512]{3,2,1,0:T(8,128)(2,1)} %broadcast_select_fusion), calls=%async_computation.1 | async-start | bytes 8388608 | tf_op jit(solution)/shard_map/all_to_all | solution.py:34
  55.3 5.3 %copy-start.5 = (s32[256]{0:T(256)S(1)}, s32[256]{0:T(256)}, u32[]{:S(2)}) copy-start(s32[256]{0:T(256)} %param.7) | copy-start | bytes 3076
  55.3 102.9 %reduce-scatter.2.cloned.1.call-start = ((), (), s32[]{:S(2)}) async-start(), calls=%async_computation.3 | async-start | bytes 2228224 | tf_op jit(solution)/shard_map/reduce_scatter | solution.py:70
  57.5 208.6 %all-reduce.2.cloned.1.call-start = ((), (), s32[]{:S(2)}) async-start(), calls=%async_computation.4 | async-start | bytes 131072 | tf_op jit(solution)/shard_map/psum | solution.py:69
  152.0 2.2 copy-start.1
  155.9 1.3 copy-start.3
  155.9 110.1 %copy-start.2 = (bf16[32,64,128]{2,1,0:T(8,128)(2,1)S(1)}, bf16[32,64,128]{2,1,0:T(8,128)(2,1)}, u32[]{:S(2)}) copy-start(bf16[32,64,128]{2,1,0:T(8,128)(2,1)} %param.11) | copy-start | bytes 1572868
Sparse Core Ops, SparseCore 0:
  58.9 67.7 reduce-scatter.1
  157.3 108.6 all-reduce.1
where the time goes:
time: 279 us; the launch traced here: 278 us
  waiting for transfers between devices  211 us (76%)
  starting transfers between devices  17.1 us (6%)
  other arithmetic  15.2 us (5%)
  between operations  13.6 us (5%)
  local copies, waits for them, and re-layouts  12.6 us (5%)
  matrix products  8.54 us (3%)
    psum x1, waiting for transfers between devices, shards(): shrink = lax.psum(shrink_part, 'tensor')  108 us
    all_to_all x1, waiting for transfers between devices, shards(): lax.all_to_all(down_outgoing, 'replica', split_axis=0, concat_axis=0, til...  85.9 us
    all_to_all x1, waiting for transfers between devices, shards(): lax.all_to_all(up_outgoing, 'replica', split_axis=0, concat_axis=0, tiled...  17.3 us
    all_to_all x1, starting transfers between devices, shards(): lax.all_to_all(up_outgoing, 'replica', split_axis=0, concat_axis=0, tiled...  10.5 us
    all_to_all x1, starting transfers between devices, shards(): lax.all_to_all(down_outgoing, 'replica', split_axis=0, concat_axis=0, til...  6.49 us
  transfers between devices with their start and end apart: 4, of which 3 were waited for; matrix products, arithmetic and copies ran while one was open for 9% of the time, Pallas kernels for 0%

commit v1 on v0

v1 whole, which is shorter than its diff:
```python
import functools

import jax
import jax.numpy as jnp
from jax import lax
from jax.experimental import pallas as pl
from jax.experimental.pallas import tpu as pltpu
from jax.sharding import Mesh, PartitionSpec as P

Y, X, Z, C = 8, 4, 8, 2
T = Z * C
GROUPS = Y * X
LIMIT = 2
VMEM_LIMIT = 48 * 1024 * 1024


def copies(count, source_of, target_of, sems):
    def start(i, carry):
        pltpu.make_async_copy(source_of(i), target_of(i), sems.at[i]).start()
        return carry

    def wait(i, carry):
        pltpu.make_async_copy(source_of(i), target_of(i), sems.at[i]).wait()
        return carry

    lax.fori_loop(0, count, start, 0)
    lax.fori_loop(0, count, wait, 0)


def pick_down_kernel(picked, down, out, sems):
    def source(i):
        x, rest = i // (Y * LIMIT), i % (Y * LIMIT)
        y, j = rest // LIMIT, rest % LIMIT
        return down.at[picked[(y * X + x) * LIMIT + j]]

    copies(GROUPS * LIMIT, source, lambda i: out.at[i], sems)


def pick_up_kernel(picked, up, out, sems):
    copies(GROUPS * LIMIT, lambda i: up.at[picked[i]], lambda i: out.at[i], sems)


def pick(kernel, picked, table):
    count = GROUPS * LIMIT
    out = jax.ShapeDtypeStruct((count,) + table.shape[1:], table.dtype)
    return pl.pallas_call(
        kernel,
        out_shape=out,
        in_specs=[
            pl.BlockSpec(memory_space=pltpu.SMEM),
            pl.BlockSpec(memory_space=pl.ANY),
        ],
        out_specs=pl.BlockSpec(memory_space=pl.ANY),
        scratch_shapes=[pltpu.SemaphoreType.DMA((count,))],
        cost_estimate=pl.CostEstimate(
            flops=0, bytes_accessed=2 * out.size * out.dtype.itemsize, transcendentals=0
        ),
    )(picked, table)


def prepare_kernel(resident, place, plan, slots, rows, rows_out, code_out):
    count = rows.shape[0]
    slot = slots[...]
    code = slot
    before = jnp.int32(-1)
    for k in range(plan.shape[1]):
        home = plan[place[0], k] // resident
        second = (home == before).astype(jnp.int32)
        code = jnp.where(slot == resident + k, resident + home * LIMIT + second, code)
        before = home
    code_out[...] = code
    rows_out[0:count, :] = rows[...]
    wide = jnp.concatenate([code.astype(jnp.float32), jnp.zeros((1, rows.shape[1] - count), jnp.float32)], axis=1)
    rows_out[count:, :] = jnp.broadcast_to(wide, (rows_out.shape[0] - count, rows.shape[1])).astype(rows_out.dtype)


def prepare(resident, group, plan, slots, rows):
    count, width = rows.shape
    smem = pl.BlockSpec(memory_space=pltpu.SMEM)
    vmem = pl.BlockSpec(memory_space=pltpu.VMEM)
    return pl.pallas_call(
        functools.partial(prepare_kernel, resident),
        out_shape=(
            jax.ShapeDtypeStruct((count + 16, width), rows.dtype),
            jax.ShapeDtypeStruct((1, count), jnp.int32),
        ),
        in_specs=[smem, smem, vmem, vmem],
        out_specs=(vmem, vmem),
    )(group, plan, slots, rows)


NT = (((1,), (1,)), ((), ()))


def local_kernel(code, rows, down, out):
    rank = out.shape[0]
    resident = down.shape[0] // rank
    total = jnp.zeros(out.shape, jnp.float32)
    step = 4
    for first in range(0, resident, step):
        product = lax.dot_general(
            down[first * rank : (first + step) * rank, :], rows[...], NT, preferred_element_type=jnp.float32
        )
        for k in range(step):
            total = total + jnp.where(code[...] == first + k, product[k * rank : (k + 1) * rank, :], 0.0)
    out[...] = total


def local_shrink(code, rows, down):
    resident, rank, width = down.shape
    vmem = pl.BlockSpec(memory_space=pltpu.VMEM)
    return pl.pallas_call(
        local_kernel,
        out_shape=jax.ShapeDtypeStruct((rank, rows.shape[0]), jnp.float32),
        in_specs=[vmem] * 3,
        out_specs=vmem,
        compiler_params=pltpu.CompilerParams(vmem_limit_bytes=VMEM_LIMIT),
        cost_estimate=pl.CostEstimate(
            flops=2 * rows.size * resident * rank, bytes_accessed=2 * down.size, transcendentals=0
        ),
    )(code, rows, down.reshape(resident * rank, width))


def imported_kernel(resident, place, rows, down, own, out):
    group = pl.program_id(0)
    rank, count = own.shape
    code = rows[0, count : count + 1, :count].astype(jnp.float32)
    base = (resident + place[0] * X * LIMIT).astype(jnp.float32)
    total = jnp.where(group == place[0], own[...], 0.0)
    for x in range(X):
        product = lax.dot_general(
            down[x, 0], rows[0, 0:count, :], NT, preferred_element_type=jnp.float32
        )
        for j in range(LIMIT):
            hit = code == base + (x * LIMIT + j)
            total = total + jnp.where(hit, product[j * rank : (j + 1) * rank, :], 0.0)
    for i in range(rank // 8):
        for k in range(count // 128):
            out[0, i * (count // 128) + k] = total[i * 8 : (i + 1) * 8, k * 128 : (k + 1) * 128]


def imported_shrink(resident, y, rows, down, own):
    rank, count = own.shape
    width = rows.shape[-1]
    height = rows.shape[1]
    blocks = rank * count // 1024
    return pl.pallas_call(
        functools.partial(imported_kernel, resident),
        grid=(Y,),
        out_shape=jax.ShapeDtypeStruct((Y, blocks, 8, 128), jnp.float32),
        in_specs=[
            pl.BlockSpec(memory_space=pltpu.SMEM),
            pl.BlockSpec((1, height, width), lambda i: (i, 0, 0)),
            pl.BlockSpec((X, 1, LIMIT * rank, width), lambda i: (0, i, 0, 0)),
            pl.BlockSpec((rank, count), lambda i: (0, 0)),
        ],
        out_specs=pl.BlockSpec((1, blocks, 8, 128), lambda i: (i, 0, 0, 0)),
        compiler_params=pltpu.CompilerParams(vmem_limit_bytes=VMEM_LIMIT),
        cost_estimate=pl.CostEstimate(
            flops=2 * down.size * count, bytes_accessed=2 * (down.size + rows.size), transcendentals=0
        ),
    )(y, rows, down, own)


def add_kernel(parts, out):
    total = jnp.sum(parts[...], axis=0)
    for t in range(out.shape[0]):
        out[t] = total


def add_and_spread(parts):
    vmem = pl.BlockSpec(memory_space=pltpu.VMEM)
    return pl.pallas_call(
        add_kernel,
        out_shape=jax.ShapeDtypeStruct((T,) + parts.shape[1:], jnp.float32),
        in_specs=[vmem],
        out_specs=vmem,
    )(parts)


def expand_kernel(shrink, code, up, up_in, base, out):
    count = out.shape[0]
    lanes = count // 128
    rank = shrink.shape[0] // lanes * 8
    resident, imported = up.shape[0], up_in.shape[0]
    rows = jnp.concatenate(
        [jnp.concatenate([shrink[i * lanes + k] for k in range(lanes)], axis=1) for i in range(rank // 8)], axis=0
    )
    rows = jnp.transpose(rows)
    column = jnp.transpose(jnp.broadcast_to(code[...], (8, count)).astype(jnp.float32))[:, :1]
    pair = jnp.concatenate([rows, rows], axis=1)
    high = pair.astype(jnp.bfloat16).astype(jnp.float32)
    low = pair - high
    half = lax.broadcasted_iota(jnp.int32, pair.shape, 1) // rank
    wanted = jnp.broadcast_to(column, pair.shape) - half.astype(jnp.float32)
    both = jnp.concatenate([high, low], axis=0)
    wanted = jnp.concatenate([wanted, wanted], axis=0)
    total = jnp.zeros((2 * count, out.shape[1]), jnp.float32)
    step = 4
    for table, start in ((up, 0), (up_in, resident)):
        pairs = table.shape[0] // 2
        for first in range(0, pairs, step):
            placed = jnp.concatenate(
                [
                    jnp.where(wanted == float(start + 2 * p), both, 0.0).astype(jnp.bfloat16)
                    for p in range(first, first + step)
                ],
                axis=1,
            )
            maps = table[2 * first : 2 * (first + step)].reshape(2 * step * rank, out.shape[1])
            total = total + jnp.dot(placed, maps, preferred_element_type=jnp.float32)
    out[...] = (base[...] + (total[:count] + total[count:])).astype(out.dtype)


def expand(shrink, code, up, up_in, base):
    vmem = pl.BlockSpec(memory_space=pltpu.VMEM)
    return pl.pallas_call(
        expand_kernel,
        out_shape=jax.ShapeDtypeStruct(base.shape, jnp.bfloat16),
        in_specs=[vmem] * 5,
        out_specs=vmem,
        compiler_params=pltpu.CompilerParams(vmem_limit_bytes=VMEM_LIMIT),
    )(shrink, code, up, up_in, base)


def shards(inputs, row_adapter_slot, transfer_plan, key_value_weight, adapter_down, adapter_up):
    count, width = inputs.shape
    resident, rank, _ = adapter_down.shape
    y, x = lax.axis_index("y"), lax.axis_index("x")
    group = y * X + x

    mine = transfer_plan // resident == group
    after = jnp.pad(mine[:, :-1], ((0, 0), (1, 0)))
    number = transfer_plan % resident
    picked = jnp.stack(
        [
            jnp.sum(jnp.where(mine & ~after, number, 0), axis=1),
            jnp.sum(jnp.where(mine & after, number, 0), axis=1),
        ],
        axis=1,
    ).reshape(-1)

    down_out = pick(pick_down_kernel, picked, adapter_down).reshape(X, Y * LIMIT, rank, width)
    down_in = lax.all_to_all(down_out, "x", 0, 0, tiled=True)

    sent_rows, code = prepare(
        resident, group.reshape(1), transfer_plan, row_adapter_slot.reshape(1, count), inputs
    )
    rows = lax.all_gather(sent_rows, "y")

    base_part = jnp.dot(inputs, key_value_weight, preferred_element_type=jnp.float32)
    base = lax.psum_scatter(base_part, ("z", "c"), scatter_dimension=1, tiled=True)

    own = local_shrink(code, inputs, adapter_down)
    parts = imported_shrink(
        resident, y.reshape(1), rows, down_in.reshape(X, Y, LIMIT * rank, width), own
    )
    parts = lax.all_to_all(parts.reshape(Y * T, 8, 128), ("y", "z", "c"), 0, 0, tiled=True)
    shrink = lax.all_to_all(add_and_spread(parts), ("z", "c"), 0, 0, tiled=True)

    up_out = pick(pick_up_kernel, picked, adapter_up)
    up_in = lax.all_to_all(up_out, ("y", "x"), 0, 0, tiled=True)
    return expand(shrink, code, adapter_up, up_in, base)


def solution(mesh):
    grid = Mesh(mesh.devices.reshape(Y, X, Z, C), ("y", "x", "z", "c"))
    replica, tensor = ("y", "x"), ("z", "c")
    placed = (
        P(replica, tensor),
        P(replica),
        P(),
        P(tensor, None),
        P(replica, None, tensor),
        P(replica, None, tensor),
    )
    return jax.shard_map(
        shards, mesh=grid, in_specs=placed, out_specs=P(replica, tensor), check_vma=False
    )
```

time: 279 us -> 322 us (1.15)
  Pallas kernels: 0 us -> 178 us
  waiting for transfers between devices: 211 us -> 70.4 us
  starting transfers between devices: 17.1 us -> 46.6 us
  other arithmetic: 15.2 us -> 1.65 us
  matrix products: 8.54 us -> 2.09 us
  local copies, waits for them, and re-layouts: 12.6 us -> 7.43 us
    pallas_call x0 -> x7, Pallas kernels: none -> 178 us  [the longest x2 164 us: pick(): pl.pallas_call(kernel, out_shape=out, in_specs=[pl.BlockSpec(memory_space...]
    psum x1 -> x0, waiting for transfers between devices: 108 us -> none  [shards(): shrink = lax.psum(shrink_part, 'tensor')]
    all_to_all x2 -> x4, waiting for transfers between devices: 103 us -> 70.3 us  [the longest x1 38 us: shards(): down_in = lax.all_to_all(down_out, 'x', 0, 0, tiled=True)]
    all_to_all x2 -> x4, starting transfers between devices: 17 us -> 46.6 us  [the longest x1 24.3 us: shards(): lax.all_to_all(parts.reshape(Y * T, 8, 128), ('y', 'z', 'c'), 0, 0, tiled...]
    gather x4 -> x0, local copies, waits for them, and re-layouts: 11.8 us -> none  [the longest x1 4.38 us: shards(): jnp.take(adapter_down, outgoing_selection, axis=0)]
    select_n x8 -> x0, other arithmetic: 10.9 us -> none  [the longest x2 4.55 us: shards(): jnp.take(adapter_down, outgoing_selection, axis=0)]
    dot_general x2 -> x0, matrix products: 6.43 us -> none  [the longest x1 5.16 us: shards(): jnp.dot(placed, up_wide, preferred_element_type=jnp.float32, precision=la...]
    unnamed x12 -> x16, local copies, waits for them, and re-layouts: 0.26 us -> 6.66 us
  transfers between devices with their start and end apart: 4 -> 6, of which waited for: 3 -> 3; matrix products, arithmetic and copies ran while one was open for 9% -> 1% of each run, Pallas kernels for 0% -> 54%
where the time goes in v1:
time: 322 us; the launch traced here: 321 us
  Pallas kernels  178 us (55%)
  waiting for transfers between devices  70.4 us (22%)
  starting transfers between devices  46.6 us (14%)
  between operations  14.9 us (5%)
  local copies, waits for them, and re-layouts  7.43 us (2%)
    pallas_call x2, Pallas kernels, pick(): pl.pallas_call(kernel, out_shape=out, in_specs=[pl.BlockSpec(memory_space...  164 us
    all_to_all x1, waiting for transfers between devices, shards(): down_in = lax.all_to_all(down_out, 'x', 0, 0, tiled=True)  38 us
    all_to_all x1, waiting for transfers between devices, shards(): up_in = lax.all_to_all(up_out, ('y', 'x'), 0, 0, tiled=True)  24.5 us
    all_to_all x1, starting transfers between devices, shards(): lax.all_to_all(parts.reshape(Y * T, 8, 128), ('y', 'z', 'c'), 0, 0, tiled...  24.3 us
    all_to_all x1, starting transfers between devices, shards(): shrink = lax.all_to_all(add_and_spread(parts), ('z', 'c'), 0, 0, tiled=True)  9.36 us
    all_to_all x1, starting transfers between devices, shards(): up_in = lax.all_to_all(up_out, ('y', 'x'), 0, 0, tiled=True)  7.86 us
    all_to_all x1, waiting for transfers between devices, shards(): shrink = lax.all_to_all(add_and_spread(parts), ('z', 'c'), 0, 0, tiled=True)  7.78 us
    pallas_call x1, Pallas kernels, imported_shrink(): pl.pallas_call(functools.partial(imported_kernel, resident), grid=(Y,), o...  7.5 us
  transfers between devices with their start and end apart: 6, of which 3 were waited for; matrix products, arithmetic and copies ran while one was open for 1% of the time, Pallas kernels for 54%

profile of v1, /device:TPU:1, one launch (start us, length us, event | category | flops | bytes accessed | tf_op | source)
XLA Modules:
  0.0 321.4 jit_solution(17376658104762812396)
XLA Ops:
  7.4 0.0 copy-start
  7.4 2.1 shard_map.64
  9.4 0.0 all-gather.3.cloned.1.call-update
  9.5 0.7 fusion
  10.2 0.9 select_reduce_fusion.1
  11.1 0.1 copy.8
  11.2 0.7 reshape.27.picked
  11.9 129.4 %shard_map.65 = bf16[64,64,512]{2,1,0:T(8,128)(2,1)} custom-call(s32[64]{0:T(128)} %reshape.27.picked, bf16[32,64,512]{2,1,0:T(8,128)(2,1)} %down.1), custom_call_target="tpu_custom_call" | custom-call | bytes 8388608 | tf_op jit(solution)/shard_map/pallas_call | solution.py:46
  141.3 0.0 copy-start.2
  141.3 5.0 %all-to-all-start = ((bf16[4,16,64,512]{3,2,1,0:T(8,128)(2,1)}), bf16[4,16,64,512]{3,2,1,0:T(8,128)(2,1)}, u32[]{:S(2)}, u32[]{:S(2)}) async-start(bf16[4,16,64,512]{3,2,1,0:T(8,128)(2,1)} %bitcast.15), calls=%async_computation | async-start | bytes 8388608 | tf_op jit(solution)/shard_map/all_to_all | solution.py:244
  146.3 0.0 reduce-scatter.2.cloned.1.call-start
  146.4 2.1 fusion.3
  148.5 0.0 reduce-scatter.2.cloned.1.call-update
  148.5 0.7 copy-done.6
  149.2 1.6 copy-done.1
  150.8 0.8 shard_map.66.own
  151.5 38.0 %all-to-all-done = bf16[4,16,64,512]{3,2,1,0:T(8,128)(2,1)} async-done(((bf16[4,16,64,512]{3,2,1,0:T(8,128)(2,1)}), bf16[4,16,64,512]{3,2,1,0:T(8,128)(2,1)}, u32[]{:S(2)}, u32[]{:S(2)}) %all-to-all-start) | async-done | bytes 4194336 | tf_op jit(solution)/shard_map/all_to_all | solution.py:244
  189.5 1.6 copy-done.3
  191.2 7.5 %shard_map.67 = f32[8,16,8,128]{3,2,1,0:T(8,128)} custom-call(s32[1]{0:T(128)} %bitcast.place, bf16[8,272,512]{2,1,0:T(8,128)(2,1)S(1)} %bitcast.14, bf16[4,8,128,512]{3,2,1,0:T(8,128)(2,1)} %bitcast.7.down, f32[64,256]{1,0:T(8,128)S(1)} %shard_map.66.own), custom_call_target="tpu_custom_call" | custom-call | flops 1073741824 | bytes 6422528 | tf_op jit(solution)/shard_map/pallas_call | solution.py:147
  198.7 24.3 %all-to-all-start.1 = ((f32[128,8,128]{2,1,0:T(8,128)}), f32[128,8,128]{2,1,0:T(8,128)S(1)}, u32[]{:S(2)}, u32[]{:S(2)}) async-start(f32[128,8,128]{2,1,0:T(8,128)} %bitcast.9), calls=%async_computation.1 | async-start | bytes 1048576 | tf_op jit(solution)/shard_map/all_to_all | solution.py:258
  223.0 34.1 %shard_map.69 = bf16[64,64,128]{2,1,0:T(8,128)(2,1)} custom-call(s32[64]{0:T(128)} %reshape.27.picked, bf16[32,64,128]{2,1,0:T(8,128)(2,1)} %up.3), custom_call_target="tpu_custom_call" | custom-call | bytes 2097152 | tf_op jit(solution)/shard_map/pallas_call | solution.py:46
  257.2 0.0 all-to-all-done.1.parts
  257.2 0.8 copy-done.7
  258.0 7.9 %all-to-all-start.3 = ((bf16[64,64,128]{2,1,0:T(8,128)(2,1)}), bf16[64,64,128]{2,1,0:T(8,128)(2,1)S(1)}, u32[]{:S(2)}, u32[]{:S(2)}) async-start(bf16[64,64,128]{2,1,0:T(8,128)(2,1)} %shard_map.69), calls=%async_computation.3 | async-start | bytes 2097152 | tf_op jit(solution)/shard_map/all_to_all | solution.py:262
  265.9 1.8 shard_map.68
  267.7 24.5 %all-to-all-done.3.up_in = bf16[64,64,128]{2,1,0:T(8,128)(2,1)S(1)} async-done(((bf16[64,64,128]{2,1,0:T(8,128)(2,1)}), bf16[64,64,128]{2,1,0:T(8,128)(2,1)S(1)}, u32[]{:S(2)}, u32[]{:S(2)}) %all-to-all-start.3) | async-done | bytes 1048608 | tf_op jit(solution)/shard_map/all_to_all | solution.py:262
  292.2 9.4 %all-to-all-start.2 = ((f32[16,8,128]{2,1,0:T(8,128)}), f32[16,8,128]{2,1,0:T(8,128)S(1)}, u32[]{:S(2)}, u32[]{:S(2)}) async-start(f32[16,8,128]{2,1,0:T(8,128)} %shard_map.68), calls=%async_computation.2 | async-start | bytes 131072 | tf_op jit(solution)/shard_map/all_to_all | solution.py:259
  301.6 0.0 reduce-scatter.2.cloned.1.call-done.base
  301.6 7.8 %all-to-all-done.2.shrink = f32[16,8,128]{2,1,0:T(8,128)S(1)} async-done(((f32[16,8,128]{2,1,0:T(8,128)}), f32[16,8,128]{2,1,0:T(8,128)S(1)}, u32[]{:S(2)}, u32[]{:S(2)}) %all-to-all-start.2) | async-done | bytes 65568 | tf_op jit(solution)/shard_map/all_to_all | solution.py:259
  309.4 1.0 copy-done.4
  310.4 0.9 copy-done.5
  311.3 2.6 shard_map.70
  (11 shorter events, 0.0 us)
Async XLA Ops:
  7.4 139.0 %copy-start = (bf16[512,2048]{1,0:T(8,128)(2,1)S(1)}, bf16[512,2048]{1,0:T(8,128)(2,1)}, u32[]{:S(2)}) copy-start(bf16[512,2048]{1,0:T(8,128)(2,1)} %param.9) | copy-start | bytes 6291460
  7.4 182.2 %all-gather.3.cloned.1.call-start = ((), (), s32[]{:S(2)}) async-start(), calls=%async_computation.6 | async-start | bytes 2506752 | tf_op jit(solution)/shard_map/all_gather | solution.py:249
  141.3 5.1 %copy-start.2 = (bf16[256,512]{1,0:T(8,128)(2,1)S(1)}, bf16[256,512]{1,0:T(8,128)(2,1)}, u32[]{:S(2)}) copy-start(bf16[256,512]{1,0:T(8,128)(2,1)} %rows.3) | copy-start | bytes 786436
  141.3 48.2 %all-to-all-start = ((bf16[4,16,64,512]{3,2,1,0:T(8,128)(2,1)}), bf16[4,16,64,512]{3,2,1,0:T(8,128)(2,1)}, u32[]{:S(2)}, u32[]{:S(2)}) async-start(bf16[4,16,64,512]{3,2,1,0:T(8,128)(2,1)} %bitcast.15), calls=%async_computation | async-start | bytes 8388608 | tf_op jit(solution)/shard_map/all_to_all | solution.py:244
  146.3 155.3 %reduce-scatter.2.cloned.1.call-start = ((), (), s32[]{:S(2)}) async-start(), calls=%async_computation.5 | async-start | bytes 2228224 | tf_op jit(solution)/shard_map/reduce_scatter | solution.py:252
  148.5 0.7 copy-start.6
  149.2 1.6 copy-start.1
  189.5 1.6 copy-start.3
  198.7 58.5 %all-to-all-start.1 = ((f32[128,8,128]{2,1,0:T(8,128)}), f32[128,8,128]{2,1,0:T(8,128)S(1)}, u32[]{:S(2)}, u32[]{:S(2)}) async-start(f32[128,8,128]{2,1,0:T(8,128)} %bitcast.9), calls=%async_computation.1 | async-start | bytes 1048576 | tf_op jit(solution)/shard_map/all_to_all | solution.py:258
  257.2 0.8 copy-start.7
  258.0 34.2 %all-to-all-start.3 = ((bf16[64,64,128]{2,1,0:T(8,128)(2,1)}), bf16[64,64,128]{2,1,0:T(8,128)(2,1)S(1)}, u32[]{:S(2)}, u32[]{:S(2)}) async-start(bf16[64,64,128]{2,1,0:T(8,128)(2,1)} %shard_map.69), calls=%async_computation.3 | async-start | bytes 2097152 | tf_op jit(solution)/shard_map/all_to_all | solution.py:262
  292.2 17.2 %all-to-all-start.2 = ((f32[16,8,128]{2,1,0:T(8,128)}), f32[16,8,128]{2,1,0:T(8,128)S(1)}, u32[]{:S(2)}, u32[]{:S(2)}) async-start(f32[16,8,128]{2,1,0:T(8,128)} %shard_map.68), calls=%async_computation.2 | async-start | bytes 131072 | tf_op jit(solution)/shard_map/all_to_all | solution.py:259
  309.4 1.0 copy-start.4
  310.4 0.9 copy-start.5
Sparse Core Ops, SparseCore 0:
  10.3 139.1 all-gather.2
Sparse Core Ops, SparseCore 1:
  149.6 67.1 reduce-scatter.1

commit v2 on v1

v2 whole, which is shorter than its diff:
```python
import functools

import jax
import jax.numpy as jnp
from jax import lax
from jax.experimental import pallas as pl
from jax.experimental.pallas import tpu as pltpu
from jax.sharding import Mesh, PartitionSpec as P

Y, X, Z, C = 8, 4, 8, 2
T = Z * C
GROUPS = Y * X
LIMIT = 2
VMEM_LIMIT = 48 * 1024 * 1024


def dispatch_kernel(place, plan, plan_row, slots, rows, down, down_out, rows_out, code_out, picked_out,
                    staged, picked, read_sems, write_sems, picked_sem):
    resident = down.shape[0]
    group = place[0] * X + place[1]
    table = plan[...]
    home = table // resident
    number = table - home * resident
    mine = (home == group).astype(jnp.int32)
    after = jnp.concatenate([jnp.zeros((mine.shape[0], 1), jnp.int32), mine[:, :-1]], axis=1)
    first = jnp.sum(mine * (1 - after) * number, axis=1, keepdims=True)
    second = jnp.sum(mine * after * number, axis=1, keepdims=True)
    lane = lax.broadcasted_iota(jnp.int32, picked_out.shape, 1)
    picked_out[...] = jnp.where(lane == 0, first, jnp.where(lane == 1, second, 0))
    to_scalars = pltpu.make_async_copy(picked_out, picked, picked_sem)
    to_scalars.start()
    to_scalars.wait()

    def read(i):
        x, rest = i // (Y * LIMIT), i % (Y * LIMIT)
        wanted = picked[rest // LIMIT * X + x, rest % LIMIT]
        return pltpu.make_async_copy(down.at[wanted], staged.at[i], read_sems.at[i])

    def write(i):
        return pltpu.make_async_copy(staged.at[i], down_out.at[i], write_sems.at[i])

    def begin(i, carry):
        read(i).start()
        return carry

    def forward(i, carry):
        read(i).wait()
        write(i).start()
        return carry

    def finish(i, carry):
        write(i).wait()
        return carry

    count = GROUPS * LIMIT
    lax.fori_loop(0, count, begin, 0)

    height = rows.shape[0]
    slot = slots[...]
    code = slot
    before = jnp.int32(-1)
    for k in range(plan_row.shape[1]):
        its_home = plan_row[group, k] // resident
        again = (its_home == before).astype(jnp.int32)
        code = jnp.where(slot == resident + k, resident + its_home * LIMIT + again, code)
        before = its_home
    code_out[...] = code
    rows_out[0:height, :] = rows[...]
    wide = jnp.concatenate(
        [code.astype(jnp.float32), jnp.zeros((1, rows.shape[1] - height), jnp.float32)], axis=1
    )
    tail = (rows_out.shape[0] - height, rows.shape[1])
    rows_out[height:, :] = jnp.broadcast_to(wide, tail).astype(rows_out.dtype)

    lax.fori_loop(0, count, forward, 0)
    lax.fori_loop(0, count, finish, 0)


def dispatch(place, plan, slots, rows, down):
    height, width = rows.shape
    count = GROUPS * LIMIT
    smem = pl.BlockSpec(memory_space=pltpu.SMEM)
    vmem = pl.BlockSpec(memory_space=pltpu.VMEM)
    hbm = pl.BlockSpec(memory_space=pl.ANY)
    return pl.pallas_call(
        dispatch_kernel,
        out_shape=(
            jax.ShapeDtypeStruct((count,) + down.shape[1:], down.dtype),
            jax.ShapeDtypeStruct((height + 16, width), rows.dtype),
            jax.ShapeDtypeStruct((1, height), jnp.int32),
            jax.ShapeDtypeStruct((GROUPS, 128), jnp.int32),
        ),
        in_specs=[smem, vmem, smem, vmem, vmem, hbm],
        out_specs=(hbm, vmem, vmem, vmem),
        scratch_shapes=[
            pltpu.VMEM((count,) + down.shape[1:], down.dtype),
            pltpu.SMEM((GROUPS, 128), jnp.int32),
            pltpu.SemaphoreType.DMA((count,)),
            pltpu.SemaphoreType.DMA((count,)),
            pltpu.SemaphoreType.DMA,
        ],
        compiler_params=pltpu.CompilerParams(vmem_limit_bytes=VMEM_LIMIT),
        cost_estimate=pl.CostEstimate(flops=0, bytes_accessed=4 * count * down[0].size, transcendentals=0),
    )(place, plan, plan, slots, rows, down)


def pick_up_kernel(place, picked, up, *outs):
    for d in range(Y):
        y = (place[0] + d) % Y
        for x in range(X):
            for j in range(LIMIT):
                outs[d][x * LIMIT + j] = up[picked[y * X + x, j]]


def pick_up(place, picked, up):
    smem = pl.BlockSpec(memory_space=pltpu.SMEM)
    vmem = pl.BlockSpec(memory_space=pltpu.VMEM)
    shape = jax.ShapeDtypeStruct((X * LIMIT,) + up.shape[1:], up.dtype)
    return pl.pallas_call(
        pick_up_kernel,
        out_shape=(shape,) * Y,
        in_specs=[smem, smem, vmem],
        out_specs=(vmem,) * Y,
        cost_estimate=pl.CostEstimate(flops=0, bytes_accessed=6 * up.size, transcendentals=0),
    )(place, picked, up)


def turn_kernel(place, *refs):
    arrived, outs = refs[:Y], refs[Y:]
    for e in range(X):
        x = (place[1] + e) % X
        for d in range(Y):
            outs[e][d * LIMIT : (d + 1) * LIMIT] = arrived[d][pl.ds(x * LIMIT, LIMIT)]


def turn(place, arrived):
    vmem = pl.BlockSpec(memory_space=pltpu.VMEM)
    shape = jax.ShapeDtypeStruct((Y * LIMIT,) + arrived[0].shape[1:], arrived[0].dtype)
    return pl.pallas_call(
        turn_kernel,
        out_shape=(shape,) * X,
        in_specs=[pl.BlockSpec(memory_space=pltpu.SMEM)] + [vmem] * Y,
        out_specs=(vmem,) * X,
        cost_estimate=pl.CostEstimate(
            flops=0, bytes_accessed=4 * Y * arrived[0].size, transcendentals=0
        ),
    )(place, *arrived)


NT = (((1,), (1,)), ((), ()))


def local_kernel(code, rows, down, out):
    rank = out.shape[0]
    resident = down.shape[0] // rank
    total = jnp.zeros(out.shape, jnp.float32)
    step = 4
    for first in range(0, resident, step):
        product = lax.dot_general(
            down[first * rank : (first + step) * rank, :], rows[...], NT, preferred_element_type=jnp.float32
        )
        for k in range(step):
            total = total + jnp.where(code[...] == first + k, product[k * rank : (k + 1) * rank, :], 0.0)
    out[...] = total


def local_shrink(code, rows, down):
    resident, rank, width = down.shape
    vmem = pl.BlockSpec(memory_space=pltpu.VMEM)
    return pl.pallas_call(
        local_kernel,
        out_shape=jax.ShapeDtypeStruct((rank, rows.shape[0]), jnp.float32),
        in_specs=[vmem] * 3,
        out_specs=vmem,
        cost_estimate=pl.CostEstimate(
            flops=2 * rows.size * resident * rank, bytes_accessed=2 * down.size, transcendentals=0
        ),
    )(code, rows, down.reshape(resident * rank, width))


def imported_kernel(resident, place, rows, down, own, keep, give):
    group = pl.program_id(0)
    rank, count = own.shape
    half = count // C
    code = rows[0, count : count + 1, :count].astype(jnp.float32)
    base = (resident + place[0] * X * LIMIT).astype(jnp.float32)
    total = jnp.where(group == place[0], own[...], 0.0)
    product = lax.dot_general(
        down[...].reshape(X * LIMIT * rank, down.shape[-1]),
        rows[0, 0:count, :],
        NT,
        preferred_element_type=jnp.float32,
    )
    for k in range(X * LIMIT):
        total = total + jnp.where(code == base + k, product[k * rank : (k + 1) * rank, :], 0.0)
    mine = place[2] == 0
    left, right = total[:, :half], total[:, half:]
    keep[...] = jnp.where(mine, left, right).reshape(keep.shape)
    give[...] = jnp.where(mine, right, left).reshape(give.shape)


def imported_shrink(resident, place, rows, down, own):
    rank, count = own.shape
    width = rows.shape[-1]
    height = rows.shape[1]
    shape = jax.ShapeDtypeStruct((Y, rank // 8, 8, count // C), jnp.float32)
    block = pl.BlockSpec((1, rank // 8, 8, count // C), lambda i: (i, 0, 0, 0))
    return pl.pallas_call(
        functools.partial(imported_kernel, resident),
        grid=(Y,),
        out_shape=(shape, shape),
        in_specs=[
            pl.BlockSpec(memory_space=pltpu.SMEM),
            pl.BlockSpec((1, height, width), lambda i: (i, 0, 0)),
            pl.BlockSpec((X, 1, LIMIT * rank, width), lambda i: (0, i, 0, 0)),
            pl.BlockSpec((rank, count), lambda i: (0, 0)),
        ],
        out_specs=(block, block),
        cost_estimate=pl.CostEstimate(
            flops=2 * down.size * count, bytes_accessed=2 * (down.size + rows.size), transcendentals=0
        ),
    )(place, rows, down, own)


def add_kernel(parts, out):
    total = jnp.sum(parts[...], axis=0)
    for t in range(out.shape[0]):
        out[t] = total


def add_and_spread(parts):
    vmem = pl.BlockSpec(memory_space=pltpu.VMEM)
    return pl.pallas_call(
        add_kernel,
        out_shape=jax.ShapeDtypeStruct((T,) + parts.shape[1:], jnp.float32),
        in_specs=[vmem],
        out_specs=vmem,
    )(parts)


def expand_kernel(place, shrink, code, base, up, *refs):
    tables, out = refs[:-1], refs[-1]
    count = out.shape[0]
    lanes = count // 128
    rank = shrink.shape[0] // lanes * 8
    resident = up.shape[0]
    imported = code[...] - resident
    home = imported // LIMIT
    e = (place[1] - home % X + X) % X
    d = (place[0] - home // X + Y) % Y
    at = jnp.where(imported < 0, code[...], resident + (e * Y + d) * LIMIT + imported % LIMIT)
    rows = jnp.concatenate(
        [jnp.concatenate([shrink[i * lanes + k] for k in range(lanes)], axis=1) for i in range(rank // 8)], axis=0
    )
    rows = jnp.transpose(rows)
    column = jnp.transpose(jnp.broadcast_to(at, (8, count)).astype(jnp.float32))[:, :1]
    pair = jnp.concatenate([rows, rows], axis=1)
    high = pair.astype(jnp.bfloat16).astype(jnp.float32)
    low = pair - high
    half = lax.broadcasted_iota(jnp.int32, pair.shape, 1) // rank
    wanted = jnp.broadcast_to(column, pair.shape) - half.astype(jnp.float32)
    both = jnp.concatenate([high, low], axis=0)
    wanted = jnp.concatenate([wanted, wanted], axis=0)
    total = jnp.zeros((2 * count, out.shape[1]), jnp.float32)
    step = 4
    start = 0
    for table in (up,) + tables:
        for first in range(0, table.shape[0] // 2, step):
            placed = jnp.concatenate(
                [
                    jnp.where(wanted == float(start + 2 * p), both, 0.0).astype(jnp.bfloat16)
                    for p in range(first, first + step)
                ],
                axis=1,
            )
            maps = table[2 * first : 2 * (first + step)].reshape(2 * step * rank, out.shape[1])
            total = total + jnp.dot(placed, maps, preferred_element_type=jnp.float32)
        start += table.shape[0]
    out[...] = (base[...] + (total[:count] + total[count:])).astype(out.dtype)


def expand(place, shrink, code, base, up, tables):
    vmem = pl.BlockSpec(memory_space=pltpu.VMEM)
    return pl.pallas_call(
        expand_kernel,
        out_shape=jax.ShapeDtypeStruct(base.shape, jnp.bfloat16),
        in_specs=[pl.BlockSpec(memory_space=pltpu.SMEM)] + [vmem] * (4 + len(tables)),
        out_specs=vmem,
    )(place, shrink, code, base, up, *tables)


def shift(array, axis, size, by):
    return lax.ppermute(array, axis, [(i, (i + by) % size) for i in range(size)])


def shards(inputs, row_adapter_slot, transfer_plan, key_value_weight, adapter_down, adapter_up):
    count, width = inputs.shape
    resident, rank, _ = adapter_down.shape
    place = jnp.stack([lax.axis_index("y"), lax.axis_index("x"), lax.axis_index("c")])

    down_out, sent_rows, code, picked = dispatch(
        place, transfer_plan, row_adapter_slot.reshape(1, count), inputs, adapter_down
    )
    down_in = lax.all_to_all(down_out.reshape(X, Y * LIMIT, rank, width), "x", 0, 0, tiled=True)
    rows = lax.all_gather(sent_rows, "y")

    base_part = jnp.dot(inputs, key_value_weight, preferred_element_type=jnp.float32)
    base = lax.psum_scatter(base_part, ("z", "c"), scatter_dimension=1, tiled=True)
    own = local_shrink(code, inputs, adapter_down)

    ups = pick_up(place, picked, adapter_up)
    arrived = [ups[0]] + [shift(ups[d], "y", Y, d) for d in range(1, Y)]
    ups = turn(place, arrived)
    tables = [ups[0]] + [shift(ups[e], "x", X, e) for e in range(1, X)]

    keep, give = imported_shrink(
        resident, place, rows, down_in.reshape(X, Y, LIMIT * rank, width), own
    )
    parts = keep + shift(give, "c", C, 1)
    parts = lax.all_to_all(parts.reshape(Y * Z, 8, 128), ("y", "z"), 0, 0, tiled=True)
    shrink = lax.all_to_all(add_and_spread(parts), ("z", "c"), 0, 0, tiled=True)
    return expand(place, shrink, code, base, adapter_up, tables)


def solution(mesh):
    grid = Mesh(mesh.devices.reshape(Y, X, Z, C), ("y", "x", "z", "c"))
    replica, tensor = ("y", "x"), ("z", "c")
    placed = (
        P(replica, tensor),
        P(replica),
        P(),
        P(tensor, None),
        P(replica, None, tensor),
        P(replica, None, tensor),
    )
    return jax.shard_map(
        shards, mesh=grid, in_specs=placed, out_specs=P(replica, tensor), check_vma=False
    )
```

time: 322 us -> 198 us (0.61)
  Pallas kernels: 178 us -> 33.4 us
  starting transfers between devices: 46.6 us -> 74.4 us
  waiting for transfers between devices: 70.4 us -> 61.9 us
    pallas_call x3, Pallas kernels: 166 us -> 17.2 us  [the longest x1 12.7 us: dispatch(): pl.pallas_call(dispatch_kernel, out_shape=(jax.ShapeDtypeStruct((count,)...]
    ppermute x0 -> x11, starting transfers between devices: none -> 44.8 us  [shift(): lax.ppermute(array, axis, [(i, (i + by) % size) for i in range(size)])]
    all_to_all x3 -> x2, waiting for transfers between devices: 62.5 us -> 40.1 us  [the longest x1 40.1 us: shards(): lax.all_to_all(down_out.reshape(X, Y * LIMIT, rank, width), 'x', 0, 0, ti...]
    all_to_all x3 -> x2, starting transfers between devices: 37.2 us -> 21.4 us  [the longest x1 16.5 us: shards(): lax.all_to_all(parts.reshape(Y * Z, 8, 128), ('y', 'z'), 0, 0, tiled=True)]
    ppermute x0 -> x11, waiting for transfers between devices: none -> 14 us  [shift(): lax.ppermute(array, axis, [(i, (i + by) % size) for i in range(size)])]
    unnamed x16 -> x42, local copies, waits for them, and re-layouts: 6.66 us -> 7.15 us
  transfers between devices with their start and end apart: 6 -> 16, of which waited for: 3 -> 7; matrix products, arithmetic and copies ran while one was open for 1% -> 2% of each run, Pallas kernels for 54% -> 8%
where the time goes in v2:
time: 198 us; the launch traced here: 196 us
  starting transfers between devices  74.4 us (38%)
  waiting for transfers between devices  61.9 us (31%)
  Pallas kernels  33.4 us (17%)
  between operations  15.1 us (8%)
  local copies, waits for them, and re-layouts  7.15 us (4%)
  matrix products  2.16 us (1%)
    ppermute x11, starting transfers between devices, shift(): lax.ppermute(array, axis, [(i, (i + by) % size) for i in range(size)])  44.8 us
    all_to_all x1, waiting for transfers between devices, shards(): lax.all_to_all(down_out.reshape(X, Y * LIMIT, rank, width), 'x', 0, 0, ti...  40.1 us
    all_to_all x1, starting transfers between devices, shards(): lax.all_to_all(parts.reshape(Y * Z, 8, 128), ('y', 'z'), 0, 0, tiled=True)  16.5 us
    ppermute x11, waiting for transfers between devices, shift(): lax.ppermute(array, axis, [(i, (i + by) % size) for i in range(size)])  14 us
    pallas_call x1, Pallas kernels, dispatch(): pl.pallas_call(dispatch_kernel, out_shape=(jax.ShapeDtypeStruct((count,)...  12.7 us
    all_to_all x1, starting transfers between devices, shards(): shrink = lax.all_to_all(add_and_spread(parts), ('z', 'c'), 0, 0, tiled=True)  8.17 us
    all_to_all x1, waiting for transfers between devices, shards(): shrink = lax.all_to_all(add_and_spread(parts), ('z', 'c'), 0, 0, tiled=True)  7.72 us
    pallas_call x1, Pallas kernels, imported_shrink(): pl.pallas_call(functools.partial(imported_kernel, resident), grid=(Y,), o...  7.38 us
  transfers between devices with their start and end apart: 16, of which 7 were waited for; matrix products, arithmetic and copies ran while one was open for 2% of the time, Pallas kernels for 8%

profile of v2, /device:TPU:1, one launch (start us, length us, event | category | flops | bytes accessed | tf_op | source)
XLA Modules:
  0.0 195.9 jit_solution(12270411231571005929)
XLA Ops:
  7.5 1.7 copy-done.1
  9.2 0.9 copy-done.2
  10.1 0.7 copy-done.4
  11.5 12.7 %shard_map.64 = (bf16[64,64,512]{2,1,0:T(8,128)(2,1)}, bf16[272,512]{1,0:T(8,128)(2,1)}, s32[1,256]{1,0:T(1,128)S(1)}, s32[32,128]{1,0:T(8,128)S(1)}) custom-call(s32[3]{0:T(128)S(1)} %pad_add_fusion.place, s32[32,31]{1,0:T(8,128)S(1)} %copy-done.4, s32[32,31]{1,0:T(8,128)S(1)} %copy-done.4, s32[1,256]{1,0:T(1,128)S(1)} %bitcast.12, ...), custom_call_target="tpu_custom_call" | custom-call | bytes 8388608 | tf_op jit(solution)/shard_map/pallas_call | solution.py:85
  25.4 2.2 %fusion = f32[256,2048]{1,0:T(8,128)} fusion(bf16[256,512]{1,0:T(8,128)(2,1)S(1)} %copy-done.3, bf16[512,2048]{1,0:T(8,128)(2,1)S(1)} %copy-done), kind=kOutput, calls=%fused_computation.1 | convolution fusion | flops 536870912 | bytes 4456448 | tf_op jit(solution)/shard_map/dot_general | solution.py:307
  27.6 4.9 %all-to-all-start = ((bf16[4,16,64,512]{3,2,1,0:T(8,128)(2,1)}), bf16[4,16,64,512]{3,2,1,0:T(8,128)(2,1)}, u32[]{:S(2)}, u32[]{:S(2)}) async-start(bf16[4,16,64,512]{3,2,1,0:T(8,128)(2,1)} %bitcast.13), calls=%async_computation | async-start | bytes 8388608 | tf_op jit(solution)/shard_map/all_to_all | solution.py:304
  32.5 3.1 %shard_map.65.own = f32[64,256]{1,0:T(8,128)} custom-call(s32[1,256]{1,0:T(1,128)} %copy-done.7, bf16[256,512]{1,0:T(8,128)(2,1)} %rows.3, bf16[2048,512]{1,0:T(8,128)(2,1)} %bitcast.11), custom_call_target="tpu_custom_call" | custom-call | flops 536870912 | bytes 2097152 | tf_op jit(solution)/shard_map/pallas_call | solution.py:170
  35.6 40.1 %all-to-all-done = bf16[4,16,64,512]{3,2,1,0:T(8,128)(2,1)} async-done(((bf16[4,16,64,512]{3,2,1,0:T(8,128)(2,1)}), bf16[4,16,64,512]{3,2,1,0:T(8,128)(2,1)}, u32[]{:S(2)}, u32[]{:S(2)}) %all-to-all-start) | async-done | bytes 4194336 | tf_op jit(solution)/shard_map/all_to_all | solution.py:304
  75.7 7.4 %shard_map.66 = (f32[8,8,8,128]{3,2,1,0:T(8,128)}, f32[8,8,8,128]{3,2,1,0:T(8,128)}) custom-call(s32[3]{0:T(128)} %copy-done.5, bf16[8,272,512]{2,1,0:T(8,128)(2,1)} %bitcast.14, bf16[4,8,128,512]{3,2,1,0:T(8,128)(2,1)} %bitcast.6.down, f32[64,256]{1,0:T(8,128)} %shard_map.65.own), custom_call_target="tpu_custom_call" | custom-call | flops 1073741824 | bytes 6422528 | tf_op jit(solution)/shard_map/pallas_call | solution.py:208
  83.1 9.1 %collective-permute-start = (f32[8,8,8,128]{3,2,1,0:T(8,128)}, f32[8,8,8,128]{3,2,1,0:T(8,128)S(1)}, u32[]{:S(2)}, u32[]{:S(2)}) collective-permute-start(f32[8,8,8,128]{3,2,1,0:T(8,128)} %get-tuple-element.27), channel_id=1, source_target_pairs={{0,1},{1,0},{2,3},{3,2},{4,5},{5,4},{6,7},{7,6},{8,9},{9,8},{10,11... | collective-permute-start | bytes 786440 | tf_op jit(solution)/shard_map/ppermute | solution.py:293
  92.2 1.4 collective-permute-done
  93.6 1.7 add.5
  95.3 16.5 %all-to-all-start.1 = ((f32[64,8,128]{2,1,0:T(8,128)}), f32[64,8,128]{2,1,0:T(8,128)S(1)}, u32[]{:S(2)}, u32[]{:S(2)}) async-start(f32[64,8,128]{2,1,0:T(8,128)} %bitcast.8), calls=%async_computation.1 | async-start | bytes 524288 | tf_op jit(solution)/shard_map/all_to_all | solution.py:320
  111.8 2.1 %shard_map.68 = (bf16[8,64,128]{2,1,0:T(8,128)(2,1)}, bf16[8,64,128]{2,1,0:T(8,128)(2,1)}, bf16[8,64,128]{2,1,0:T(8,128)(2,1)}, bf16[8,64,128]{2,1,0:T(8,128)(2,...) custom-call(s32[3]{0:T(128)} %copy-done.5, ...), custom_call_target="tpu_custom_call" | custom-call | bytes 1572864 | tf_op jit(solution)/shard_map/pallas_call | solution.py:119
  113.9 2.9 %collective-permute-start.1 = (bf16[8,64,128]{2,1,0:T(8,128)(2,1)}, bf16[8,64,128]{2,1,0:T(8,128)(2,1)S(1)}, u32[]{:S(2)}, u32[]{:S(2)}) collective-permute-start(bf16[8,64,128]{2,1,0:T(8,128)(2,1)} %get-tuple-element.30), channel_id=1, source_target_pairs={{0,64},{64,128},{128,192},{192,256},{256,320},{320,384},{384,448},... | collective-permute-start | bytes 393224 | tf_op jit(solution)/shard_map/ppermute | solution.py:293
  116.9 4.0 %collective-permute-start.2 = (bf16[8,64,128]{2,1,0:T(8,128)(2,1)}, bf16[8,64,128]{2,1,0:T(8,128)(2,1)S(1)}, u32[]{:S(2)}, u32[]{:S(2)}) collective-permute-start(bf16[8,64,128]{2,1,0:T(8,128)(2,1)} %get-tuple-element.31), channel_id=1, source_target_pairs={{0,128},{64,192},{128,256},{192,320},{256,384},{320,448},{384,0},{... | collective-permute-start | bytes 393224 | tf_op jit(solution)/shard_map/ppermute | solution.py:293
  120.9 4.5 %collective-permute-start.3 = (bf16[8,64,128]{2,1,0:T(8,128)(2,1)}, bf16[8,64,128]{2,1,0:T(8,128)(2,1)S(1)}, u32[]{:S(2)}, u32[]{:S(2)}) collective-permute-start(bf16[8,64,128]{2,1,0:T(8,128)(2,1)} %get-tuple-element.32), channel_id=1, source_target_pairs={{0,192},{64,256},{128,320},{192,384},{256,448},{320,0},{384,64},{4... | collective-permute-start | bytes 393224 | tf_op jit(solution)/shard_map/ppermute | solution.py:293
  125.4 3.8 %collective-permute-start.4 = (bf16[8,64,128]{2,1,0:T(8,128)(2,1)}, bf16[8,64,128]{2,1,0:T(8,128)(2,1)S(1)}, u32[]{:S(2)}, u32[]{:S(2)}) collective-permute-start(bf16[8,64,128]{2,1,0:T(8,128)(2,1)} %get-tuple-element.33), channel_id=1, source_target_pairs={{0,256},{64,320},{128,384},{192,448},{256,0},{320,64},{384,128},{4... | collective-permute-start | bytes 393224 | tf_op jit(solution)/shard_map/ppermute | solution.py:293
  129.2 4.6 %collective-permute-start.5 = (bf16[8,64,128]{2,1,0:T(8,128)(2,1)}, bf16[8,64,128]{2,1,0:T(8,128)(2,1)S(1)}, u32[]{:S(2)}, u32[]{:S(2)}) collective-permute-start(bf16[8,64,128]{2,1,0:T(8,128)(2,1)} %get-tuple-element.34), channel_id=1, source_target_pairs={{0,320},{64,384},{128,448},{192,0},{256,64},{320,128},{384,192},{4... | collective-permute-start | bytes 393224 | tf_op jit(solution)/shard_map/ppermute | solution.py:293
  133.8 5.1 %collective-permute-start.6 = (bf16[8,64,128]{2,1,0:T(8,128)(2,1)}, bf16[8,64,128]{2,1,0:T(8,128)(2,1)S(1)}, u32[]{:S(2)}, u32[]{:S(2)}) collective-permute-start(bf16[8,64,128]{2,1,0:T(8,128)(2,1)} %get-tuple-element.35), channel_id=1, source_target_pairs={{0,384},{64,448},{128,0},{192,64},{256,128},{320,192},{384,256},{4... | collective-permute-start | bytes 393224 | tf_op jit(solution)/shard_map/ppermute | solution.py:293
  138.9 3.0 %collective-permute-start.7 = (bf16[8,64,128]{2,1,0:T(8,128)(2,1)}, bf16[8,64,128]{2,1,0:T(8,128)(2,1)S(1)}, u32[]{:S(2)}, u32[]{:S(2)}) collective-permute-start(bf16[8,64,128]{2,1,0:T(8,128)(2,1)} %get-tuple-element.36), channel_id=1, source_target_pairs={{0,448},{64,0},{128,64},{192,128},{256,192},{320,256},{384,320},{4... | collective-permute-start | bytes 393224 | tf_op jit(solution)/shard_map/ppermute | solution.py:293
  142.1 5.4 %collective-permute-done.5.refs_5_ = bf16[8,64,128]{2,1,0:T(8,128)(2,1)S(1)} collective-permute-done((bf16[8,64,128]{2,1,0:T(8,128)(2,1)}, bf16[8,64,128]{2,1,0:T(8,128)(2,1)S(1)}, u32[]{:S(2)}, u32[]{:S(2)}) %collective-permute-start.5) | collective-permute-done | bytes 131104 | tf_op jit(solution)/shard_map/ppermute | solution.py:293
  147.5 5.2 %collective-permute-done.6.refs_6_ = bf16[8,64,128]{2,1,0:T(8,128)(2,1)S(1)} collective-permute-done((bf16[8,64,128]{2,1,0:T(8,128)(2,1)}, bf16[8,64,128]{2,1,0:T(8,128)(2,1)S(1)}, u32[]{:S(2)}, u32[]{:S(2)}) %collective-permute-start.6) | collective-permute-done | bytes 131104 | tf_op jit(solution)/shard_map/ppermute | solution.py:293
  152.7 1.9 collective-permute-done.7.refs_7_
  155.2 2.4 %shard_map.69 = (bf16[16,64,128]{2,1,0:T(8,128)(2,1)}, bf16[16,64,128]{2,1,0:T(8,128)(2,1)}, bf16[16,64,128]{2,1,0:T(8,128)(2,1)}, bf16[16,64,128]{2,1,0:T(8,128)(2,1)}) custom-call(s32[3]{0:T(128)} %copy-done.5, bf16[8,64,128]{2,1,0:T(8,128)(2,1)} %get-tuple-element.29.refs_0_, bf16[8,64,128]{2,1,0:T(8,128)(2,1)} %copy-done.14, ...), custom_call_target="tpu_custom_call" | custom-call | bytes 2097152 | tf_op jit(solution)/shard_map/pallas_call | solution.py:139
  157.6 2.8 %collective-permute-start.10 = (bf16[16,64,128]{2,1,0:T(8,128)(2,1)}, bf16[16,64,128]{2,1,0:T(8,128)(2,1)S(1)}, u32[]{:S(2)}, u32[]{:S(2)}) collective-permute-start(bf16[16,64,128]{2,1,0:T(8,128)(2,1)} %get-tuple-element.40), channel_id=1, source_target_pairs={{0,48},{16,0},{32,16},{48,32},{1,49},{17,1},{33,17},{49,33},{2,50}... | collective-permute-start | bytes 786440 | tf_op jit(solution)/shard_map/ppermute | solution.py:293
  160.4 2.5 %collective-permute-start.8 = (bf16[16,64,128]{2,1,0:T(8,128)(2,1)}, bf16[16,64,128]{2,1,0:T(8,128)(2,1)S(1)}, u32[]{:S(2)}, u32[]{:S(2)}) collective-permute-start(bf16[16,64,128]{2,1,0:T(8,128)(2,1)} %get-tuple-element.38), channel_id=1, source_target_pairs={{0,16},{16,32},{32,48},{48,0},{1,17},{17,33},{33,49},{49,1},{2,18}... | collective-permute-start | bytes 786440 | tf_op jit(solution)/shard_map/ppermute | solution.py:293
  162.9 2.5 %collective-permute-start.9 = (bf16[16,64,128]{2,1,0:T(8,128)(2,1)}, bf16[16,64,128]{2,1,0:T(8,128)(2,1)S(1)}, u32[]{:S(2)}, u32[]{:S(2)}) collective-permute-start(bf16[16,64,128]{2,1,0:T(8,128)(2,1)} %get-tuple-element.39), channel_id=1, source_target_pairs={{0,32},{16,48},{32,0},{48,16},{1,33},{17,49},{33,1},{49,17},{2,34}... | collective-permute-start | bytes 786440 | tf_op jit(solution)/shard_map/ppermute | solution.py:293
  166.1 1.6 shard_map.67
  167.8 8.2 %all-to-all-start.2 = ((f32[16,8,128]{2,1,0:T(8,128)}), f32[16,8,128]{2,1,0:T(8,128)S(1)}, u32[]{:S(2)}, u32[]{:S(2)}) async-start(f32[16,8,128]{2,1,0:T(8,128)} %shard_map.67), calls=%async_computation.2 | async-start | bytes 131072 | tf_op jit(solution)/shard_map/all_to_all | solution.py:321
  176.1 7.7 %all-to-all-done.2.shrink = f32[16,8,128]{2,1,0:T(8,128)S(1)} async-done(((f32[16,8,128]{2,1,0:T(8,128)}), f32[16,8,128]{2,1,0:T(8,128)S(1)}, u32[]{:S(2)}, u32[]{:S(2)}) %all-to-all-start.2) | async-done | bytes 65568 | tf_op jit(solution)/shard_map/all_to_all | solution.py:321
  184.4 4.1 %shard_map.70 = bf16[256,128]{1,0:T(8,128)(2,1)} custom-call(s32[3]{0:T(128)} %copy-done.5, f32[16,8,128]{2,1,0:T(8,128)} %copy-done.13, s32[1,256]{1,0:T(1,128)} %copy-done.7, f32[256,128]{1,0:T(8,128)} %reduce-scatter.2.cloned.1.call-done.base, bf16[32,64,128]{2,1,0:T(8,128)(2,1)} %up.3, bf16[16,64,128]{2,1,0:T(8,128)(2,1)} %get-tuple-element.37.refs_0_, ...), custom_call_target="tpu_custom_call" | custom-call | tf_op jit(solution)/shard_map/pallas_call | solution.py:284
  (54 shorter events, 4.2 us)
Async XLA Ops:
  7.4 18.0 %copy-start = (bf16[512,2048]{1,0:T(8,128)(2,1)S(1)}, bf16[512,2048]{1,0:T(8,128)(2,1)}, u32[]{:S(2)}) copy-start(bf16[512,2048]{1,0:T(8,128)(2,1)} %param.9) | copy-start | bytes 6291460
  7.4 68.3 %all-gather.3.cloned.1.call-start = ((), (), s32[]{:S(2)}) async-start(), calls=%async_computation.5 | async-start | bytes 2506752 | tf_op jit(solution)/shard_map/all_gather | solution.py:305
  7.4 20.1 %copy-start.5 = (s32[3]{0:T(128)}, s32[3]{0:T(128)S(1)}, u32[]{:S(2)}) copy-start(s32[3]{0:T(128)S(1)} %pad_add_fusion.place) | copy-start | bytes 40
  7.5 1.7 copy-start.1
  9.2 0.9 copy-start.2
  10.1 0.7 copy-start.4
  11.5 13.9 %copy-start.3 = (bf16[256,512]{1,0:T(8,128)(2,1)S(1)}, bf16[256,512]{1,0:T(8,128)(2,1)}, u32[]{:S(2)}) copy-start(bf16[256,512]{1,0:T(8,128)(2,1)} %rows.3) | copy-start | bytes 786436
  25.4 150.7 %reduce-scatter.2.cloned.1.call-start = ((), (), s32[]{:S(2)}) async-start(), calls=%async_computation.4 | async-start | bytes 2228224 | tf_op jit(solution)/shard_map/reduce_scatter | solution.py:308
  27.6 48.1 %all-to-all-start = ((bf16[4,16,64,512]{3,2,1,0:T(8,128)(2,1)}), bf16[4,16,64,512]{3,2,1,0:T(8,128)(2,1)}, u32[]{:S(2)}, u32[]{:S(2)}) async-start(bf16[4,16,64,512]{3,2,1,0:T(8,128)(2,1)} %bitcast.13), calls=%async_computation | async-start | bytes 8388608 | tf_op jit(solution)/shard_map/all_to_all | solution.py:304
  83.1 10.5 %collective-permute-start = (f32[8,8,8,128]{3,2,1,0:T(8,128)}, f32[8,8,8,128]{3,2,1,0:T(8,128)S(1)}, u32[]{:S(2)}, u32[]{:S(2)}) collective-permute-start(f32[8,8,8,128]{3,2,1,0:T(8,128)} %get-tuple-element.27), channel_id=1, source_target_pairs={{0,1},{1,0},{2,3},{3,2},{4,5},{5,4},{6,7},{7,6},{8,9},{9,8},{10,11... | collective-permute-start | bytes 786440 | tf_op jit(solution)/shard_map/ppermute | solution.py:293
  95.3 70.2 %all-to-all-start.1 = ((f32[64,8,128]{2,1,0:T(8,128)}), f32[64,8,128]{2,1,0:T(8,128)S(1)}, u32[]{:S(2)}, u32[]{:S(2)}) async-start(f32[64,8,128]{2,1,0:T(8,128)} %bitcast.8), calls=%async_computation.1 | async-start | bytes 524288 | tf_op jit(solution)/shard_map/all_to_all | solution.py:320
  113.9 19.8 %collective-permute-start.1 = (bf16[8,64,128]{2,1,0:T(8,128)(2,1)}, bf16[8,64,128]{2,1,0:T(8,128)(2,1)S(1)}, u32[]{:S(2)}, u32[]{:S(2)}) collective-permute-start(bf16[8,64,128]{2,1,0:T(8,128)(2,1)} %get-tuple-element.30), channel_id=1, source_target_pairs={{0,64},{64,128},{128,192},{192,256},{256,320},{320,384},{384,448},... | collective-permute-start | bytes 393224 | tf_op jit(solution)/shard_map/ppermute | solution.py:293
  116.9 22.0 %collective-permute-start.2 = (bf16[8,64,128]{2,1,0:T(8,128)(2,1)}, bf16[8,64,128]{2,1,0:T(8,128)(2,1)S(1)}, u32[]{:S(2)}, u32[]{:S(2)}) collective-permute-start(bf16[8,64,128]{2,1,0:T(8,128)(2,1)} %get-tuple-element.31), channel_id=1, source_target_pairs={{0,128},{64,192},{128,256},{192,320},{256,384},{320,448},{384,0},{... | collective-permute-start | bytes 393224 | tf_op jit(solution)/shard_map/ppermute | solution.py:293
  120.9 21.0 %collective-permute-start.3 = (bf16[8,64,128]{2,1,0:T(8,128)(2,1)}, bf16[8,64,128]{2,1,0:T(8,128)(2,1)S(1)}, u32[]{:S(2)}, u32[]{:S(2)}) collective-permute-start(bf16[8,64,128]{2,1,0:T(8,128)(2,1)} %get-tuple-element.32), channel_id=1, source_target_pairs={{0,192},{64,256},{128,320},{192,384},{256,448},{320,0},{384,64},{4... | collective-permute-start | bytes 393224 | tf_op jit(solution)/shard_map/ppermute | solution.py:293
  125.4 16.8 %collective-permute-start.4 = (bf16[8,64,128]{2,1,0:T(8,128)(2,1)}, bf16[8,64,128]{2,1,0:T(8,128)(2,1)S(1)}, u32[]{:S(2)}, u32[]{:S(2)}) collective-permute-start(bf16[8,64,128]{2,1,0:T(8,128)(2,1)} %get-tuple-element.33), channel_id=1, source_target_pairs={{0,256},{64,320},{128,384},{192,448},{256,0},{320,64},{384,128},{4... | collective-permute-start | bytes 393224 | tf_op jit(solution)/shard_map/ppermute | solution.py:293
  129.2 18.3 %collective-permute-start.5 = (bf16[8,64,128]{2,1,0:T(8,128)(2,1)}, bf16[8,64,128]{2,1,0:T(8,128)(2,1)S(1)}, u32[]{:S(2)}, u32[]{:S(2)}) collective-permute-start(bf16[8,64,128]{2,1,0:T(8,128)(2,1)} %get-tuple-element.34), channel_id=1, source_target_pairs={{0,320},{64,384},{128,448},{192,0},{256,64},{320,128},{384,192},{4... | collective-permute-start | bytes 393224 | tf_op jit(solution)/shard_map/ppermute | solution.py:293
  133.7 20.8 %copy-start.14 = (bf16[8,64,128]{2,1,0:T(8,128)(2,1)}, bf16[8,64,128]{2,1,0:T(8,128)(2,1)S(1)}, u32[]{:S(2)}) copy-start(bf16[8,64,128]{2,1,0:T(8,128)(2,1)S(1)} %collective-permute-done.1.refs_1_) | copy-start | bytes 393220
  133.8 18.9 %collective-permute-start.6 = (bf16[8,64,128]{2,1,0:T(8,128)(2,1)}, bf16[8,64,128]{2,1,0:T(8,128)(2,1)S(1)}, u32[]{:S(2)}, u32[]{:S(2)}) collective-permute-start(bf16[8,64,128]{2,1,0:T(8,128)(2,1)} %get-tuple-element.35), channel_id=1, source_target_pairs={{0,384},{64,448},{128,0},{192,64},{256,128},{320,192},{384,256},{4... | collective-permute-start | bytes 393224 | tf_op jit(solution)/shard_map/ppermute | solution.py:293
  138.9 15.7 %copy-start.15 = (bf16[8,64,128]{2,1,0:T(8,128)(2,1)}, bf16[8,64,128]{2,1,0:T(8,128)(2,1)S(1)}, u32[]{:S(2)}) copy-start(bf16[8,64,128]{2,1,0:T(8,128)(2,1)S(1)} %collective-permute-done.2.refs_2_) | copy-start | bytes 393220
  138.9 15.7 %collective-permute-start.7 = (bf16[8,64,128]{2,1,0:T(8,128)(2,1)}, bf16[8,64,128]{2,1,0:T(8,128)(2,1)S(1)}, u32[]{:S(2)}, u32[]{:S(2)}) collective-permute-start(bf16[8,64,128]{2,1,0:T(8,128)(2,1)} %get-tuple-element.36), channel_id=1, source_target_pairs={{0,448},{64,0},{128,64},{192,128},{256,192},{320,256},{384,320},{4... | collective-permute-start | bytes 393224 | tf_op jit(solution)/shard_map/ppermute | solution.py:293
  141.9 12.7 %copy-start.16 = (bf16[8,64,128]{2,1,0:T(8,128)(2,1)}, bf16[8,64,128]{2,1,0:T(8,128)(2,1)S(1)}, u32[]{:S(2)}) copy-start(bf16[8,64,128]{2,1,0:T(8,128)(2,1)S(1)} %collective-permute-done.3.refs_3_) | copy-start | bytes 393220
  142.1 12.5 %copy-start.17 = (bf16[8,64,128]{2,1,0:T(8,128)(2,1)}, bf16[8,64,128]{2,1,0:T(8,128)(2,1)S(1)}, u32[]{:S(2)}) copy-start(bf16[8,64,128]{2,1,0:T(8,128)(2,1)S(1)} %collective-permute-done.4.refs_4_) | copy-start | bytes 393220
  147.5 7.1 %copy-start.18 = (bf16[8,64,128]{2,1,0:T(8,128)(2,1)}, bf16[8,64,128]{2,1,0:T(8,128)(2,1)S(1)}, u32[]{:S(2)}) copy-start(bf16[8,64,128]{2,1,0:T(8,128)(2,1)S(1)} %collective-permute-done.5.refs_5_) | copy-start | bytes 393220
  152.7 1.9 copy-start.19
  157.6 18.4 %collective-permute-start.10 = (bf16[16,64,128]{2,1,0:T(8,128)(2,1)}, bf16[16,64,128]{2,1,0:T(8,128)(2,1)S(1)}, u32[]{:S(2)}, u32[]{:S(2)}) collective-permute-start(bf16[16,64,128]{2,1,0:T(8,128)(2,1)} %get-tuple-element.40), channel_id=1, source_target_pairs={{0,48},{16,0},{32,16},{48,32},{1,49},{17,1},{33,17},{49,33},{2,50}... | collective-permute-start | bytes 786440 | tf_op jit(solution)/shard_map/ppermute | solution.py:293
  160.4 15.6 %collective-permute-start.8 = (bf16[16,64,128]{2,1,0:T(8,128)(2,1)}, bf16[16,64,128]{2,1,0:T(8,128)(2,1)S(1)}, u32[]{:S(2)}, u32[]{:S(2)}) collective-permute-start(bf16[16,64,128]{2,1,0:T(8,128)(2,1)} %get-tuple-element.38), channel_id=1, source_target_pairs={{0,16},{16,32},{32,48},{48,0},{1,17},{17,33},{33,49},{49,1},{2,18}... | collective-permute-start | bytes 786440 | tf_op jit(solution)/shard_map/ppermute | solution.py:293
  162.9 13.1 %collective-permute-start.9 = (bf16[16,64,128]{2,1,0:T(8,128)(2,1)}, bf16[16,64,128]{2,1,0:T(8,128)(2,1)S(1)}, u32[]{:S(2)}, u32[]{:S(2)}) collective-permute-start(bf16[16,64,128]{2,1,0:T(8,128)(2,1)} %get-tuple-element.39), channel_id=1, source_target_pairs={{0,32},{16,48},{32,0},{48,16},{1,33},{17,49},{33,1},{49,17},{2,34}... | collective-permute-start | bytes 786440 | tf_op jit(solution)/shard_map/ppermute | solution.py:293
  165.4 0.7 copy-start.9
  167.8 16.0 %all-to-all-start.2 = ((f32[16,8,128]{2,1,0:T(8,128)}), f32[16,8,128]{2,1,0:T(8,128)S(1)}, u32[]{:S(2)}, u32[]{:S(2)}) async-start(f32[16,8,128]{2,1,0:T(8,128)} %shard_map.67), calls=%async_computation.2 | async-start | bytes 131072 | tf_op jit(solution)/shard_map/all_to_all | solution.py:321
  176.0 7.8 %copy-start.10 = (bf16[16,64,128]{2,1,0:T(8,128)(2,1)}, bf16[16,64,128]{2,1,0:T(8,128)(2,1)S(1)}, u32[]{:S(2)}) copy-start(bf16[16,64,128]{2,1,0:T(8,128)(2,1)S(1)} %collective-permute-done.10.refs_3_) | copy-start | bytes 786436
  176.0 7.8 %copy-start.11 = (bf16[16,64,128]{2,1,0:T(8,128)(2,1)}, bf16[16,64,128]{2,1,0:T(8,128)(2,1)S(1)}, u32[]{:S(2)}) copy-start(bf16[16,64,128]{2,1,0:T(8,128)(2,1)S(1)} %collective-permute-done.8.refs_1_) | copy-start | bytes 786436
  176.0 7.8 %copy-start.12 = (bf16[16,64,128]{2,1,0:T(8,128)(2,1)}, bf16[16,64,128]{2,1,0:T(8,128)(2,1)S(1)}, u32[]{:S(2)}) copy-start(bf16[16,64,128]{2,1,0:T(8,128)(2,1)S(1)} %collective-permute-done.9.refs_2_) | copy-start | bytes 786436
  (5 other events, 3.1 us)
Sparse Core Ops, SparseCore 0:
  25.5 45.7 all-gather.2
Sparse Core Ops, SparseCore 1:
  28.7 67.1 reduce-scatter.1

commit v3 on v2

--- a/solution.py
+++ b/solution.py
@@ -15,92 +15,73 @@
 
 
 def dispatch_kernel(place, plan, plan_row, slots, rows, down, down_out, rows_out, code_out, picked_out,
-                    staged, picked, read_sems, write_sems, picked_sem):
+                    picked, picked_sem):
     resident = down.shape[0]
     group = place[0] * X + place[1]
-    table = plan[...]
-    home = table // resident
-    number = table - home * resident
-    mine = (home == group).astype(jnp.int32)
-    after = jnp.concatenate([jnp.zeros((mine.shape[0], 1), jnp.int32), mine[:, :-1]], axis=1)
-    first = jnp.sum(mine * (1 - after) * number, axis=1, keepdims=True)
-    second = jnp.sum(mine * after * number, axis=1, keepdims=True)
-    lane = lax.broadcasted_iota(jnp.int32, picked_out.shape, 1)
-    picked_out[...] = jnp.where(lane == 0, first, jnp.where(lane == 1, second, 0))
-    to_scalars = pltpu.make_async_copy(picked_out, picked, picked_sem)
-    to_scalars.start()
-    to_scalars.wait()
-
-    def read(i):
-        x, rest = i // (Y * LIMIT), i % (Y * LIMIT)
-        wanted = picked[rest // LIMIT * X + x, rest % LIMIT]
-        return pltpu.make_async_copy(down.at[wanted], staged.at[i], read_sems.at[i])
-
-    def write(i):
-        return pltpu.make_async_copy(staged.at[i], down_out.at[i], write_sems.at[i])
-
-    def begin(i, carry):
-        read(i).start()
-        return carry
-
-    def forward(i, carry):
-        read(i).wait()
-        write(i).start()
-        return carry
-
-    def finish(i, carry):
-        write(i).wait()
-        return carry
-
-    count = GROUPS * LIMIT
-    lax.fori_loop(0, count, begin, 0)
-
-    height = rows.shape[0]
-    slot = slots[...]
-    code = slot
-    before = jnp.int32(-1)
-    for k in range(plan_row.shape[1]):
-        its_home = plan_row[group, k] // resident
-        again = (its_home == before).astype(jnp.int32)
-        code = jnp.where(slot == resident + k, resident + its_home * LIMIT + again, code)
-        before = its_home
-    code_out[...] = code
-    rows_out[0:height, :] = rows[...]
-    wide = jnp.concatenate(
-        [code.astype(jnp.float32), jnp.zeros((1, rows.shape[1] - height), jnp.float32)], axis=1
-    )
-    tail = (rows_out.shape[0] - height, rows.shape[1])
-    rows_out[height:, :] = jnp.broadcast_to(wide, tail).astype(rows_out.dtype)
-
-    lax.fori_loop(0, count, forward, 0)
-    lax.fori_loop(0, count, finish, 0)
+    x = pl.program_id(0)
+
+    @pl.when(x == 0)
+    def _():
+        table = plan[...]
+        home = table // resident
+        number = table - home * resident
+        mine = (home == group).astype(jnp.int32)
+        after = jnp.concatenate([jnp.zeros((mine.shape[0], 1), jnp.int32), mine[:, :-1]], axis=1)
+        first = jnp.sum(mine * (1 - after) * number, axis=1, keepdims=True)
+        second = jnp.sum(mine * after * number, axis=1, keepdims=True)
+        lane = lax.broadcasted_iota(jnp.int32, picked_out.shape, 1)
+        picked_out[...] = jnp.where(lane == 0, first, jnp.where(lane == 1, second, 0))
+        to_scalars = pltpu.make_async_copy(picked_out, picked, picked_sem)
+        to_scalars.start()
+
+        height = rows.shape[0]
+        slot = slots[...]
+        code = slot
+        before = jnp.int32(-1)
+        for k in range(plan_row.shape[1]):
+            its_home = plan_row[group, k] // resident
+            again = (its_home == before).astype(jnp.int32)
+            code = jnp.where(slot == resident + k, resident + its_home * LIMIT + again, code)
+            before = its_home
+        code_out[...] = code
+        rows_out[0:height, :] = rows[...]
+        wide = jnp.concatenate(
+            [code.astype(jnp.float32), jnp.zeros((1, rows.shape[1] - height), jnp.float32)], axis=1
+        )
+        tail = (rows_out.shape[0] - height, rows.shape[1])
+        rows_out[height:, :] = jnp.broadcast_to(wide, tail).astype(rows_out.dtype)
+        to_scalars.wait()
+
+    for y in range(Y):
+        for j in range(LIMIT):
+            down_out[0, y * LIMIT + j] = down[picked[y * X + x, j]]
 
 
 def dispatch(place, plan, slots, rows, down):
     height, width = rows.shape
-    count = GROUPS * LIMIT
     smem = pl.BlockSpec(memory_space=pltpu.SMEM)
-    vmem = pl.BlockSpec(memory_space=pltpu.VMEM)
-    hbm = pl.BlockSpec(memory_space=pl.ANY)
+
+    def whole(shape):
+        return pl.BlockSpec(shape, lambda i: (0,) * len(shape))
+
     return pl.pallas_call(
         dispatch_kernel,
+        grid=(X,),
         out_shape=(
-            jax.ShapeDtypeStruct((count,) + down.shape[1:], down.dtype),
+            jax.ShapeDtypeStruct((X, Y * LIMIT) + down.shape[1:], down.dtype),
             jax.ShapeDtypeStruct((height + 16, width), rows.dtype),
             jax.ShapeDtypeStruct((1, height), jnp.int32),
             jax.ShapeDtypeStruct((GROUPS, 128), jnp.int32),
         ),
-        in_specs=[smem, vmem, smem, vmem, vmem, hbm],
-        out_specs=(hbm, vmem, vmem, vmem),
-        scratch_shapes=[
-            pltpu.VMEM((count,) + down.shape[1:], down.dtype),
-            pltpu.SMEM((GROUPS, 128), jnp.int32),
-            pltpu.SemaphoreType.DMA((count,)),
-            pltpu.SemaphoreType.DMA((count,)),
-            pltpu.SemaphoreType.DMA,
-        ],
-        compiler_params=pltpu.CompilerParams(vmem_limit_bytes=VMEM_LIMIT),
-        cost_estimate=pl.CostEstimate(flops=0, bytes_accessed=4 * count * down[0].size, transcendentals=0),
+        in_specs=[smem, whole(plan.shape), smem, whole(slots.shape), whole(rows.shape), whole(down.shape)],
+        out_specs=(
+            pl.BlockSpec((1, Y * LIMIT) + down.shape[1:], lambda i: (i, 0, 0, 0)),
+            whole((height + 16, width)),
+            whole((1, height)),
+            whole((GROUPS, 128)),
+        ),
+        scratch_shapes=[pltpu.SMEM((GROUPS, 128), jnp.int32), pltpu.SemaphoreType.DMA],
+        cost_estimate=pl.CostEstimate(flops=0, bytes_accessed=6 * down.size, transcendentals=0),
     )(place, plan, plan, slots, rows, down)
 
 
@@ -178,7 +159,8 @@
     )(code, rows, down.reshape(resident * rank, width))
 
 
-def imported_kernel(resident, place, rows, down, own, keep, give):
+def imported_kernel(resident, place, rows, *refs):
+    down, (own, keep, give) = refs[:X], refs[X:]
     group = pl.program_id(0)
     rank, count = own.shape
     half = count // C
@@ -186,7 +168,7 @@
     base = (resident + place[0] * X * LIMIT).astype(jnp.float32)
     total = jnp.where(group == place[0], own[...], 0.0)
     product = lax.dot_general(
-        down[...].reshape(X * LIMIT * rank, down.shape[-1]),
+        jnp.concatenate([part[0, 0] for part in down], axis=0),
         rows[0, 0:count, :],
         NT,
         preferred_element_type=jnp.float32,
@@ -212,14 +194,19 @@
         in_specs=[
             pl.BlockSpec(memory_space=pltpu.SMEM),
             pl.BlockSpec((1, height, width), lambda i: (i, 0, 0)),
-            pl.BlockSpec((X, 1, LIMIT * rank, width), lambda i: (0, i, 0, 0)),
+        ]
+        + [
+            pl.BlockSpec((1, 1, LIMIT * rank, width), functools.partial(lambda x, i: (x, i, 0, 0), x))
+            for x in range(X)
+        ]
+        + [
             pl.BlockSpec((rank, count), lambda i: (0, 0)),
         ],
         out_specs=(block, block),
         cost_estimate=pl.CostEstimate(
             flops=2 * down.size * count, bytes_accessed=2 * (down.size + rows.size), transcendentals=0
         ),
-    )(place, rows, down, own)
+    )(place, rows, *([down] * X), own)
 
 
 def add_kernel(parts, out):
@@ -301,7 +288,7 @@
     down_out, sent_rows, code, picked = dispatch(
         place, transfer_plan, row_adapter_slot.reshape(1, count), inputs, adapter_down
     )
-    down_in = lax.all_to_all(down_out.reshape(X, Y * LIMIT, rank, width), "x", 0, 0, tiled=True)
+    down_in = lax.all_to_all(down_out, "x", 0, 0, tiled=True)
     rows = lax.all_gather(sent_rows, "y")
 
     base_part = jnp.dot(inputs, key_value_weight, preferred_element_type=jnp.float32)
@@ -310,6 +297,7 @@
 
     ups = pick_up(place, picked, adapter_up)
     arrived = [ups[0]] + [shift(ups[d], "y", Y, d) for d in range(1, Y)]
+    down_in, arrived = lax.optimization_barrier((down_in, arrived))
     ups = turn(place, arrived)
     tables = [ups[0]] + [shift(ups[e], "x", X, e) for e in range(1, X)]
 

time: 198 us -> 153 us (0.77)
  waiting for transfers between devices: 61.9 us -> 37.7 us
  Pallas kernels: 33.4 us -> 26.1 us
  starting transfers between devices: 74.4 us -> 67.6 us
  local copies, waits for them, and re-layouts: 7.15 us -> 1.35 us
    all_to_all x1, waiting for transfers between devices: 40.1 us -> 0.01 us  [shards(): down_in = lax.all_to_all(down_out, 'x', 0, 0, tiled=True)]
    all_gather x1, waiting for transfers between devices: 0.01 us -> 10 us  [shards(): rows = lax.all_gather(sent_rows, 'y')]
    pallas_call x1, Pallas kernels: 12.7 us -> 5.38 us  [dispatch(): pl.pallas_call(dispatch_kernel, grid=(X,), out_shape=(jax.ShapeDtypeStruc...]
    unnamed x42 -> x28, local copies, waits for them, and re-layouts: 7.15 us -> 1.35 us
    ppermute x11, waiting for transfers between devices: 14 us -> 19.4 us  [shift(): lax.ppermute(array, axis, [(i, (i + by) % size) for i in range(size)])]
    all_to_all x1, starting transfers between devices: 16.5 us -> 11.9 us  [shards(): lax.all_to_all(parts.reshape(Y * Z, 8, 128), ('y', 'z'), 0, 0, tiled=True)]
  transfers between devices with their start and end apart: 16 -> 16, of which waited for: 7 -> 8; matrix products, arithmetic and copies ran while one was open for 2% -> 2% of each run, Pallas kernels for 8% -> 11%
where the time goes in v3:
time: 153 us; the launch traced here: 152 us
  starting transfers between devices  67.6 us (44%)
  waiting for transfers between devices  37.7 us (25%)
  Pallas kernels  26.1 us (17%)
  between operations  15.1 us (10%)
  other arithmetic  2.35 us (2%)
  matrix products  2.12 us (1%)
    ppermute x11, starting transfers between devices, shift(): lax.ppermute(array, axis, [(i, (i + by) % size) for i in range(size)])  42.9 us
    ppermute x11, waiting for transfers between devices, shift(): lax.ppermute(array, axis, [(i, (i + by) % size) for i in range(size)])  19.4 us
    all_to_all x1, starting transfers between devices, shards(): lax.all_to_all(parts.reshape(Y * Z, 8, 128), ('y', 'z'), 0, 0, tiled=True)  11.9 us
    all_gather x1, waiting for transfers between devices, shards(): rows = lax.all_gather(sent_rows, 'y')  10 us
    all_to_all x1, starting transfers between devices, shards(): shrink = lax.all_to_all(add_and_spread(parts), ('z', 'c'), 0, 0, tiled=True)  7.81 us
    all_to_all x1, waiting for transfers between devices, shards(): shrink = lax.all_to_all(add_and_spread(parts), ('z', 'c'), 0, 0, tiled=True)  7.72 us
    pallas_call x1, Pallas kernels, imported_shrink(): pl.pallas_call(functools.partial(imported_kernel, resident), grid=(Y,), o...  7.41 us
    pallas_call x1, Pallas kernels, dispatch(): pl.pallas_call(dispatch_kernel, grid=(X,), out_shape=(jax.ShapeDtypeStruc...  5.38 us
  transfers between devices with their start and end apart: 16, of which 8 were waited for; matrix products, arithmetic and copies ran while one was open for 2% of the time, Pallas kernels for 11%

profile of v3, /device:TPU:1, one launch (start us, length us, event | category | flops | bytes accessed | tf_op | source)
XLA Modules:
  0.0 152.3 jit_solution(7256366404649790484)
XLA Ops:
  7.4 0.7 pad_add_fusion.place
  8.0 5.4 %shard_map.64 = (bf16[4,16,64,512]{3,2,1,0:T(8,128)(2,1)}, bf16[272,512]{1,0:T(8,128)(2,1)}, s32[1,256]{1,0:T(1,128)}, s32[32,128]{1,0:T(8,128)}) custom-call(s32[3]{0:T(128)} %pad_add_fusion.place, s32[32,31]{1,0:T(8,128)} %plan_row.1, s32[32,31]{1,0:T(8,128)} %plan_row.1, s32[1,256]{1,0:T(1,128)} %bitcast.12, bf16[256,512]{1,0:T(8,128)(2,1)} %rows.3, ...), custom_call_target="tpu_custom_call" | custom-call | bytes 6291456 | tf_op jit(solution)/shard_map/pallas_call | solution.py:67
  13.5 2.1 %fusion = f32[256,2048]{1,0:T(8,128)} fusion(bf16[256,512]{1,0:T(8,128)(2,1)S(1)} %copy-done.1, bf16[512,2048]{1,0:T(8,128)(2,1)S(1)} %copy-done), kind=kOutput, calls=%fused_computation.1 | convolution fusion | flops 536870912 | bytes 4456448 | tf_op jit(solution)/shard_map/dot_general | solution.py:294
  15.7 4.9 %all-to-all-start = ((bf16[4,16,64,512]{3,2,1,0:T(8,128)(2,1)}), bf16[4,16,64,512]{3,2,1,0:T(8,128)(2,1)}, u32[]{:S(2)}, u32[]{:S(2)}) async-start(bf16[4,16,64,512]{3,2,1,0:T(8,128)(2,1)} %get-tuple-element.33), calls=%async_computation | async-start | bytes 8388608 | tf_op jit(solution)/shard_map/all_to_all | solution.py:291
  20.6 2.1 %shard_map.65 = (bf16[8,64,128]{2,1,0:T(8,128)(2,1)}, bf16[8,64,128]{2,1,0:T(8,128)(2,1)}, bf16[8,64,128]{2,1,0:T(8,128)(2,1)}, bf16[8,64,128]{2,1,0:T(8,128)(2,...) custom-call(s32[3]{0:T(128)} %pad_add_fusion.place, ...), custom_call_target="tpu_custom_call" | custom-call | bytes 1572864 | tf_op jit(solution)/shard_map/pallas_call | solution.py:100
  22.7 4.0 %collective-permute-start = (bf16[8,64,128]{2,1,0:T(8,128)(2,1)}, bf16[8,64,128]{2,1,0:T(8,128)(2,1)S(1)}, u32[]{:S(2)}, u32[]{:S(2)}) collective-permute-start(bf16[8,64,128]{2,1,0:T(8,128)(2,1)} %get-tuple-element.36), channel_id=1, source_target_pairs={{0,64},{64,128},{128,192},{192,256},{256,320},{320,384},{384,448},... | collective-permute-start | bytes 393224 | tf_op jit(solution)/shard_map/ppermute | solution.py:280
  26.7 4.2 %collective-permute-start.1 = (bf16[8,64,128]{2,1,0:T(8,128)(2,1)}, bf16[8,64,128]{2,1,0:T(8,128)(2,1)S(1)}, u32[]{:S(2)}, u32[]{:S(2)}) collective-permute-start(bf16[8,64,128]{2,1,0:T(8,128)(2,1)} %get-tuple-element.37), channel_id=1, source_target_pairs={{0,128},{64,192},{128,256},{192,320},{256,384},{320,448},{384,0},{... | collective-permute-start | bytes 393224 | tf_op jit(solution)/shard_map/ppermute | solution.py:280
  31.0 4.6 %collective-permute-start.2 = (bf16[8,64,128]{2,1,0:T(8,128)(2,1)}, bf16[8,64,128]{2,1,0:T(8,128)(2,1)S(1)}, u32[]{:S(2)}, u32[]{:S(2)}) collective-permute-start(bf16[8,64,128]{2,1,0:T(8,128)(2,1)} %get-tuple-element.38), channel_id=1, source_target_pairs={{0,192},{64,256},{128,320},{192,384},{256,448},{320,0},{384,64},{4... | collective-permute-start | bytes 393224 | tf_op jit(solution)/shard_map/ppermute | solution.py:280
  35.6 3.5 %collective-permute-start.3 = (bf16[8,64,128]{2,1,0:T(8,128)(2,1)}, bf16[8,64,128]{2,1,0:T(8,128)(2,1)S(1)}, u32[]{:S(2)}, u32[]{:S(2)}) collective-permute-start(bf16[8,64,128]{2,1,0:T(8,128)(2,1)} %get-tuple-element.39), channel_id=1, source_target_pairs={{0,256},{64,320},{128,384},{192,448},{256,0},{320,64},{384,128},{4... | collective-permute-start | bytes 393224 | tf_op jit(solution)/shard_map/ppermute | solution.py:280
  39.2 4.9 %collective-permute-start.4 = (bf16[8,64,128]{2,1,0:T(8,128)(2,1)}, bf16[8,64,128]{2,1,0:T(8,128)(2,1)S(1)}, u32[]{:S(2)}, u32[]{:S(2)}) collective-permute-start(bf16[8,64,128]{2,1,0:T(8,128)(2,1)} %get-tuple-element.40), channel_id=1, source_target_pairs={{0,320},{64,384},{128,448},{192,0},{256,64},{320,128},{384,192},{4... | collective-permute-start | bytes 393224 | tf_op jit(solution)/shard_map/ppermute | solution.py:280
  44.0 5.0 %collective-permute-start.5 = (bf16[8,64,128]{2,1,0:T(8,128)(2,1)}, bf16[8,64,128]{2,1,0:T(8,128)(2,1)S(1)}, u32[]{:S(2)}, u32[]{:S(2)}) collective-permute-start(bf16[8,64,128]{2,1,0:T(8,128)(2,1)} %get-tuple-element.41), channel_id=1, source_target_pairs={{0,384},{64,448},{128,0},{192,64},{256,128},{320,192},{384,256},{4... | collective-permute-start | bytes 393224 | tf_op jit(solution)/shard_map/ppermute | solution.py:280
  49.0 3.0 %collective-permute-start.6 = (bf16[8,64,128]{2,1,0:T(8,128)(2,1)}, bf16[8,64,128]{2,1,0:T(8,128)(2,1)S(1)}, u32[]{:S(2)}, u32[]{:S(2)}) collective-permute-start(bf16[8,64,128]{2,1,0:T(8,128)(2,1)} %get-tuple-element.42), channel_id=1, source_target_pairs={{0,448},{64,0},{128,64},{192,128},{256,192},{320,256},{384,320},{4... | collective-permute-start | bytes 393224 | tf_op jit(solution)/shard_map/ppermute | solution.py:280
  52.0 3.1 %shard_map.66.refs_4_ = f32[64,256]{1,0:T(8,128)} custom-call(s32[1,256]{1,0:T(1,128)} %get-tuple-element.44.code, bf16[256,512]{1,0:T(8,128)(2,1)} %rows.3, bf16[2048,512]{1,0:T(8,128)(2,1)} %bitcast.10), custom_call_target="tpu_custom_call" | custom-call | flops 536870912 | bytes 2097152 | tf_op jit(solution)/shard_map/pallas_call | solution.py:151
  55.1 0.7 collective-permute-done.3.refs_4_
  55.8 4.0 %collective-permute-done.4.refs_5_ = bf16[8,64,128]{2,1,0:T(8,128)(2,1)S(1)} collective-permute-done((bf16[8,64,128]{2,1,0:T(8,128)(2,1)}, bf16[8,64,128]{2,1,0:T(8,128)(2,1)S(1)}, u32[]{:S(2)}, u32[]{:S(2)}) %collective-permute-start.4) | collective-permute-done | bytes 131104 | tf_op jit(solution)/shard_map/ppermute | solution.py:280
  59.8 9.0 %collective-permute-done.5.refs_6_ = bf16[8,64,128]{2,1,0:T(8,128)(2,1)S(1)} collective-permute-done((bf16[8,64,128]{2,1,0:T(8,128)(2,1)}, bf16[8,64,128]{2,1,0:T(8,128)(2,1)S(1)}, u32[]{:S(2)}, u32[]{:S(2)}) %collective-permute-start.5) | collective-permute-done | bytes 131104 | tf_op jit(solution)/shard_map/ppermute | solution.py:280
  68.7 4.4 %collective-permute-done.6.refs_7_ = bf16[8,64,128]{2,1,0:T(8,128)(2,1)S(1)} collective-permute-done((bf16[8,64,128]{2,1,0:T(8,128)(2,1)}, bf16[8,64,128]{2,1,0:T(8,128)(2,1)S(1)}, u32[]{:S(2)}, u32[]{:S(2)}) %collective-permute-start.6) | collective-permute-done | bytes 131104 | tf_op jit(solution)/shard_map/ppermute | solution.py:280
  73.2 10.0 %all-gather.3.cloned.1.call-done = bf16[2176,512]{1,0:T(8,128)(2,1)} async-done(((bf16[272,512]{1,0:T(8,128)(2,1)}), bf16[2176,512]{1,0:T(8,128)(2,1)}) %all-gather.3.cloned.1.call-update) | async-done | bytes 2228240 | tf_op jit(solution)/shard_map/all_gather | solution.py:292
  83.2 7.4 %shard_map.67 = (f32[8,8,8,128]{3,2,1,0:T(8,128)}, f32[8,8,8,128]{3,2,1,0:T(8,128)}) custom-call(s32[3]{0:T(128)} %pad_add_fusion.place, bf16[8,272,512]{2,1,0:T(8,128)(2,1)} %bitcast.11, bf16[4,8,128,512]{3,2,1,0:T(8,128)(2,1)} %bitcast.5.refs_0_.refs_1_.refs_2_.refs_3_, bf16[4,8,128,512]{3,2,1,0:T(8,128)(2,1)} %bitcast.5.refs_0_.refs_1_.refs_2_.refs_3_, ...), custom_call_target="tpu_custom_call" | custom-call | flops 1073741824 | bytes 6422528 | tf_op jit(solution)/shard_map/pallas_call | solution.py:190
  90.7 3.5 %collective-permute-start.7 = (f32[8,8,8,128]{3,2,1,0:T(8,128)}, f32[8,8,8,128]{3,2,1,0:T(8,128)S(1)}, u32[]{:S(2)}, u32[]{:S(2)}) collective-permute-start(f32[8,8,8,128]{3,2,1,0:T(8,128)} %get-tuple-element.46), channel_id=1, source_target_pairs={{0,1},{1,0},{2,3},{3,2},{4,5},{5,4},{6,7},{7,6},{8,9},{9,8},{10,11... | collective-permute-start | bytes 786440 | tf_op jit(solution)/shard_map/ppermute | solution.py:280
  94.2 1.4 collective-permute-done.7
  95.5 1.7 %add.5 = f32[8,8,8,128]{3,2,1,0:T(8,128)} add(f32[8,8,8,128]{3,2,1,0:T(8,128)} %get-tuple-element.45, f32[8,8,8,128]{3,2,1,0:T(8,128)S(1)} %collective-permute-done.7) | non-fusion elementwise | flops 65536 | bytes 786432 | tf_op jit(solution)/shard_map/add | solution.py:307
  97.2 11.9 %all-to-all-start.1 = ((f32[64,8,128]{2,1,0:T(8,128)}), f32[64,8,128]{2,1,0:T(8,128)S(1)}, u32[]{:S(2)}, u32[]{:S(2)}) async-start(f32[64,8,128]{2,1,0:T(8,128)} %bitcast.7), calls=%async_computation.1 | async-start | bytes 524288 | tf_op jit(solution)/shard_map/all_to_all | solution.py:308
  109.1 2.3 %shard_map.69 = (bf16[16,64,128]{2,1,0:T(8,128)(2,1)}, bf16[16,64,128]{2,1,0:T(8,128)(2,1)}, bf16[16,64,128]{2,1,0:T(8,128)(2,1)}, bf16[16,64,128]{2,1,0:T(8,128)(2,1)}) custom-call(s32[3]{0:T(128)} %pad_add_fusion.place, bf16[8,64,128]{2,1,0:T(8,128)(2,1)} %get-tuple-element.47.refs_0_, bf16[8,64,128]{2,1,0:T(8,128)(2,1)} %copy-done.7, ...), custom_call_target="tpu_custom_call" | custom-call | bytes 2097152 | tf_op jit(solution)/shard_map/pallas_call | solution.py:120
  111.5 4.2 %collective-permute-start.10 = (bf16[16,64,128]{2,1,0:T(8,128)(2,1)}, bf16[16,64,128]{2,1,0:T(8,128)(2,1)S(1)}, u32[]{:S(2)}, u32[]{:S(2)}) collective-permute-start(bf16[16,64,128]{2,1,0:T(8,128)(2,1)} %get-tuple-element.58), channel_id=1, source_target_pairs={{0,48},{16,0},{32,16},{48,32},{1,49},{17,1},{33,17},{49,33},{2,50}... | collective-permute-start | bytes 786440 | tf_op jit(solution)/shard_map/ppermute | solution.py:280
  115.7 1.9 %collective-permute-start.8 = (bf16[16,64,128]{2,1,0:T(8,128)(2,1)}, bf16[16,64,128]{2,1,0:T(8,128)(2,1)S(1)}, u32[]{:S(2)}, u32[]{:S(2)}) collective-permute-start(bf16[16,64,128]{2,1,0:T(8,128)(2,1)} %get-tuple-element.56), channel_id=1, source_target_pairs={{0,16},{16,32},{32,48},{48,0},{1,17},{17,33},{33,49},{49,1},{2,18}... | collective-permute-start | bytes 786440 | tf_op jit(solution)/shard_map/ppermute | solution.py:280
  117.6 4.1 %collective-permute-start.9 = (bf16[16,64,128]{2,1,0:T(8,128)(2,1)}, bf16[16,64,128]{2,1,0:T(8,128)(2,1)S(1)}, u32[]{:S(2)}, u32[]{:S(2)}) collective-permute-start(bf16[16,64,128]{2,1,0:T(8,128)(2,1)} %get-tuple-element.57), channel_id=1, source_target_pairs={{0,32},{16,48},{32,0},{48,16},{1,33},{17,49},{33,1},{49,17},{2,34}... | collective-permute-start | bytes 786440 | tf_op jit(solution)/shard_map/ppermute | solution.py:280
  122.2 0.7 copy-done.2
  122.9 1.6 %shard_map.68 = f32[16,8,128]{2,1,0:T(8,128)} custom-call(f32[64,8,128]{2,1,0:T(8,128)} %copy-done.2), custom_call_target="tpu_custom_call" | custom-call | tf_op jit(solution)/shard_map/pallas_call | solution.py:220
  124.5 7.8 %all-to-all-start.2 = ((f32[16,8,128]{2,1,0:T(8,128)}), f32[16,8,128]{2,1,0:T(8,128)S(1)}, u32[]{:S(2)}, u32[]{:S(2)}) async-start(f32[16,8,128]{2,1,0:T(8,128)} %shard_map.68), calls=%async_computation.2 | async-start | bytes 131072 | tf_op jit(solution)/shard_map/all_to_all | solution.py:309
  132.4 7.7 %all-to-all-done.2.shrink = f32[16,8,128]{2,1,0:T(8,128)S(1)} async-done(((f32[16,8,128]{2,1,0:T(8,128)}), f32[16,8,128]{2,1,0:T(8,128)S(1)}, u32[]{:S(2)}, u32[]{:S(2)}) %all-to-all-start.2) | async-done | bytes 65568 | tf_op jit(solution)/shard_map/all_to_all | solution.py:309
  140.7 4.1 %shard_map.70 = bf16[256,128]{1,0:T(8,128)(2,1)} custom-call(s32[3]{0:T(128)} %pad_add_fusion.place, f32[16,8,128]{2,1,0:T(8,128)} %copy-done.6, s32[1,256]{1,0:T(1,128)} %get-tuple-element.44.code, f32[256,128]{1,0:T(8,128)} %reduce-scatter.2.cloned.1.call-done.base, bf16[32,64,128]{2,1,0:T(8,128)(2,1)} %up.3, ...), custom_call_target="tpu_custom_call" | custom-call | tf_op jit(solution)/shard_map/pallas_call | solution.py:271
  (40 shorter events, 1.2 us)
Async XLA Ops:
  7.4 6.1 %copy-start = (bf16[512,2048]{1,0:T(8,128)(2,1)S(1)}, bf16[512,2048]{1,0:T(8,128)(2,1)}, u32[]{:S(2)}) copy-start(bf16[512,2048]{1,0:T(8,128)(2,1)} %param.9) | copy-start | bytes 6291460
  7.4 6.1 %copy-start.1 = (bf16[256,512]{1,0:T(8,128)(2,1)S(1)}, bf16[256,512]{1,0:T(8,128)(2,1)}, u32[]{:S(2)}) copy-start(bf16[256,512]{1,0:T(8,128)(2,1)} %rows.3) | copy-start | bytes 786436
  7.4 75.9 %all-gather.3.cloned.1.call-start = ((), (), s32[]{:S(2)}) async-start(), calls=%async_computation.5 | async-start | bytes 2506752 | tf_op jit(solution)/shard_map/all_gather | solution.py:292
  13.5 118.9 %reduce-scatter.2.cloned.1.call-start = ((), (), s32[]{:S(2)}) async-start(), calls=%async_computation.4 | async-start | bytes 2228224 | tf_op jit(solution)/shard_map/reduce_scatter | solution.py:295
  15.7 57.5 %all-to-all-start = ((bf16[4,16,64,512]{3,2,1,0:T(8,128)(2,1)}), bf16[4,16,64,512]{3,2,1,0:T(8,128)(2,1)}, u32[]{:S(2)}, u32[]{:S(2)}) async-start(bf16[4,16,64,512]{3,2,1,0:T(8,128)(2,1)} %get-tuple-element.33), calls=%async_computation | async-start | bytes 8388608 | tf_op jit(solution)/shard_map/all_to_all | solution.py:291
  22.7 21.3 %collective-permute-start = (bf16[8,64,128]{2,1,0:T(8,128)(2,1)}, bf16[8,64,128]{2,1,0:T(8,128)(2,1)S(1)}, u32[]{:S(2)}, u32[]{:S(2)}) collective-permute-start(bf16[8,64,128]{2,1,0:T(8,128)(2,1)} %get-tuple-element.36), channel_id=1, source_target_pairs={{0,64},{64,128},{128,192},{192,256},{256,320},{320,384},{384,448},... | collective-permute-start | bytes 393224 | tf_op jit(solution)/shard_map/ppermute | solution.py:280
  26.7 22.3 %collective-permute-start.1 = (bf16[8,64,128]{2,1,0:T(8,128)(2,1)}, bf16[8,64,128]{2,1,0:T(8,128)(2,1)S(1)}, u32[]{:S(2)}, u32[]{:S(2)}) collective-permute-start(bf16[8,64,128]{2,1,0:T(8,128)(2,1)} %get-tuple-element.37), channel_id=1, source_target_pairs={{0,128},{64,192},{128,256},{192,320},{256,384},{320,448},{384,0},{... | collective-permute-start | bytes 393224 | tf_op jit(solution)/shard_map/ppermute | solution.py:280
  31.0 24.2 %collective-permute-start.2 = (bf16[8,64,128]{2,1,0:T(8,128)(2,1)}, bf16[8,64,128]{2,1,0:T(8,128)(2,1)S(1)}, u32[]{:S(2)}, u32[]{:S(2)}) collective-permute-start(bf16[8,64,128]{2,1,0:T(8,128)(2,1)} %get-tuple-element.38), channel_id=1, source_target_pairs={{0,192},{64,256},{128,320},{192,384},{256,448},{320,0},{384,64},{4... | collective-permute-start | bytes 393224 | tf_op jit(solution)/shard_map/ppermute | solution.py:280
  35.6 20.2 %collective-permute-start.3 = (bf16[8,64,128]{2,1,0:T(8,128)(2,1)}, bf16[8,64,128]{2,1,0:T(8,128)(2,1)S(1)}, u32[]{:S(2)}, u32[]{:S(2)}) collective-permute-start(bf16[8,64,128]{2,1,0:T(8,128)(2,1)} %get-tuple-element.39), channel_id=1, source_target_pairs={{0,256},{64,320},{128,384},{192,448},{256,0},{320,64},{384,128},{4... | collective-permute-start | bytes 393224 | tf_op jit(solution)/shard_map/ppermute | solution.py:280
  39.2 20.6 %collective-permute-start.4 = (bf16[8,64,128]{2,1,0:T(8,128)(2,1)}, bf16[8,64,128]{2,1,0:T(8,128)(2,1)S(1)}, u32[]{:S(2)}, u32[]{:S(2)}) collective-permute-start(bf16[8,64,128]{2,1,0:T(8,128)(2,1)} %get-tuple-element.40), channel_id=1, source_target_pairs={{0,320},{64,384},{128,448},{192,0},{256,64},{320,128},{384,192},{4... | collective-permute-start | bytes 393224 | tf_op jit(solution)/shard_map/ppermute | solution.py:280
  44.0 46.6 %copy-start.7 = (bf16[8,64,128]{2,1,0:T(8,128)(2,1)}, bf16[8,64,128]{2,1,0:T(8,128)(2,1)S(1)}, u32[]{:S(2)}) copy-start(bf16[8,64,128]{2,1,0:T(8,128)(2,1)S(1)} %collective-permute-done.refs_1_) | copy-start | bytes 393220
  44.0 24.7 %collective-permute-start.5 = (bf16[8,64,128]{2,1,0:T(8,128)(2,1)}, bf16[8,64,128]{2,1,0:T(8,128)(2,1)S(1)}, u32[]{:S(2)}, u32[]{:S(2)}) collective-permute-start(bf16[8,64,128]{2,1,0:T(8,128)(2,1)} %get-tuple-element.41), channel_id=1, source_target_pairs={{0,384},{64,448},{128,0},{192,64},{256,128},{320,192},{384,256},{4... | collective-permute-start | bytes 393224 | tf_op jit(solution)/shard_map/ppermute | solution.py:280
  49.0 41.6 %copy-start.8 = (bf16[8,64,128]{2,1,0:T(8,128)(2,1)}, bf16[8,64,128]{2,1,0:T(8,128)(2,1)S(1)}, u32[]{:S(2)}) copy-start(bf16[8,64,128]{2,1,0:T(8,128)(2,1)S(1)} %collective-permute-done.1.refs_2_) | copy-start | bytes 393220
  49.0 24.1 %collective-permute-start.6 = (bf16[8,64,128]{2,1,0:T(8,128)(2,1)}, bf16[8,64,128]{2,1,0:T(8,128)(2,1)S(1)}, u32[]{:S(2)}, u32[]{:S(2)}) collective-permute-start(bf16[8,64,128]{2,1,0:T(8,128)(2,1)} %get-tuple-element.42), channel_id=1, source_target_pairs={{0,448},{64,0},{128,64},{192,128},{256,192},{320,256},{384,320},{4... | collective-permute-start | bytes 393224 | tf_op jit(solution)/shard_map/ppermute | solution.py:280
  55.1 35.5 %copy-start.9 = (bf16[8,64,128]{2,1,0:T(8,128)(2,1)}, bf16[8,64,128]{2,1,0:T(8,128)(2,1)S(1)}, u32[]{:S(2)}) copy-start(bf16[8,64,128]{2,1,0:T(8,128)(2,1)S(1)} %collective-permute-done.2.refs_3_) | copy-start | bytes 393220
  55.8 34.8 %copy-start.10 = (bf16[8,64,128]{2,1,0:T(8,128)(2,1)}, bf16[8,64,128]{2,1,0:T(8,128)(2,1)S(1)}, u32[]{:S(2)}) copy-start(bf16[8,64,128]{2,1,0:T(8,128)(2,1)S(1)} %collective-permute-done.3.refs_4_) | copy-start | bytes 393220
  59.8 30.9 %copy-start.11 = (bf16[8,64,128]{2,1,0:T(8,128)(2,1)}, bf16[8,64,128]{2,1,0:T(8,128)(2,1)S(1)}, u32[]{:S(2)}) copy-start(bf16[8,64,128]{2,1,0:T(8,128)(2,1)S(1)} %collective-permute-done.4.refs_5_) | copy-start | bytes 393220
  68.7 21.9 %copy-start.12 = (bf16[8,64,128]{2,1,0:T(8,128)(2,1)}, bf16[8,64,128]{2,1,0:T(8,128)(2,1)S(1)}, u32[]{:S(2)}) copy-start(bf16[8,64,128]{2,1,0:T(8,128)(2,1)S(1)} %collective-permute-done.5.refs_6_) | copy-start | bytes 393220
  73.2 17.5 %copy-start.13 = (bf16[8,64,128]{2,1,0:T(8,128)(2,1)}, bf16[8,64,128]{2,1,0:T(8,128)(2,1)S(1)}, u32[]{:S(2)}) copy-start(bf16[8,64,128]{2,1,0:T(8,128)(2,1)S(1)} %collective-permute-done.6.refs_7_) | copy-start | bytes 393220
  90.7 4.8 %collective-permute-start.7 = (f32[8,8,8,128]{3,2,1,0:T(8,128)}, f32[8,8,8,128]{3,2,1,0:T(8,128)S(1)}, u32[]{:S(2)}, u32[]{:S(2)}) collective-permute-start(f32[8,8,8,128]{3,2,1,0:T(8,128)} %get-tuple-element.46), channel_id=1, source_target_pairs={{0,1},{1,0},{2,3},{3,2},{4,5},{5,4},{6,7},{7,6},{8,9},{9,8},{10,11... | collective-permute-start | bytes 786440 | tf_op jit(solution)/shard_map/ppermute | solution.py:280
  97.2 25.0 %all-to-all-start.1 = ((f32[64,8,128]{2,1,0:T(8,128)}), f32[64,8,128]{2,1,0:T(8,128)S(1)}, u32[]{:S(2)}, u32[]{:S(2)}) async-start(f32[64,8,128]{2,1,0:T(8,128)} %bitcast.7), calls=%async_computation.1 | async-start | bytes 524288 | tf_op jit(solution)/shard_map/all_to_all | solution.py:308
  111.5 20.8 %collective-permute-start.10 = (bf16[16,64,128]{2,1,0:T(8,128)(2,1)}, bf16[16,64,128]{2,1,0:T(8,128)(2,1)S(1)}, u32[]{:S(2)}, u32[]{:S(2)}) collective-permute-start(bf16[16,64,128]{2,1,0:T(8,128)(2,1)} %get-tuple-element.58), channel_id=1, source_target_pairs={{0,48},{16,0},{32,16},{48,32},{1,49},{17,1},{33,17},{49,33},{2,50}... | collective-permute-start | bytes 786440 | tf_op jit(solution)/shard_map/ppermute | solution.py:280
  115.7 16.6 %collective-permute-start.8 = (bf16[16,64,128]{2,1,0:T(8,128)(2,1)}, bf16[16,64,128]{2,1,0:T(8,128)(2,1)S(1)}, u32[]{:S(2)}, u32[]{:S(2)}) collective-permute-start(bf16[16,64,128]{2,1,0:T(8,128)(2,1)} %get-tuple-element.56), channel_id=1, source_target_pairs={{0,16},{16,32},{32,48},{48,0},{1,17},{17,33},{33,49},{49,1},{2,18}... | collective-permute-start | bytes 786440 | tf_op jit(solution)/shard_map/ppermute | solution.py:280
  117.6 14.7 %collective-permute-start.9 = (bf16[16,64,128]{2,1,0:T(8,128)(2,1)}, bf16[16,64,128]{2,1,0:T(8,128)(2,1)S(1)}, u32[]{:S(2)}, u32[]{:S(2)}) collective-permute-start(bf16[16,64,128]{2,1,0:T(8,128)(2,1)} %get-tuple-element.57), channel_id=1, source_target_pairs={{0,32},{16,48},{32,0},{48,16},{1,33},{17,49},{33,1},{49,17},{2,34}... | collective-permute-start | bytes 786440 | tf_op jit(solution)/shard_map/ppermute | solution.py:280
  122.2 0.7 copy-start.2
  124.5 15.6 %all-to-all-start.2 = ((f32[16,8,128]{2,1,0:T(8,128)}), f32[16,8,128]{2,1,0:T(8,128)S(1)}, u32[]{:S(2)}, u32[]{:S(2)}) async-start(f32[16,8,128]{2,1,0:T(8,128)} %shard_map.68), calls=%async_computation.2 | async-start | bytes 131072 | tf_op jit(solution)/shard_map/all_to_all | solution.py:309
  132.3 7.8 %copy-start.3 = (bf16[16,64,128]{2,1,0:T(8,128)(2,1)}, bf16[16,64,128]{2,1,0:T(8,128)(2,1)S(1)}, u32[]{:S(2)}) copy-start(bf16[16,64,128]{2,1,0:T(8,128)(2,1)S(1)} %collective-permute-done.10.refs_3_) | copy-start | bytes 786436
  132.3 7.8 %copy-start.4 = (bf16[16,64,128]{2,1,0:T(8,128)(2,1)}, bf16[16,64,128]{2,1,0:T(8,128)(2,1)S(1)}, u32[]{:S(2)}) copy-start(bf16[16,64,128]{2,1,0:T(8,128)(2,1)S(1)} %collective-permute-done.8.refs_1_) | copy-start | bytes 786436
  132.4 7.8 %copy-start.5 = (bf16[16,64,128]{2,1,0:T(8,128)(2,1)}, bf16[16,64,128]{2,1,0:T(8,128)(2,1)S(1)}, u32[]{:S(2)}) copy-start(bf16[16,64,128]{2,1,0:T(8,128)(2,1)S(1)} %collective-permute-done.9.refs_2_) | copy-start | bytes 786436
  140.1 0.6 copy-start.6
Sparse Core Ops, SparseCore 0:
  13.6 69.6 all-gather.2
Sparse Core Ops, SparseCore 1:
  16.7 67.3 reduce-scatter.1

commit v4 on v1

v4 whole, which is shorter than its diff:
```python
import functools

import jax
import jax.numpy as jnp
from jax import lax
from jax.experimental import pallas as pl
from jax.experimental.pallas import tpu as pltpu
from jax.sharding import Mesh, PartitionSpec as P

Y, X, Z, C = 8, 4, 8, 2
T = Z * C
GROUPS = Y * X
LIMIT = 2
CODE_ROWS = 16
NT = (((1,), (1,)), ((), ()))


def spot():
    return lax.axis_index("y"), lax.axis_index("x")


def dispatch_kernel(plan, down, *refs):
    outs, (picked_out, held, staged, picked, in_sems, out_sems, picked_sem) = refs[:X], refs[X:]
    resident = down.shape[0]
    y, x = spot()
    pieces = in_sems.shape[0]
    part = resident // pieces

    def read(i):
        rows = pl.ds(i * part, part)
        return pltpu.make_async_copy(down.at[rows], held.at[rows], in_sems.at[i])

    def write(e):
        return pltpu.make_async_copy(staged.at[e], outs[e], out_sems.at[e])

    for i in range(pieces):
        read(i).start()
    table = plan[...]
    home = table // resident
    number = table - home * resident
    mine = (home == y * X + x).astype(jnp.int32)
    after = jnp.concatenate([jnp.zeros((mine.shape[0], 1), jnp.int32), mine[:, :-1]], axis=1)
    first = jnp.sum(mine * (1 - after) * number, axis=1, keepdims=True)
    second = jnp.sum(mine * after * number, axis=1, keepdims=True)
    lane = lax.broadcasted_iota(jnp.int32, picked_out.shape, 1)
    picked_out[...] = jnp.where(lane == 0, first, jnp.where(lane == 1, second, 0))
    to_scalars = pltpu.make_async_copy(picked_out, picked, picked_sem)
    to_scalars.start()
    to_scalars.wait()
    for i in range(pieces):
        read(i).wait()
    for e in range(X):
        column = lax.rem(x + e, X)
        for row in range(Y):
            for j in range(LIMIT):
                staged[e, row * LIMIT + j] = held[picked[row * X + column, j]]
        write(e).start()
    for e in range(X):
        write(e).wait()


def dispatch(plan, down):
    vmem = pl.BlockSpec(memory_space=pltpu.VMEM)
    hbm = pl.BlockSpec(memory_space=pl.ANY)
    shape = (Y * LIMIT,) + down.shape[1:]
    return pl.pallas_call(
        dispatch_kernel,
        out_shape=(jax.ShapeDtypeStruct(shape, down.dtype),) * X
        + (jax.ShapeDtypeStruct((GROUPS, 128), jnp.int32),),
        in_specs=[vmem, hbm],
        out_specs=(hbm,) * X + (vmem,),
        scratch_shapes=[
            pltpu.VMEM(down.shape, down.dtype),
            pltpu.VMEM((X,) + shape, down.dtype),
            pltpu.SMEM((GROUPS, 128), jnp.int32),
            pltpu.SemaphoreType.DMA((4,)),
            pltpu.SemaphoreType.DMA((X,)),
            pltpu.SemaphoreType.DMA,
        ],
        cost_estimate=pl.CostEstimate(flops=0, bytes_accessed=6 * down.size, transcendentals=0),
    )(plan, down)


def pick_up_kernel(picked, plan, slots, up, out, code_out):
    resident, rank, _ = up.shape
    y, x = spot()
    slot = slots[...]
    code = slot
    before = jnp.int32(-1)
    for k in range(plan.shape[1]):
        home = plan[y * X + x, k] // resident
        again = (home == before).astype(jnp.int32)
        code = jnp.where(slot == resident + k, resident + home * LIMIT + again, code)
        before = home
    code_out[...] = code
    lanes = out.shape[2]
    tail = [code[:, k * lanes : (k + 1) * lanes].astype(jnp.float32) for k in range(code.shape[1] // lanes)]
    tail.append(jnp.zeros((CODE_ROWS - len(tail), lanes), jnp.float32))
    tail = jnp.concatenate(tail, axis=0).astype(out.dtype)
    for group in range(GROUPS):
        for j in range(LIMIT):
            out[group, j * rank : (j + 1) * rank, :] = up[picked[group, j]]
        out[group, LIMIT * rank :, :] = tail


def pick_up(picked, plan, slots, up):
    smem = pl.BlockSpec(memory_space=pltpu.SMEM)
    vmem = pl.BlockSpec(memory_space=pltpu.VMEM)
    _, rank, width = up.shape
    return pl.pallas_call(
        pick_up_kernel,
        out_shape=(
            jax.ShapeDtypeStruct((GROUPS, LIMIT * rank + CODE_ROWS, width), up.dtype),
            jax.ShapeDtypeStruct(slots.shape, jnp.int32),
        ),
        in_specs=[smem, smem, vmem, vmem],
        out_specs=(vmem, vmem),
        cost_estimate=pl.CostEstimate(flops=0, bytes_accessed=6 * up.size, transcendentals=0),
    )(picked, plan, slots, up)


def local_kernel(code, rows, down, out):
    rank = out.shape[0]
    resident = down.shape[0] // rank
    total = jnp.zeros(out.shape, jnp.float32)
    step = 4
    for first in range(0, resident, step):
        product = lax.dot_general(
            down[first * rank : (first + step) * rank, :], rows[...], NT, preferred_element_type=jnp.float32
        )
        for k in range(step):
            total = total + jnp.where(code[...] == first + k, product[k * rank : (k + 1) * rank, :], 0.0)
    out[...] = total


def local_shrink(code, rows, down):
    resident, rank, width = down.shape
    vmem = pl.BlockSpec(memory_space=pltpu.VMEM)
    return pl.pallas_call(
        local_kernel,
        out_shape=jax.ShapeDtypeStruct((rank, rows.shape[0]), jnp.float32),
        in_specs=[vmem] * 3,
        out_specs=vmem,
        cost_estimate=pl.CostEstimate(
            flops=2 * rows.size * resident * rank, bytes_accessed=2 * down.size, transcendentals=0
        ),
    )(code, rows, down.reshape(resident * rank, width))


def imported_kernel(resident, rows, codes, *refs):
    down, (own, out, rows_held, codes_held, down_held, sems) = refs[:X], refs[X:]
    rank, count = own.shape
    lanes = out.shape[-1]
    y, x = spot()

    def reads(g):
        wanted = pl.ds(g * LIMIT * rank, LIMIT * rank)
        pairs = [(rows.at[pl.ds(g * count, count)], rows_held.at[g])]
        pairs.append((codes.at[g * X + x, pl.ds(LIMIT * rank, CODE_ROWS)], codes_held.at[g]))
        pairs += [(down[e].at[wanted], down_held.at[g, pl.ds(e * LIMIT * rank, LIMIT * rank)]) for e in range(X)]
        return [pltpu.make_async_copy(a, b, sems.at[g, i]) for i, (a, b) in enumerate(pairs)]

    for g in range(Y):
        for read in reads(g):
            read.start()
    for g in range(Y):
        for read in reads(g):
            read.wait()
        tail = codes_held[g].astype(jnp.float32)
        code = jnp.concatenate([tail[k : k + 1] for k in range(count // lanes)], axis=1)
        total = jnp.where(y == g, own[...], 0.0)
        product = lax.dot_general(down_held[g], rows_held[g], NT, preferred_element_type=jnp.float32)
        for e in range(X):
            home = y * X + lax.rem(x - e + X, X)
            for j in range(LIMIT):
                at = (e * LIMIT + j) * rank
                hit = code == (resident + home * LIMIT + j).astype(jnp.float32)
                total = total + jnp.where(hit, product[at : at + rank, :], 0.0)
        for i in range(rank // 8):
            for k in range(count // lanes):
                out[g, i * (count // lanes) + k] = total[i * 8 : (i + 1) * 8, k * lanes : (k + 1) * lanes]


def imported_shrink(resident, rows, codes, down, own):
    rank, count = own.shape
    width = rows.shape[-1]
    blocks = rank * count // 1024
    vmem = pl.BlockSpec(memory_space=pltpu.VMEM)
    hbm = pl.BlockSpec(memory_space=pl.ANY)
    return pl.pallas_call(
        functools.partial(imported_kernel, resident),
        out_shape=jax.ShapeDtypeStruct((Y, blocks, 8, 128), jnp.float32),
        in_specs=[hbm] * (2 + X) + [vmem],
        out_specs=vmem,
        scratch_shapes=[
            pltpu.VMEM((Y, count, width), rows.dtype),
            pltpu.VMEM((Y, CODE_ROWS, codes.shape[-1]), codes.dtype),
            pltpu.VMEM((Y, X * LIMIT * rank, width), rows.dtype),
            pltpu.SemaphoreType.DMA((Y, X + 2)),
        ],
        cost_estimate=pl.CostEstimate(
            flops=2 * X * down[0].size * count, bytes_accessed=2 * (X * down[0].size + rows.size), transcendentals=0
        ),
    )(rows, codes, *[part.reshape(-1, width) for part in down], own)


def add_kernel(parts, out):
    total = jnp.sum(parts[...], axis=0)
    for t in range(out.shape[0]):
        out[t] = total


def add_and_spread(parts):
    vmem = pl.BlockSpec(memory_space=pltpu.VMEM)
    return pl.pallas_call(
        add_kernel,
        out_shape=jax.ShapeDtypeStruct((T,) + parts.shape[1:], jnp.float32),
        in_specs=[vmem],
        out_specs=vmem,
    )(parts)


def expand_kernel(shrink, code, base, up, up_in, out):
    count = out.shape[0]
    lanes = count // 128
    rank = shrink.shape[0] // lanes * 8
    rows = jnp.concatenate(
        [jnp.concatenate([shrink[i * lanes + k] for k in range(lanes)], axis=1) for i in range(rank // 8)], axis=0
    )
    rows = jnp.transpose(rows)
    column = jnp.transpose(jnp.broadcast_to(code[...], (8, count)).astype(jnp.float32))[:, :1]
    pair = jnp.concatenate([rows, rows], axis=1)
    high = pair.astype(jnp.bfloat16).astype(jnp.float32)
    low = pair - high
    half = lax.broadcasted_iota(jnp.int32, pair.shape, 1) // rank
    wanted = jnp.broadcast_to(column, pair.shape) - half.astype(jnp.float32)
    both = jnp.concatenate([high, low], axis=0)
    wanted = jnp.concatenate([wanted, wanted], axis=0)
    total = jnp.zeros((2 * count, out.shape[1]), jnp.float32)
    step = 4
    pairs = [up[2 * p : 2 * p + 2].reshape(2 * rank, -1) for p in range(up.shape[0] // 2)]
    pairs += [up_in[p, : 2 * rank, :] for p in range(up_in.shape[0])]
    for first in range(0, len(pairs), step):
        placed = jnp.concatenate(
            [
                jnp.where(wanted == float(2 * p), both, 0.0).astype(jnp.bfloat16)
                for p in range(first, first + step)
            ],
            axis=1,
        )
        maps = jnp.concatenate(pairs[first : first + step], axis=0)
        total = total + jnp.dot(placed, maps, preferred_element_type=jnp.float32)
    out[...] = (base[...] + (total[:count] + total[count:])).astype(out.dtype)


def expand(shrink, code, base, up, up_in):
    vmem = pl.BlockSpec(memory_space=pltpu.VMEM)
    return pl.pallas_call(
        expand_kernel,
        out_shape=jax.ShapeDtypeStruct(base.shape, jnp.bfloat16),
        in_specs=[vmem] * 5,
        out_specs=vmem,
    )(shrink, code, base, up, up_in)


def shift(array, axis, size, by):
    return lax.ppermute(array, axis, [(i, (i + by) % size) for i in range(size)])


def shards(inputs, row_adapter_slot, transfer_plan, key_value_weight, adapter_down, adapter_up):
    count = inputs.shape[0]
    resident = adapter_down.shape[0]
    slots = row_adapter_slot.reshape(1, count)

    rows = lax.all_gather(inputs, "y", tiled=True)
    *down, picked = dispatch(transfer_plan, adapter_down)
    down = [down[0]] + [shift(down[e], "x", X, e) for e in range(1, X)]

    up_out, code = pick_up(picked, transfer_plan, slots, adapter_up)
    up_in = lax.all_to_all(up_out, ("y", "x"), 0, 0, tiled=True)

    base_part = jnp.dot(inputs, key_value_weight, preferred_element_type=jnp.float32)
    base = lax.psum_scatter(base_part, ("z", "c"), scatter_dimension=1, tiled=True)
    own = local_shrink(code, inputs, adapter_down)

    parts = imported_shrink(resident, rows, up_in, down, own)
    parts = lax.all_to_all(parts.reshape(Y * T, 8, 128), ("y", "z", "c"), 0, 0, tiled=True)
    shrink = lax.all_to_all(add_and_spread(parts), ("z", "c"), 0, 0, tiled=True)
    return expand(shrink, code, base, adapter_up, up_in)


def solution(mesh):
    grid = Mesh(mesh.devices.reshape(Y, X, Z, C), ("y", "x", "z", "c"))
    replica, tensor = ("y", "x"), ("z", "c")
    placed = (
        P(replica, tensor),
        P(replica),
        P(),
        P(tensor, None),
        P(replica, None, tensor),
        P(replica, None, tensor),
    )
    return jax.shard_map(
        shards, mesh=grid, in_specs=placed, out_specs=P(replica, tensor), check_vma=False
    )
```

time: 322 us -> 165 us (0.51)
  Pallas kernels: 178 us -> 23.5 us
  blocking collectives: 0 us -> 36.1 us
  starting transfers between devices: 46.6 us -> 26.4 us
  waiting for transfers between devices: 70.4 us -> 58.2 us
  local copies, waits for them, and re-layouts: 7.43 us -> 2.46 us
    pallas_call x4 -> x3, Pallas kernels: 173 us -> 14.4 us  [the longest x1 6.91 us: imported_shrink(): pl.pallas_call(functools.partial(imported_kernel, resident), out_shape=ja...]
    ppermute x0 -> x3, waiting for transfers between devices: none -> 49.6 us  [shift(): lax.ppermute(array, axis, [(i, (i + by) % size) for i in range(size)])]
    all_to_all x2 -> x0, waiting for transfers between devices: 38 us -> none  [the longest x1 38 us: shards(): down_in = lax.all_to_all(down_out, 'x', 0, 0, tiled=True)]
    all_to_all x0 -> x1, blocking collectives: none -> 36.1 us  [shards(): lax.all_to_all(parts.reshape(Y * T, 8, 128), ('y', 'z', 'c'), 0, 0, tiled...]
    all_to_all x2 -> x0, starting transfers between devices: 29.3 us -> none  [the longest x1 24.3 us: shards(): lax.all_to_all(parts.reshape(Y * T, 8, 128), ('y', 'z', 'c'), 0, 0, tiled...]
    all_to_all x1, waiting for transfers between devices: 24.5 us -> 0.01 us  [shards(): up_in = lax.all_to_all(up_out, ('y', 'x'), 0, 0, tiled=True)]
    ppermute x0 -> x3, starting transfers between devices: none -> 10.5 us  [shift(): lax.ppermute(array, axis, [(i, (i + by) % size) for i in range(size)])]
    unnamed x16 -> x6, local copies, waits for them, and re-layouts: 6.66 us -> 2.46 us
  transfers between devices with their start and end apart: 6 -> 7, of which waited for: 3 -> 4; matrix products, arithmetic and copies ran while one was open for 1% -> 2% of each run, Pallas kernels for 54% -> 12%
where the time goes in v4:
time: 165 us
  waiting for transfers between devices  58.2 us (35%)
  blocking collectives  36.1 us (22%)
  starting transfers between devices  26.4 us (16%)
  Pallas kernels  23.5 us (14%)
  between operations  14.9 us (9%)
  matrix products  3 us (2%)
  local copies, waits for them, and re-layouts  2.46 us (1%)
    ppermute x3, waiting for transfers between devices, shift(): lax.ppermute(array, axis, [(i, (i + by) % size) for i in range(size)])  49.6 us
    all_to_all x1, blocking collectives, shards(): lax.all_to_all(parts.reshape(Y * T, 8, 128), ('y', 'z', 'c'), 0, 0, tiled...  36.1 us
    ppermute x3, starting transfers between devices, shift(): lax.ppermute(array, axis, [(i, (i + by) % size) for i in range(size)])  10.5 us
    all_to_all x1, starting transfers between devices, shards(): up_in = lax.all_to_all(up_out, ('y', 'x'), 0, 0, tiled=True)  10.5 us
    all_to_all x1, waiting for transfers between devices, shards(): shrink = lax.all_to_all(add_and_spread(parts), ('z', 'c'), 0, 0, tiled=True)  7.81 us
    pallas_call x1, Pallas kernels, imported_shrink(): pl.pallas_call(functools.partial(imported_kernel, resident), out_shape=ja...  6.91 us
    all_to_all x1, starting transfers between devices, shards(): shrink = lax.all_to_all(add_and_spread(parts), ('z', 'c'), 0, 0, tiled=True)  5.36 us
    pallas_call x1, Pallas kernels, dispatch(): pl.pallas_call(dispatch_kernel, out_shape=(jax.ShapeDtypeStruct(shape, do...  5 us
  transfers between devices with their start and end apart: 7, of which 4 were waited for; matrix products, arithmetic and copies ran while one was open for 2% of the time, Pallas kernels for 12%

profile of v4, /device:TPU:1, one launch (start us, length us, event | category | flops | bytes accessed | tf_op | source)
XLA Modules:
  0.0 164.6 jit_solution(11338987980073710571)
XLA Ops:
  7.4 0.0 copy-start
  7.4 0.0 all-gather.2.cloned.1.call-start
  7.4 0.7 all-gather.2.cloned.1.call-update
  8.1 0.0 reduce-scatter.2.cloned.1.call-start
  8.1 0.8 copy-done
  9.0 3.0 %fusion = f32[256,2048]{1,0:T(8,128)} fusion(bf16[256,512]{1,0:T(8,128)(2,1)} %rows.1, bf16[512,2048]{1,0:T(8,128)(2,1)S(1)} %copy-done), kind=kOutput, calls=%fused_computation | convolution fusion | flops 536870912 | bytes 4456448 | tf_op jit(solution)/shard_map/dot_general | solution.py:282
  12.0 0.0 reduce-scatter.2.cloned.1.call-update
  12.0 5.0 %shard_map.64 = (bf16[16,64,512]{2,1,0:T(8,128)(2,1)}, bf16[16,64,512]{2,1,0:T(8,128)(2,1)}, bf16[16,64,512]{2,1,0:T(8,128)(2,1)}, bf16[16,64,512]{2,1,0:T(8,128)(2,1)}, s32[32,128]{1,0:T(8,128)}) custom-call(s32[32,31]{1,0:T(8,128)} %plan.3, bf16[32,64,512]{2,1,0:T(8,128)(2,1)} %down.1), custom_call_target="tpu_custom_call" | custom-call | bytes 6291456 | tf_op jit(solution)/shard_map/pallas_call | solution.py:66
  17.0 2.5 %shard_map.65 = (bf16[32,144,128]{2,1,0:T(8,128)(2,1)}, s32[1,256]{1,0:T(1,128)}) custom-call(s32[32,128]{1,0:T(8,128)} %get-tuple-element.12.picked, s32[32,31]{1,0:T(8,128)} %plan.3, s32[1,256]{1,0:T(1,128)} %bitcast.12, bf16[32,64,128]{2,1,0:T(8,128)(2,1)} %up.3), custom_call_target="tpu_custom_call" | custom-call | bytes 1572864 | tf_op jit(solution)/shard_map/pallas_call | solution.py:110
  19.5 10.5 %all-to-all-start = ((bf16[32,144,128]{2,1,0:T(8,128)(2,1)}), bf16[32,144,128]{2,1,0:T(8,128)(2,1)S(1)}, u32[]{:S(2)}, u32[]{:S(2)}) async-start(bf16[32,144,128]{2,1,0:T(8,128)(2,1)} %get-tuple-element.13), calls=%async_computation | async-start | bytes 2359296 | tf_op jit(solution)/shard_map/all_to_all | solution.py:280
  30.0 3.1 %collective-permute-start = (bf16[16,64,512]{2,1,0:T(8,128)(2,1)}, bf16[16,64,512]{2,1,0:T(8,128)(2,1)}, u32[]{:S(2)}, u32[]{:S(2)}) collective-permute-start(bf16[16,64,512]{2,1,0:T(8,128)(2,1)} %get-tuple-element.15), channel_id=1, source_target_pairs={{0,16},{16,32},{32,48},{48,0},{1,17},{17,33},{33,49},{49,1},{2,18}... | collective-permute-start | bytes 3145736 | tf_op jit(solution)/shard_map/ppermute | solution.py:267
  33.2 4.3 %collective-permute-start.1 = (bf16[16,64,512]{2,1,0:T(8,128)(2,1)}, bf16[16,64,512]{2,1,0:T(8,128)(2,1)}, u32[]{:S(2)}, u32[]{:S(2)}) collective-permute-start(bf16[16,64,512]{2,1,0:T(8,128)(2,1)} %get-tuple-element.16), channel_id=1, source_target_pairs={{0,32},{16,48},{32,0},{48,16},{1,33},{17,49},{33,1},{49,17},{2,34}... | collective-permute-start | bytes 3145736 | tf_op jit(solution)/shard_map/ppermute | solution.py:267
  37.5 3.1 %collective-permute-start.2 = (bf16[16,64,512]{2,1,0:T(8,128)(2,1)}, bf16[16,64,512]{2,1,0:T(8,128)(2,1)}, u32[]{:S(2)}, u32[]{:S(2)}) collective-permute-start(bf16[16,64,512]{2,1,0:T(8,128)(2,1)} %get-tuple-element.17), channel_id=1, source_target_pairs={{0,48},{16,0},{32,16},{48,32},{1,49},{17,1},{33,17},{49,33},{2,50}... | collective-permute-start | bytes 3145736 | tf_op jit(solution)/shard_map/ppermute | solution.py:267
  40.6 3.1 %shard_map.66.refs_4_ = f32[64,256]{1,0:T(8,128)} custom-call(s32[1,256]{1,0:T(1,128)} %get-tuple-element.18.code, bf16[256,512]{1,0:T(8,128)(2,1)} %rows.1, bf16[2048,512]{1,0:T(8,128)(2,1)} %bitcast.9), custom_call_target="tpu_custom_call" | custom-call | flops 536870912 | bytes 2097152 | tf_op jit(solution)/shard_map/pallas_call | solution.py:139
  43.7 23.7 %collective-permute-done = bf16[16,64,512]{2,1,0:T(8,128)(2,1)} collective-permute-done((bf16[16,64,512]{2,1,0:T(8,128)(2,1)}, bf16[16,64,512]{2,1,0:T(8,128)(2,1)}, u32[]{:S(2)}, u32[]{:S(2)}) %collective-permute-start) | collective-permute-done | bytes 1048608 | tf_op jit(solution)/shard_map/ppermute | solution.py:267
  67.4 23.8 %collective-permute-done.1 = bf16[16,64,512]{2,1,0:T(8,128)(2,1)} collective-permute-done((bf16[16,64,512]{2,1,0:T(8,128)(2,1)}, bf16[16,64,512]{2,1,0:T(8,128)(2,1)}, u32[]{:S(2)}, u32[]{:S(2)}) %collective-permute-start.1) | collective-permute-done | bytes 1048608 | tf_op jit(solution)/shard_map/ppermute | solution.py:267
  91.2 2.1 %collective-permute-done.2 = bf16[16,64,512]{2,1,0:T(8,128)(2,1)} collective-permute-done((bf16[16,64,512]{2,1,0:T(8,128)(2,1)}, bf16[16,64,512]{2,1,0:T(8,128)(2,1)}, u32[]{:S(2)}, u32[]{:S(2)}) %collective-permute-start.2) | collective-permute-done | bytes 1048608 | tf_op jit(solution)/shard_map/ppermute | solution.py:267
  93.3 0.0 all-to-all-done.codes.up_in
  93.3 0.0 copy-start.1
  93.3 0.0 all-gather.2.cloned.1.call-done.rows
  93.3 1.0 copy-done.1
  94.3 6.9 %shard_map.67 = f32[8,16,8,128]{3,2,1,0:T(8,128)} custom-call(bf16[2048,512]{1,0:T(8,128)(2,1)} %all-gather.2.cloned.1.call-done.rows, bf16[32,144,128]{2,1,0:T(8,128)(2,1)} %copy-done.1, bf16[1024,512]{1,0:T(8,128)(2,1)} %bitcast.11, bf16[1024,512]{1,0:T(8,128)(2,1)} %bitcast.2.refs_1_, bf16[1024,512]{1,0:T(8,128)(2,1)} %bitcast.3.refs_2_, ...), custom_call_target="tpu_custom_call" | custom-call | flops 1073741824 | bytes 6291456 | tf_op jit(solution)/shard_map/pallas_call | solution.py:190
  101.2 36.1 %all_to_all.15.parts = f32[128,8,128]{2,1,0:T(8,128)} all-to-all(f32[128,8,128]{2,1,0:T(8,128)} %bitcast.10), channel_id=1, replica_groups=mesh['y'=8,'x'=4,'z'=8,'c'=2] {'y','z','c'}, dimensions={0} | all-to-all | bytes 1048576 | tf_op jit(solution)/shard_map/all_to_all | solution.py:287
  137.4 1.8 %shard_map.68 = f32[16,8,128]{2,1,0:T(8,128)} custom-call(f32[128,8,128]{2,1,0:T(8,128)} %all_to_all.15.parts), custom_call_target="tpu_custom_call" | custom-call | tf_op jit(solution)/shard_map/pallas_call | solution.py:215
  139.2 5.4 %all-to-all-start.2 = ((f32[16,8,128]{2,1,0:T(8,128)}), f32[16,8,128]{2,1,0:T(8,128)S(1)}, u32[]{:S(2)}, u32[]{:S(2)}) async-start(f32[16,8,128]{2,1,0:T(8,128)} %shard_map.68), calls=%async_computation.2 | async-start | bytes 131072 | tf_op jit(solution)/shard_map/all_to_all | solution.py:288
  144.5 0.0 reduce-scatter.2.cloned.1.call-done.base
  144.5 7.8 %all-to-all-done.2.shrink = f32[16,8,128]{2,1,0:T(8,128)S(1)} async-done(((f32[16,8,128]{2,1,0:T(8,128)}), f32[16,8,128]{2,1,0:T(8,128)S(1)}, u32[]{:S(2)}, u32[]{:S(2)}) %all-to-all-start.2) | async-done | bytes 65568 | tf_op jit(solution)/shard_map/all_to_all | solution.py:288
  152.4 0.0 copy-start.2
  152.4 0.6 copy-done.2
  153.0 4.1 %shard_map.69 = bf16[256,128]{1,0:T(8,128)(2,1)} custom-call(f32[16,8,128]{2,1,0:T(8,128)} %copy-done.2, s32[1,256]{1,0:T(1,128)} %get-tuple-element.18.code, f32[256,128]{1,0:T(8,128)} %reduce-scatter.2.cloned.1.call-done.base, bf16[32,64,128]{2,1,0:T(8,128)(2,1)} %up.3, bf16[32,144,128]{2,1,0:T(8,128)(2,1)} %copy-done.1), custom_call_target="tpu_custom_call" | custom-call | tf_op jit(solution)/shard_map/pallas_call | solution.py:258
Async XLA Ops:
  7.4 1.6 copy-start
  7.4 85.9 %all-gather.2.cloned.1.call-start = ((), (), s32[]{:S(2)}) async-start(), calls=%async_computation.4 | async-start | bytes 2359296 | tf_op jit(solution)/shard_map/all_gather | solution.py:275
  8.1 136.4 %reduce-scatter.2.cloned.1.call-start = ((), (), s32[]{:S(2)}) async-start(), calls=%async_computation.5 | async-start | bytes 2228224 | tf_op jit(solution)/shard_map/reduce_scatter | solution.py:283
  19.5 73.8 %all-to-all-start = ((bf16[32,144,128]{2,1,0:T(8,128)(2,1)}), bf16[32,144,128]{2,1,0:T(8,128)(2,1)S(1)}, u32[]{:S(2)}, u32[]{:S(2)}) async-start(bf16[32,144,128]{2,1,0:T(8,128)(2,1)} %get-tuple-element.13), calls=%async_computation | async-start | bytes 2359296 | tf_op jit(solution)/shard_map/all_to_all | solution.py:280
  30.0 37.3 %collective-permute-start = (bf16[16,64,512]{2,1,0:T(8,128)(2,1)}, bf16[16,64,512]{2,1,0:T(8,128)(2,1)}, u32[]{:S(2)}, u32[]{:S(2)}) collective-permute-start(bf16[16,64,512]{2,1,0:T(8,128)(2,1)} %get-tuple-element.15), channel_id=1, source_target_pairs={{0,16},{16,32},{32,48},{48,0},{1,17},{17,33},{33,49},{49,1},{2,18}... | collective-permute-start | bytes 3145736 | tf_op jit(solution)/shard_map/ppermute | solution.py:267
  33.2 58.0 %collective-permute-start.1 = (bf16[16,64,512]{2,1,0:T(8,128)(2,1)}, bf16[16,64,512]{2,1,0:T(8,128)(2,1)}, u32[]{:S(2)}, u32[]{:S(2)}) collective-permute-start(bf16[16,64,512]{2,1,0:T(8,128)(2,1)} %get-tuple-element.16), channel_id=1, source_target_pairs={{0,32},{16,48},{32,0},{48,16},{1,33},{17,49},{33,1},{49,17},{2,34}... | collective-permute-start | bytes 3145736 | tf_op jit(solution)/shard_map/ppermute | solution.py:267
  37.5 55.8 %collective-permute-start.2 = (bf16[16,64,512]{2,1,0:T(8,128)(2,1)}, bf16[16,64,512]{2,1,0:T(8,128)(2,1)}, u32[]{:S(2)}, u32[]{:S(2)}) collective-permute-start(bf16[16,64,512]{2,1,0:T(8,128)(2,1)} %get-tuple-element.17), channel_id=1, source_target_pairs={{0,48},{16,0},{32,16},{48,32},{1,49},{17,1},{33,17},{49,33},{2,50}... | collective-permute-start | bytes 3145736 | tf_op jit(solution)/shard_map/ppermute | solution.py:267
  93.3 1.0 copy-start.1
  139.2 13.2 %all-to-all-start.2 = ((f32[16,8,128]{2,1,0:T(8,128)}), f32[16,8,128]{2,1,0:T(8,128)S(1)}, u32[]{:S(2)}, u32[]{:S(2)}) async-start(f32[16,8,128]{2,1,0:T(8,128)} %shard_map.68), calls=%async_computation.2 | async-start | bytes 131072 | tf_op jit(solution)/shard_map/all_to_all | solution.py:288
  152.4 0.6 copy-start.2
Sparse Core Ops, SparseCore 0:
  10.3 68.7 all-gather.1
Sparse Core Ops, SparseCore 1:
  12.1 67.0 reduce-scatter.1

commit v5 on v4

v5 whole, which is shorter than its diff:
```python
import functools

import jax
import jax.numpy as jnp
from jax import lax
from jax.experimental import pallas as pl
from jax.experimental.pallas import tpu as pltpu
from jax.sharding import Mesh, PartitionSpec as P

Y, X, Z, C = 8, 4, 8, 2
T = Z * C
GROUPS = Y * X
LIMIT = 2
CODE_ROWS = 16
NT = (((1,), (1,)), ((), ()))


def spot():
    return lax.axis_index("y"), lax.axis_index("x")


def dispatch_kernel(plan, down, up, *refs):
    outs, (held, held_up, staged, picked_rows, picked, in_sems, out_sems, picked_sem) = refs[:X], refs[X:]
    resident, _, width = down.shape
    y, x = spot()
    pieces = in_sems.shape[0] - 1
    part = resident // pieces

    def read(i):
        if i == pieces:
            return pltpu.make_async_copy(up, held_up, in_sems.at[i])
        rows = pl.ds(i * part, part)
        return pltpu.make_async_copy(down.at[rows], held.at[rows], in_sems.at[i])

    def write(e):
        return pltpu.make_async_copy(staged.at[e], outs[e], out_sems.at[e])

    for i in range(pieces + 1):
        read(i).start()
    table = plan[...]
    home = table // resident
    number = table - home * resident
    mine = (home == y * X + x).astype(jnp.int32)
    after = jnp.concatenate([jnp.zeros((mine.shape[0], 1), jnp.int32), mine[:, :-1]], axis=1)
    first = jnp.sum(mine * (1 - after) * number, axis=1, keepdims=True)
    second = jnp.sum(mine * after * number, axis=1, keepdims=True)
    lane = lax.broadcasted_iota(jnp.int32, picked_rows.shape, 1)
    picked_rows[...] = jnp.where(lane == 0, first, jnp.where(lane == 1, second, 0))
    to_scalars = pltpu.make_async_copy(picked_rows, picked, picked_sem)
    to_scalars.start()
    to_scalars.wait()
    for i in range(pieces + 1):
        read(i).wait()
    for e in range(X):
        column = lax.rem(x + e, X)
        for row in range(Y):
            for j in range(LIMIT):
                wanted = picked[row * X + column, j]
                staged[e, row * LIMIT + j, :, :width] = held[wanted]
                staged[e, row * LIMIT + j, :, width:] = held_up[wanted]
        write(e).start()
    for e in range(X):
        write(e).wait()


def dispatch(plan, down, up):
    vmem = pl.BlockSpec(memory_space=pltpu.VMEM)
    hbm = pl.BlockSpec(memory_space=pl.ANY)
    shape = (Y * LIMIT, down.shape[1], down.shape[2] + up.shape[2])
    return pl.pallas_call(
        dispatch_kernel,
        out_shape=(jax.ShapeDtypeStruct(shape, down.dtype),) * X,
        in_specs=[vmem, hbm, hbm],
        out_specs=(hbm,) * X,
        scratch_shapes=[
            pltpu.VMEM(down.shape, down.dtype),
            pltpu.VMEM(up.shape, up.dtype),
            pltpu.VMEM((X,) + shape, down.dtype),
            pltpu.VMEM((GROUPS, 128), jnp.int32),
            pltpu.SMEM((GROUPS, 128), jnp.int32),
            pltpu.SemaphoreType.DMA((5,)),
            pltpu.SemaphoreType.DMA((X,)),
            pltpu.SemaphoreType.DMA,
        ],
        cost_estimate=pl.CostEstimate(flops=0, bytes_accessed=6 * down.size, transcendentals=0),
    )(plan, down, up)


def prepare_kernel(resident, plan, slots, rows, out, code_out, sent, sems):
    y, x = spot()
    height, width = rows.shape
    slot = slots[...]
    code = slot
    before = jnp.int32(-1)
    for k in range(plan.shape[1]):
        home = plan[y * X + x, k] // resident
        again = (home == before).astype(jnp.int32)
        code = jnp.where(slot == resident + k, resident + home * LIMIT + again, code)
        before = home
    code_out[...] = code
    sent[0:height, :] = rows[...]
    wide = jnp.concatenate([code.astype(jnp.float32), jnp.zeros((1, width - height), jnp.float32)], axis=1)
    sent[height:, :] = jnp.broadcast_to(wide, (CODE_ROWS, width)).astype(sent.dtype)
    copies = [pltpu.make_async_copy(sent, out.at[i], sems.at[i]) for i in range(Y)]
    for copy in copies:
        copy.start()
    for copy in copies:
        copy.wait()


def prepare(resident, plan, slots, rows):
    height, width = rows.shape
    smem = pl.BlockSpec(memory_space=pltpu.SMEM)
    vmem = pl.BlockSpec(memory_space=pltpu.VMEM)
    return pl.pallas_call(
        functools.partial(prepare_kernel, resident),
        out_shape=(
            jax.ShapeDtypeStruct((Y, height + CODE_ROWS, width), rows.dtype),
            jax.ShapeDtypeStruct(slots.shape, jnp.int32),
        ),
        in_specs=[smem, vmem, vmem],
        out_specs=(pl.BlockSpec(memory_space=pl.ANY), vmem),
        scratch_shapes=[
            pltpu.VMEM((height + CODE_ROWS, width), rows.dtype),
            pltpu.SemaphoreType.DMA((Y,)),
        ],
        cost_estimate=pl.CostEstimate(flops=0, bytes_accessed=2 * Y * rows.size, transcendentals=0),
    )(plan, slots, rows)


def base_kernel(rows, weight, keep, give):
    product = jnp.dot(rows[...], weight[...], preferred_element_type=jnp.float32)
    width = keep.shape[-1]
    left, right = product[:, :width], product[:, width:]
    first = lax.axis_index("c") == 0
    keep[0] = jnp.where(first, left, right)
    give[0] = jnp.where(first, right, left)


def base_product(rows, weight):
    count, depth = rows.shape
    width = weight.shape[1] // T
    shape = jax.ShapeDtypeStruct((Z, count, width), jnp.float32)
    block = pl.BlockSpec((1, count, width), lambda i: (i, 0, 0))
    return pl.pallas_call(
        base_kernel,
        grid=(Z,),
        out_shape=(shape, shape),
        in_specs=[
            pl.BlockSpec((count, depth), lambda i: (0, 0)),
            pl.BlockSpec((depth, C * width), lambda i: (0, i)),
        ],
        out_specs=(block, block),
        cost_estimate=pl.CostEstimate(
            flops=2 * rows.size * weight.shape[1], bytes_accessed=2 * weight.size + 8 * Z * count * width, transcendentals=0
        ),
    )(rows, weight)


def halve_kernel(bit, mine, arrived, keep, give):
    half = keep.shape[0]
    side = lax.rem(lax.axis_index("z") // bit, 2)
    for i in range(half):
        at = side * half + i
        keep[i] = mine[at] + arrived[at]
        at = (1 - side) * half + i
        give[i] = mine[at] + arrived[at]


def halve(bit, mine, arrived):
    vmem = pl.BlockSpec(memory_space=pltpu.VMEM)
    shape = jax.ShapeDtypeStruct((mine.shape[0] // 2,) + mine.shape[1:], jnp.float32)
    return pl.pallas_call(
        functools.partial(halve_kernel, bit),
        out_shape=(shape, shape),
        in_specs=[vmem, vmem],
        out_specs=(vmem, vmem),
        cost_estimate=pl.CostEstimate(flops=mine.size, bytes_accessed=12 * mine.size, transcendentals=0),
    )(mine, arrived)


def turn_kernel(*refs):
    arrived, outs, (sems,) = refs[:X], refs[X:-1], refs[-1:]
    y, _ = spot()
    width = outs[0].shape[-1]
    copies = []
    for d in range(Y):
        row = lax.rem(y + d, Y)
        for e in range(X):
            source = arrived[e].at[pl.ds(row * LIMIT, LIMIT), :, pl.ds(arrived[e].shape[-1] - width, width)]
            target = outs[d].at[pl.ds(e * LIMIT, LIMIT)]
            copies.append(pltpu.make_async_copy(source, target, sems.at[d, e]))
    for copy in copies:
        copy.start()
    for copy in copies:
        copy.wait()


def turn(width, arrived):
    hbm = pl.BlockSpec(memory_space=pl.ANY)
    vmem = pl.BlockSpec(memory_space=pltpu.VMEM)
    shape = jax.ShapeDtypeStruct((X * LIMIT, arrived[0].shape[1], width), arrived[0].dtype)
    return pl.pallas_call(
        turn_kernel,
        out_shape=(shape,) * Y,
        in_specs=[hbm] * X,
        out_specs=(vmem,) * Y,
        scratch_shapes=[pltpu.SemaphoreType.DMA((Y, X))],
        cost_estimate=pl.CostEstimate(flops=0, bytes_accessed=4 * Y * shape.size, transcendentals=0),
    )(*arrived)


def local_kernel(code, rows, down, out):
    rank = out.shape[0]
    resident = down.shape[0] // rank
    total = jnp.zeros(out.shape, jnp.float32)
    step = 4
    for first in range(0, resident, step):
        product = lax.dot_general(
            down[first * rank : (first + step) * rank, :], rows[...], NT, preferred_element_type=jnp.float32
        )
        for k in range(step):
            total = total + jnp.where(code[...] == first + k, product[k * rank : (k + 1) * rank, :], 0.0)
    out[...] = total


def local_shrink(code, rows, down):
    resident, rank, width = down.shape
    vmem = pl.BlockSpec(memory_space=pltpu.VMEM)
    return pl.pallas_call(
        local_kernel,
        out_shape=jax.ShapeDtypeStruct((rank, rows.shape[0]), jnp.float32),
        in_specs=[vmem] * 3,
        out_specs=vmem,
        cost_estimate=pl.CostEstimate(
            flops=2 * rows.size * resident * rank, bytes_accessed=2 * down.size, transcendentals=0
        ),
    )(code, rows, down.reshape(resident * rank, width))


def imported_kernel(resident, rows, *refs):
    arrived, (own, out, rows_held, down_held, sems) = refs[:X], refs[X:]
    rank, count = own.shape
    lanes = out.shape[-1]
    width = rows.shape[-1]
    y, x = spot()

    def reads(g):
        wanted = pl.ds(g * LIMIT * rank, LIMIT * rank)
        pairs = [(rows.at[g], rows_held.at[g])]
        pairs += [
            (arrived[e].at[wanted, pl.ds(0, width)], down_held.at[g, pl.ds(e * LIMIT * rank, LIMIT * rank)])
            for e in range(X)
        ]
        return [pltpu.make_async_copy(a, b, sems.at[g, i]) for i, (a, b) in enumerate(pairs)]

    for g in range(Y):
        for read in reads(g):
            read.start()
    for g in range(Y):
        for read in reads(g):
            read.wait()
        code = rows_held[g, count : count + 1, :count].astype(jnp.float32)
        total = jnp.where(y == g, own[...], 0.0)
        product = lax.dot_general(
            down_held[g], rows_held[g, 0:count, :], NT, preferred_element_type=jnp.float32
        )
        for e in range(X):
            home = y * X + lax.rem(x - e + X, X)
            for j in range(LIMIT):
                at = (e * LIMIT + j) * rank
                hit = code == (resident + home * LIMIT + j).astype(jnp.float32)
                total = total + jnp.where(hit, product[at : at + rank, :], 0.0)
        for i in range(rank // 8):
            for k in range(count // lanes):
                out[g, i * (count // lanes) + k] = total[i * 8 : (i + 1) * 8, k * lanes : (k + 1) * lanes]


def imported_shrink(resident, rows, arrived, own):
    rank, count = own.shape
    height, width = rows.shape[1:]
    wide = arrived[0].shape[-1]
    blocks = rank * count // 1024
    vmem = pl.BlockSpec(memory_space=pltpu.VMEM)
    hbm = pl.BlockSpec(memory_space=pl.ANY)
    return pl.pallas_call(
        functools.partial(imported_kernel, resident),
        out_shape=jax.ShapeDtypeStruct((Y, blocks, 8, 128), jnp.float32),
        in_specs=[hbm] * (1 + X) + [vmem],
        out_specs=vmem,
        scratch_shapes=[
            pltpu.VMEM((Y, height, width), rows.dtype),
            pltpu.VMEM((Y, X * LIMIT * rank, width), rows.dtype),
            pltpu.SemaphoreType.DMA((Y, X + 1)),
        ],
        cost_estimate=pl.CostEstimate(
            flops=2 * X * arrived[0].size * count,
            bytes_accessed=2 * (X * arrived[0].size + rows.size),
            transcendentals=0,
        ),
    )(rows, *[part.reshape(-1, wide) for part in arrived], own)


def add_kernel(parts, out):
    total = jnp.sum(parts[...], axis=0)
    for t in range(out.shape[0]):
        out[t] = total


def add_and_spread(parts):
    vmem = pl.BlockSpec(memory_space=pltpu.VMEM)
    return pl.pallas_call(
        add_kernel,
        out_shape=jax.ShapeDtypeStruct((T,) + parts.shape[1:], jnp.float32),
        in_specs=[vmem],
        out_specs=vmem,
    )(parts)


def expand_kernel(shrink, code, mine, arrived, up, *refs):
    tables, out = refs[:-1], refs[-1]
    count = out.shape[0]
    lanes = count // 128
    rank = shrink.shape[0] // lanes * 8
    resident = up.shape[0]
    y, x = spot()
    imported = code[...] - resident
    home = imported // LIMIT
    d = (y - home // X + Y) % Y
    e = (x - home % X + X) % X
    at = jnp.where(imported < 0, code[...], resident + (d * X + e) * LIMIT + imported % LIMIT)
    rows = jnp.concatenate(
        [jnp.concatenate([shrink[i * lanes + k] for k in range(lanes)], axis=1) for i in range(rank // 8)], axis=0
    )
    rows = jnp.transpose(rows)
    column = jnp.transpose(jnp.broadcast_to(at, (8, count)).astype(jnp.float32))[:, :1]
    pair = jnp.concatenate([rows, rows], axis=1)
    high = pair.astype(jnp.bfloat16).astype(jnp.float32)
    low = pair - high
    half = lax.broadcasted_iota(jnp.int32, pair.shape, 1) // rank
    wanted = jnp.broadcast_to(column, pair.shape) - half.astype(jnp.float32)
    both = jnp.concatenate([high, low], axis=0)
    wanted = jnp.concatenate([wanted, wanted], axis=0)
    total = jnp.zeros((2 * count, out.shape[1]), jnp.float32)
    step = 4
    start = 0
    for table in (up,) + tables:
        for first in range(0, table.shape[0] // 2, step):
            placed = jnp.concatenate(
                [
                    jnp.where(wanted == float(start + 2 * p), both, 0.0).astype(jnp.bfloat16)
                    for p in range(first, first + step)
                ],
                axis=1,
            )
            maps = table[2 * first : 2 * (first + step)].reshape(2 * step * rank, out.shape[1])
            total = total + jnp.dot(placed, maps, preferred_element_type=jnp.float32)
        start += table.shape[0]
    base = mine[0] + arrived[0]
    out[...] = (base + (total[:count] + total[count:])).astype(out.dtype)


def expand(shrink, code, mine, arrived, up, tables):
    vmem = pl.BlockSpec(memory_space=pltpu.VMEM)
    return pl.pallas_call(
        expand_kernel,
        out_shape=jax.ShapeDtypeStruct(mine.shape[1:], jnp.bfloat16),
        in_specs=[vmem] * (5 + len(tables)),
        out_specs=vmem,
    )(shrink, code, mine, arrived, up, *tables)


def shift(array, axis, size, by):
    return lax.ppermute(array, axis, [(i, (i + by) % size) for i in range(size)])


def swap(array, axis, size, bit):
    return lax.ppermute(array, axis, [(i, i ^ bit) for i in range(size)])


def shards(inputs, row_adapter_slot, transfer_plan, key_value_weight, adapter_down, adapter_up):
    count = inputs.shape[0]
    resident = adapter_down.shape[0]
    slots = row_adapter_slot.reshape(1, count)

    arrived = dispatch(transfer_plan, adapter_down, adapter_up)
    arrived = [arrived[0]] + [shift(arrived[e], "x", X, e) for e in range(1, X)]
    sent, code = prepare(resident, transfer_plan, slots, inputs)
    rows = lax.all_to_all(sent, "y", 0, 0, tiled=True)

    keep, give = base_product(inputs, key_value_weight)
    other = swap(give, "c", C, 1)
    for bit in (4, 2, 1):
        keep, give = halve(bit, keep, other)
        other = swap(give, "z", Z, bit)

    own = local_shrink(code, inputs, adapter_down)
    parts = imported_shrink(resident, rows, arrived, own)
    parts = lax.all_to_all(parts.reshape(Y * T, 8, 128), ("y", "z", "c"), 0, 0, tiled=True)

    ups = turn(adapter_up.shape[-1], arrived)
    tables = [ups[0]] + [shift(ups[d], "y", Y, d) for d in range(1, Y)]
    shrink = lax.all_to_all(add_and_spread(parts), ("z", "c"), 0, 0, tiled=True)
    return expand(shrink, code, keep, other, adapter_up, tables)


def solution(mesh):
    grid = Mesh(mesh.devices.reshape(Y, X, Z, C), ("y", "x", "z", "c"))
    replica, tensor = ("y", "x"), ("z", "c")
    placed = (
        P(replica, tensor),
        P(replica),
        P(),
        P(tensor, None),
        P(replica, None, tensor),
        P(replica, None, tensor),
    )
    return jax.shard_map(
        shards, mesh=grid, in_specs=placed, out_specs=P(replica, tensor), check_vma=False
    )
```

time: 165 us -> 209 us (1.27)
  starting transfers between devices: 26.4 us -> 86.3 us
  blocking collectives: 36.1 us -> 0 us
  waiting for transfers between devices: 58.2 us -> 78 us
  Pallas kernels: 23.5 us -> 39.7 us
  between operations: 14.9 us -> 0.36 us
  matrix products: 3 us -> 0 us
    all_to_all x1 -> x0, blocking collectives: 36.1 us -> none  [shards(): lax.all_to_all(parts.reshape(Y * T, 8, 128), ('y', 'z', 'c'), 0, 0, tiled...]
    ppermute x0 -> x4, waiting for transfers between devices: none -> 30.5 us  [swap(): return lax.ppermute(array, axis, [(i, i ^ bit) for i in range(size)])]
    ppermute x3 -> x10, starting transfers between devices: 10.5 us -> 36.7 us  [shift(): lax.ppermute(array, axis, [(i, (i + by) % size) for i in range(size)])]
    pallas_call x2 -> x7, Pallas kernels: 6.67 us -> 22.9 us  [the longest x3 6.53 us: halve(): pl.pallas_call(functools.partial(halve_kernel, bit), out_shape=(shape, sh...]
    ppermute x0 -> x4, starting transfers between devices: none -> 16 us  [swap(): return lax.ppermute(array, axis, [(i, i ^ bit) for i in range(size)])]
    all_to_all x1 -> x2, starting transfers between devices: 10.5 us -> 26 us  [the longest x1 18.3 us: shards(): lax.all_to_all(parts.reshape(Y * T, 8, 128), ('y', 'z', 'c'), 0, 0, tiled...]
    ppermute x3 -> x10, waiting for transfers between devices: 49.6 us -> 39.9 us  [shift(): lax.ppermute(array, axis, [(i, (i + by) % size) for i in range(size)])]
    dot_general x1 -> x0, matrix products: 3 us -> none  [shards(): jnp.dot(inputs, key_value_weight, preferred_element_type=jnp.float32)]
  transfers between devices with their start and end apart: 7 -> 17, of which waited for: 4 -> 5; matrix products, arithmetic and copies ran while one was open for 2% -> 0% of each run, Pallas kernels for 12% -> 16%
where the time goes in v5:
time: 209 us; the launch traced here: 208 us
  starting transfers between devices  86.3 us (41%)
  waiting for transfers between devices  78 us (37%)
  Pallas kernels  39.7 us (19%)
  local copies, waits for them, and re-layouts  3.57 us (2%)
    ppermute x10, waiting for transfers between devices, shift(): lax.ppermute(array, axis, [(i, (i + by) % size) for i in range(size)])  39.9 us
    ppermute x10, starting transfers between devices, shift(): lax.ppermute(array, axis, [(i, (i + by) % size) for i in range(size)])  36.7 us
    ppermute x4, waiting for transfers between devices, swap(): return lax.ppermute(array, axis, [(i, i ^ bit) for i in range(size)])  30.5 us
    all_to_all x1, starting transfers between devices, shards(): lax.all_to_all(parts.reshape(Y * T, 8, 128), ('y', 'z', 'c'), 0, 0, tiled...  18.3 us
    ppermute x4, starting transfers between devices, swap(): return lax.ppermute(array, axis, [(i, i ^ bit) for i in range(size)])  16 us
    all_to_all x1, waiting for transfers between devices, shards(): shrink = lax.all_to_all(add_and_spread(parts), ('z', 'c'), 0, 0, tiled=True)  7.71 us
    all_to_all x1, starting transfers between devices, shards(): rows = lax.all_to_all(sent, 'y', 0, 0, tiled=True)  7.66 us
    all_to_all x1, starting transfers between devices, shards(): shrink = lax.all_to_all(add_and_spread(parts), ('z', 'c'), 0, 0, tiled=True)  7.55 us
  transfers between devices with their start and end apart: 17, of which 5 were waited for; matrix products, arithmetic and copies ran while one was open for 0% of the time, Pallas kernels for 16%

profile of v5, /device:TPU:1, one launch (start us, length us, event | category | flops | bytes accessed | tf_op | source)
XLA Modules:
  0.0 207.9 jit_solution(16471385513742646929)
XLA Ops:
  0.0 3.2 %shard_map.64 = (bf16[8,272,512]{2,1,0:T(8,128)(2,1)}, s32[1,256]{1,0:T(1,128)}) custom-call(s32[32,31]{1,0:T(8,128)} %plan.3, s32[1,256]{1,0:T(1,128)} %bitcast.11, bf16[256,512]{1,0:T(8,128)(2,1)} %rows.5), custom_call_target="tpu_custom_call" | custom-call | bytes 2097152 | tf_op jit(solution)/shard_map/pallas_call | solution.py:115
  3.2 7.7 %all-to-all-start = ((bf16[8,272,512]{2,1,0:T(8,128)(2,1)}), bf16[8,272,512]{2,1,0:T(8,128)(2,1)S(1)}, u32[]{:S(2)}, u32[]{:S(2)}) async-start(bf16[8,272,512]{2,1,0:T(8,128)(2,1)} %get-tuple-element.27), calls=%async_computation | async-start | bytes 4456448 | tf_op jit(solution)/shard_map/all_to_all | solution.py:389
  10.9 5.0 %shard_map.65 = (bf16[16,64,640]{2,1,0:T(8,128)(2,1)}, bf16[16,64,640]{2,1,0:T(8,128)(2,1)}, bf16[16,64,640]{2,1,0:T(8,128)(2,1)}, bf16[16,64,640]{2,1,0:T(8,128)(2,1)}) custom-call(s32[32,31]{1,0:T(8,128)} %plan.3, bf16[32,64,512]{2,1,0:T(8,128)(2,1)} %down.1, bf16[32,64,128]{2,1,0:T(8,128)(2,1)} %up.3), custom_call_target="tpu_custom_call" | custom-call | bytes 6291456 | tf_op jit(solution)/shard_map/pallas_call | solution.py:70
  15.8 3.1 %collective-permute-start = (bf16[16,64,640]{2,1,0:T(8,128)(2,1)}, bf16[16,64,640]{2,1,0:T(8,128)(2,1)S(1)}, u32[]{:S(2)}, u32[]{:S(2)}) collective-permute-start(bf16[16,64,640]{2,1,0:T(8,128)(2,1)} %get-tuple-element.29), channel_id=1, source_target_pairs={{0,16},{16,32},{32,48},{48,0},{1,17},{17,33},{33,49},{49,1},{2,18}... | collective-permute-start | bytes 3932168 | tf_op jit(solution)/shard_map/ppermute | solution.py:374
  19.0 4.4 %collective-permute-start.1 = (bf16[16,64,640]{2,1,0:T(8,128)(2,1)}, bf16[16,64,640]{2,1,0:T(8,128)(2,1)}, u32[]{:S(2)}, u32[]{:S(2)}) collective-permute-start(bf16[16,64,640]{2,1,0:T(8,128)(2,1)} %get-tuple-element.30), channel_id=1, source_target_pairs={{0,32},{16,48},{32,0},{48,16},{1,33},{17,49},{33,1},{49,17},{2,34}... | collective-permute-start | bytes 3932168 | tf_op jit(solution)/shard_map/ppermute | solution.py:374
  23.3 3.1 %collective-permute-start.2 = (bf16[16,64,640]{2,1,0:T(8,128)(2,1)}, bf16[16,64,640]{2,1,0:T(8,128)(2,1)}, u32[]{:S(2)}, u32[]{:S(2)}) collective-permute-start(bf16[16,64,640]{2,1,0:T(8,128)(2,1)} %get-tuple-element.31), channel_id=1, source_target_pairs={{0,48},{16,0},{32,16},{48,32},{1,49},{17,1},{33,17},{49,33},{2,50}... | collective-permute-start | bytes 3932168 | tf_op jit(solution)/shard_map/ppermute | solution.py:374
  26.4 6.5 %shard_map.69 = (f32[8,256,128]{2,1,0:T(8,128)}, f32[8,256,128]{2,1,0:T(8,128)}) custom-call(bf16[256,512]{1,0:T(8,128)(2,1)} %rows.5, bf16[512,2048]{1,0:T(8,128)(2,1)} %weight.1), custom_call_target="tpu_custom_call" | custom-call | flops 536870912 | bytes 4194304 | tf_op jit(solution)/shard_map/pallas_call | solution.py:145
  32.9 3.7 %collective-permute-start.3 = (f32[8,256,128]{2,1,0:T(8,128)}, f32[8,256,128]{2,1,0:T(8,128)}, u32[]{:S(2)}, u32[]{:S(2)}) collective-permute-start(f32[8,256,128]{2,1,0:T(8,128)} %get-tuple-element.34), channel_id=1, source_target_pairs={{0,1},{1,0},{2,3},{3,2},{4,5},{5,4},{6,7},{7,6},{8,9},{9,8},{10,11... | collective-permute-start | bytes 3145736 | tf_op jit(solution)/shard_map/ppermute | solution.py:378
  36.6 3.1 %shard_map.66.refs_4_ = f32[64,256]{1,0:T(8,128)} custom-call(s32[1,256]{1,0:T(1,128)} %get-tuple-element.32.code, bf16[256,512]{1,0:T(8,128)(2,1)} %rows.5, bf16[2048,512]{1,0:T(8,128)(2,1)} %bitcast.7), custom_call_target="tpu_custom_call" | custom-call | flops 536870912 | bytes 2097152 | tf_op jit(solution)/shard_map/pallas_call | solution.py:230
  39.7 6.9 %collective-permute-done.refs_1_ = bf16[16,64,640]{2,1,0:T(8,128)(2,1)S(1)} collective-permute-done((bf16[16,64,640]{2,1,0:T(8,128)(2,1)}, bf16[16,64,640]{2,1,0:T(8,128)(2,1)S(1)}, u32[]{:S(2)}, u32[]{:S(2)}) %collective-permute-start) | collective-permute-done | bytes 1310752 | tf_op jit(solution)/shard_map/ppermute | solution.py:374
  46.6 31.1 %collective-permute-done.1.refs_2_ = bf16[16,64,640]{2,1,0:T(8,128)(2,1)} collective-permute-done((bf16[16,64,640]{2,1,0:T(8,128)(2,1)}, bf16[16,64,640]{2,1,0:T(8,128)(2,1)}, u32[]{:S(2)}, u32[]{:S(2)}) %collective-permute-start.1) | collective-permute-done | bytes 1310752 | tf_op jit(solution)/shard_map/ppermute | solution.py:374
  77.7 1.9 collective-permute-done.2.refs_3_
  80.9 6.9 %shard_map.67 = f32[8,16,8,128]{3,2,1,0:T(8,128)} custom-call(bf16[8,272,512]{2,1,0:T(8,128)(2,1)} %copy-done, bf16[1024,640]{1,0:T(8,128)(2,1)} %bitcast.8, bf16[1024,640]{1,0:T(8,128)(2,1)} %bitcast.9, bf16[1024,640]{1,0:T(8,128)(2,1)} %bitcast.3.refs_2_, bf16[1024,640]{1,0:T(8,128)(2,1)} %bitcast.4.refs_3_, f32[64,256]{1,0:T(8,128)} %shard_map.66.refs_4_), custom_call_target="tpu_custom_call" | custom-call | flops 1342177280 | bytes 7471104 | tf_op jit(solution)/shard_map/pallas_call | solution.py:286
  87.8 18.3 %all-to-all-start.1 = ((f32[128,8,128]{2,1,0:T(8,128)}), f32[128,8,128]{2,1,0:T(8,128)S(1)}, u32[]{:S(2)}, u32[]{:S(2)}) async-start(f32[128,8,128]{2,1,0:T(8,128)} %bitcast.10), calls=%async_computation.1 | async-start | bytes 1048576 | tf_op jit(solution)/shard_map/all_to_all | solution.py:399
  106.1 2.7 %shard_map.70 = (f32[4,256,128]{2,1,0:T(8,128)}, f32[4,256,128]{2,1,0:T(8,128)}) custom-call(f32[8,256,128]{2,1,0:T(8,128)} %get-tuple-element.33.mine, f32[8,256,128]{2,1,0:T(8,128)} %collective-permute-done.3.arrived), custom_call_target="tpu_custom_call" | custom-call | flops 262144 | bytes 3145728 | tf_op jit(solution)/shard_map/pallas_call | solution.py:173
  108.8 7.2 %collective-permute-start.4 = (f32[4,256,128]{2,1,0:T(8,128)}, f32[4,256,128]{2,1,0:T(8,128)S(1)}, u32[]{:S(2)}, u32[]{:S(2)}) collective-permute-start(f32[4,256,128]{2,1,0:T(8,128)} %get-tuple-element.36), channel_id=1, source_target_pairs={{0,8},{2,10},{4,12},{6,14},{8,0},{10,2},{12,4},{14,6},{1,9},{3,11}... | collective-permute-start | bytes 1572872 | tf_op jit(solution)/shard_map/ppermute | solution.py:378
  116.0 30.5 %collective-permute-done.4.arrived = f32[4,256,128]{2,1,0:T(8,128)S(1)} collective-permute-done((f32[4,256,128]{2,1,0:T(8,128)}, f32[4,256,128]{2,1,0:T(8,128)S(1)}, u32[]{:S(2)}, u32[]{:S(2)}) %collective-permute-start.4) | collective-permute-done | bytes 524320 | tf_op jit(solution)/shard_map/ppermute | solution.py:378
  147.3 2.1 shard_map.71
  149.4 2.8 %collective-permute-start.5 = (f32[2,256,128]{2,1,0:T(8,128)}, f32[2,256,128]{2,1,0:T(8,128)S(1)}, u32[]{:S(2)}, u32[]{:S(2)}) collective-permute-start(f32[2,256,128]{2,1,0:T(8,128)} %get-tuple-element.38), channel_id=1, source_target_pairs={{0,4},{2,6},{4,0},{6,2},{8,12},{10,14},{12,8},{14,10},{1,5},{3,7},... | collective-permute-start | bytes 786440 | tf_op jit(solution)/shard_map/ppermute | solution.py:378
  152.1 2.5 %shard_map.73 = (bf16[8,64,128]{2,1,0:T(8,128)(2,1)}, bf16[8,64,128]{2,1,0:T(8,128)(2,1)}, bf16[8,64,128]{2,1,0:T(8,128)(2,1)}, bf16[8,64,128]{2,1,0:T(8,128)(2,...) custom-call(bf16[16,64,640]{2,1,0:T(8,128)(2,1)} %get-tuple-element., ...), custom_call_target="tpu_custom_call" | custom-call | bytes 2097152 | tf_op jit(solution)/shard_map/pallas_call | solution.py:203
  154.6 3.3 %collective-permute-start.7 = (bf16[8,64,128]{2,1,0:T(8,128)(2,1)}, bf16[8,64,128]{2,1,0:T(8,128)(2,1)S(1)}, u32[]{:S(2)}, u32[]{:S(2)}) collective-permute-start(bf16[8,64,128]{2,1,0:T(8,128)(2,1)} %get-tuple-element.42), channel_id=1, source_target_pairs={{0,64},{64,128},{128,192},{192,256},{256,320},{320,384},{384,448},... | collective-permute-start | bytes 393224 | tf_op jit(solution)/shard_map/ppermute | solution.py:374
  158.0 3.3 %collective-permute-start.8 = (bf16[8,64,128]{2,1,0:T(8,128)(2,1)}, bf16[8,64,128]{2,1,0:T(8,128)(2,1)S(1)}, u32[]{:S(2)}, u32[]{:S(2)}) collective-permute-start(bf16[8,64,128]{2,1,0:T(8,128)(2,1)} %get-tuple-element.43), channel_id=1, source_target_pairs={{0,128},{64,192},{128,256},{192,320},{256,384},{320,448},{384,0},{... | collective-permute-start | bytes 393224 | tf_op jit(solution)/shard_map/ppermute | solution.py:374
  161.3 3.6 %collective-permute-start.9 = (bf16[8,64,128]{2,1,0:T(8,128)(2,1)}, bf16[8,64,128]{2,1,0:T(8,128)(2,1)S(1)}, u32[]{:S(2)}, u32[]{:S(2)}) collective-permute-start(bf16[8,64,128]{2,1,0:T(8,128)(2,1)} %get-tuple-element.44), channel_id=1, source_target_pairs={{0,192},{64,256},{128,320},{192,384},{256,448},{320,0},{384,64},{4... | collective-permute-start | bytes 393224 | tf_op jit(solution)/shard_map/ppermute | solution.py:374
  164.9 4.2 %collective-permute-start.10 = (bf16[8,64,128]{2,1,0:T(8,128)(2,1)}, bf16[8,64,128]{2,1,0:T(8,128)(2,1)S(1)}, u32[]{:S(2)}, u32[]{:S(2)}) collective-permute-start(bf16[8,64,128]{2,1,0:T(8,128)(2,1)} %get-tuple-element.45), channel_id=1, source_target_pairs={{0,256},{64,320},{128,384},{192,448},{256,0},{320,64},{384,128},{4... | collective-permute-start | bytes 393224 | tf_op jit(solution)/shard_map/ppermute | solution.py:374
  169.1 4.1 %collective-permute-start.11 = (bf16[8,64,128]{2,1,0:T(8,128)(2,1)}, bf16[8,64,128]{2,1,0:T(8,128)(2,1)S(1)}, u32[]{:S(2)}, u32[]{:S(2)}) collective-permute-start(bf16[8,64,128]{2,1,0:T(8,128)(2,1)} %get-tuple-element.46), channel_id=1, source_target_pairs={{0,320},{64,384},{128,448},{192,0},{256,64},{320,128},{384,192},{4... | collective-permute-start | bytes 393224 | tf_op jit(solution)/shard_map/ppermute | solution.py:374
  175.0 5.2 %collective-permute-start.12 = (bf16[8,64,128]{2,1,0:T(8,128)(2,1)}, bf16[8,64,128]{2,1,0:T(8,128)(2,1)S(1)}, u32[]{:S(2)}, u32[]{:S(2)}) collective-permute-start(bf16[8,64,128]{2,1,0:T(8,128)(2,1)} %get-tuple-element.47), channel_id=1, source_target_pairs={{0,384},{64,448},{128,0},{192,64},{256,128},{320,192},{384,256},{4... | collective-permute-start | bytes 393224 | tf_op jit(solution)/shard_map/ppermute | solution.py:374
  180.3 2.4 %collective-permute-start.13 = (bf16[8,64,128]{2,1,0:T(8,128)(2,1)}, bf16[8,64,128]{2,1,0:T(8,128)(2,1)S(1)}, u32[]{:S(2)}, u32[]{:S(2)}) collective-permute-start(bf16[8,64,128]{2,1,0:T(8,128)(2,1)} %get-tuple-element.48), channel_id=1, source_target_pairs={{0,448},{64,0},{128,64},{192,128},{256,192},{320,256},{384,320},{4... | collective-permute-start | bytes 393224 | tf_op jit(solution)/shard_map/ppermute | solution.py:374
  182.7 2.4 %collective-permute-start.6 = (f32[1,256,128]{2,1,0:T(8,128)}, f32[1,256,128]{2,1,0:T(8,128)S(1)}, u32[]{:S(2)}, u32[]{:S(2)}) collective-permute-start(f32[1,256,128]{2,1,0:T(8,128)} %get-tuple-element.40), channel_id=1, source_target_pairs={{0,2},{2,0},{4,6},{6,4},{8,10},{10,8},{12,14},{14,12},{1,3},{3,1},... | collective-permute-start | bytes 393224 | tf_op jit(solution)/shard_map/ppermute | solution.py:378
  185.9 1.8 shard_map.68
  187.7 7.6 %all-to-all-start.2 = ((f32[16,8,128]{2,1,0:T(8,128)}), f32[16,8,128]{2,1,0:T(8,128)S(1)}, u32[]{:S(2)}, u32[]{:S(2)}) async-start(f32[16,8,128]{2,1,0:T(8,128)} %shard_map.68), calls=%async_computation.2 | async-start | bytes 131072 | tf_op jit(solution)/shard_map/all_to_all | solution.py:403
  195.4 7.7 %all-to-all-done.2.shrink = f32[16,8,128]{2,1,0:T(8,128)S(1)} async-done(((f32[16,8,128]{2,1,0:T(8,128)}), f32[16,8,128]{2,1,0:T(8,128)S(1)}, u32[]{:S(2)}, u32[]{:S(2)}) %all-to-all-start.2) | async-done | bytes 65568 | tf_op jit(solution)/shard_map/all_to_all | solution.py:403
  203.7 4.2 %shard_map.74 = bf16[256,128]{1,0:T(8,128)(2,1)} custom-call(f32[16,8,128]{2,1,0:T(8,128)} %copy-done.4, s32[1,256]{1,0:T(1,128)} %get-tuple-element.32.code, f32[1,256,128]{2,1,0:T(8,128)} %get-tuple-element.39.mine, f32[1,256,128]{2,1,0:T(8,128)} %copy-done.13, bf16[32,64,128]{2,1,0:T(8,128)(2,1)} %up.3, bf16[8,64,128]{2,1,0:T(8,128)(2,1)} %get-tuple-element.41.refs_0_, ...), custom_call_target="tpu_custom_call" | custom-call | tf_op jit(solution)/shard_map/pallas_call | solution.py:365
  (41 shorter events, 5.4 us)
Async XLA Ops:
  3.2 76.3 %all-to-all-start = ((bf16[8,272,512]{2,1,0:T(8,128)(2,1)}), bf16[8,272,512]{2,1,0:T(8,128)(2,1)S(1)}, u32[]{:S(2)}, u32[]{:S(2)}) async-start(bf16[8,272,512]{2,1,0:T(8,128)(2,1)} %get-tuple-element.27), calls=%async_computation | async-start | bytes 4456448 | tf_op jit(solution)/shard_map/all_to_all | solution.py:389
  15.8 30.7 %collective-permute-start = (bf16[16,64,640]{2,1,0:T(8,128)(2,1)}, bf16[16,64,640]{2,1,0:T(8,128)(2,1)S(1)}, u32[]{:S(2)}, u32[]{:S(2)}) collective-permute-start(bf16[16,64,640]{2,1,0:T(8,128)(2,1)} %get-tuple-element.29), channel_id=1, source_target_pairs={{0,16},{16,32},{32,48},{48,0},{1,17},{17,33},{33,49},{49,1},{2,18}... | collective-permute-start | bytes 3932168 | tf_op jit(solution)/shard_map/ppermute | solution.py:374
  19.0 58.7 %collective-permute-start.1 = (bf16[16,64,640]{2,1,0:T(8,128)(2,1)}, bf16[16,64,640]{2,1,0:T(8,128)(2,1)}, u32[]{:S(2)}, u32[]{:S(2)}) collective-permute-start(bf16[16,64,640]{2,1,0:T(8,128)(2,1)} %get-tuple-element.30), channel_id=1, source_target_pairs={{0,32},{16,48},{32,0},{48,16},{1,33},{17,49},{33,1},{49,17},{2,34}... | collective-permute-start | bytes 3932168 | tf_op jit(solution)/shard_map/ppermute | solution.py:374
  23.3 56.2 %collective-permute-start.2 = (bf16[16,64,640]{2,1,0:T(8,128)(2,1)}, bf16[16,64,640]{2,1,0:T(8,128)(2,1)}, u32[]{:S(2)}, u32[]{:S(2)}) collective-permute-start(bf16[16,64,640]{2,1,0:T(8,128)(2,1)} %get-tuple-element.31), channel_id=1, source_target_pairs={{0,48},{16,0},{32,16},{48,32},{1,49},{17,1},{33,17},{49,33},{2,50}... | collective-permute-start | bytes 3932168 | tf_op jit(solution)/shard_map/ppermute | solution.py:374
  32.9 73.2 %collective-permute-start.3 = (f32[8,256,128]{2,1,0:T(8,128)}, f32[8,256,128]{2,1,0:T(8,128)}, u32[]{:S(2)}, u32[]{:S(2)}) collective-permute-start(f32[8,256,128]{2,1,0:T(8,128)} %get-tuple-element.34), channel_id=1, source_target_pairs={{0,1},{1,0},{2,3},{3,2},{4,5},{5,4},{6,7},{7,6},{8,9},{9,8},{10,11... | collective-permute-start | bytes 3145736 | tf_op jit(solution)/shard_map/ppermute | solution.py:378
  46.6 33.0 %copy-start.1 = (bf16[16,64,640]{2,1,0:T(8,128)(2,1)}, bf16[16,64,640]{2,1,0:T(8,128)(2,1)S(1)}, u32[]{:S(2)}) copy-start(bf16[16,64,640]{2,1,0:T(8,128)(2,1)S(1)} %collective-permute-done.refs_1_) | copy-start | bytes 3932164
  79.5 1.4 copy-start
  87.8 97.3 %all-to-all-start.1 = ((f32[128,8,128]{2,1,0:T(8,128)}), f32[128,8,128]{2,1,0:T(8,128)S(1)}, u32[]{:S(2)}, u32[]{:S(2)}) async-start(f32[128,8,128]{2,1,0:T(8,128)} %bitcast.10), calls=%async_computation.1 | async-start | bytes 1048576 | tf_op jit(solution)/shard_map/all_to_all | solution.py:399
  108.8 37.7 %collective-permute-start.4 = (f32[4,256,128]{2,1,0:T(8,128)}, f32[4,256,128]{2,1,0:T(8,128)S(1)}, u32[]{:S(2)}, u32[]{:S(2)}) collective-permute-start(f32[4,256,128]{2,1,0:T(8,128)} %get-tuple-element.36), channel_id=1, source_target_pairs={{0,8},{2,10},{4,12},{6,14},{8,0},{10,2},{12,4},{14,6},{1,9},{3,11}... | collective-permute-start | bytes 1572872 | tf_op jit(solution)/shard_map/ppermute | solution.py:378
  146.5 0.8 copy-start.3
  149.4 19.7 %collective-permute-start.5 = (f32[2,256,128]{2,1,0:T(8,128)}, f32[2,256,128]{2,1,0:T(8,128)S(1)}, u32[]{:S(2)}, u32[]{:S(2)}) collective-permute-start(f32[2,256,128]{2,1,0:T(8,128)} %get-tuple-element.38), channel_id=1, source_target_pairs={{0,4},{2,6},{4,0},{6,2},{8,12},{10,14},{12,8},{14,10},{1,5},{3,7},... | collective-permute-start | bytes 786440 | tf_op jit(solution)/shard_map/ppermute | solution.py:378
  154.6 20.4 %collective-permute-start.7 = (bf16[8,64,128]{2,1,0:T(8,128)(2,1)}, bf16[8,64,128]{2,1,0:T(8,128)(2,1)S(1)}, u32[]{:S(2)}, u32[]{:S(2)}) collective-permute-start(bf16[8,64,128]{2,1,0:T(8,128)(2,1)} %get-tuple-element.42), channel_id=1, source_target_pairs={{0,64},{64,128},{128,192},{192,256},{256,320},{320,384},{384,448},... | collective-permute-start | bytes 393224 | tf_op jit(solution)/shard_map/ppermute | solution.py:374
  158.0 22.3 %collective-permute-start.8 = (bf16[8,64,128]{2,1,0:T(8,128)(2,1)}, bf16[8,64,128]{2,1,0:T(8,128)(2,1)S(1)}, u32[]{:S(2)}, u32[]{:S(2)}) collective-permute-start(bf16[8,64,128]{2,1,0:T(8,128)(2,1)} %get-tuple-element.43), channel_id=1, source_target_pairs={{0,128},{64,192},{128,256},{192,320},{256,384},{320,448},{384,0},{... | collective-permute-start | bytes 393224 | tf_op jit(solution)/shard_map/ppermute | solution.py:374
  161.3 21.4 %collective-permute-start.9 = (bf16[8,64,128]{2,1,0:T(8,128)(2,1)}, bf16[8,64,128]{2,1,0:T(8,128)(2,1)S(1)}, u32[]{:S(2)}, u32[]{:S(2)}) collective-permute-start(bf16[8,64,128]{2,1,0:T(8,128)(2,1)} %get-tuple-element.44), channel_id=1, source_target_pairs={{0,192},{64,256},{128,320},{192,384},{256,448},{320,0},{384,64},{4... | collective-permute-start | bytes 393224 | tf_op jit(solution)/shard_map/ppermute | solution.py:374
  164.9 30.4 %collective-permute-start.10 = (bf16[8,64,128]{2,1,0:T(8,128)(2,1)}, bf16[8,64,128]{2,1,0:T(8,128)(2,1)S(1)}, u32[]{:S(2)}, u32[]{:S(2)}) collective-permute-start(bf16[8,64,128]{2,1,0:T(8,128)(2,1)} %get-tuple-element.45), channel_id=1, source_target_pairs={{0,256},{64,320},{128,384},{192,448},{256,0},{320,64},{384,128},{4... | collective-permute-start | bytes 393224 | tf_op jit(solution)/shard_map/ppermute | solution.py:374
  169.1 4.1 %copy-start.5 = (f32[2,256,128]{2,1,0:T(8,128)}, f32[2,256,128]{2,1,0:T(8,128)S(1)}, u32[]{:S(2)}) copy-start(f32[2,256,128]{2,1,0:T(8,128)S(1)} %collective-permute-done.5.arrived) | copy-start | bytes 786436
  169.1 26.2 %collective-permute-start.11 = (bf16[8,64,128]{2,1,0:T(8,128)(2,1)}, bf16[8,64,128]{2,1,0:T(8,128)(2,1)S(1)}, u32[]{:S(2)}, u32[]{:S(2)}) collective-permute-start(bf16[8,64,128]{2,1,0:T(8,128)(2,1)} %get-tuple-element.46), channel_id=1, source_target_pairs={{0,320},{64,384},{128,448},{192,0},{256,64},{320,128},{384,192},{4... | collective-permute-start | bytes 393224 | tf_op jit(solution)/shard_map/ppermute | solution.py:374
  175.0 28.1 %copy-start.6 = (bf16[8,64,128]{2,1,0:T(8,128)(2,1)}, bf16[8,64,128]{2,1,0:T(8,128)(2,1)S(1)}, u32[]{:S(2)}) copy-start(bf16[8,64,128]{2,1,0:T(8,128)(2,1)S(1)} %collective-permute-done.7.refs_1_) | copy-start | bytes 393220
  175.0 20.3 %collective-permute-start.12 = (bf16[8,64,128]{2,1,0:T(8,128)(2,1)}, bf16[8,64,128]{2,1,0:T(8,128)(2,1)S(1)}, u32[]{:S(2)}, u32[]{:S(2)}) collective-permute-start(bf16[8,64,128]{2,1,0:T(8,128)(2,1)} %get-tuple-element.47), channel_id=1, source_target_pairs={{0,384},{64,448},{128,0},{192,64},{256,128},{320,192},{384,256},{4... | collective-permute-start | bytes 393224 | tf_op jit(solution)/shard_map/ppermute | solution.py:374
  180.3 22.8 %copy-start.7 = (bf16[8,64,128]{2,1,0:T(8,128)(2,1)}, bf16[8,64,128]{2,1,0:T(8,128)(2,1)S(1)}, u32[]{:S(2)}) copy-start(bf16[8,64,128]{2,1,0:T(8,128)(2,1)S(1)} %collective-permute-done.8.refs_2_) | copy-start | bytes 393220
  180.3 15.1 %collective-permute-start.13 = (bf16[8,64,128]{2,1,0:T(8,128)(2,1)}, bf16[8,64,128]{2,1,0:T(8,128)(2,1)S(1)}, u32[]{:S(2)}, u32[]{:S(2)}) collective-permute-start(bf16[8,64,128]{2,1,0:T(8,128)(2,1)} %get-tuple-element.48), channel_id=1, source_target_pairs={{0,448},{64,0},{128,64},{192,128},{256,192},{320,256},{384,320},{4... | collective-permute-start | bytes 393224 | tf_op jit(solution)/shard_map/ppermute | solution.py:374
  182.7 20.4 %copy-start.8 = (bf16[8,64,128]{2,1,0:T(8,128)(2,1)}, bf16[8,64,128]{2,1,0:T(8,128)(2,1)S(1)}, u32[]{:S(2)}) copy-start(bf16[8,64,128]{2,1,0:T(8,128)(2,1)S(1)} %collective-permute-done.9.refs_3_) | copy-start | bytes 393220
  182.7 12.6 %collective-permute-start.6 = (f32[1,256,128]{2,1,0:T(8,128)}, f32[1,256,128]{2,1,0:T(8,128)S(1)}, u32[]{:S(2)}, u32[]{:S(2)}) collective-permute-start(f32[1,256,128]{2,1,0:T(8,128)} %get-tuple-element.40), channel_id=1, source_target_pairs={{0,2},{2,0},{4,6},{6,4},{8,10},{10,8},{12,14},{14,12},{1,3},{3,1},... | collective-permute-start | bytes 393224 | tf_op jit(solution)/shard_map/ppermute | solution.py:378
  185.1 0.8 copy-start.2
  187.7 15.4 %all-to-all-start.2 = ((f32[16,8,128]{2,1,0:T(8,128)}), f32[16,8,128]{2,1,0:T(8,128)S(1)}, u32[]{:S(2)}, u32[]{:S(2)}) async-start(f32[16,8,128]{2,1,0:T(8,128)} %shard_map.68), calls=%async_computation.2 | async-start | bytes 131072 | tf_op jit(solution)/shard_map/all_to_all | solution.py:403
  195.3 7.8 %copy-start.9 = (bf16[8,64,128]{2,1,0:T(8,128)(2,1)}, bf16[8,64,128]{2,1,0:T(8,128)(2,1)S(1)}, u32[]{:S(2)}) copy-start(bf16[8,64,128]{2,1,0:T(8,128)(2,1)S(1)} %collective-permute-done.10.refs_4_) | copy-start | bytes 393220
  195.3 7.8 %copy-start.10 = (bf16[8,64,128]{2,1,0:T(8,128)(2,1)}, bf16[8,64,128]{2,1,0:T(8,128)(2,1)S(1)}, u32[]{:S(2)}) copy-start(bf16[8,64,128]{2,1,0:T(8,128)(2,1)S(1)} %collective-permute-done.11.refs_5_) | copy-start | bytes 393220
  195.3 7.8 %copy-start.11 = (bf16[8,64,128]{2,1,0:T(8,128)(2,1)}, bf16[8,64,128]{2,1,0:T(8,128)(2,1)S(1)}, u32[]{:S(2)}) copy-start(bf16[8,64,128]{2,1,0:T(8,128)(2,1)S(1)} %collective-permute-done.12.refs_6_) | copy-start | bytes 393220
  195.3 7.8 %copy-start.12 = (bf16[8,64,128]{2,1,0:T(8,128)(2,1)}, bf16[8,64,128]{2,1,0:T(8,128)(2,1)S(1)}, u32[]{:S(2)}) copy-start(bf16[8,64,128]{2,1,0:T(8,128)(2,1)S(1)} %collective-permute-done.13.refs_7_) | copy-start | bytes 393220
  195.4 7.8 %copy-start.13 = (f32[1,256,128]{2,1,0:T(8,128)}, f32[1,256,128]{2,1,0:T(8,128)S(1)}, u32[]{:S(2)}) copy-start(f32[1,256,128]{2,1,0:T(8,128)S(1)} %collective-permute-done.6.arrived) | copy-start | bytes 393220
  203.1 0.6 copy-start.4

commit v6 on v4

--- a/solution.py
+++ b/solution.py
@@ -12,6 +12,7 @@
 GROUPS = Y * X
 LIMIT = 2
 CODE_ROWS = 16
+MIB = 1024 * 1024
 NT = (((1,), (1,)), ((), ()))
 
 
@@ -81,9 +82,9 @@
     )(plan, down)
 
 
-def pick_up_kernel(picked, plan, slots, up, out, code_out):
-    resident, rank, _ = up.shape
+def prepare_kernel(resident, plan, slots, rows, out, code_out):
     y, x = spot()
+    height, width = rows.shape
     slot = slots[...]
     code = slot
     before = jnp.int32(-1)
@@ -93,30 +94,91 @@
         code = jnp.where(slot == resident + k, resident + home * LIMIT + again, code)
         before = home
     code_out[...] = code
-    lanes = out.shape[2]
-    tail = [code[:, k * lanes : (k + 1) * lanes].astype(jnp.float32) for k in range(code.shape[1] // lanes)]
-    tail.append(jnp.zeros((CODE_ROWS - len(tail), lanes), jnp.float32))
-    tail = jnp.concatenate(tail, axis=0).astype(out.dtype)
+    out[0:height, :] = rows[...]
+    wide = jnp.concatenate([code.astype(jnp.float32), jnp.zeros((1, width - height), jnp.float32)], axis=1)
+    out[height:, :] = jnp.broadcast_to(wide, (CODE_ROWS, width)).astype(out.dtype)
+
+
+def prepare(resident, plan, slots, rows):
+    height, width = rows.shape
+    smem = pl.BlockSpec(memory_space=pltpu.SMEM)
+    vmem = pl.BlockSpec(memory_space=pltpu.VMEM)
+    return pl.pallas_call(
+        functools.partial(prepare_kernel, resident),
+        out_shape=(
+            jax.ShapeDtypeStruct((height + CODE_ROWS, width), rows.dtype),
+            jax.ShapeDtypeStruct(slots.shape, jnp.int32),
+        ),
+        in_specs=[smem, vmem, vmem],
+        out_specs=(vmem, vmem),
+        cost_estimate=pl.CostEstimate(flops=0, bytes_accessed=4 * rows.size, transcendentals=0),
+    )(plan, slots, rows)
+
+
+def pick_up_kernel(picked, up, out):
     for group in range(GROUPS):
         for j in range(LIMIT):
-            out[group, j * rank : (j + 1) * rank, :] = up[picked[group, j]]
-        out[group, LIMIT * rank :, :] = tail
-
-
-def pick_up(picked, plan, slots, up):
+            out[group * LIMIT + j] = up[picked[group, j]]
+
+
+def pick_up(picked, up):
     smem = pl.BlockSpec(memory_space=pltpu.SMEM)
     vmem = pl.BlockSpec(memory_space=pltpu.VMEM)
-    _, rank, width = up.shape
     return pl.pallas_call(
         pick_up_kernel,
-        out_shape=(
-            jax.ShapeDtypeStruct((GROUPS, LIMIT * rank + CODE_ROWS, width), up.dtype),
-            jax.ShapeDtypeStruct(slots.shape, jnp.int32),
+        out_shape=jax.ShapeDtypeStruct((GROUPS * LIMIT,) + up.shape[1:], up.dtype),
+        in_specs=[smem, vmem],
+        out_specs=vmem,
+        cost_estimate=pl.CostEstimate(flops=0, bytes_accessed=6 * up.size, transcendentals=0),
+    )(picked, up)
+
+
+def base_kernel(rows, weight, out):
+    out[...] = jnp.dot(rows[...], weight[...], preferred_element_type=jnp.float32)
+
+
+def base_product(rows, weight):
+    count, depth = rows.shape
+    width = weight.shape[1]
+    step = 512
+    return pl.pallas_call(
+        base_kernel,
+        grid=(width // step,),
+        out_shape=jax.ShapeDtypeStruct((count, width), jnp.float32),
+        in_specs=[
+            pl.BlockSpec((count, depth), lambda i: (0, 0)),
+            pl.BlockSpec((depth, step), lambda i: (0, i)),
+        ],
+        out_specs=pl.BlockSpec((count, step), lambda i: (0, i)),
+        cost_estimate=pl.CostEstimate(
+            flops=2 * rows.size * width, bytes_accessed=2 * weight.size + 4 * count * width, transcendentals=0
         ),
-        in_specs=[smem, smem, vmem, vmem],
-        out_specs=(vmem, vmem),
-        cost_estimate=pl.CostEstimate(flops=0, bytes_accessed=6 * up.size, transcendentals=0),
-    )(picked, plan, slots, up)
+    )(rows, weight)
+
+
+def turn_kernel(arrived, *refs):
+    outs, (held, sem) = refs[:X], refs[X:]
+    _, x = spot()
+    copy = pltpu.make_async_copy(arrived, held, sem)
+    copy.start()
+    copy.wait()
+    for e in range(X):
+        column = lax.rem(x + e, X)
+        for row in range(Y):
+            for j in range(LIMIT):
+                outs[e][row * LIMIT + j] = held[(row * X + column) * LIMIT + j]
+
+
+def turn(arrived):
+    vmem = pl.BlockSpec(memory_space=pltpu.VMEM)
+    return pl.pallas_call(
+        turn_kernel,
+        out_shape=(jax.ShapeDtypeStruct((Y * LIMIT,) + arrived.shape[1:], arrived.dtype),) * X,
+        in_specs=[pl.BlockSpec(memory_space=pltpu.HBM)],
+        out_specs=(vmem,) * X,
+        scratch_shapes=[pltpu.VMEM(arrived.shape, arrived.dtype), pltpu.SemaphoreType.DMA],
+        cost_estimate=pl.CostEstimate(flops=0, bytes_accessed=4 * arrived.size, transcendentals=0),
+    )(arrived)
 
 
 def local_kernel(code, rows, down, out):
@@ -147,16 +209,15 @@
     )(code, rows, down.reshape(resident * rank, width))
 
 
-def imported_kernel(resident, rows, codes, *refs):
-    down, (own, out, rows_held, codes_held, down_held, sems) = refs[:X], refs[X:]
+def imported_kernel(resident, rows, *refs):
+    down, (own, out, rows_held, down_held, sems) = refs[:X], refs[X:]
     rank, count = own.shape
     lanes = out.shape[-1]
     y, x = spot()
 
     def reads(g):
         wanted = pl.ds(g * LIMIT * rank, LIMIT * rank)
-        pairs = [(rows.at[pl.ds(g * count, count)], rows_held.at[g])]
-        pairs.append((codes.at[g * X + x, pl.ds(LIMIT * rank, CODE_ROWS)], codes_held.at[g]))
+        pairs = [(rows.at[g], rows_held.at[g])]
         pairs += [(down[e].at[wanted], down_held.at[g, pl.ds(e * LIMIT * rank, LIMIT * rank)]) for e in range(X)]
         return [pltpu.make_async_copy(a, b, sems.at[g, i]) for i, (a, b) in enumerate(pairs)]
 
@@ -166,10 +227,11 @@
     for g in range(Y):
         for read in reads(g):
             read.wait()
-        tail = codes_held[g].astype(jnp.float32)
-        code = jnp.concatenate([tail[k : k + 1] for k in range(count // lanes)], axis=1)
+        code = rows_held[g, count : count + 1, :count].astype(jnp.float32)
         total = jnp.where(y == g, own[...], 0.0)
-        product = lax.dot_general(down_held[g], rows_held[g], NT, preferred_element_type=jnp.float32)
+        product = lax.dot_general(
+            down_held[g], rows_held[g, 0:count, :], NT, preferred_element_type=jnp.float32
+        )
         for e in range(X):
             home = y * X + lax.rem(x - e + X, X)
             for j in range(LIMIT):
@@ -181,27 +243,28 @@
                 out[g, i * (count // lanes) + k] = total[i * 8 : (i + 1) * 8, k * lanes : (k + 1) * lanes]
 
 
-def imported_shrink(resident, rows, codes, down, own):
+def imported_shrink(resident, rows, down, own):
     rank, count = own.shape
-    width = rows.shape[-1]
+    height, width = rows.shape[1:]
     blocks = rank * count // 1024
     vmem = pl.BlockSpec(memory_space=pltpu.VMEM)
-    hbm = pl.BlockSpec(memory_space=pl.ANY)
+    hbm = pl.BlockSpec(memory_space=pltpu.HBM)
     return pl.pallas_call(
         functools.partial(imported_kernel, resident),
         out_shape=jax.ShapeDtypeStruct((Y, blocks, 8, 128), jnp.float32),
-        in_specs=[hbm] * (2 + X) + [vmem],
+        in_specs=[hbm] * (1 + X) + [vmem],
         out_specs=vmem,
         scratch_shapes=[
-            pltpu.VMEM((Y, count, width), rows.dtype),
-            pltpu.VMEM((Y, CODE_ROWS, codes.shape[-1]), codes.dtype),
+            pltpu.VMEM((Y, height, width), rows.dtype),
             pltpu.VMEM((Y, X * LIMIT * rank, width), rows.dtype),
-            pltpu.SemaphoreType.DMA((Y, X + 2)),
+            pltpu.SemaphoreType.DMA((Y, X + 1)),
         ],
         cost_estimate=pl.CostEstimate(
-            flops=2 * X * down[0].size * count, bytes_accessed=2 * (X * down[0].size + rows.size), transcendentals=0
+            flops=2 * X * down[0].size * count,
+            bytes_accessed=2 * (X * down[0].size + rows.size),
+            transcendentals=0,
         ),
-    )(rows, codes, *[part.reshape(-1, width) for part in down], own)
+    )(rows, *[part.reshape(-1, width) for part in down], own)
 
 
 def add_kernel(parts, out):
@@ -217,18 +280,33 @@
         out_shape=jax.ShapeDtypeStruct((T,) + parts.shape[1:], jnp.float32),
         in_specs=[vmem],
         out_specs=vmem,
+        compiler_params=pltpu.CompilerParams(vmem_limit_bytes=2 * MIB),
     )(parts)
 
 
-def expand_kernel(shrink, code, base, up, up_in, out):
+def expand_kernel(shrink, code, base, up, *refs):
+    tables, (out, held, base_held, sems) = refs[:X], refs[X:]
     count = out.shape[0]
     lanes = count // 128
     rank = shrink.shape[0] // lanes * 8
+    resident, imported_each = up.shape[0], tables[0].shape[0]
+    copies = [pltpu.make_async_copy(up, held.at[pl.ds(0, resident)], sems.at[0])]
+    for e in range(X):
+        place = pl.ds(resident + e * imported_each, imported_each)
+        copies.append(pltpu.make_async_copy(tables[e], held.at[place], sems.at[1 + e]))
+    copies.append(pltpu.make_async_copy(base, base_held, sems.at[1 + X]))
+    for copy in copies:
+        copy.start()
     rows = jnp.concatenate(
         [jnp.concatenate([shrink[i * lanes + k] for k in range(lanes)], axis=1) for i in range(rank // 8)], axis=0
     )
     rows = jnp.transpose(rows)
-    column = jnp.transpose(jnp.broadcast_to(code[...], (8, count)).astype(jnp.float32))[:, :1]
+    _, x = spot()
+    imported = code[...] - resident
+    home = imported // LIMIT
+    e = (x - home % X + X) % X
+    at = jnp.where(imported < 0, code[...], resident + (e * Y + home // X) * LIMIT + imported % LIMIT)
+    column = jnp.transpose(jnp.broadcast_to(at, (8, count)).astype(jnp.float32))[:, :1]
     pair = jnp.concatenate([rows, rows], axis=1)
     high = pair.astype(jnp.bfloat16).astype(jnp.float32)
     low = pair - high
@@ -238,9 +316,12 @@
     wanted = jnp.concatenate([wanted, wanted], axis=0)
     total = jnp.zeros((2 * count, out.shape[1]), jnp.float32)
     step = 4
-    pairs = [up[2 * p : 2 * p + 2].reshape(2 * rank, -1) for p in range(up.shape[0] // 2)]
-    pairs += [up_in[p, : 2 * rank, :] for p in range(up_in.shape[0])]
-    for first in range(0, len(pairs), step):
+    bounds = [resident + e * imported_each for e in range(X + 1)]
+    for first in range(0, held.shape[0] // 2, step):
+        if first == 0:
+            copies[0].wait()
+        if 2 * first in bounds:
+            copies[1 + bounds.index(2 * first)].wait()
         placed = jnp.concatenate(
             [
                 jnp.where(wanted == float(2 * p), both, 0.0).astype(jnp.bfloat16)
@@ -248,19 +329,28 @@
             ],
             axis=1,
         )
-        maps = jnp.concatenate(pairs[first : first + step], axis=0)
+        maps = held[2 * first : 2 * (first + step)].reshape(2 * step * rank, out.shape[1])
         total = total + jnp.dot(placed, maps, preferred_element_type=jnp.float32)
-    out[...] = (base[...] + (total[:count] + total[count:])).astype(out.dtype)
-
-
-def expand(shrink, code, base, up, up_in):
-    vmem = pl.BlockSpec(memory_space=pltpu.VMEM)
+    copies[-1].wait()
+    out[...] = (base_held[...] + (total[:count] + total[count:])).astype(out.dtype)
+
+
+def expand(shrink, code, base, up, tables):
+    vmem = pl.BlockSpec(memory_space=pltpu.VMEM)
+    hbm = pl.BlockSpec(memory_space=pltpu.HBM)
+    maps = up.shape[0] + X * tables[0].shape[0]
     return pl.pallas_call(
         expand_kernel,
         out_shape=jax.ShapeDtypeStruct(base.shape, jnp.bfloat16),
-        in_specs=[vmem] * 5,
-        out_specs=vmem,
-    )(shrink, code, base, up, up_in)
+        in_specs=[vmem, vmem] + [hbm] * (2 + X),
+        out_specs=vmem,
+        scratch_shapes=[
+            pltpu.VMEM((maps,) + up.shape[1:], up.dtype),
+            pltpu.VMEM(base.shape, base.dtype),
+            pltpu.SemaphoreType.DMA((2 + X,)),
+        ],
+        compiler_params=pltpu.CompilerParams(vmem_limit_bytes=12 * MIB),
+    )(shrink, code, base, up, *tables)
 
 
 def shift(array, axis, size, by):
@@ -272,21 +362,23 @@
     resident = adapter_down.shape[0]
     slots = row_adapter_slot.reshape(1, count)
 
-    rows = lax.all_gather(inputs, "y", tiled=True)
+    sent, code = prepare(resident, transfer_plan, slots, inputs)
+    rows = lax.all_gather(sent, "y")
     *down, picked = dispatch(transfer_plan, adapter_down)
     down = [down[0]] + [shift(down[e], "x", X, e) for e in range(1, X)]
 
-    up_out, code = pick_up(picked, transfer_plan, slots, adapter_up)
-    up_in = lax.all_to_all(up_out, ("y", "x"), 0, 0, tiled=True)
-
-    base_part = jnp.dot(inputs, key_value_weight, preferred_element_type=jnp.float32)
+    ups = turn(lax.all_to_all(pick_up(picked, adapter_up), "y", 0, 0, tiled=True))
+    tables = [ups[0]] + [shift(ups[e], "x", X, e) for e in range(1, X)]
+
+    late, picked = lax.optimization_barrier((inputs, picked))
+    base_part = base_product(late, key_value_weight)
     base = lax.psum_scatter(base_part, ("z", "c"), scatter_dimension=1, tiled=True)
-    own = local_shrink(code, inputs, adapter_down)
-
-    parts = imported_shrink(resident, rows, up_in, down, own)
+    own = local_shrink(code, late, adapter_down)
+
+    parts = imported_shrink(resident, rows, down, own)
     parts = lax.all_to_all(parts.reshape(Y * T, 8, 128), ("y", "z", "c"), 0, 0, tiled=True)
     shrink = lax.all_to_all(add_and_spread(parts), ("z", "c"), 0, 0, tiled=True)
-    return expand(shrink, code, base, adapter_up, up_in)
+    return expand(shrink, code, base, adapter_up, tables)
 
 
 def solution(mesh):

time: 165 us -> 154 us (0.933)
  blocking collectives: 36.1 us -> 0 us
  starting transfers between devices: 26.4 us -> 52.6 us
  Pallas kernels: 23.5 us -> 30.2 us
  waiting for transfers between devices: 58.2 us -> 53.3 us
  matrix products: 3 us -> 0 us
    all_to_all x1 -> x0, blocking collectives: 36.1 us -> none  [shards(): lax.all_to_all(parts.reshape(Y * T, 8, 128), ('y', 'z', 'c'), 0, 0, tiled...]
    all_to_all x1 -> x2, starting transfers between devices: 10.5 us -> 26.1 us  [the longest x1 18.4 us: shards(): lax.all_to_all(parts.reshape(Y * T, 8, 128), ('y', 'z', 'c'), 0, 0, tiled...]
    ppermute x3 -> x6, waiting for transfers between devices: 49.6 us -> 38.8 us  [shift(): lax.ppermute(array, axis, [(i, (i + by) % size) for i in range(size)])]
    ppermute x3 -> x6, starting transfers between devices: 10.5 us -> 21.1 us  [shift(): lax.ppermute(array, axis, [(i, (i + by) % size) for i in range(size)])]
    pallas_call x1 -> x4, Pallas kernels: 2.53 us -> 10.8 us  [the longest x1 4.48 us: base_product(): pl.pallas_call(base_kernel, grid=(width // step,), out_shape=jax.ShapeDty...]
    all_to_all x1 -> x2, waiting for transfers between devices: 0.01 us -> 6.61 us  [the longest x1 6.61 us: shards(): lax.all_to_all(parts.reshape(Y * T, 8, 128), ('y', 'z', 'c'), 0, 0, tiled...]
    dot_general x1 -> x0, matrix products: 3 us -> none  [shards(): jnp.dot(inputs, key_value_weight, preferred_element_type=jnp.float32)]
  transfers between devices with their start and end apart: 7 -> 11, of which waited for: 4 -> 5; matrix products, arithmetic and copies ran while one was open for 2% -> 0% of each run, Pallas kernels for 12% -> 16%
where the time goes in v6:
time: 154 us; the launch traced here: 153 us
  waiting for transfers between devices  53.3 us (35%)
  starting transfers between devices  52.6 us (34%)
  Pallas kernels  30.2 us (20%)
  between operations  15 us (10%)
  local copies, waits for them, and re-layouts  1.88 us (1%)
    ppermute x6, waiting for transfers between devices, shift(): lax.ppermute(array, axis, [(i, (i + by) % size) for i in range(size)])  38.8 us
    ppermute x6, starting transfers between devices, shift(): lax.ppermute(array, axis, [(i, (i + by) % size) for i in range(size)])  21.1 us
    all_to_all x1, starting transfers between devices, shards(): lax.all_to_all(parts.reshape(Y * T, 8, 128), ('y', 'z', 'c'), 0, 0, tiled...  18.4 us
    all_to_all x1, waiting for transfers between devices, shards(): shrink = lax.all_to_all(add_and_spread(parts), ('z', 'c'), 0, 0, tiled=True)  7.78 us
    all_to_all x1, starting transfers between devices, shards(): lax.all_to_all(pick_up(picked, adapter_up), 'y', 0, 0, tiled=True)  7.65 us
    pallas_call x1, Pallas kernels, imported_shrink(): pl.pallas_call(functools.partial(imported_kernel, resident), out_shape=ja...  6.84 us
    all_to_all x1, waiting for transfers between devices, shards(): lax.all_to_all(parts.reshape(Y * T, 8, 128), ('y', 'z', 'c'), 0, 0, tiled...  6.61 us
    all_to_all x1, starting transfers between devices, shards(): shrink = lax.all_to_all(add_and_spread(parts), ('z', 'c'), 0, 0, tiled=True)  5.36 us
  transfers between devices with their start and end apart: 11, of which 5 were waited for; matrix products, arithmetic and copies ran while one was open for 0% of the time, Pallas kernels for 16%

profile of v6, /device:TPU:1, one launch (start us, length us, event | category | flops | bytes accessed | tf_op | source)
XLA Modules:
  0.0 152.9 jit_solution(2927580235235928788)
XLA Ops:
  7.4 1.9 %shard_map.64 = (bf16[272,512]{1,0:T(8,128)(2,1)}, s32[1,256]{1,0:T(1,128)}) custom-call(s32[32,31]{1,0:T(8,128)} %plan.3, s32[1,256]{1,0:T(1,128)} %bitcast.14, bf16[256,512]{1,0:T(8,128)(2,1)} %rows.3), custom_call_target="tpu_custom_call" | custom-call | bytes 524288 | tf_op jit(solution)/shard_map/pallas_call | solution.py:106
  9.3 0.0 all-gather.3.cloned.1.call-update
  9.3 0.0 reduce-scatter.2.cloned.1.call-start
  9.4 5.0 %shard_map.65 = (bf16[16,64,512]{2,1,0:T(8,128)(2,1)}, bf16[16,64,512]{2,1,0:T(8,128)(2,1)}, bf16[16,64,512]{2,1,0:T(8,128)(2,1)}, bf16[16,64,512]{2,1,0:T(8,128)(2,1)}, s32[32,128]{1,0:T(8,128)}) custom-call(s32[32,31]{1,0:T(8,128)} %plan.3, bf16[32,64,512]{2,1,0:T(8,128)(2,1)} %down.1), custom_call_target="tpu_custom_call" | custom-call | bytes 6291456 | tf_op jit(solution)/shard_map/pallas_call | solution.py:67
  14.4 4.5 %shard_map.69 = f32[256,2048]{1,0:T(8,128)} custom-call(bf16[256,512]{1,0:T(8,128)(2,1)} %rows.3, bf16[512,2048]{1,0:T(8,128)(2,1)} %weight.1), custom_call_target="tpu_custom_call" | custom-call | flops 536870912 | bytes 4194304 | tf_op jit(solution)/shard_map/pallas_call | solution.py:144
  18.8 0.0 reduce-scatter.2.cloned.1.call-update
  18.9 2.2 %shard_map.70 = bf16[64,64,128]{2,1,0:T(8,128)(2,1)} custom-call(s32[32,128]{1,0:T(8,128)} %get-tuple-element.23.picked, bf16[32,64,128]{2,1,0:T(8,128)(2,1)} %up.3), custom_call_target="tpu_custom_call" | custom-call | bytes 1572864 | tf_op jit(solution)/shard_map/pallas_call | solution.py:127
  21.0 7.7 %all-to-all-start.2 = ((bf16[64,64,128]{2,1,0:T(8,128)(2,1)}), bf16[64,64,128]{2,1,0:T(8,128)(2,1)S(1)}, u32[]{:S(2)}, u32[]{:S(2)}) async-start(bf16[64,64,128]{2,1,0:T(8,128)(2,1)} %shard_map.70), calls=%async_computation.3 | async-start | bytes 2097152 | tf_op jit(solution)/shard_map/all_to_all | solution.py:370
  28.7 3.1 %collective-permute-start = (bf16[16,64,512]{2,1,0:T(8,128)(2,1)}, bf16[16,64,512]{2,1,0:T(8,128)(2,1)S(1)}, u32[]{:S(2)}, u32[]{:S(2)}) collective-permute-start(bf16[16,64,512]{2,1,0:T(8,128)(2,1)} %get-tuple-element.19), channel_id=1, source_target_pairs={{0,16},{16,32},{32,48},{48,0},{1,17},{17,33},{33,49},{49,1},{2,18}... | collective-permute-start | bytes 3145736 | tf_op jit(solution)/shard_map/ppermute | solution.py:357
  31.8 4.4 %collective-permute-start.1 = (bf16[16,64,512]{2,1,0:T(8,128)(2,1)}, bf16[16,64,512]{2,1,0:T(8,128)(2,1)S(1)}, u32[]{:S(2)}, u32[]{:S(2)}) collective-permute-start(bf16[16,64,512]{2,1,0:T(8,128)(2,1)} %get-tuple-element.20), channel_id=1, source_target_pairs={{0,32},{16,48},{32,0},{48,16},{1,33},{17,49},{33,1},{49,17},{2,34}... | collective-permute-start | bytes 3145736 | tf_op jit(solution)/shard_map/ppermute | solution.py:357
  36.1 3.1 %collective-permute-start.2 = (bf16[16,64,512]{2,1,0:T(8,128)(2,1)}, bf16[16,64,512]{2,1,0:T(8,128)(2,1)}, u32[]{:S(2)}, u32[]{:S(2)}) collective-permute-start(bf16[16,64,512]{2,1,0:T(8,128)(2,1)} %get-tuple-element.21), channel_id=1, source_target_pairs={{0,48},{16,0},{32,16},{48,32},{1,49},{17,1},{33,17},{49,33},{2,50}... | collective-permute-start | bytes 3145736 | tf_op jit(solution)/shard_map/ppermute | solution.py:357
  39.2 3.1 %shard_map.66.refs_4_ = f32[64,256]{1,0:T(8,128)} custom-call(s32[1,256]{1,0:T(1,128)} %get-tuple-element.22.code, bf16[256,512]{1,0:T(8,128)(2,1)} %rows.3, bf16[2048,512]{1,0:T(8,128)(2,1)} %bitcast.8), custom_call_target="tpu_custom_call" | custom-call | flops 536870912 | bytes 2097152 | tf_op jit(solution)/shard_map/pallas_call | solution.py:201
  42.3 11.6 %collective-permute-done = bf16[16,64,512]{2,1,0:T(8,128)(2,1)S(1)} collective-permute-done((bf16[16,64,512]{2,1,0:T(8,128)(2,1)}, bf16[16,64,512]{2,1,0:T(8,128)(2,1)S(1)}, u32[]{:S(2)}, u32[]{:S(2)}) %collective-permute-start) | collective-permute-done | bytes 1048608 | tf_op jit(solution)/shard_map/ppermute | solution.py:357
  53.9 25.2 %collective-permute-done.1 = bf16[16,64,512]{2,1,0:T(8,128)(2,1)S(1)} collective-permute-done((bf16[16,64,512]{2,1,0:T(8,128)(2,1)}, bf16[16,64,512]{2,1,0:T(8,128)(2,1)S(1)}, u32[]{:S(2)}, u32[]{:S(2)}) %collective-permute-start.1) | collective-permute-done | bytes 1048608 | tf_op jit(solution)/shard_map/ppermute | solution.py:357
  79.1 2.0 %collective-permute-done.2 = bf16[16,64,512]{2,1,0:T(8,128)(2,1)} collective-permute-done((bf16[16,64,512]{2,1,0:T(8,128)(2,1)}, bf16[16,64,512]{2,1,0:T(8,128)(2,1)}, u32[]{:S(2)}, u32[]{:S(2)}) %collective-permute-start.2) | collective-permute-done | bytes 1048608 | tf_op jit(solution)/shard_map/ppermute | solution.py:357
  81.1 6.8 %shard_map.67 = f32[8,16,8,128]{3,2,1,0:T(8,128)} custom-call(bf16[8,272,512]{2,1,0:T(8,128)(2,1)} %bitcast.9, bf16[1024,512]{1,0:T(8,128)(2,1)} %bitcast.11, bf16[1024,512]{1,0:T(8,128)(2,1)} %bitcast.12, bf16[1024,512]{1,0:T(8,128)(2,1)} %bitcast.13, bf16[1024,512]{1,0:T(8,128)(2,1)} %bitcast.5.refs_3_, f32[64,256]{1,0:T(8,128)} %shard_map.66.refs_4_), custom_call_target="tpu_custom_call" | custom-call | flops 1073741824 | bytes 6422528 | tf_op jit(solution)/shard_map/pallas_call | solution.py:252
  87.9 0.0 copy-start
  88.0 0.0 all-to-all-done.2.arrived
  88.0 18.4 %all-to-all-start = ((f32[128,8,128]{2,1,0:T(8,128)}), f32[128,8,128]{2,1,0:T(8,128)S(1)}, u32[]{:S(2)}, u32[]{:S(2)}) async-start(f32[128,8,128]{2,1,0:T(8,128)} %bitcast.10), calls=%async_computation | async-start | bytes 1048576 | tf_op jit(solution)/shard_map/all_to_all | solution.py:379
  106.4 2.3 %shard_map.71 = (bf16[16,64,128]{2,1,0:T(8,128)(2,1)}, bf16[16,64,128]{2,1,0:T(8,128)(2,1)}, bf16[16,64,128]{2,1,0:T(8,128)(2,1)}, bf16[16,64,128]{2,1,0:T(8,128)(2,1)}) custom-call(bf16[64,64,128]{2,1,0:T(8,128)(2,1)} %copy-done.4), custom_call_target="tpu_custom_call" | custom-call | bytes 2097152 | tf_op jit(solution)/shard_map/pallas_call | solution.py:174
  108.7 4.0 %collective-permute-start.3 = (bf16[16,64,128]{2,1,0:T(8,128)(2,1)}, bf16[16,64,128]{2,1,0:T(8,128)(2,1)S(1)}, u32[]{:S(2)}, u32[]{:S(2)}) collective-permute-start(bf16[16,64,128]{2,1,0:T(8,128)(2,1)} %get-tuple-element.26), channel_id=1, source_target_pairs={{0,16},{16,32},{32,48},{48,0},{1,17},{17,33},{33,49},{49,1},{2,18}... | collective-permute-start | bytes 786440 | tf_op jit(solution)/shard_map/ppermute | solution.py:357
  112.7 3.3 %collective-permute-start.4 = (bf16[16,64,128]{2,1,0:T(8,128)(2,1)}, bf16[16,64,128]{2,1,0:T(8,128)(2,1)S(1)}, u32[]{:S(2)}, u32[]{:S(2)}) collective-permute-start(bf16[16,64,128]{2,1,0:T(8,128)(2,1)} %get-tuple-element.27), channel_id=1, source_target_pairs={{0,32},{16,48},{32,0},{48,16},{1,33},{17,49},{33,1},{49,17},{2,34}... | collective-permute-start | bytes 786440 | tf_op jit(solution)/shard_map/ppermute | solution.py:357
  116.1 3.2 %collective-permute-start.5 = (bf16[16,64,128]{2,1,0:T(8,128)(2,1)}, bf16[16,64,128]{2,1,0:T(8,128)(2,1)S(1)}, u32[]{:S(2)}, u32[]{:S(2)}) collective-permute-start(bf16[16,64,128]{2,1,0:T(8,128)(2,1)} %get-tuple-element.28), channel_id=1, source_target_pairs={{0,48},{16,0},{32,16},{48,32},{1,49},{17,1},{33,17},{49,33},{2,50}... | collective-permute-start | bytes 786440 | tf_op jit(solution)/shard_map/ppermute | solution.py:357
  119.3 6.6 %all-to-all-done.parts = f32[128,8,128]{2,1,0:T(8,128)S(1)} async-done(((f32[128,8,128]{2,1,0:T(8,128)}), f32[128,8,128]{2,1,0:T(8,128)S(1)}, u32[]{:S(2)}, u32[]{:S(2)}) %all-to-all-start) | async-done | bytes 524320 | tf_op jit(solution)/shard_map/all_to_all | solution.py:379
  125.9 0.8 shard_map.68
  126.7 5.4 %all-to-all-start.1 = ((f32[16,8,128]{2,1,0:T(8,128)}), f32[16,8,128]{2,1,0:T(8,128)S(1)}, u32[]{:S(2)}, u32[]{:S(2)}) async-start(f32[16,8,128]{2,1,0:T(8,128)} %shard_map.68), calls=%async_computation.1 | async-start | bytes 131072 | tf_op jit(solution)/shard_map/all_to_all | solution.py:380
  132.0 0.0 collective-permute-done.3.refs_1_
  132.1 0.0 reduce-scatter.2.cloned.1.call-done.base
  132.1 7.8 %all-to-all-done.1.shrink = f32[16,8,128]{2,1,0:T(8,128)S(1)} async-done(((f32[16,8,128]{2,1,0:T(8,128)}), f32[16,8,128]{2,1,0:T(8,128)S(1)}, u32[]{:S(2)}, u32[]{:S(2)}) %all-to-all-start.1) | async-done | bytes 65568 | tf_op jit(solution)/shard_map/all_to_all | solution.py:380
  139.9 0.9 copy-done.1
  140.8 0.9 copy-done.2
  141.7 3.7 %shard_map.72 = bf16[256,128]{1,0:T(8,128)(2,1)} custom-call(f32[16,8,128]{2,1,0:T(8,128)S(1)} %all-to-all-done.1.shrink, s32[1,256]{1,0:T(1,128)S(1)} %copy-done.3, f32[256,128]{1,0:T(8,128)S(1)} %copy-done.2, bf16[32,64,128]{2,1,0:T(8,128)(2,1)S(1)} %copy-done, bf16[16,64,128]{2,1,0:T(8,128)(2,1)S(1)} %copy-done.1, ...), custom_call_target="tpu_custom_call" | custom-call | tf_op jit(solution)/shard_map/pallas_call | solution.py:342
  (15 shorter events, 0.0 us)
Async XLA Ops:
  7.4 73.7 %all-gather.3.cloned.1.call-start = ((), (), s32[]{:S(2)}) async-start(), calls=%async_computation.5 | async-start | bytes 2506752 | tf_op jit(solution)/shard_map/all_gather | solution.py:366
  9.3 122.7 %reduce-scatter.2.cloned.1.call-start = ((), (), s32[]{:S(2)}) async-start(), calls=%async_computation.4 | async-start | bytes 2228224 | tf_op jit(solution)/shard_map/reduce_scatter | solution.py:375
  21.0 67.0 %all-to-all-start.2 = ((bf16[64,64,128]{2,1,0:T(8,128)(2,1)}), bf16[64,64,128]{2,1,0:T(8,128)(2,1)S(1)}, u32[]{:S(2)}, u32[]{:S(2)}) async-start(bf16[64,64,128]{2,1,0:T(8,128)(2,1)} %shard_map.70), calls=%async_computation.3 | async-start | bytes 2097152 | tf_op jit(solution)/shard_map/all_to_all | solution.py:370
  28.7 25.3 %collective-permute-start = (bf16[16,64,512]{2,1,0:T(8,128)(2,1)}, bf16[16,64,512]{2,1,0:T(8,128)(2,1)S(1)}, u32[]{:S(2)}, u32[]{:S(2)}) collective-permute-start(bf16[16,64,512]{2,1,0:T(8,128)(2,1)} %get-tuple-element.19), channel_id=1, source_target_pairs={{0,16},{16,32},{32,48},{48,0},{1,17},{17,33},{33,49},{49,1},{2,18}... | collective-permute-start | bytes 3145736 | tf_op jit(solution)/shard_map/ppermute | solution.py:357
  31.8 47.4 %collective-permute-start.1 = (bf16[16,64,512]{2,1,0:T(8,128)(2,1)}, bf16[16,64,512]{2,1,0:T(8,128)(2,1)S(1)}, u32[]{:S(2)}, u32[]{:S(2)}) collective-permute-start(bf16[16,64,512]{2,1,0:T(8,128)(2,1)} %get-tuple-element.20), channel_id=1, source_target_pairs={{0,32},{16,48},{32,0},{48,16},{1,33},{17,49},{33,1},{49,17},{2,34}... | collective-permute-start | bytes 3145736 | tf_op jit(solution)/shard_map/ppermute | solution.py:357
  36.1 45.0 %collective-permute-start.2 = (bf16[16,64,512]{2,1,0:T(8,128)(2,1)}, bf16[16,64,512]{2,1,0:T(8,128)(2,1)}, u32[]{:S(2)}, u32[]{:S(2)}) collective-permute-start(bf16[16,64,512]{2,1,0:T(8,128)(2,1)} %get-tuple-element.21), channel_id=1, source_target_pairs={{0,48},{16,0},{32,16},{48,32},{1,49},{17,1},{33,17},{49,33},{2,50}... | collective-permute-start | bytes 3145736 | tf_op jit(solution)/shard_map/ppermute | solution.py:357
  53.9 27.2 %copy-start.5 = (bf16[16,64,512]{2,1,0:T(8,128)(2,1)}, bf16[16,64,512]{2,1,0:T(8,128)(2,1)S(1)}, u32[]{:S(2)}) copy-start(bf16[16,64,512]{2,1,0:T(8,128)(2,1)S(1)} %collective-permute-done) | copy-start | bytes 3145732
  79.1 2.0 %copy-start.6 = (bf16[16,64,512]{2,1,0:T(8,128)(2,1)}, bf16[16,64,512]{2,1,0:T(8,128)(2,1)S(1)}, u32[]{:S(2)}) copy-start(bf16[16,64,512]{2,1,0:T(8,128)(2,1)S(1)} %collective-permute-done.1) | copy-start | bytes 3145732
  87.9 51.9 %copy-start = (bf16[32,64,128]{2,1,0:T(8,128)(2,1)S(1)}, bf16[32,64,128]{2,1,0:T(8,128)(2,1)}, u32[]{:S(2)}) copy-start(bf16[32,64,128]{2,1,0:T(8,128)(2,1)} %up.3) | copy-start | bytes 1572868
  88.0 51.9 %copy-start.3 = (s32[1,256]{1,0:T(1,128)S(1)}, s32[1,256]{1,0:T(1,128)}, u32[]{:S(2)}) copy-start(s32[1,256]{1,0:T(1,128)} %get-tuple-element.22.code) | copy-start | bytes 3076
  88.0 18.5 %copy-start.4 = (bf16[64,64,128]{2,1,0:T(8,128)(2,1)}, bf16[64,64,128]{2,1,0:T(8,128)(2,1)S(1)}, u32[]{:S(2)}) copy-start(bf16[64,64,128]{2,1,0:T(8,128)(2,1)S(1)} %all-to-all-done.2.arrived) | copy-start | bytes 3145732
  88.0 37.9 %all-to-all-start = ((f32[128,8,128]{2,1,0:T(8,128)}), f32[128,8,128]{2,1,0:T(8,128)S(1)}, u32[]{:S(2)}, u32[]{:S(2)}) async-start(f32[128,8,128]{2,1,0:T(8,128)} %bitcast.10), calls=%async_computation | async-start | bytes 1048576 | tf_op jit(solution)/shard_map/all_to_all | solution.py:379
  108.7 23.3 %collective-permute-start.3 = (bf16[16,64,128]{2,1,0:T(8,128)(2,1)}, bf16[16,64,128]{2,1,0:T(8,128)(2,1)S(1)}, u32[]{:S(2)}, u32[]{:S(2)}) collective-permute-start(bf16[16,64,128]{2,1,0:T(8,128)(2,1)} %get-tuple-element.26), channel_id=1, source_target_pairs={{0,16},{16,32},{32,48},{48,0},{1,17},{17,33},{33,49},{49,1},{2,18}... | collective-permute-start | bytes 786440 | tf_op jit(solution)/shard_map/ppermute | solution.py:357
  112.7 19.3 %collective-permute-start.4 = (bf16[16,64,128]{2,1,0:T(8,128)(2,1)}, bf16[16,64,128]{2,1,0:T(8,128)(2,1)S(1)}, u32[]{:S(2)}, u32[]{:S(2)}) collective-permute-start(bf16[16,64,128]{2,1,0:T(8,128)(2,1)} %get-tuple-element.27), channel_id=1, source_target_pairs={{0,32},{16,48},{32,0},{48,16},{1,33},{17,49},{33,1},{49,17},{2,34}... | collective-permute-start | bytes 786440 | tf_op jit(solution)/shard_map/ppermute | solution.py:357
  116.1 15.9 %collective-permute-start.5 = (bf16[16,64,128]{2,1,0:T(8,128)(2,1)}, bf16[16,64,128]{2,1,0:T(8,128)(2,1)S(1)}, u32[]{:S(2)}, u32[]{:S(2)}) collective-permute-start(bf16[16,64,128]{2,1,0:T(8,128)(2,1)} %get-tuple-element.28), channel_id=1, source_target_pairs={{0,48},{16,0},{32,16},{48,32},{1,49},{17,1},{33,17},{49,33},{2,50}... | collective-permute-start | bytes 786440 | tf_op jit(solution)/shard_map/ppermute | solution.py:357
  126.7 13.2 %all-to-all-start.1 = ((f32[16,8,128]{2,1,0:T(8,128)}), f32[16,8,128]{2,1,0:T(8,128)S(1)}, u32[]{:S(2)}, u32[]{:S(2)}) async-start(f32[16,8,128]{2,1,0:T(8,128)} %shard_map.68), calls=%async_computation.1 | async-start | bytes 131072 | tf_op jit(solution)/shard_map/all_to_all | solution.py:380
  139.9 1.0 copy-start.1
  140.8 0.9 copy-start.2
Sparse Core Ops, SparseCore 0:
  10.3 67.1 all-gather.2
Sparse Core Ops, SparseCore 1:
  18.9 67.3 reduce-scatter.1

commit v7 on v6

--- a/solution.py
+++ b/solution.py
@@ -21,7 +21,7 @@
 
 
 def dispatch_kernel(plan, down, *refs):
-    outs, (picked_out, held, staged, picked, in_sems, out_sems, picked_sem) = refs[:X], refs[X:]
+    out, picked_out, held, staged, picked, in_sems, out_sems, picked_sem = refs
     resident = down.shape[0]
     y, x = spot()
     pieces = in_sems.shape[0]
@@ -32,7 +32,7 @@
         return pltpu.make_async_copy(down.at[rows], held.at[rows], in_sems.at[i])
 
     def write(e):
-        return pltpu.make_async_copy(staged.at[e], outs[e], out_sems.at[e])
+        return pltpu.make_async_copy(staged.at[e], out.at[e], out_sems.at[e])
 
     for i in range(pieces):
         read(i).start()
@@ -51,10 +51,9 @@
     for i in range(pieces):
         read(i).wait()
     for e in range(X):
-        column = lax.rem(x + e, X)
         for row in range(Y):
             for j in range(LIMIT):
-                staged[e, row * LIMIT + j] = held[picked[row * X + column, j]]
+                staged[e, row * LIMIT + j] = held[picked[row * X + e, j]]
         write(e).start()
     for e in range(X):
         write(e).wait()
@@ -63,16 +62,18 @@
 def dispatch(plan, down):
     vmem = pl.BlockSpec(memory_space=pltpu.VMEM)
     hbm = pl.BlockSpec(memory_space=pl.ANY)
-    shape = (Y * LIMIT,) + down.shape[1:]
+    shape = (X, Y * LIMIT) + down.shape[1:]
     return pl.pallas_call(
         dispatch_kernel,
-        out_shape=(jax.ShapeDtypeStruct(shape, down.dtype),) * X
-        + (jax.ShapeDtypeStruct((GROUPS, 128), jnp.int32),),
+        out_shape=(
+            jax.ShapeDtypeStruct(shape, down.dtype),
+            jax.ShapeDtypeStruct((GROUPS, 128), jnp.int32),
+        ),
         in_specs=[vmem, hbm],
-        out_specs=(hbm,) * X + (vmem,),
+        out_specs=(hbm, vmem),
         scratch_shapes=[
             pltpu.VMEM(down.shape, down.dtype),
-            pltpu.VMEM((X,) + shape, down.dtype),
+            pltpu.VMEM(shape, down.dtype),
             pltpu.SMEM((GROUPS, 128), jnp.int32),
             pltpu.SemaphoreType.DMA((4,)),
             pltpu.SemaphoreType.DMA((X,)),
@@ -115,10 +116,13 @@
     )(plan, slots, rows)
 
 
-def pick_up_kernel(picked, up, out):
-    for group in range(GROUPS):
-        for j in range(LIMIT):
-            out[group * LIMIT + j] = up[picked[group, j]]
+def pick_up_kernel(picked, up, *outs):
+    y, _ = spot()
+    for d in range(Y):
+        row = lax.rem(y + d, Y)
+        for x in range(X):
+            for j in range(LIMIT):
+                outs[d][x * LIMIT + j] = up[picked[row * X + x, j]]
 
 
 def pick_up(picked, up):
@@ -126,59 +130,34 @@
     vmem = pl.BlockSpec(memory_space=pltpu.VMEM)
     return pl.pallas_call(
         pick_up_kernel,
-        out_shape=jax.ShapeDtypeStruct((GROUPS * LIMIT,) + up.shape[1:], up.dtype),
+        out_shape=(jax.ShapeDtypeStruct((X * LIMIT,) + up.shape[1:], up.dtype),) * Y,
         in_specs=[smem, vmem],
-        out_specs=vmem,
+        out_specs=(vmem,) * Y,
         cost_estimate=pl.CostEstimate(flops=0, bytes_accessed=6 * up.size, transcendentals=0),
     )(picked, up)
 
 
-def base_kernel(rows, weight, out):
-    out[...] = jnp.dot(rows[...], weight[...], preferred_element_type=jnp.float32)
-
-
-def base_product(rows, weight):
-    count, depth = rows.shape
-    width = weight.shape[1]
-    step = 512
-    return pl.pallas_call(
-        base_kernel,
-        grid=(width // step,),
-        out_shape=jax.ShapeDtypeStruct((count, width), jnp.float32),
-        in_specs=[
-            pl.BlockSpec((count, depth), lambda i: (0, 0)),
-            pl.BlockSpec((depth, step), lambda i: (0, i)),
-        ],
-        out_specs=pl.BlockSpec((count, step), lambda i: (0, i)),
-        cost_estimate=pl.CostEstimate(
-            flops=2 * rows.size * width, bytes_accessed=2 * weight.size + 4 * count * width, transcendentals=0
-        ),
-    )(rows, weight)
-
-
-def turn_kernel(arrived, *refs):
-    outs, (held, sem) = refs[:X], refs[X:]
+def turn_kernel(*refs):
+    arrived, outs = refs[:Y], refs[Y:]
     _, x = spot()
-    copy = pltpu.make_async_copy(arrived, held, sem)
-    copy.start()
-    copy.wait()
     for e in range(X):
         column = lax.rem(x + e, X)
-        for row in range(Y):
+        for d in range(Y):
             for j in range(LIMIT):
-                outs[e][row * LIMIT + j] = held[(row * X + column) * LIMIT + j]
+                outs[e][d * LIMIT + j] = arrived[d][column * LIMIT + j]
 
 
 def turn(arrived):
     vmem = pl.BlockSpec(memory_space=pltpu.VMEM)
+    shape = jax.ShapeDtypeStruct((Y * LIMIT,) + arrived[0].shape[1:], arrived[0].dtype)
     return pl.pallas_call(
         turn_kernel,
-        out_shape=(jax.ShapeDtypeStruct((Y * LIMIT,) + arrived.shape[1:], arrived.dtype),) * X,
-        in_specs=[pl.BlockSpec(memory_space=pltpu.HBM)],
+        out_shape=(shape,) * X,
+        in_specs=[vmem] * Y,
         out_specs=(vmem,) * X,
-        scratch_shapes=[pltpu.VMEM(arrived.shape, arrived.dtype), pltpu.SemaphoreType.DMA],
-        cost_estimate=pl.CostEstimate(flops=0, bytes_accessed=4 * arrived.size, transcendentals=0),
-    )(arrived)
+        compiler_params=pltpu.CompilerParams(vmem_limit_bytes=6 * MIB),
+        cost_estimate=pl.CostEstimate(flops=0, bytes_accessed=4 * Y * arrived[0].size, transcendentals=0),
+    )(*arrived)
 
 
 def local_kernel(code, rows, down, out):
@@ -209,21 +188,23 @@
     )(code, rows, down.reshape(resident * rank, width))
 
 
-def imported_kernel(resident, rows, *refs):
-    down, (own, out, rows_held, down_held, sems) = refs[:X], refs[X:]
+def imported_kernel(resident, rows, down, own, out, rows_held, down_held, sems):
     rank, count = own.shape
     lanes = out.shape[-1]
-    y, x = spot()
+    y, _ = spot()
+    odd = lax.axis_index("c")
 
     def reads(g):
         wanted = pl.ds(g * LIMIT * rank, LIMIT * rank)
-        pairs = [(rows.at[g], rows_held.at[g])]
-        pairs += [(down[e].at[wanted], down_held.at[g, pl.ds(e * LIMIT * rank, LIMIT * rank)]) for e in range(X)]
+        at = g + odd * (Y - 1 - 2 * g)
+        pairs = [(rows.at[at], rows_held.at[g])]
+        pairs += [(down.at[x, wanted], down_held.at[g, pl.ds(x * LIMIT * rank, LIMIT * rank)]) for x in range(X)]
         return [pltpu.make_async_copy(a, b, sems.at[g, i]) for i, (a, b) in enumerate(pairs)]
 
     for g in range(Y):
         for read in reads(g):
             read.start()
+    base = (resident + y * X * LIMIT).astype(jnp.float32)
     for g in range(Y):
         for read in reads(g):
             read.wait()
@@ -232,12 +213,8 @@
         product = lax.dot_general(
             down_held[g], rows_held[g, 0:count, :], NT, preferred_element_type=jnp.float32
         )
-        for e in range(X):
-            home = y * X + lax.rem(x - e + X, X)
-            for j in range(LIMIT):
-                at = (e * LIMIT + j) * rank
-                hit = code == (resident + home * LIMIT + j).astype(jnp.float32)
-                total = total + jnp.where(hit, product[at : at + rank, :], 0.0)
+        for k in range(X * LIMIT):
+            total = total + jnp.where(code == base + k, product[k * rank : (k + 1) * rank, :], 0.0)
         for i in range(rank // 8):
             for k in range(count // lanes):
                 out[g, i * (count // lanes) + k] = total[i * 8 : (i + 1) * 8, k * lanes : (k + 1) * lanes]
@@ -248,11 +225,11 @@
     height, width = rows.shape[1:]
     blocks = rank * count // 1024
     vmem = pl.BlockSpec(memory_space=pltpu.VMEM)
-    hbm = pl.BlockSpec(memory_space=pltpu.HBM)
+    hbm = pl.BlockSpec(memory_space=pl.ANY)
     return pl.pallas_call(
         functools.partial(imported_kernel, resident),
         out_shape=jax.ShapeDtypeStruct((Y, blocks, 8, 128), jnp.float32),
-        in_specs=[hbm] * (1 + X) + [vmem],
+        in_specs=[hbm, hbm, vmem],
         out_specs=vmem,
         scratch_shapes=[
             pltpu.VMEM((Y, height, width), rows.dtype),
@@ -260,11 +237,9 @@
             pltpu.SemaphoreType.DMA((Y, X + 1)),
         ],
         cost_estimate=pl.CostEstimate(
-            flops=2 * X * down[0].size * count,
-            bytes_accessed=2 * (X * down[0].size + rows.size),
-            transcendentals=0,
+            flops=2 * down.size * count, bytes_accessed=2 * (down.size + rows.size), transcendentals=0
         ),
-    )(rows, *[part.reshape(-1, width) for part in down], own)
+    )(rows, down.reshape(X, -1, width), own)
 
 
 def add_kernel(parts, out):
@@ -301,11 +276,12 @@
         [jnp.concatenate([shrink[i * lanes + k] for k in range(lanes)], axis=1) for i in range(rank // 8)], axis=0
     )
     rows = jnp.transpose(rows)
-    _, x = spot()
+    y, x = spot()
     imported = code[...] - resident
     home = imported // LIMIT
     e = (x - home % X + X) % X
-    at = jnp.where(imported < 0, code[...], resident + (e * Y + home // X) * LIMIT + imported % LIMIT)
+    d = (y - home // X + Y) % Y
+    at = jnp.where(imported < 0, code[...], resident + (e * Y + d) * LIMIT + imported % LIMIT)
     column = jnp.transpose(jnp.broadcast_to(at, (8, count)).astype(jnp.float32))[:, :1]
     pair = jnp.concatenate([rows, rows], axis=1)
     high = pair.astype(jnp.bfloat16).astype(jnp.float32)
@@ -349,7 +325,6 @@
             pltpu.VMEM(base.shape, base.dtype),
             pltpu.SemaphoreType.DMA((2 + X,)),
         ],
-        compiler_params=pltpu.CompilerParams(vmem_limit_bytes=12 * MIB),
     )(shrink, code, base, up, *tables)
 
 
@@ -363,17 +338,21 @@
     slots = row_adapter_slot.reshape(1, count)
 
     sent, code = prepare(resident, transfer_plan, slots, inputs)
-    rows = lax.all_gather(sent, "y")
-    *down, picked = dispatch(transfer_plan, adapter_down)
-    down = [down[0]] + [shift(down[e], "x", X, e) for e in range(1, X)]
-
-    ups = turn(lax.all_to_all(pick_up(picked, adapter_up), "y", 0, 0, tiled=True))
-    tables = [ups[0]] + [shift(ups[e], "x", X, e) for e in range(1, X)]
+    rings = [[i * C for i in range(Y)], [i * C + 1 for i in reversed(range(Y))]]
+    rows = lax.all_gather(sent, ("y", "c"), axis_index_groups=rings)
+    down, picked = dispatch(transfer_plan, adapter_down)
+    down = lax.all_to_all(down, "x", 0, 0, tiled=True)
 
     late, picked = lax.optimization_barrier((inputs, picked))
-    base_part = base_product(late, key_value_weight)
+    base_part = jnp.dot(late, key_value_weight, preferred_element_type=jnp.float32)
     base = lax.psum_scatter(base_part, ("z", "c"), scatter_dimension=1, tiled=True)
     own = local_shrink(code, late, adapter_down)
+
+    ups = pick_up(picked, adapter_up)
+    ups = [ups[0]] + [shift(ups[d], "y", Y, d) for d in range(1, Y)]
+    down, ups = lax.optimization_barrier((down, ups))
+    ups = turn(ups)
+    tables = [ups[0]] + [shift(ups[e], "x", X, e) for e in range(1, X)]
 
     parts = imported_shrink(resident, rows, down, own)
     parts = lax.all_to_all(parts.reshape(Y * T, 8, 128), ("y", "z", "c"), 0, 0, tiled=True)

time: 154 us -> 149 us (0.968)
  waiting for transfers between devices: 53.3 us -> 39.6 us
  starting transfers between devices: 52.6 us -> 63.3 us
  Pallas kernels: 30.2 us -> 26 us
  matrix products: 0 us -> 2.09 us
    ppermute x6 -> x10, waiting for transfers between devices: 38.8 us -> 17.8 us  [shift(): lax.ppermute(array, axis, [(i, (i + by) % size) for i in range(size)])]
    ppermute x6 -> x10, starting transfers between devices: 21.1 us -> 39.6 us  [shift(): lax.ppermute(array, axis, [(i, (i + by) % size) for i in range(size)])]
    all_gather x1, waiting for transfers between devices: 0.01 us -> 7.41 us  [shards(): rows = lax.all_gather(sent, ('y', 'c'), axis_index_groups=rings)]
    pallas_call x3 -> x2, Pallas kernels: 8.91 us -> 3.09 us  [the longest x1 2.13 us: pick_up(): pl.pallas_call(pick_up_kernel, out_shape=(jax.ShapeDtypeStruct((X * LIMIT...]
    all_to_all x1, starting transfers between devices: 18.4 us -> 13.3 us  [shards(): lax.all_to_all(parts.reshape(Y * T, 8, 128), ('y', 'z', 'c'), 0, 0, tiled...]
    all_to_all x1, starting transfers between devices: 7.65 us -> 4.99 us  [shards(): down = lax.all_to_all(down, 'x', 0, 0, tiled=True)]
    dot_general x0 -> x1, matrix products: none -> 2.09 us  [shards(): jnp.dot(late, key_value_weight, preferred_element_type=jnp.float32)]
  transfers between devices with their start and end apart: 11 -> 15, of which waited for: 5 -> 7; matrix products, arithmetic and copies ran while one was open for 0% -> 1% of each run, Pallas kernels for 16% -> 13%
where the time goes in v7:
time: 149 us; the launch traced here: 148 us
  starting transfers between devices  63.3 us (42%)
  waiting for transfers between devices  39.6 us (27%)
  Pallas kernels  26 us (17%)
  between operations  15.1 us (10%)
  local copies, waits for them, and re-layouts  2.22 us (1%)
  matrix products  2.09 us (1%)
    ppermute x10, starting transfers between devices, shift(): lax.ppermute(array, axis, [(i, (i + by) % size) for i in range(size)])  39.6 us
    ppermute x10, waiting for transfers between devices, shift(): lax.ppermute(array, axis, [(i, (i + by) % size) for i in range(size)])  17.8 us
    all_to_all x1, starting transfers between devices, shards(): lax.all_to_all(parts.reshape(Y * T, 8, 128), ('y', 'z', 'c'), 0, 0, tiled...  13.3 us
    all_to_all x1, waiting for transfers between devices, shards(): shrink = lax.all_to_all(add_and_spread(parts), ('z', 'c'), 0, 0, tiled=True)  7.75 us
    all_gather x1, waiting for transfers between devices, shards(): rows = lax.all_gather(sent, ('y', 'c'), axis_index_groups=rings)  7.41 us
    pallas_call x1, Pallas kernels, imported_shrink(): pl.pallas_call(functools.partial(imported_kernel, resident), out_shape=ja...  6.88 us
    all_to_all x1, waiting for transfers between devices, shards(): lax.all_to_all(parts.reshape(Y * T, 8, 128), ('y', 'z', 'c'), 0, 0, tiled...  6.5 us
    all_to_all x1, starting transfers between devices, shards(): shrink = lax.all_to_all(add_and_spread(parts), ('z', 'c'), 0, 0, tiled=True)  5.36 us
  transfers between devices with their start and end apart: 15, of which 7 were waited for; matrix products, arithmetic and copies ran while one was open for 1% of the time, Pallas kernels for 13%

profile of v7, /device:TPU:1, one launch (start us, length us, event | category | flops | bytes accessed | tf_op | source)
XLA Modules:
  0.0 148.2 jit_solution(4848477752735987023)
XLA Ops:
  7.4 2.1 %shard_map.64 = (bf16[272,512]{1,0:T(8,128)(2,1)}, s32[1,256]{1,0:T(1,128)}) custom-call(s32[32,31]{1,0:T(8,128)} %plan.3, s32[1,256]{1,0:T(1,128)} %bitcast.10, bf16[256,512]{1,0:T(8,128)(2,1)} %rows.2), custom_call_target="tpu_custom_call" | custom-call | bytes 524288 | tf_op jit(solution)/shard_map/pallas_call | solution.py:107
  9.5 5.0 %shard_map.65 = (bf16[4,16,64,512]{3,2,1,0:T(8,128)(2,1)}, s32[32,128]{1,0:T(8,128)}) custom-call(s32[32,31]{1,0:T(8,128)} %plan.3, bf16[32,64,512]{2,1,0:T(8,128)(2,1)} %down.1), custom_call_target="tpu_custom_call" | custom-call | bytes 6291456 | tf_op jit(solution)/shard_map/pallas_call | solution.py:66
  14.5 5.0 %all-to-all-start = ((bf16[4,16,64,512]{3,2,1,0:T(8,128)(2,1)}), bf16[4,16,64,512]{3,2,1,0:T(8,128)(2,1)}, u32[]{:S(2)}, u32[]{:S(2)}) async-start(bf16[4,16,64,512]{3,2,1,0:T(8,128)(2,1)} %get-tuple-element.33), calls=%async_computation | async-start | bytes 8388608 | tf_op jit(solution)/shard_map/all_to_all | solution.py:344
  19.6 2.1 %fusion = f32[256,2048]{1,0:T(8,128)} fusion(bf16[256,512]{1,0:T(8,128)(2,1)S(1)} %copy-done.5, bf16[512,2048]{1,0:T(8,128)(2,1)S(1)} %copy-done), kind=kOutput, calls=%fused_computation | convolution fusion | flops 536870912 | bytes 4456448 | tf_op jit(solution)/shard_map/dot_general | solution.py:347
  21.7 2.1 %shard_map.66 = (bf16[8,64,128]{2,1,0:T(8,128)(2,1)}, bf16[8,64,128]{2,1,0:T(8,128)(2,1)}, bf16[8,64,128]{2,1,0:T(8,128)(2,1)}, bf16[8,64,128]{2,1,0:T(8,128)(2,...) custom-call(s32[32,128]{1,0:T(8,128)} %get-tuple-element.35.picked, ...), custom_call_target="tpu_custom_call" | custom-call | bytes 1572864 | tf_op jit(solution)/shard_map/pallas_call | solution.py:131
  23.8 4.0 %collective-permute-start = (bf16[8,64,128]{2,1,0:T(8,128)(2,1)}, bf16[8,64,128]{2,1,0:T(8,128)(2,1)S(1)}, u32[]{:S(2)}, u32[]{:S(2)}) collective-permute-start(bf16[8,64,128]{2,1,0:T(8,128)(2,1)} %get-tuple-element.37), channel_id=1, source_target_pairs={{0,64},{64,128},{128,192},{192,256},{256,320},{320,384},{384,448},... | collective-permute-start | bytes 393224 | tf_op jit(solution)/shard_map/ppermute | solution.py:332
  27.9 4.2 %collective-permute-start.1 = (bf16[8,64,128]{2,1,0:T(8,128)(2,1)}, bf16[8,64,128]{2,1,0:T(8,128)(2,1)S(1)}, u32[]{:S(2)}, u32[]{:S(2)}) collective-permute-start(bf16[8,64,128]{2,1,0:T(8,128)(2,1)} %get-tuple-element.38), channel_id=1, source_target_pairs={{0,128},{64,192},{128,256},{192,320},{256,384},{320,448},{384,0},{... | collective-permute-start | bytes 393224 | tf_op jit(solution)/shard_map/ppermute | solution.py:332
  32.1 4.6 %collective-permute-start.2 = (bf16[8,64,128]{2,1,0:T(8,128)(2,1)}, bf16[8,64,128]{2,1,0:T(8,128)(2,1)S(1)}, u32[]{:S(2)}, u32[]{:S(2)}) collective-permute-start(bf16[8,64,128]{2,1,0:T(8,128)(2,1)} %get-tuple-element.39), channel_id=1, source_target_pairs={{0,192},{64,256},{128,320},{192,384},{256,448},{320,0},{384,64},{4... | collective-permute-start | bytes 393224 | tf_op jit(solution)/shard_map/ppermute | solution.py:332
  36.7 3.5 %collective-permute-start.3 = (bf16[8,64,128]{2,1,0:T(8,128)(2,1)}, bf16[8,64,128]{2,1,0:T(8,128)(2,1)S(1)}, u32[]{:S(2)}, u32[]{:S(2)}) collective-permute-start(bf16[8,64,128]{2,1,0:T(8,128)(2,1)} %get-tuple-element.40), channel_id=1, source_target_pairs={{0,256},{64,320},{128,384},{192,448},{256,0},{320,64},{384,128},{4... | collective-permute-start | bytes 393224 | tf_op jit(solution)/shard_map/ppermute | solution.py:332
  40.3 4.9 %collective-permute-start.4 = (bf16[8,64,128]{2,1,0:T(8,128)(2,1)}, bf16[8,64,128]{2,1,0:T(8,128)(2,1)S(1)}, u32[]{:S(2)}, u32[]{:S(2)}) collective-permute-start(bf16[8,64,128]{2,1,0:T(8,128)(2,1)} %get-tuple-element.41), channel_id=1, source_target_pairs={{0,320},{64,384},{128,448},{192,0},{256,64},{320,128},{384,192},{4... | collective-permute-start | bytes 393224 | tf_op jit(solution)/shard_map/ppermute | solution.py:332
  45.2 5.0 %collective-permute-start.5 = (bf16[8,64,128]{2,1,0:T(8,128)(2,1)}, bf16[8,64,128]{2,1,0:T(8,128)(2,1)S(1)}, u32[]{:S(2)}, u32[]{:S(2)}) collective-permute-start(bf16[8,64,128]{2,1,0:T(8,128)(2,1)} %get-tuple-element.42), channel_id=1, source_target_pairs={{0,384},{64,448},{128,0},{192,64},{256,128},{320,192},{384,256},{4... | collective-permute-start | bytes 393224 | tf_op jit(solution)/shard_map/ppermute | solution.py:332
  50.2 3.0 %collective-permute-start.6 = (bf16[8,64,128]{2,1,0:T(8,128)(2,1)}, bf16[8,64,128]{2,1,0:T(8,128)(2,1)S(1)}, u32[]{:S(2)}, u32[]{:S(2)}) collective-permute-start(bf16[8,64,128]{2,1,0:T(8,128)(2,1)} %get-tuple-element.43), channel_id=1, source_target_pairs={{0,448},{64,0},{128,64},{192,128},{256,192},{320,256},{384,320},{4... | collective-permute-start | bytes 393224 | tf_op jit(solution)/shard_map/ppermute | solution.py:332
  53.1 3.1 %shard_map.67.own = f32[64,256]{1,0:T(8,128)} custom-call(s32[1,256]{1,0:T(1,128)} %get-tuple-element.45.code, bf16[256,512]{1,0:T(8,128)(2,1)} %rows.2, bf16[2048,512]{1,0:T(8,128)(2,1)} %bitcast.7), custom_call_target="tpu_custom_call" | custom-call | flops 536870912 | bytes 2097152 | tf_op jit(solution)/shard_map/pallas_call | solution.py:180
  56.2 2.9 %collective-permute-done.3.refs_4_ = bf16[8,64,128]{2,1,0:T(8,128)(2,1)S(1)} collective-permute-done((bf16[8,64,128]{2,1,0:T(8,128)(2,1)}, bf16[8,64,128]{2,1,0:T(8,128)(2,1)S(1)}, u32[]{:S(2)}, u32[]{:S(2)}) %collective-permute-start.3) | collective-permute-done | bytes 131104 | tf_op jit(solution)/shard_map/ppermute | solution.py:332
  59.1 0.3 collective-permute-done.4.refs_5_
  59.4 9.5 %collective-permute-done.5.refs_6_ = bf16[8,64,128]{2,1,0:T(8,128)(2,1)S(1)} collective-permute-done((bf16[8,64,128]{2,1,0:T(8,128)(2,1)}, bf16[8,64,128]{2,1,0:T(8,128)(2,1)S(1)}, u32[]{:S(2)}, u32[]{:S(2)}) %collective-permute-start.5) | collective-permute-done | bytes 131104 | tf_op jit(solution)/shard_map/ppermute | solution.py:332
  68.9 5.2 %collective-permute-done.6.refs_7_ = bf16[8,64,128]{2,1,0:T(8,128)(2,1)S(1)} collective-permute-done((bf16[8,64,128]{2,1,0:T(8,128)(2,1)}, bf16[8,64,128]{2,1,0:T(8,128)(2,1)S(1)}, u32[]{:S(2)}, u32[]{:S(2)}) %collective-permute-start.6) | collective-permute-done | bytes 131104 | tf_op jit(solution)/shard_map/ppermute | solution.py:332
  74.1 7.4 %all-gather.3.cloned.1.call-done = bf16[2176,512]{1,0:T(8,128)(2,1)} async-done(((bf16[272,512]{1,0:T(8,128)(2,1)}), bf16[2176,512]{1,0:T(8,128)(2,1)}) %all-gather.3.cloned.1.call-update) | async-done | bytes 2228240 | tf_op jit(solution)/shard_map/all_gather | solution.py:342
  81.5 6.9 %shard_map.68 = f32[8,16,8,128]{3,2,1,0:T(8,128)} custom-call(bf16[8,272,512]{2,1,0:T(8,128)(2,1)} %bitcast.8, bf16[4,1024,512]{2,1,0:T(8,128)(2,1)} %bitcast.2.down, f32[64,256]{1,0:T(8,128)} %shard_map.67.own), custom_call_target="tpu_custom_call" | custom-call | flops 1073741824 | bytes 6422528 | tf_op jit(solution)/shard_map/pallas_call | solution.py:229
  88.4 13.3 %all-to-all-start.1 = ((f32[128,8,128]{2,1,0:T(8,128)}), f32[128,8,128]{2,1,0:T(8,128)S(1)}, u32[]{:S(2)}, u32[]{:S(2)}) async-start(f32[128,8,128]{2,1,0:T(8,128)} %bitcast.9), calls=%async_computation.1 | async-start | bytes 1048576 | tf_op jit(solution)/shard_map/all_to_all | solution.py:358
  101.7 0.9 copy-done.4
  102.6 1.0 shard_map.70
  103.5 0.7 copy-done.1
  104.2 3.0 %collective-permute-start.7 = (bf16[16,64,128]{2,1,0:T(8,128)(2,1)}, bf16[16,64,128]{2,1,0:T(8,128)(2,1)S(1)}, u32[]{:S(2)}, u32[]{:S(2)}) collective-permute-start(bf16[16,64,128]{2,1,0:T(8,128)(2,1)} %get-tuple-element.56), channel_id=1, source_target_pairs={{0,16},{16,32},{32,48},{48,0},{1,17},{17,33},{33,49},{49,1},{2,18}... | collective-permute-start | bytes 786440 | tf_op jit(solution)/shard_map/ppermute | solution.py:332
  107.2 4.3 %collective-permute-start.8 = (bf16[16,64,128]{2,1,0:T(8,128)(2,1)}, bf16[16,64,128]{2,1,0:T(8,128)(2,1)S(1)}, u32[]{:S(2)}, u32[]{:S(2)}) collective-permute-start(bf16[16,64,128]{2,1,0:T(8,128)(2,1)} %get-tuple-element.57), channel_id=1, source_target_pairs={{0,32},{16,48},{32,0},{48,16},{1,33},{17,49},{33,1},{49,17},{2,34}... | collective-permute-start | bytes 786440 | tf_op jit(solution)/shard_map/ppermute | solution.py:332
  111.5 3.1 %collective-permute-start.9 = (bf16[16,64,128]{2,1,0:T(8,128)(2,1)}, bf16[16,64,128]{2,1,0:T(8,128)(2,1)S(1)}, u32[]{:S(2)}, u32[]{:S(2)}) collective-permute-start(bf16[16,64,128]{2,1,0:T(8,128)(2,1)} %get-tuple-element.58), channel_id=1, source_target_pairs={{0,48},{16,0},{32,16},{48,32},{1,49},{17,1},{33,17},{49,33},{2,50}... | collective-permute-start | bytes 786440 | tf_op jit(solution)/shard_map/ppermute | solution.py:332
  114.6 6.5 %all-to-all-done.1.parts = f32[128,8,128]{2,1,0:T(8,128)S(1)} async-done(((f32[128,8,128]{2,1,0:T(8,128)}), f32[128,8,128]{2,1,0:T(8,128)S(1)}, u32[]{:S(2)}, u32[]{:S(2)}) %all-to-all-start.1) | async-done | bytes 524320 | tf_op jit(solution)/shard_map/all_to_all | solution.py:358
  121.1 0.8 shard_map.69
  121.9 5.4 %all-to-all-start.2 = ((f32[16,8,128]{2,1,0:T(8,128)}), f32[16,8,128]{2,1,0:T(8,128)S(1)}, u32[]{:S(2)}, u32[]{:S(2)}) async-start(f32[16,8,128]{2,1,0:T(8,128)} %shard_map.69), calls=%async_computation.2 | async-start | bytes 131072 | tf_op jit(solution)/shard_map/all_to_all | solution.py:359
  127.3 7.7 %all-to-all-done.2.shrink = f32[16,8,128]{2,1,0:T(8,128)S(1)} async-done(((f32[16,8,128]{2,1,0:T(8,128)}), f32[16,8,128]{2,1,0:T(8,128)S(1)}, u32[]{:S(2)}, u32[]{:S(2)}) %all-to-all-start.2) | async-done | bytes 65568 | tf_op jit(solution)/shard_map/all_to_all | solution.py:359
  135.1 0.6 copy-done.9
  135.7 5.1 %shard_map.71 = bf16[256,128]{1,0:T(8,128)(2,1)} custom-call(f32[16,8,128]{2,1,0:T(8,128)} %copy-done.9, s32[1,256]{1,0:T(1,128)} %get-tuple-element.45.code, f32[256,128]{1,0:T(8,128)} %reduce-scatter.2.cloned.1.call-done.base, bf16[32,64,128]{2,1,0:T(8,128)(2,1)} %up.3, bf16[16,64,128]{2,1,0:T(8,128)(2,1)} %copy-done.1, bf16[16,64,128]{2,1,0:T(8,128)(2,1)} %copy-done.6, ...), custom_call_target="tpu_custom_call" | custom-call | tf_op jit(solution)/shard_map/pallas_call | solution.py:318
  (29 shorter events, 0.2 us)
Async XLA Ops:
  7.4 12.2 %copy-start = (bf16[512,2048]{1,0:T(8,128)(2,1)S(1)}, bf16[512,2048]{1,0:T(8,128)(2,1)}, u32[]{:S(2)}) copy-start(bf16[512,2048]{1,0:T(8,128)(2,1)} %param.9) | copy-start | bytes 6291460
  7.4 74.1 %all-gather.3.cloned.1.call-start = ((), (), s32[]{:S(2)}) async-start(), calls=%async_computation.5 | async-start | bytes 2506752 | tf_op jit(solution)/shard_map/all_gather | solution.py:342
  14.5 5.1 %copy-start.5 = (bf16[256,512]{1,0:T(8,128)(2,1)S(1)}, bf16[256,512]{1,0:T(8,128)(2,1)}, u32[]{:S(2)}) copy-start(bf16[256,512]{1,0:T(8,128)(2,1)} %rows.2) | copy-start | bytes 786436
  14.5 59.5 %all-to-all-start = ((bf16[4,16,64,512]{3,2,1,0:T(8,128)(2,1)}), bf16[4,16,64,512]{3,2,1,0:T(8,128)(2,1)}, u32[]{:S(2)}, u32[]{:S(2)}) async-start(bf16[4,16,64,512]{3,2,1,0:T(8,128)(2,1)} %get-tuple-element.33), calls=%async_computation | async-start | bytes 8388608 | tf_op jit(solution)/shard_map/all_to_all | solution.py:344
  19.5 107.8 %reduce-scatter.2.cloned.1.call-start = ((), (), s32[]{:S(2)}) async-start(), calls=%async_computation.4 | async-start | bytes 2228224 | tf_op jit(solution)/shard_map/reduce_scatter | solution.py:348
  23.8 21.3 %collective-permute-start = (bf16[8,64,128]{2,1,0:T(8,128)(2,1)}, bf16[8,64,128]{2,1,0:T(8,128)(2,1)S(1)}, u32[]{:S(2)}, u32[]{:S(2)}) collective-permute-start(bf16[8,64,128]{2,1,0:T(8,128)(2,1)} %get-tuple-element.37), channel_id=1, source_target_pairs={{0,64},{64,128},{128,192},{192,256},{256,320},{320,384},{384,448},... | collective-permute-start | bytes 393224 | tf_op jit(solution)/shard_map/ppermute | solution.py:332
  27.9 22.3 %collective-permute-start.1 = (bf16[8,64,128]{2,1,0:T(8,128)(2,1)}, bf16[8,64,128]{2,1,0:T(8,128)(2,1)S(1)}, u32[]{:S(2)}, u32[]{:S(2)}) collective-permute-start(bf16[8,64,128]{2,1,0:T(8,128)(2,1)} %get-tuple-element.38), channel_id=1, source_target_pairs={{0,128},{64,192},{128,256},{192,320},{256,384},{320,448},{384,0},{... | collective-permute-start | bytes 393224 | tf_op jit(solution)/shard_map/ppermute | solution.py:332
  32.1 24.1 %collective-permute-start.2 = (bf16[8,64,128]{2,1,0:T(8,128)(2,1)}, bf16[8,64,128]{2,1,0:T(8,128)(2,1)S(1)}, u32[]{:S(2)}, u32[]{:S(2)}) collective-permute-start(bf16[8,64,128]{2,1,0:T(8,128)(2,1)} %get-tuple-element.39), channel_id=1, source_target_pairs={{0,192},{64,256},{128,320},{192,384},{256,448},{320,0},{384,64},{4... | collective-permute-start | bytes 393224 | tf_op jit(solution)/shard_map/ppermute | solution.py:332
  36.7 22.4 %collective-permute-start.3 = (bf16[8,64,128]{2,1,0:T(8,128)(2,1)}, bf16[8,64,128]{2,1,0:T(8,128)(2,1)S(1)}, u32[]{:S(2)}, u32[]{:S(2)}) collective-permute-start(bf16[8,64,128]{2,1,0:T(8,128)(2,1)} %get-tuple-element.40), channel_id=1, source_target_pairs={{0,256},{64,320},{128,384},{192,448},{256,0},{320,64},{384,128},{4... | collective-permute-start | bytes 393224 | tf_op jit(solution)/shard_map/ppermute | solution.py:332
  40.3 19.1 %collective-permute-start.4 = (bf16[8,64,128]{2,1,0:T(8,128)(2,1)}, bf16[8,64,128]{2,1,0:T(8,128)(2,1)S(1)}, u32[]{:S(2)}, u32[]{:S(2)}) collective-permute-start(bf16[8,64,128]{2,1,0:T(8,128)(2,1)} %get-tuple-element.41), channel_id=1, source_target_pairs={{0,320},{64,384},{128,448},{192,0},{256,64},{320,128},{384,192},{4... | collective-permute-start | bytes 393224 | tf_op jit(solution)/shard_map/ppermute | solution.py:332
  45.2 23.7 %collective-permute-start.5 = (bf16[8,64,128]{2,1,0:T(8,128)(2,1)}, bf16[8,64,128]{2,1,0:T(8,128)(2,1)S(1)}, u32[]{:S(2)}, u32[]{:S(2)}) collective-permute-start(bf16[8,64,128]{2,1,0:T(8,128)(2,1)} %get-tuple-element.42), channel_id=1, source_target_pairs={{0,384},{64,448},{128,0},{192,64},{256,128},{320,192},{384,256},{4... | collective-permute-start | bytes 393224 | tf_op jit(solution)/shard_map/ppermute | solution.py:332
  50.2 23.9 %collective-permute-start.6 = (bf16[8,64,128]{2,1,0:T(8,128)(2,1)}, bf16[8,64,128]{2,1,0:T(8,128)(2,1)S(1)}, u32[]{:S(2)}, u32[]{:S(2)}) collective-permute-start(bf16[8,64,128]{2,1,0:T(8,128)(2,1)} %get-tuple-element.43), channel_id=1, source_target_pairs={{0,448},{64,0},{128,64},{192,128},{256,192},{320,256},{384,320},{4... | collective-permute-start | bytes 393224 | tf_op jit(solution)/shard_map/ppermute | solution.py:332
  74.0 14.3 %copy-start.3 = (bf16[8,64,128]{2,1,0:T(8,128)(2,1)}, bf16[8,64,128]{2,1,0:T(8,128)(2,1)S(1)}, u32[]{:S(2)}) copy-start(bf16[8,64,128]{2,1,0:T(8,128)(2,1)S(1)} %collective-permute-done.6.refs_7_) | copy-start | bytes 393220
  81.5 20.2 %copy-start.2 = (bf16[8,64,128]{2,1,0:T(8,128)(2,1)S(1)}, bf16[8,64,128]{2,1,0:T(8,128)(2,1)}, u32[]{:S(2)}) copy-start(bf16[8,64,128]{2,1,0:T(8,128)(2,1)} %get-tuple-element.47.refs_0_) | copy-start | bytes 393220
  88.4 32.7 %all-to-all-start.1 = ((f32[128,8,128]{2,1,0:T(8,128)}), f32[128,8,128]{2,1,0:T(8,128)S(1)}, u32[]{:S(2)}, u32[]{:S(2)}) async-start(f32[128,8,128]{2,1,0:T(8,128)} %bitcast.9), calls=%async_computation.1 | async-start | bytes 1048576 | tf_op jit(solution)/shard_map/all_to_all | solution.py:358
  101.6 0.9 copy-start.4
  103.5 0.7 copy-start.1
  104.2 23.0 %collective-permute-start.7 = (bf16[16,64,128]{2,1,0:T(8,128)(2,1)}, bf16[16,64,128]{2,1,0:T(8,128)(2,1)S(1)}, u32[]{:S(2)}, u32[]{:S(2)}) collective-permute-start(bf16[16,64,128]{2,1,0:T(8,128)(2,1)} %get-tuple-element.56), channel_id=1, source_target_pairs={{0,16},{16,32},{32,48},{48,0},{1,17},{17,33},{33,49},{49,1},{2,18}... | collective-permute-start | bytes 786440 | tf_op jit(solution)/shard_map/ppermute | solution.py:332
  107.2 20.1 %collective-permute-start.8 = (bf16[16,64,128]{2,1,0:T(8,128)(2,1)}, bf16[16,64,128]{2,1,0:T(8,128)(2,1)S(1)}, u32[]{:S(2)}, u32[]{:S(2)}) collective-permute-start(bf16[16,64,128]{2,1,0:T(8,128)(2,1)} %get-tuple-element.57), channel_id=1, source_target_pairs={{0,32},{16,48},{32,0},{48,16},{1,33},{17,49},{33,1},{49,17},{2,34}... | collective-permute-start | bytes 786440 | tf_op jit(solution)/shard_map/ppermute | solution.py:332
  111.5 15.8 %collective-permute-start.9 = (bf16[16,64,128]{2,1,0:T(8,128)(2,1)}, bf16[16,64,128]{2,1,0:T(8,128)(2,1)S(1)}, u32[]{:S(2)}, u32[]{:S(2)}) collective-permute-start(bf16[16,64,128]{2,1,0:T(8,128)(2,1)} %get-tuple-element.58), channel_id=1, source_target_pairs={{0,48},{16,0},{32,16},{48,32},{1,49},{17,1},{33,17},{49,33},{2,50}... | collective-permute-start | bytes 786440 | tf_op jit(solution)/shard_map/ppermute | solution.py:332
  121.9 13.2 %all-to-all-start.2 = ((f32[16,8,128]{2,1,0:T(8,128)}), f32[16,8,128]{2,1,0:T(8,128)S(1)}, u32[]{:S(2)}, u32[]{:S(2)}) async-start(f32[16,8,128]{2,1,0:T(8,128)} %shard_map.69), calls=%async_computation.2 | async-start | bytes 131072 | tf_op jit(solution)/shard_map/all_to_all | solution.py:359
  127.2 7.8 %copy-start.6 = (bf16[16,64,128]{2,1,0:T(8,128)(2,1)}, bf16[16,64,128]{2,1,0:T(8,128)(2,1)S(1)}, u32[]{:S(2)}) copy-start(bf16[16,64,128]{2,1,0:T(8,128)(2,1)S(1)} %collective-permute-done.7.refs_1_) | copy-start | bytes 786436
  127.3 7.8 %copy-start.7 = (bf16[16,64,128]{2,1,0:T(8,128)(2,1)}, bf16[16,64,128]{2,1,0:T(8,128)(2,1)S(1)}, u32[]{:S(2)}) copy-start(bf16[16,64,128]{2,1,0:T(8,128)(2,1)S(1)} %collective-permute-done.8.refs_2_) | copy-start | bytes 786436
  127.3 7.8 %copy-start.8 = (bf16[16,64,128]{2,1,0:T(8,128)(2,1)}, bf16[16,64,128]{2,1,0:T(8,128)(2,1)S(1)}, u32[]{:S(2)}) copy-start(bf16[16,64,128]{2,1,0:T(8,128)(2,1)S(1)} %collective-permute-done.9.refs_3_) | copy-start | bytes 786436
  135.1 0.6 copy-start.9
Sparse Core Ops, SparseCore 0:
  10.3 71.1 all-gather.2
Sparse Core Ops, SparseCore 1:
  22.8 67.5 reduce-scatter.1

commit v8 on v7

--- a/solution.py
+++ b/solution.py
@@ -13,6 +13,7 @@
 LIMIT = 2
 CODE_ROWS = 16
 MIB = 1024 * 1024
+AHEAD = 6
 NT = (((1,), (1,)), ((), ()))
 
 
@@ -117,46 +118,46 @@
 
 
 def pick_up_kernel(picked, up, *outs):
+    _, x = spot()
+    for e in range(X):
+        column = lax.rem(x + e, X)
+        for row in range(Y):
+            for j in range(LIMIT):
+                outs[e][row * LIMIT + j] = up[picked[row * X + column, j]]
+
+
+def pick_up(picked, up):
+    smem = pl.BlockSpec(memory_space=pltpu.SMEM)
+    vmem = pl.BlockSpec(memory_space=pltpu.VMEM)
+    return pl.pallas_call(
+        pick_up_kernel,
+        out_shape=(jax.ShapeDtypeStruct((Y * LIMIT,) + up.shape[1:], up.dtype),) * X,
+        in_specs=[smem, vmem],
+        out_specs=(vmem,) * X,
+        cost_estimate=pl.CostEstimate(flops=0, bytes_accessed=6 * up.size, transcendentals=0),
+    )(picked, up)
+
+
+def turn_kernel(*refs):
+    arrived, outs = refs[:X], refs[X:]
     y, _ = spot()
     for d in range(Y):
         row = lax.rem(y + d, Y)
-        for x in range(X):
+        for e in range(X):
             for j in range(LIMIT):
-                outs[d][x * LIMIT + j] = up[picked[row * X + x, j]]
-
-
-def pick_up(picked, up):
-    smem = pl.BlockSpec(memory_space=pltpu.SMEM)
-    vmem = pl.BlockSpec(memory_space=pltpu.VMEM)
-    return pl.pallas_call(
-        pick_up_kernel,
-        out_shape=(jax.ShapeDtypeStruct((X * LIMIT,) + up.shape[1:], up.dtype),) * Y,
-        in_specs=[smem, vmem],
+                outs[d][e * LIMIT + j] = arrived[e][row * LIMIT + j]
+
+
+def turn(arrived):
+    vmem = pl.BlockSpec(memory_space=pltpu.VMEM)
+    shape = jax.ShapeDtypeStruct((X * LIMIT,) + arrived[0].shape[1:], arrived[0].dtype)
+    return pl.pallas_call(
+        turn_kernel,
+        out_shape=(shape,) * Y,
+        in_specs=[vmem] * X,
         out_specs=(vmem,) * Y,
-        cost_estimate=pl.CostEstimate(flops=0, bytes_accessed=6 * up.size, transcendentals=0),
-    )(picked, up)
-
-
-def turn_kernel(*refs):
-    arrived, outs = refs[:Y], refs[Y:]
-    _, x = spot()
-    for e in range(X):
-        column = lax.rem(x + e, X)
-        for d in range(Y):
-            for j in range(LIMIT):
-                outs[e][d * LIMIT + j] = arrived[d][column * LIMIT + j]
-
-
-def turn(arrived):
-    vmem = pl.BlockSpec(memory_space=pltpu.VMEM)
-    shape = jax.ShapeDtypeStruct((Y * LIMIT,) + arrived[0].shape[1:], arrived[0].dtype)
-    return pl.pallas_call(
-        turn_kernel,
-        out_shape=(shape,) * X,
-        in_specs=[vmem] * Y,
-        out_specs=(vmem,) * X,
         compiler_params=pltpu.CompilerParams(vmem_limit_bytes=6 * MIB),
-        cost_estimate=pl.CostEstimate(flops=0, bytes_accessed=4 * Y * arrived[0].size, transcendentals=0),
+        cost_estimate=pl.CostEstimate(flops=0, bytes_accessed=4 * X * arrived[0].size, transcendentals=0),
     )(*arrived)
 
 
@@ -260,16 +261,16 @@
 
 
 def expand_kernel(shrink, code, base, up, *refs):
-    tables, (out, held, base_held, sems) = refs[:X], refs[X:]
+    tables, (out, held, base_held, sems) = refs[:Y], refs[Y:]
     count = out.shape[0]
     lanes = count // 128
     rank = shrink.shape[0] // lanes * 8
     resident, imported_each = up.shape[0], tables[0].shape[0]
     copies = [pltpu.make_async_copy(up, held.at[pl.ds(0, resident)], sems.at[0])]
-    for e in range(X):
-        place = pl.ds(resident + e * imported_each, imported_each)
-        copies.append(pltpu.make_async_copy(tables[e], held.at[place], sems.at[1 + e]))
-    copies.append(pltpu.make_async_copy(base, base_held, sems.at[1 + X]))
+    for d in range(Y):
+        place = pl.ds(resident + d * imported_each, imported_each)
+        copies.append(pltpu.make_async_copy(tables[d], held.at[place], sems.at[1 + d]))
+    copies.append(pltpu.make_async_copy(base, base_held, sems.at[1 + Y]))
     for copy in copies:
         copy.start()
     rows = jnp.concatenate(
@@ -281,7 +282,7 @@
     home = imported // LIMIT
     e = (x - home % X + X) % X
     d = (y - home // X + Y) % Y
-    at = jnp.where(imported < 0, code[...], resident + (e * Y + d) * LIMIT + imported % LIMIT)
+    at = jnp.where(imported < 0, code[...], resident + (d * X + e) * LIMIT + imported % LIMIT)
     column = jnp.transpose(jnp.broadcast_to(at, (8, count)).astype(jnp.float32))[:, :1]
     pair = jnp.concatenate([rows, rows], axis=1)
     high = pair.astype(jnp.bfloat16).astype(jnp.float32)
@@ -292,7 +293,7 @@
     wanted = jnp.concatenate([wanted, wanted], axis=0)
     total = jnp.zeros((2 * count, out.shape[1]), jnp.float32)
     step = 4
-    bounds = [resident + e * imported_each for e in range(X + 1)]
+    bounds = [resident + d * imported_each for d in range(Y)]
     for first in range(0, held.shape[0] // 2, step):
         if first == 0:
             copies[0].wait()
@@ -314,16 +315,16 @@
 def expand(shrink, code, base, up, tables):
     vmem = pl.BlockSpec(memory_space=pltpu.VMEM)
     hbm = pl.BlockSpec(memory_space=pltpu.HBM)
-    maps = up.shape[0] + X * tables[0].shape[0]
+    maps = up.shape[0] + Y * tables[0].shape[0]
     return pl.pallas_call(
         expand_kernel,
         out_shape=jax.ShapeDtypeStruct(base.shape, jnp.bfloat16),
-        in_specs=[vmem, vmem] + [hbm] * (2 + X),
+        in_specs=[vmem, vmem] + [hbm] * (2 + Y),
         out_specs=vmem,
         scratch_shapes=[
             pltpu.VMEM((maps,) + up.shape[1:], up.dtype),
             pltpu.VMEM(base.shape, base.dtype),
-            pltpu.SemaphoreType.DMA((2 + X,)),
+            pltpu.SemaphoreType.DMA((2 + Y,)),
         ],
     )(shrink, code, base, up, *tables)
 
@@ -349,10 +350,9 @@
     own = local_shrink(code, late, adapter_down)
 
     ups = pick_up(picked, adapter_up)
-    ups = [ups[0]] + [shift(ups[d], "y", Y, d) for d in range(1, Y)]
-    down, ups = lax.optimization_barrier((down, ups))
-    ups = turn(ups)
-    tables = [ups[0]] + [shift(ups[e], "x", X, e) for e in range(1, X)]
+    ups = turn([ups[0]] + [shift(ups[e], "x", X, e) for e in range(1, X)])
+    tables = [ups[0]] + [shift(ups[d], "y", Y, d) for d in range(1, Y)]
+    down, tables[1:AHEAD] = lax.optimization_barrier((down, tables[1:AHEAD]))
 
     parts = imported_shrink(resident, rows, down, own)
     parts = lax.all_to_all(parts.reshape(Y * T, 8, 128), ("y", "z", "c"), 0, 0, tiled=True)

time: 149 us -> 185 us (1.24)
  waiting for transfers between devices: 39.6 us -> 64.7 us
  starting transfers between devices: 63.3 us -> 74.6 us
    ppermute x10, waiting for transfers between devices: 17.8 us -> 46.3 us  [shift(): lax.ppermute(array, axis, [(i, (i + by) % size) for i in range(size)])]
    all_gather x1, waiting for transfers between devices: 7.41 us -> 0.01 us  [shards(): rows = lax.all_gather(sent, ('y', 'c'), axis_index_groups=rings)]
    ppermute x10, starting transfers between devices: 39.6 us -> 46.5 us  [shift(): lax.ppermute(array, axis, [(i, (i + by) % size) for i in range(size)])]
    all_to_all x1, starting transfers between devices: 13.3 us -> 17.8 us  [shards(): lax.all_to_all(parts.reshape(Y * T, 8, 128), ('y', 'z', 'c'), 0, 0, tiled...]
    all_to_all x1, waiting for transfers between devices: 6.5 us -> 10.5 us  [shards(): lax.all_to_all(parts.reshape(Y * T, 8, 128), ('y', 'z', 'c'), 0, 0, tiled...]
  transfers between devices with their start and end apart: 15 -> 15, of which waited for: 7 -> 6; matrix products, arithmetic and copies ran while one was open for 1% -> 1% of each run, Pallas kernels for 13% -> 10%
where the time goes in v8:
time: 185 us
  starting transfers between devices  74.6 us (40%)
  waiting for transfers between devices  64.7 us (35%)
  Pallas kernels  25.7 us (14%)
  between operations  15.1 us (8%)
  local copies, waits for them, and re-layouts  2.24 us (1%)
  matrix products  2.1 us (1%)
    ppermute x10, starting transfers between devices, shift(): lax.ppermute(array, axis, [(i, (i + by) % size) for i in range(size)])  46.5 us
    ppermute x10, waiting for transfers between devices, shift(): lax.ppermute(array, axis, [(i, (i + by) % size) for i in range(size)])  46.3 us
    all_to_all x1, starting transfers between devices, shards(): lax.all_to_all(parts.reshape(Y * T, 8, 128), ('y', 'z', 'c'), 0, 0, tiled...  17.8 us
    all_to_all x1, waiting for transfers between devices, shards(): lax.all_to_all(parts.reshape(Y * T, 8, 128), ('y', 'z', 'c'), 0, 0, tiled...  10.5 us
    all_to_all x1, waiting for transfers between devices, shards(): shrink = lax.all_to_all(add_and_spread(parts), ('z', 'c'), 0, 0, tiled=True)  7.77 us
    pallas_call x1, Pallas kernels, imported_shrink(): pl.pallas_call(functools.partial(imported_kernel, resident), out_shape=ja...  6.85 us
    pallas_call x1, Pallas kernels, expand(): pl.pallas_call(expand_kernel, out_shape=jax.ShapeDtypeStruct(base.shape,...  5.75 us
    all_to_all x1, starting transfers between devices, shards(): shrink = lax.all_to_all(add_and_spread(parts), ('z', 'c'), 0, 0, tiled=True)  5.36 us
  transfers between devices with their start and end apart: 15, of which 6 were waited for; matrix products, arithmetic and copies ran while one was open for 1% of the time, Pallas kernels for 10%

profile of v8, /device:TPU:1, one launch (start us, length us, event | category | flops | bytes accessed | tf_op | source)
XLA Modules:
  0.0 184.5 jit_solution(12377851586507968273)
XLA Ops:
  7.4 2.1 %shard_map.64 = (bf16[272,512]{1,0:T(8,128)(2,1)}, s32[1,256]{1,0:T(1,128)}) custom-call(s32[32,31]{1,0:T(8,128)} %plan.3, s32[1,256]{1,0:T(1,128)} %bitcast.10, bf16[256,512]{1,0:T(8,128)(2,1)} %rows.2), custom_call_target="tpu_custom_call" | custom-call | bytes 524288 | tf_op jit(solution)/shard_map/pallas_call | solution.py:108
  9.5 5.0 %shard_map.65 = (bf16[4,16,64,512]{3,2,1,0:T(8,128)(2,1)}, s32[32,128]{1,0:T(8,128)}) custom-call(s32[32,31]{1,0:T(8,128)} %plan.3, bf16[32,64,512]{2,1,0:T(8,128)(2,1)} %down.1), custom_call_target="tpu_custom_call" | custom-call | bytes 6291456 | tf_op jit(solution)/shard_map/pallas_call | solution.py:67
  14.5 5.0 %all-to-all-start = ((bf16[4,16,64,512]{3,2,1,0:T(8,128)(2,1)}), bf16[4,16,64,512]{3,2,1,0:T(8,128)(2,1)}, u32[]{:S(2)}, u32[]{:S(2)}) async-start(bf16[4,16,64,512]{3,2,1,0:T(8,128)(2,1)} %get-tuple-element.30), calls=%async_computation | async-start | bytes 8388608 | tf_op jit(solution)/shard_map/all_to_all | solution.py:345
  19.5 0.0 reduce-scatter.2.cloned.1.call-start
  19.6 2.1 %fusion = f32[256,2048]{1,0:T(8,128)} fusion(bf16[256,512]{1,0:T(8,128)(2,1)S(1)} %copy-done.3, bf16[512,2048]{1,0:T(8,128)(2,1)S(1)} %copy-done), kind=kOutput, calls=%fused_computation | convolution fusion | flops 536870912 | bytes 4456448 | tf_op jit(solution)/shard_map/dot_general | solution.py:348
  21.7 2.1 %shard_map.66 = (bf16[16,64,128]{2,1,0:T(8,128)(2,1)}, bf16[16,64,128]{2,1,0:T(8,128)(2,1)}, bf16[16,64,128]{2,1,0:T(8,128)(2,1)}, bf16[16,64,128]{2,1,0:T(8,128)(2,1)}) custom-call(s32[32,128]{1,0:T(8,128)} %get-tuple-element.32.picked, bf16[32,64,128]{2,1,0:T(8,128)(2,1)} %up.3), custom_call_target="tpu_custom_call" | custom-call | bytes 1572864 | tf_op jit(solution)/shard_map/pallas_call | solution.py:132
  23.8 3.9 %collective-permute-start = (bf16[16,64,128]{2,1,0:T(8,128)(2,1)}, bf16[16,64,128]{2,1,0:T(8,128)(2,1)S(1)}, u32[]{:S(2)}, u32[]{:S(2)}) collective-permute-start(bf16[16,64,128]{2,1,0:T(8,128)(2,1)} %get-tuple-element.34), channel_id=1, source_target_pairs={{0,16},{16,32},{32,48},{48,0},{1,17},{17,33},{33,49},{49,1},{2,18}... | collective-permute-start | bytes 786440 | tf_op jit(solution)/shard_map/ppermute | solution.py:333
  27.7 4.4 %collective-permute-start.1 = (bf16[16,64,128]{2,1,0:T(8,128)(2,1)}, bf16[16,64,128]{2,1,0:T(8,128)(2,1)S(1)}, u32[]{:S(2)}, u32[]{:S(2)}) collective-permute-start(bf16[16,64,128]{2,1,0:T(8,128)(2,1)} %get-tuple-element.35), channel_id=1, source_target_pairs={{0,32},{16,48},{32,0},{48,16},{1,33},{17,49},{33,1},{49,17},{2,34}... | collective-permute-start | bytes 786440 | tf_op jit(solution)/shard_map/ppermute | solution.py:333
  32.1 3.1 %collective-permute-start.2 = (bf16[16,64,128]{2,1,0:T(8,128)(2,1)}, bf16[16,64,128]{2,1,0:T(8,128)(2,1)S(1)}, u32[]{:S(2)}, u32[]{:S(2)}) collective-permute-start(bf16[16,64,128]{2,1,0:T(8,128)(2,1)} %get-tuple-element.36), channel_id=1, source_target_pairs={{0,48},{16,0},{32,16},{48,32},{1,49},{17,1},{33,17},{49,33},{2,50}... | collective-permute-start | bytes 786440 | tf_op jit(solution)/shard_map/ppermute | solution.py:333
  35.2 28.6 %collective-permute-done.refs_1_ = bf16[16,64,128]{2,1,0:T(8,128)(2,1)S(1)} collective-permute-done((bf16[16,64,128]{2,1,0:T(8,128)(2,1)}, bf16[16,64,128]{2,1,0:T(8,128)(2,1)S(1)}, u32[]{:S(2)}, u32[]{:S(2)}) %collective-permute-start) | collective-permute-done | bytes 262176 | tf_op jit(solution)/shard_map/ppermute | solution.py:333
  63.8 10.2 %collective-permute-done.1.refs_2_ = bf16[16,64,128]{2,1,0:T(8,128)(2,1)S(1)} collective-permute-done((bf16[16,64,128]{2,1,0:T(8,128)(2,1)}, bf16[16,64,128]{2,1,0:T(8,128)(2,1)S(1)}, u32[]{:S(2)}, u32[]{:S(2)}) %collective-permute-start.1) | collective-permute-done | bytes 262176 | tf_op jit(solution)/shard_map/ppermute | solution.py:333
  74.1 0.9 copy-done.1
  75.0 0.1 shard_map.67
  75.1 0.6 copy-done.2
  75.7 8.9 %collective-permute-start.3 = (bf16[8,64,128]{2,1,0:T(8,128)(2,1)S(1)}, bf16[8,64,128]{2,1,0:T(8,128)(2,1)S(1)}, u32[]{:S(2)}, u32[]{:S(2)}) collective-permute-start(bf16[8,64,128]{2,1,0:T(8,128)(2,1)S(1)} %get-tuple-element.37), channel_id=1, source_target_pairs={{0,64},{64,128},{128,192},{192,256},{256,320},{320,384},{384,448},... | collective-permute-start | bytes 393224 | tf_op jit(solution)/shard_map/ppermute | solution.py:333
  84.7 4.2 %collective-permute-start.4 = (bf16[8,64,128]{2,1,0:T(8,128)(2,1)S(1)}, bf16[8,64,128]{2,1,0:T(8,128)(2,1)S(1)}, u32[]{:S(2)}, u32[]{:S(2)}) collective-permute-start(bf16[8,64,128]{2,1,0:T(8,128)(2,1)S(1)} %get-tuple-element.38), channel_id=1, source_target_pairs={{0,128},{64,192},{128,256},{192,320},{256,384},{320,448},{384,0},{... | collective-permute-start | bytes 393224 | tf_op jit(solution)/shard_map/ppermute | solution.py:333
  88.9 4.6 %collective-permute-start.5 = (bf16[8,64,128]{2,1,0:T(8,128)(2,1)S(1)}, bf16[8,64,128]{2,1,0:T(8,128)(2,1)S(1)}, u32[]{:S(2)}, u32[]{:S(2)}) collective-permute-start(bf16[8,64,128]{2,1,0:T(8,128)(2,1)S(1)} %get-tuple-element.39), channel_id=1, source_target_pairs={{0,192},{64,256},{128,320},{192,384},{256,448},{320,0},{384,64},{4... | collective-permute-start | bytes 393224 | tf_op jit(solution)/shard_map/ppermute | solution.py:333
  93.5 3.5 %collective-permute-start.6 = (bf16[8,64,128]{2,1,0:T(8,128)(2,1)S(1)}, bf16[8,64,128]{2,1,0:T(8,128)(2,1)S(1)}, u32[]{:S(2)}, u32[]{:S(2)}) collective-permute-start(bf16[8,64,128]{2,1,0:T(8,128)(2,1)S(1)} %get-tuple-element.40), channel_id=1, source_target_pairs={{0,256},{64,320},{128,384},{192,448},{256,0},{320,64},{384,128},{4... | collective-permute-start | bytes 393224 | tf_op jit(solution)/shard_map/ppermute | solution.py:333
  97.1 4.9 %collective-permute-start.7 = (bf16[8,64,128]{2,1,0:T(8,128)(2,1)S(1)}, bf16[8,64,128]{2,1,0:T(8,128)(2,1)}, u32[]{:S(2)}, u32[]{:S(2)}) collective-permute-start(bf16[8,64,128]{2,1,0:T(8,128)(2,1)S(1)} %get-tuple-element.41), channel_id=1, source_target_pairs={{0,320},{64,384},{128,448},{192,0},{256,64},{320,128},{384,192},{4... | collective-permute-start | bytes 393224 | tf_op jit(solution)/shard_map/ppermute | solution.py:333
  102.0 3.1 %shard_map.68.own = f32[64,256]{1,0:T(8,128)} custom-call(s32[1,256]{1,0:T(1,128)} %get-tuple-element.43.code, bf16[256,512]{1,0:T(8,128)(2,1)} %rows.2, bf16[2048,512]{1,0:T(8,128)(2,1)} %bitcast.7), custom_call_target="tpu_custom_call" | custom-call | flops 536870912 | bytes 2097152 | tf_op jit(solution)/shard_map/pallas_call | solution.py:181
  105.1 4.3 %collective-permute-done.6.refs_4_ = bf16[8,64,128]{2,1,0:T(8,128)(2,1)S(1)} collective-permute-done((bf16[8,64,128]{2,1,0:T(8,128)(2,1)S(1)}, bf16[8,64,128]{2,1,0:T(8,128)(2,1)S(1)}, u32[]{:S(2)}, u32[]{:S(2)}) %collective-permute-start.6) | collective-permute-done | bytes 131104 | tf_op jit(solution)/shard_map/ppermute | solution.py:333
  109.4 3.2 %collective-permute-done.7.refs_5_ = bf16[8,64,128]{2,1,0:T(8,128)(2,1)} collective-permute-done((bf16[8,64,128]{2,1,0:T(8,128)(2,1)S(1)}, bf16[8,64,128]{2,1,0:T(8,128)(2,1)}, u32[]{:S(2)}, u32[]{:S(2)}) %collective-permute-start.7) | collective-permute-done | bytes 131104 | tf_op jit(solution)/shard_map/ppermute | solution.py:333
  112.6 6.9 %shard_map.69 = f32[8,16,8,128]{3,2,1,0:T(8,128)} custom-call(bf16[8,272,512]{2,1,0:T(8,128)(2,1)} %bitcast.8, bf16[4,1024,512]{2,1,0:T(8,128)(2,1)} %bitcast.2.down, f32[64,256]{1,0:T(8,128)} %shard_map.68.own), custom_call_target="tpu_custom_call" | custom-call | flops 1073741824 | bytes 6422528 | tf_op jit(solution)/shard_map/pallas_call | solution.py:230
  119.5 17.8 %all-to-all-start.1 = ((f32[128,8,128]{2,1,0:T(8,128)}), f32[128,8,128]{2,1,0:T(8,128)S(1)}, u32[]{:S(2)}, u32[]{:S(2)}) async-start(f32[128,8,128]{2,1,0:T(8,128)} %bitcast.9), calls=%async_computation.1 | async-start | bytes 1048576 | tf_op jit(solution)/shard_map/all_to_all | solution.py:358
  137.3 5.9 %collective-permute-start.8 = (bf16[8,64,128]{2,1,0:T(8,128)(2,1)S(1)}, bf16[8,64,128]{2,1,0:T(8,128)(2,1)S(1)}, u32[]{:S(2)}, u32[]{:S(2)}) collective-permute-start(bf16[8,64,128]{2,1,0:T(8,128)(2,1)S(1)} %get-tuple-element.51), channel_id=1, source_target_pairs={{0,384},{64,448},{128,0},{192,64},{256,128},{320,192},{384,256},{4... | collective-permute-start | bytes 393224 | tf_op jit(solution)/shard_map/ppermute | solution.py:333
  143.2 3.0 %collective-permute-start.9 = (bf16[8,64,128]{2,1,0:T(8,128)(2,1)S(1)}, bf16[8,64,128]{2,1,0:T(8,128)(2,1)S(1)}, u32[]{:S(2)}, u32[]{:S(2)}) collective-permute-start(bf16[8,64,128]{2,1,0:T(8,128)(2,1)S(1)} %get-tuple-element.52), channel_id=1, source_target_pairs={{0,448},{64,0},{128,64},{192,128},{256,192},{320,256},{384,320},{4... | collective-permute-start | bytes 393224 | tf_op jit(solution)/shard_map/ppermute | solution.py:333
  146.2 10.5 %all-to-all-done.1.parts = f32[128,8,128]{2,1,0:T(8,128)S(1)} async-done(((f32[128,8,128]{2,1,0:T(8,128)}), f32[128,8,128]{2,1,0:T(8,128)S(1)}, u32[]{:S(2)}, u32[]{:S(2)}) %all-to-all-start.1) | async-done | bytes 524320 | tf_op jit(solution)/shard_map/all_to_all | solution.py:358
  156.7 0.8 shard_map.70
  157.5 5.4 %all-to-all-start.2 = ((f32[16,8,128]{2,1,0:T(8,128)}), f32[16,8,128]{2,1,0:T(8,128)S(1)}, u32[]{:S(2)}, u32[]{:S(2)}) async-start(f32[16,8,128]{2,1,0:T(8,128)} %shard_map.70), calls=%async_computation.2 | async-start | bytes 131072 | tf_op jit(solution)/shard_map/all_to_all | solution.py:359
  162.9 7.8 %all-to-all-done.2.shrink = f32[16,8,128]{2,1,0:T(8,128)S(1)} async-done(((f32[16,8,128]{2,1,0:T(8,128)}), f32[16,8,128]{2,1,0:T(8,128)S(1)}, u32[]{:S(2)}, u32[]{:S(2)}) %all-to-all-start.2) | async-done | bytes 65568 | tf_op jit(solution)/shard_map/all_to_all | solution.py:359
  170.7 0.6 copy-done.4
  171.3 5.7 %shard_map.71 = bf16[256,128]{1,0:T(8,128)(2,1)} custom-call(f32[16,8,128]{2,1,0:T(8,128)} %copy-done.4, s32[1,256]{1,0:T(1,128)} %get-tuple-element.43.code, f32[256,128]{1,0:T(8,128)} %reduce-scatter.2.cloned.1.call-done.base, bf16[32,64,128]{2,1,0:T(8,128)(2,1)} %up.3, bf16[8,64,128]{2,1,0:T(8,128)(2,1)} %copy-done.2, bf16[8,64,128]{2,1,0:T(8,128)(2,1)} %copy-done.5, ...), custom_call_target="tpu_custom_call" | custom-call | tf_op jit(solution)/shard_map/pallas_call | solution.py:319
  (31 shorter events, 0.1 us)
Async XLA Ops:
  7.4 12.2 %copy-start = (bf16[512,2048]{1,0:T(8,128)(2,1)S(1)}, bf16[512,2048]{1,0:T(8,128)(2,1)}, u32[]{:S(2)}) copy-start(bf16[512,2048]{1,0:T(8,128)(2,1)} %param.9) | copy-start | bytes 6291460
  7.4 105.2 %all-gather.3.cloned.1.call-start = ((), (), s32[]{:S(2)}) async-start(), calls=%async_computation.5 | async-start | bytes 2506752 | tf_op jit(solution)/shard_map/all_gather | solution.py:343
  14.5 5.1 %copy-start.3 = (bf16[256,512]{1,0:T(8,128)(2,1)S(1)}, bf16[256,512]{1,0:T(8,128)(2,1)}, u32[]{:S(2)}) copy-start(bf16[256,512]{1,0:T(8,128)(2,1)} %rows.2) | copy-start | bytes 786436
  14.5 98.1 %all-to-all-start = ((bf16[4,16,64,512]{3,2,1,0:T(8,128)(2,1)}), bf16[4,16,64,512]{3,2,1,0:T(8,128)(2,1)}, u32[]{:S(2)}, u32[]{:S(2)}) async-start(bf16[4,16,64,512]{3,2,1,0:T(8,128)(2,1)} %get-tuple-element.30), calls=%async_computation | async-start | bytes 8388608 | tf_op jit(solution)/shard_map/all_to_all | solution.py:345
  19.5 143.4 %reduce-scatter.2.cloned.1.call-start = ((), (), s32[]{:S(2)}) async-start(), calls=%async_computation.4 | async-start | bytes 2228224 | tf_op jit(solution)/shard_map/reduce_scatter | solution.py:349
  23.8 40.0 %collective-permute-start = (bf16[16,64,128]{2,1,0:T(8,128)(2,1)}, bf16[16,64,128]{2,1,0:T(8,128)(2,1)S(1)}, u32[]{:S(2)}, u32[]{:S(2)}) collective-permute-start(bf16[16,64,128]{2,1,0:T(8,128)(2,1)} %get-tuple-element.34), channel_id=1, source_target_pairs={{0,16},{16,32},{32,48},{48,0},{1,17},{17,33},{33,49},{49,1},{2,18}... | collective-permute-start | bytes 786440 | tf_op jit(solution)/shard_map/ppermute | solution.py:333
  27.7 46.3 %collective-permute-start.1 = (bf16[16,64,128]{2,1,0:T(8,128)(2,1)}, bf16[16,64,128]{2,1,0:T(8,128)(2,1)S(1)}, u32[]{:S(2)}, u32[]{:S(2)}) collective-permute-start(bf16[16,64,128]{2,1,0:T(8,128)(2,1)} %get-tuple-element.35), channel_id=1, source_target_pairs={{0,32},{16,48},{32,0},{48,16},{1,33},{17,49},{33,1},{49,17},{2,34}... | collective-permute-start | bytes 786440 | tf_op jit(solution)/shard_map/ppermute | solution.py:333
  32.1 41.9 %collective-permute-start.2 = (bf16[16,64,128]{2,1,0:T(8,128)(2,1)}, bf16[16,64,128]{2,1,0:T(8,128)(2,1)S(1)}, u32[]{:S(2)}, u32[]{:S(2)}) collective-permute-start(bf16[16,64,128]{2,1,0:T(8,128)(2,1)} %get-tuple-element.36), channel_id=1, source_target_pairs={{0,48},{16,0},{32,16},{48,32},{1,49},{17,1},{33,17},{49,33},{2,50}... | collective-permute-start | bytes 786440 | tf_op jit(solution)/shard_map/ppermute | solution.py:333
  74.1 1.0 copy-start.1
  75.1 0.6 copy-start.2
  75.7 29.3 %collective-permute-start.3 = (bf16[8,64,128]{2,1,0:T(8,128)(2,1)S(1)}, bf16[8,64,128]{2,1,0:T(8,128)(2,1)S(1)}, u32[]{:S(2)}, u32[]{:S(2)}) collective-permute-start(bf16[8,64,128]{2,1,0:T(8,128)(2,1)S(1)} %get-tuple-element.37), channel_id=1, source_target_pairs={{0,64},{64,128},{128,192},{192,256},{256,320},{320,384},{384,448},... | collective-permute-start | bytes 393224 | tf_op jit(solution)/shard_map/ppermute | solution.py:333
  84.7 20.4 %collective-permute-start.4 = (bf16[8,64,128]{2,1,0:T(8,128)(2,1)S(1)}, bf16[8,64,128]{2,1,0:T(8,128)(2,1)S(1)}, u32[]{:S(2)}, u32[]{:S(2)}) collective-permute-start(bf16[8,64,128]{2,1,0:T(8,128)(2,1)S(1)} %get-tuple-element.38), channel_id=1, source_target_pairs={{0,128},{64,192},{128,256},{192,320},{256,384},{320,448},{384,0},{... | collective-permute-start | bytes 393224 | tf_op jit(solution)/shard_map/ppermute | solution.py:333
  88.9 16.2 %collective-permute-start.5 = (bf16[8,64,128]{2,1,0:T(8,128)(2,1)S(1)}, bf16[8,64,128]{2,1,0:T(8,128)(2,1)S(1)}, u32[]{:S(2)}, u32[]{:S(2)}) collective-permute-start(bf16[8,64,128]{2,1,0:T(8,128)(2,1)S(1)} %get-tuple-element.39), channel_id=1, source_target_pairs={{0,192},{64,256},{128,320},{192,384},{256,448},{320,0},{384,64},{4... | collective-permute-start | bytes 393224 | tf_op jit(solution)/shard_map/ppermute | solution.py:333
  93.5 15.8 %collective-permute-start.6 = (bf16[8,64,128]{2,1,0:T(8,128)(2,1)S(1)}, bf16[8,64,128]{2,1,0:T(8,128)(2,1)S(1)}, u32[]{:S(2)}, u32[]{:S(2)}) collective-permute-start(bf16[8,64,128]{2,1,0:T(8,128)(2,1)S(1)} %get-tuple-element.40), channel_id=1, source_target_pairs={{0,256},{64,320},{128,384},{192,448},{256,0},{320,64},{384,128},{4... | collective-permute-start | bytes 393224 | tf_op jit(solution)/shard_map/ppermute | solution.py:333
  97.1 15.5 %collective-permute-start.7 = (bf16[8,64,128]{2,1,0:T(8,128)(2,1)S(1)}, bf16[8,64,128]{2,1,0:T(8,128)(2,1)}, u32[]{:S(2)}, u32[]{:S(2)}) collective-permute-start(bf16[8,64,128]{2,1,0:T(8,128)(2,1)S(1)} %get-tuple-element.41), channel_id=1, source_target_pairs={{0,320},{64,384},{128,448},{192,0},{256,64},{320,128},{384,192},{4... | collective-permute-start | bytes 393224 | tf_op jit(solution)/shard_map/ppermute | solution.py:333
  105.0 14.4 %copy-start.5 = (bf16[8,64,128]{2,1,0:T(8,128)(2,1)}, bf16[8,64,128]{2,1,0:T(8,128)(2,1)S(1)}, u32[]{:S(2)}) copy-start(bf16[8,64,128]{2,1,0:T(8,128)(2,1)S(1)} %collective-permute-done.3.refs_1_) | copy-start | bytes 393220
  105.0 14.4 %copy-start.6 = (bf16[8,64,128]{2,1,0:T(8,128)(2,1)}, bf16[8,64,128]{2,1,0:T(8,128)(2,1)S(1)}, u32[]{:S(2)}) copy-start(bf16[8,64,128]{2,1,0:T(8,128)(2,1)S(1)} %collective-permute-done.4.refs_2_) | copy-start | bytes 393220
  105.1 14.4 %copy-start.7 = (bf16[8,64,128]{2,1,0:T(8,128)(2,1)}, bf16[8,64,128]{2,1,0:T(8,128)(2,1)S(1)}, u32[]{:S(2)}) copy-start(bf16[8,64,128]{2,1,0:T(8,128)(2,1)S(1)} %collective-permute-done.5.refs_3_) | copy-start | bytes 393220
  109.3 10.1 %copy-start.8 = (bf16[8,64,128]{2,1,0:T(8,128)(2,1)}, bf16[8,64,128]{2,1,0:T(8,128)(2,1)S(1)}, u32[]{:S(2)}) copy-start(bf16[8,64,128]{2,1,0:T(8,128)(2,1)S(1)} %collective-permute-done.6.refs_4_) | copy-start | bytes 393220
  119.5 37.2 %all-to-all-start.1 = ((f32[128,8,128]{2,1,0:T(8,128)}), f32[128,8,128]{2,1,0:T(8,128)S(1)}, u32[]{:S(2)}, u32[]{:S(2)}) async-start(f32[128,8,128]{2,1,0:T(8,128)} %bitcast.9), calls=%async_computation.1 | async-start | bytes 1048576 | tf_op jit(solution)/shard_map/all_to_all | solution.py:358
  137.3 25.6 %collective-permute-start.8 = (bf16[8,64,128]{2,1,0:T(8,128)(2,1)S(1)}, bf16[8,64,128]{2,1,0:T(8,128)(2,1)S(1)}, u32[]{:S(2)}, u32[]{:S(2)}) collective-permute-start(bf16[8,64,128]{2,1,0:T(8,128)(2,1)S(1)} %get-tuple-element.51), channel_id=1, source_target_pairs={{0,384},{64,448},{128,0},{192,64},{256,128},{320,192},{384,256},{4... | collective-permute-start | bytes 393224 | tf_op jit(solution)/shard_map/ppermute | solution.py:333
  143.2 19.7 %collective-permute-start.9 = (bf16[8,64,128]{2,1,0:T(8,128)(2,1)S(1)}, bf16[8,64,128]{2,1,0:T(8,128)(2,1)S(1)}, u32[]{:S(2)}, u32[]{:S(2)}) collective-permute-start(bf16[8,64,128]{2,1,0:T(8,128)(2,1)S(1)} %get-tuple-element.52), channel_id=1, source_target_pairs={{0,448},{64,0},{128,64},{192,128},{256,192},{320,256},{384,320},{4... | collective-permute-start | bytes 393224 | tf_op jit(solution)/shard_map/ppermute | solution.py:333
  157.5 13.2 %all-to-all-start.2 = ((f32[16,8,128]{2,1,0:T(8,128)}), f32[16,8,128]{2,1,0:T(8,128)S(1)}, u32[]{:S(2)}, u32[]{:S(2)}) async-start(f32[16,8,128]{2,1,0:T(8,128)} %shard_map.70), calls=%async_computation.2 | async-start | bytes 131072 | tf_op jit(solution)/shard_map/all_to_all | solution.py:359
  162.8 7.8 %copy-start.9 = (bf16[8,64,128]{2,1,0:T(8,128)(2,1)}, bf16[8,64,128]{2,1,0:T(8,128)(2,1)S(1)}, u32[]{:S(2)}) copy-start(bf16[8,64,128]{2,1,0:T(8,128)(2,1)S(1)} %collective-permute-done.8.refs_6_) | copy-start | bytes 393220
  162.9 7.8 %copy-start.10 = (bf16[8,64,128]{2,1,0:T(8,128)(2,1)}, bf16[8,64,128]{2,1,0:T(8,128)(2,1)S(1)}, u32[]{:S(2)}) copy-start(bf16[8,64,128]{2,1,0:T(8,128)(2,1)S(1)} %collective-permute-done.9.refs_7_) | copy-start | bytes 393220
  170.7 0.6 copy-start.4
Sparse Core Ops, SparseCore 0:
  10.3 46.4 all-gather.2
Sparse Core Ops, SparseCore 1:
  22.8 67.4 reduce-scatter.1

commit v9 on v7

--- a/solution.py
+++ b/solution.py
@@ -349,8 +349,13 @@
     own = local_shrink(code, late, adapter_down)
 
     ups = pick_up(picked, adapter_up)
-    ups = [ups[0]] + [shift(ups[d], "y", Y, d) for d in range(1, Y)]
-    down, ups = lax.optimization_barrier((down, ups))
+    near, far = (1, 7, 2, 6), (3, 5, 4)
+    moved = {d: shift(ups[d], "y", Y, d) for d in near}
+    moved, later = lax.optimization_barrier((moved, {d: ups[d] for d in far}))
+    moved |= {d: shift(later[d], "y", Y, d) for d in far}
+    moved[0] = ups[0]
+    down, moved = lax.optimization_barrier((down, moved))
+    ups = [moved[d] for d in range(Y)]
     ups = turn(ups)
     tables = [ups[0]] + [shift(ups[e], "x", X, e) for e in range(1, X)]
 

time: 149 us -> 147 us (0.987)
  waiting for transfers between devices: 39.6 us -> 34.8 us
  starting transfers between devices: 63.3 us -> 66.3 us
    all_gather x1, waiting for transfers between devices: 7.41 us -> 0.01 us  [shards(): rows = lax.all_gather(sent, ('y', 'c'), axis_index_groups=rings)]
    all_to_all x1, starting transfers between devices: 13.3 us -> 17.2 us  [shards(): lax.all_to_all(parts.reshape(Y * T, 8, 128), ('y', 'z', 'c'), 0, 0, tiled...]
    ppermute x10, waiting for transfers between devices: 17.8 us -> 20.5 us  [shift(): lax.ppermute(array, axis, [(i, (i + by) % size) for i in range(size)])]
where the time goes in v9:
time: 147 us; the launch traced here: 146 us
  starting transfers between devices  66.3 us (45%)
  waiting for transfers between devices  34.8 us (24%)
  Pallas kernels  26 us (18%)
  between operations  15.1 us (10%)
  local copies, waits for them, and re-layouts  2.22 us (2%)
  matrix products  2.09 us (1%)
    ppermute x10, starting transfers between devices, shift(): lax.ppermute(array, axis, [(i, (i + by) % size) for i in range(size)])  38.7 us
    ppermute x10, waiting for transfers between devices, shift(): lax.ppermute(array, axis, [(i, (i + by) % size) for i in range(size)])  20.5 us
    all_to_all x1, starting transfers between devices, shards(): lax.all_to_all(parts.reshape(Y * T, 8, 128), ('y', 'z', 'c'), 0, 0, tiled...  17.2 us
    all_to_all x1, waiting for transfers between devices, shards(): shrink = lax.all_to_all(add_and_spread(parts), ('z', 'c'), 0, 0, tiled=True)  7.75 us
    pallas_call x1, Pallas kernels, imported_shrink(): pl.pallas_call(functools.partial(imported_kernel, resident), out_shape=ja...  6.91 us
    all_to_all x1, waiting for transfers between devices, shards(): lax.all_to_all(parts.reshape(Y * T, 8, 128), ('y', 'z', 'c'), 0, 0, tiled...  6.52 us
    all_to_all x1, starting transfers between devices, shards(): shrink = lax.all_to_all(add_and_spread(parts), ('z', 'c'), 0, 0, tiled=True)  5.36 us
    pallas_call x1, Pallas kernels, expand(): pl.pallas_call(expand_kernel, out_shape=jax.ShapeDtypeStruct(base.shape,...  5.06 us
  transfers between devices with their start and end apart: 15, of which 7 were waited for; matrix products, arithmetic and copies ran while one was open for 1% of the time, Pallas kernels for 13%

profile of v9, /device:TPU:1, one launch (start us, length us, event | category | flops | bytes accessed | tf_op | source)
XLA Modules:
  0.0 146.5 jit_solution(2908016566681935231)
XLA Ops:
  7.4 2.1 %shard_map.64 = (bf16[272,512]{1,0:T(8,128)(2,1)}, s32[1,256]{1,0:T(1,128)}) custom-call(s32[32,31]{1,0:T(8,128)} %plan.3, s32[1,256]{1,0:T(1,128)} %bitcast.10, bf16[256,512]{1,0:T(8,128)(2,1)} %rows.2), custom_call_target="tpu_custom_call" | custom-call | bytes 524288 | tf_op jit(solution)/shard_map/pallas_call | solution.py:107
  9.5 5.0 %shard_map.65 = (bf16[4,16,64,512]{3,2,1,0:T(8,128)(2,1)}, s32[32,128]{1,0:T(8,128)}) custom-call(s32[32,31]{1,0:T(8,128)} %plan.3, bf16[32,64,512]{2,1,0:T(8,128)(2,1)} %down.1), custom_call_target="tpu_custom_call" | custom-call | bytes 6291456 | tf_op jit(solution)/shard_map/pallas_call | solution.py:66
  14.5 5.0 %all-to-all-start = ((bf16[4,16,64,512]{3,2,1,0:T(8,128)(2,1)}), bf16[4,16,64,512]{3,2,1,0:T(8,128)(2,1)}, u32[]{:S(2)}, u32[]{:S(2)}) async-start(bf16[4,16,64,512]{3,2,1,0:T(8,128)(2,1)} %get-tuple-element.40), calls=%async_computation | async-start | bytes 8388608 | tf_op jit(solution)/shard_map/all_to_all | solution.py:344
  19.6 2.1 %fusion = f32[256,2048]{1,0:T(8,128)} fusion(bf16[256,512]{1,0:T(8,128)(2,1)S(1)} %copy-done.5, bf16[512,2048]{1,0:T(8,128)(2,1)S(1)} %copy-done), kind=kOutput, calls=%fused_computation | convolution fusion | flops 536870912 | bytes 4456448 | tf_op jit(solution)/shard_map/dot_general | solution.py:347
  21.7 2.1 %shard_map.66 = (bf16[8,64,128]{2,1,0:T(8,128)(2,1)}, bf16[8,64,128]{2,1,0:T(8,128)(2,1)}, bf16[8,64,128]{2,1,0:T(8,128)(2,1)}, bf16[8,64,128]{2,1,0:T(8,128)(2,...) custom-call(s32[32,128]{1,0:T(8,128)} %get-tuple-element.42.picked, ...), custom_call_target="tpu_custom_call" | custom-call | bytes 1572864 | tf_op jit(solution)/shard_map/pallas_call | solution.py:131
  23.8 4.0 %collective-permute-start = (bf16[8,64,128]{2,1,0:T(8,128)(2,1)}, bf16[8,64,128]{2,1,0:T(8,128)(2,1)S(1)}, u32[]{:S(2)}, u32[]{:S(2)}) collective-permute-start(bf16[8,64,128]{2,1,0:T(8,128)(2,1)} %get-tuple-element.44), channel_id=1, source_target_pairs={{0,64},{64,128},{128,192},{192,256},{256,320},{320,384},{384,448},... | collective-permute-start | bytes 393224 | tf_op jit(solution)/shard_map/ppermute | solution.py:332
  27.9 4.2 %collective-permute-start.1 = (bf16[8,64,128]{2,1,0:T(8,128)(2,1)}, bf16[8,64,128]{2,1,0:T(8,128)(2,1)S(1)}, u32[]{:S(2)}, u32[]{:S(2)}) collective-permute-start(bf16[8,64,128]{2,1,0:T(8,128)(2,1)} %get-tuple-element.45), channel_id=1, source_target_pairs={{0,128},{64,192},{128,256},{192,320},{256,384},{320,448},{384,0},{... | collective-permute-start | bytes 393224 | tf_op jit(solution)/shard_map/ppermute | solution.py:332
  32.1 3.2 %collective-permute-start.2 = (bf16[8,64,128]{2,1,0:T(8,128)(2,1)}, bf16[8,64,128]{2,1,0:T(8,128)(2,1)S(1)}, u32[]{:S(2)}, u32[]{:S(2)}) collective-permute-start(bf16[8,64,128]{2,1,0:T(8,128)(2,1)} %get-tuple-element.46), channel_id=1, source_target_pairs={{0,384},{64,448},{128,0},{192,64},{256,128},{320,192},{384,256},{4... | collective-permute-start | bytes 393224 | tf_op jit(solution)/shard_map/ppermute | solution.py:332
  35.3 2.6 %collective-permute-start.3 = (bf16[8,64,128]{2,1,0:T(8,128)(2,1)}, bf16[8,64,128]{2,1,0:T(8,128)(2,1)S(1)}, u32[]{:S(2)}, u32[]{:S(2)}) collective-permute-start(bf16[8,64,128]{2,1,0:T(8,128)(2,1)} %get-tuple-element.47), channel_id=1, source_target_pairs={{0,448},{64,0},{128,64},{192,128},{256,192},{320,256},{384,320},{4... | collective-permute-start | bytes 393224 | tf_op jit(solution)/shard_map/ppermute | solution.py:332
  37.9 2.7 %collective-permute-done.1.refs_2_ = bf16[8,64,128]{2,1,0:T(8,128)(2,1)S(1)} collective-permute-done((bf16[8,64,128]{2,1,0:T(8,128)(2,1)}, bf16[8,64,128]{2,1,0:T(8,128)(2,1)S(1)}, u32[]{:S(2)}, u32[]{:S(2)}) %collective-permute-start.1) | collective-permute-done | bytes 131104 | tf_op jit(solution)/shard_map/ppermute | solution.py:332
  40.6 0.6 collective-permute-done.2.refs_6_
  41.2 9.5 %collective-permute-done.3.refs_7_ = bf16[8,64,128]{2,1,0:T(8,128)(2,1)S(1)} collective-permute-done((bf16[8,64,128]{2,1,0:T(8,128)(2,1)}, bf16[8,64,128]{2,1,0:T(8,128)(2,1)S(1)}, u32[]{:S(2)}, u32[]{:S(2)}) %collective-permute-start.3) | collective-permute-done | bytes 131104 | tf_op jit(solution)/shard_map/ppermute | solution.py:332
  50.8 5.1 %collective-permute-start.4 = (bf16[8,64,128]{2,1,0:T(8,128)(2,1)}, bf16[8,64,128]{2,1,0:T(8,128)(2,1)S(1)}, u32[]{:S(2)}, u32[]{:S(2)}) collective-permute-start(bf16[8,64,128]{2,1,0:T(8,128)(2,1)} %get-tuple-element.53), channel_id=1, source_target_pairs={{0,192},{64,256},{128,320},{192,384},{256,448},{320,0},{384,64},{4... | collective-permute-start | bytes 393224 | tf_op jit(solution)/shard_map/ppermute | solution.py:332
  55.8 2.9 %collective-permute-start.5 = (bf16[8,64,128]{2,1,0:T(8,128)(2,1)}, bf16[8,64,128]{2,1,0:T(8,128)(2,1)S(1)}, u32[]{:S(2)}, u32[]{:S(2)}) collective-permute-start(bf16[8,64,128]{2,1,0:T(8,128)(2,1)} %get-tuple-element.54), channel_id=1, source_target_pairs={{0,256},{64,320},{128,384},{192,448},{256,0},{320,64},{384,128},{4... | collective-permute-start | bytes 393224 | tf_op jit(solution)/shard_map/ppermute | solution.py:332
  58.7 6.4 %collective-permute-start.6 = (bf16[8,64,128]{2,1,0:T(8,128)(2,1)}, bf16[8,64,128]{2,1,0:T(8,128)(2,1)S(1)}, u32[]{:S(2)}, u32[]{:S(2)}) collective-permute-start(bf16[8,64,128]{2,1,0:T(8,128)(2,1)} %get-tuple-element.55), channel_id=1, source_target_pairs={{0,320},{64,384},{128,448},{192,0},{256,64},{320,128},{384,192},{4... | collective-permute-start | bytes 393224 | tf_op jit(solution)/shard_map/ppermute | solution.py:332
  65.1 3.1 %shard_map.67.own = f32[64,256]{1,0:T(8,128)} custom-call(s32[1,256]{1,0:T(1,128)} %get-tuple-element.59.code, bf16[256,512]{1,0:T(8,128)(2,1)} %rows.2, bf16[2048,512]{1,0:T(8,128)(2,1)} %bitcast.7), custom_call_target="tpu_custom_call" | custom-call | flops 536870912 | bytes 2097152 | tf_op jit(solution)/shard_map/pallas_call | solution.py:180
  68.2 6.9 %collective-permute-done.5.refs_4_ = bf16[8,64,128]{2,1,0:T(8,128)(2,1)S(1)} collective-permute-done((bf16[8,64,128]{2,1,0:T(8,128)(2,1)}, bf16[8,64,128]{2,1,0:T(8,128)(2,1)S(1)}, u32[]{:S(2)}, u32[]{:S(2)}) %collective-permute-start.5) | collective-permute-done | bytes 131104 | tf_op jit(solution)/shard_map/ppermute | solution.py:332
  75.0 0.7 collective-permute-done.6.refs_5_
  75.8 6.9 %shard_map.68 = f32[8,16,8,128]{3,2,1,0:T(8,128)} custom-call(bf16[8,272,512]{2,1,0:T(8,128)(2,1)} %bitcast.8, bf16[4,1024,512]{2,1,0:T(8,128)(2,1)} %bitcast.2.down, f32[64,256]{1,0:T(8,128)} %shard_map.67.own), custom_call_target="tpu_custom_call" | custom-call | flops 1073741824 | bytes 6422528 | tf_op jit(solution)/shard_map/pallas_call | solution.py:229
  82.7 17.2 %all-to-all-start.1 = ((f32[128,8,128]{2,1,0:T(8,128)}), f32[128,8,128]{2,1,0:T(8,128)S(1)}, u32[]{:S(2)}, u32[]{:S(2)}) async-start(f32[128,8,128]{2,1,0:T(8,128)} %bitcast.9), calls=%async_computation.1 | async-start | bytes 1048576 | tf_op jit(solution)/shard_map/all_to_all | solution.py:363
  99.9 0.9 copy-done.4
  100.8 1.0 shard_map.70
  101.8 0.7 copy-done.1
  102.5 3.3 %collective-permute-start.7 = (bf16[16,64,128]{2,1,0:T(8,128)(2,1)}, bf16[16,64,128]{2,1,0:T(8,128)(2,1)S(1)}, u32[]{:S(2)}, u32[]{:S(2)}) collective-permute-start(bf16[16,64,128]{2,1,0:T(8,128)(2,1)} %get-tuple-element.70), channel_id=1, source_target_pairs={{0,16},{16,32},{32,48},{48,0},{1,17},{17,33},{33,49},{49,1},{2,18}... | collective-permute-start | bytes 786440 | tf_op jit(solution)/shard_map/ppermute | solution.py:332
  105.7 3.8 %collective-permute-start.8 = (bf16[16,64,128]{2,1,0:T(8,128)(2,1)}, bf16[16,64,128]{2,1,0:T(8,128)(2,1)S(1)}, u32[]{:S(2)}, u32[]{:S(2)}) collective-permute-start(bf16[16,64,128]{2,1,0:T(8,128)(2,1)} %get-tuple-element.71), channel_id=1, source_target_pairs={{0,32},{16,48},{32,0},{48,16},{1,33},{17,49},{33,1},{49,17},{2,34}... | collective-permute-start | bytes 786440 | tf_op jit(solution)/shard_map/ppermute | solution.py:332
  109.5 3.3 %collective-permute-start.9 = (bf16[16,64,128]{2,1,0:T(8,128)(2,1)}, bf16[16,64,128]{2,1,0:T(8,128)(2,1)S(1)}, u32[]{:S(2)}, u32[]{:S(2)}) collective-permute-start(bf16[16,64,128]{2,1,0:T(8,128)(2,1)} %get-tuple-element.72), channel_id=1, source_target_pairs={{0,48},{16,0},{32,16},{48,32},{1,49},{17,1},{33,17},{49,33},{2,50}... | collective-permute-start | bytes 786440 | tf_op jit(solution)/shard_map/ppermute | solution.py:332
  112.8 6.5 %all-to-all-done.1.parts = f32[128,8,128]{2,1,0:T(8,128)S(1)} async-done(((f32[128,8,128]{2,1,0:T(8,128)}), f32[128,8,128]{2,1,0:T(8,128)S(1)}, u32[]{:S(2)}, u32[]{:S(2)}) %all-to-all-start.1) | async-done | bytes 524320 | tf_op jit(solution)/shard_map/all_to_all | solution.py:363
  119.4 0.8 shard_map.69
  120.1 5.4 %all-to-all-start.2 = ((f32[16,8,128]{2,1,0:T(8,128)}), f32[16,8,128]{2,1,0:T(8,128)S(1)}, u32[]{:S(2)}, u32[]{:S(2)}) async-start(f32[16,8,128]{2,1,0:T(8,128)} %shard_map.69), calls=%async_computation.2 | async-start | bytes 131072 | tf_op jit(solution)/shard_map/all_to_all | solution.py:364
  125.6 7.7 %all-to-all-done.2.shrink = f32[16,8,128]{2,1,0:T(8,128)S(1)} async-done(((f32[16,8,128]{2,1,0:T(8,128)}), f32[16,8,128]{2,1,0:T(8,128)S(1)}, u32[]{:S(2)}, u32[]{:S(2)}) %all-to-all-start.2) | async-done | bytes 65568 | tf_op jit(solution)/shard_map/all_to_all | solution.py:364
  133.3 0.6 copy-done.9
  133.9 5.1 %shard_map.71 = bf16[256,128]{1,0:T(8,128)(2,1)} custom-call(f32[16,8,128]{2,1,0:T(8,128)} %copy-done.9, s32[1,256]{1,0:T(1,128)} %get-tuple-element.59.code, f32[256,128]{1,0:T(8,128)} %reduce-scatter.2.cloned.1.call-done.base, bf16[32,64,128]{2,1,0:T(8,128)(2,1)} %up.3, bf16[16,64,128]{2,1,0:T(8,128)(2,1)} %copy-done.1, bf16[16,64,128]{2,1,0:T(8,128)(2,1)} %copy-done.6, ...), custom_call_target="tpu_custom_call" | custom-call | tf_op jit(solution)/shard_map/pallas_call | solution.py:318
  (29 shorter events, 0.2 us)
Async XLA Ops:
  7.4 12.2 %copy-start = (bf16[512,2048]{1,0:T(8,128)(2,1)S(1)}, bf16[512,2048]{1,0:T(8,128)(2,1)}, u32[]{:S(2)}) copy-start(bf16[512,2048]{1,0:T(8,128)(2,1)} %param.9) | copy-start | bytes 6291460
  7.4 68.4 %all-gather.3.cloned.1.call-start = ((), (), s32[]{:S(2)}) async-start(), calls=%async_computation.5 | async-start | bytes 2506752 | tf_op jit(solution)/shard_map/all_gather | solution.py:342
  14.5 5.1 %copy-start.5 = (bf16[256,512]{1,0:T(8,128)(2,1)S(1)}, bf16[256,512]{1,0:T(8,128)(2,1)}, u32[]{:S(2)}) copy-start(bf16[256,512]{1,0:T(8,128)(2,1)} %rows.2) | copy-start | bytes 786436
  14.5 61.3 %all-to-all-start = ((bf16[4,16,64,512]{3,2,1,0:T(8,128)(2,1)}), bf16[4,16,64,512]{3,2,1,0:T(8,128)(2,1)}, u32[]{:S(2)}, u32[]{:S(2)}) async-start(bf16[4,16,64,512]{3,2,1,0:T(8,128)(2,1)} %get-tuple-element.40), calls=%async_computation | async-start | bytes 8388608 | tf_op jit(solution)/shard_map/all_to_all | solution.py:344
  19.5 106.1 %reduce-scatter.2.cloned.1.call-start = ((), (), s32[]{:S(2)}) async-start(), calls=%async_computation.4 | async-start | bytes 2228224 | tf_op jit(solution)/shard_map/reduce_scatter | solution.py:348
  23.8 14.0 %collective-permute-start = (bf16[8,64,128]{2,1,0:T(8,128)(2,1)}, bf16[8,64,128]{2,1,0:T(8,128)(2,1)S(1)}, u32[]{:S(2)}, u32[]{:S(2)}) collective-permute-start(bf16[8,64,128]{2,1,0:T(8,128)(2,1)} %get-tuple-element.44), channel_id=1, source_target_pairs={{0,64},{64,128},{128,192},{192,256},{256,320},{320,384},{384,448},... | collective-permute-start | bytes 393224 | tf_op jit(solution)/shard_map/ppermute | solution.py:332
  27.9 12.8 %collective-permute-start.1 = (bf16[8,64,128]{2,1,0:T(8,128)(2,1)}, bf16[8,64,128]{2,1,0:T(8,128)(2,1)S(1)}, u32[]{:S(2)}, u32[]{:S(2)}) collective-permute-start(bf16[8,64,128]{2,1,0:T(8,128)(2,1)} %get-tuple-element.45), channel_id=1, source_target_pairs={{0,128},{64,192},{128,256},{192,320},{256,384},{320,448},{384,0},{... | collective-permute-start | bytes 393224 | tf_op jit(solution)/shard_map/ppermute | solution.py:332
  32.1 9.2 %collective-permute-start.2 = (bf16[8,64,128]{2,1,0:T(8,128)(2,1)}, bf16[8,64,128]{2,1,0:T(8,128)(2,1)S(1)}, u32[]{:S(2)}, u32[]{:S(2)}) collective-permute-start(bf16[8,64,128]{2,1,0:T(8,128)(2,1)} %get-tuple-element.46), channel_id=1, source_target_pairs={{0,384},{64,448},{128,0},{192,64},{256,128},{320,192},{384,256},{4... | collective-permute-start | bytes 393224 | tf_op jit(solution)/shard_map/ppermute | solution.py:332
  35.3 15.5 %collective-permute-start.3 = (bf16[8,64,128]{2,1,0:T(8,128)(2,1)}, bf16[8,64,128]{2,1,0:T(8,128)(2,1)S(1)}, u32[]{:S(2)}, u32[]{:S(2)}) collective-permute-start(bf16[8,64,128]{2,1,0:T(8,128)(2,1)} %get-tuple-element.47), channel_id=1, source_target_pairs={{0,448},{64,0},{128,64},{192,128},{256,192},{320,256},{384,320},{4... | collective-permute-start | bytes 393224 | tf_op jit(solution)/shard_map/ppermute | solution.py:332
  50.8 17.4 %collective-permute-start.4 = (bf16[8,64,128]{2,1,0:T(8,128)(2,1)}, bf16[8,64,128]{2,1,0:T(8,128)(2,1)S(1)}, u32[]{:S(2)}, u32[]{:S(2)}) collective-permute-start(bf16[8,64,128]{2,1,0:T(8,128)(2,1)} %get-tuple-element.53), channel_id=1, source_target_pairs={{0,192},{64,256},{128,320},{192,384},{256,448},{320,0},{384,64},{4... | collective-permute-start | bytes 393224 | tf_op jit(solution)/shard_map/ppermute | solution.py:332
  55.8 19.2 %collective-permute-start.5 = (bf16[8,64,128]{2,1,0:T(8,128)(2,1)}, bf16[8,64,128]{2,1,0:T(8,128)(2,1)S(1)}, u32[]{:S(2)}, u32[]{:S(2)}) collective-permute-start(bf16[8,64,128]{2,1,0:T(8,128)(2,1)} %get-tuple-element.54), channel_id=1, source_target_pairs={{0,256},{64,320},{128,384},{192,448},{256,0},{320,64},{384,128},{4... | collective-permute-start | bytes 393224 | tf_op jit(solution)/shard_map/ppermute | solution.py:332
  58.7 17.1 %collective-permute-start.6 = (bf16[8,64,128]{2,1,0:T(8,128)(2,1)}, bf16[8,64,128]{2,1,0:T(8,128)(2,1)S(1)}, u32[]{:S(2)}, u32[]{:S(2)}) collective-permute-start(bf16[8,64,128]{2,1,0:T(8,128)(2,1)} %get-tuple-element.55), channel_id=1, source_target_pairs={{0,320},{64,384},{128,448},{192,0},{256,64},{320,128},{384,192},{4... | collective-permute-start | bytes 393224 | tf_op jit(solution)/shard_map/ppermute | solution.py:332
  75.8 6.9 %copy-start.3 = (bf16[8,64,128]{2,1,0:T(8,128)(2,1)}, bf16[8,64,128]{2,1,0:T(8,128)(2,1)S(1)}, u32[]{:S(2)}) copy-start(bf16[8,64,128]{2,1,0:T(8,128)(2,1)S(1)} %collective-permute-done.6.refs_5_) | copy-start | bytes 393220
  75.8 24.1 %copy-start.2 = (bf16[8,64,128]{2,1,0:T(8,128)(2,1)S(1)}, bf16[8,64,128]{2,1,0:T(8,128)(2,1)}, u32[]{:S(2)}) copy-start(bf16[8,64,128]{2,1,0:T(8,128)(2,1)} %get-tuple-element.61.refs_0_) | copy-start | bytes 393220
  82.7 36.7 %all-to-all-start.1 = ((f32[128,8,128]{2,1,0:T(8,128)}), f32[128,8,128]{2,1,0:T(8,128)S(1)}, u32[]{:S(2)}, u32[]{:S(2)}) async-start(f32[128,8,128]{2,1,0:T(8,128)} %bitcast.9), calls=%async_computation.1 | async-start | bytes 1048576 | tf_op jit(solution)/shard_map/all_to_all | solution.py:363
  99.9 0.9 copy-start.4
  101.8 0.7 copy-start.1
  102.5 23.0 %collective-permute-start.7 = (bf16[16,64,128]{2,1,0:T(8,128)(2,1)}, bf16[16,64,128]{2,1,0:T(8,128)(2,1)S(1)}, u32[]{:S(2)}, u32[]{:S(2)}) collective-permute-start(bf16[16,64,128]{2,1,0:T(8,128)(2,1)} %get-tuple-element.70), channel_id=1, source_target_pairs={{0,16},{16,32},{32,48},{48,0},{1,17},{17,33},{33,49},{49,1},{2,18}... | collective-permute-start | bytes 786440 | tf_op jit(solution)/shard_map/ppermute | solution.py:332
  105.7 19.8 %collective-permute-start.8 = (bf16[16,64,128]{2,1,0:T(8,128)(2,1)}, bf16[16,64,128]{2,1,0:T(8,128)(2,1)S(1)}, u32[]{:S(2)}, u32[]{:S(2)}) collective-permute-start(bf16[16,64,128]{2,1,0:T(8,128)(2,1)} %get-tuple-element.71), channel_id=1, source_target_pairs={{0,32},{16,48},{32,0},{48,16},{1,33},{17,49},{33,1},{49,17},{2,34}... | collective-permute-start | bytes 786440 | tf_op jit(solution)/shard_map/ppermute | solution.py:332
  109.5 16.0 %collective-permute-start.9 = (bf16[16,64,128]{2,1,0:T(8,128)(2,1)}, bf16[16,64,128]{2,1,0:T(8,128)(2,1)S(1)}, u32[]{:S(2)}, u32[]{:S(2)}) collective-permute-start(bf16[16,64,128]{2,1,0:T(8,128)(2,1)} %get-tuple-element.72), channel_id=1, source_target_pairs={{0,48},{16,0},{32,16},{48,32},{1,49},{17,1},{33,17},{49,33},{2,50}... | collective-permute-start | bytes 786440 | tf_op jit(solution)/shard_map/ppermute | solution.py:332
  120.1 13.2 %all-to-all-start.2 = ((f32[16,8,128]{2,1,0:T(8,128)}), f32[16,8,128]{2,1,0:T(8,128)S(1)}, u32[]{:S(2)}, u32[]{:S(2)}) async-start(f32[16,8,128]{2,1,0:T(8,128)} %shard_map.69), calls=%async_computation.2 | async-start | bytes 131072 | tf_op jit(solution)/shard_map/all_to_all | solution.py:364
  125.5 7.8 %copy-start.6 = (bf16[16,64,128]{2,1,0:T(8,128)(2,1)}, bf16[16,64,128]{2,1,0:T(8,128)(2,1)S(1)}, u32[]{:S(2)}) copy-start(bf16[16,64,128]{2,1,0:T(8,128)(2,1)S(1)} %collective-permute-done.7.refs_1_) | copy-start | bytes 786436
  125.5 7.8 %copy-start.7 = (bf16[16,64,128]{2,1,0:T(8,128)(2,1)}, bf16[16,64,128]{2,1,0:T(8,128)(2,1)S(1)}, u32[]{:S(2)}) copy-start(bf16[16,64,128]{2,1,0:T(8,128)(2,1)S(1)} %collective-permute-done.8.refs_2_) | copy-start | bytes 786436
  125.5 7.8 %copy-start.8 = (bf16[16,64,128]{2,1,0:T(8,128)(2,1)}, bf16[16,64,128]{2,1,0:T(8,128)(2,1)S(1)}, u32[]{:S(2)}) copy-start(bf16[16,64,128]{2,1,0:T(8,128)(2,1)S(1)} %collective-permute-done.9.refs_3_) | copy-start | bytes 786436
  133.3 0.6 copy-start.9
Sparse Core Ops, SparseCore 0:
  10.3 65.1 all-gather.2
Sparse Core Ops, SparseCore 1:
  22.8 67.4 reduce-scatter.1

commit v10 on v9

--- a/solution.py
+++ b/solution.py
@@ -83,9 +83,10 @@
     )(plan, down)
 
 
-def prepare_kernel(resident, plan, slots, rows, out, code_out):
+def pick_up_kernel(picked, plan, slots, up, *refs):
+    outs, code_out = refs[:Y], refs[Y]
+    resident, rank, lanes = up.shape
     y, x = spot()
-    height, width = rows.shape
     slot = slots[...]
     code = slot
     before = jnp.int32(-1)
@@ -95,66 +96,55 @@
         code = jnp.where(slot == resident + k, resident + home * LIMIT + again, code)
         before = home
     code_out[...] = code
-    out[0:height, :] = rows[...]
-    wide = jnp.concatenate([code.astype(jnp.float32), jnp.zeros((1, width - height), jnp.float32)], axis=1)
-    out[height:, :] = jnp.broadcast_to(wide, (CODE_ROWS, width)).astype(out.dtype)
-
-
-def prepare(resident, plan, slots, rows):
-    height, width = rows.shape
-    smem = pl.BlockSpec(memory_space=pltpu.SMEM)
-    vmem = pl.BlockSpec(memory_space=pltpu.VMEM)
-    return pl.pallas_call(
-        functools.partial(prepare_kernel, resident),
-        out_shape=(
-            jax.ShapeDtypeStruct((height + CODE_ROWS, width), rows.dtype),
-            jax.ShapeDtypeStruct(slots.shape, jnp.int32),
-        ),
-        in_specs=[smem, vmem, vmem],
-        out_specs=(vmem, vmem),
-        cost_estimate=pl.CostEstimate(flops=0, bytes_accessed=4 * rows.size, transcendentals=0),
-    )(plan, slots, rows)
-
-
-def pick_up_kernel(picked, up, *outs):
-    y, _ = spot()
+    tail = [code[:, k * lanes : (k + 1) * lanes].astype(jnp.float32) for k in range(code.shape[1] // lanes)]
+    tail.append(jnp.zeros((CODE_ROWS - len(tail), lanes), jnp.float32))
+    tail = jnp.concatenate(tail, axis=0).astype(up.dtype)
     for d in range(Y):
         row = lax.rem(y + d, Y)
-        for x in range(X):
+        for column in range(X):
             for j in range(LIMIT):
-                outs[d][x * LIMIT + j] = up[picked[row * X + x, j]]
-
-
-def pick_up(picked, up):
+                at = (column * LIMIT + j) * rank
+                outs[d][at : at + rank, :] = up[picked[row * X + column, j]]
+        outs[d][X * LIMIT * rank :, :] = tail
+
+
+def pick_up(picked, plan, slots, up):
     smem = pl.BlockSpec(memory_space=pltpu.SMEM)
     vmem = pl.BlockSpec(memory_space=pltpu.VMEM)
+    _, rank, lanes = up.shape
+    shape = jax.ShapeDtypeStruct((X * LIMIT * rank + CODE_ROWS, lanes), up.dtype)
     return pl.pallas_call(
         pick_up_kernel,
-        out_shape=(jax.ShapeDtypeStruct((X * LIMIT,) + up.shape[1:], up.dtype),) * Y,
-        in_specs=[smem, vmem],
-        out_specs=(vmem,) * Y,
+        out_shape=(shape,) * Y + (jax.ShapeDtypeStruct(slots.shape, jnp.int32),),
+        in_specs=[smem, smem, vmem, vmem],
+        out_specs=(vmem,) * (Y + 1),
         cost_estimate=pl.CostEstimate(flops=0, bytes_accessed=6 * up.size, transcendentals=0),
-    )(picked, up)
+    )(picked, plan, slots, up)
 
 
 def turn_kernel(*refs):
-    arrived, outs = refs[:Y], refs[Y:]
+    arrived, outs, codes = refs[:Y], refs[Y:-1], refs[-1]
     _, x = spot()
+    rank = outs[0].shape[1]
+    for d in range(Y):
+        codes[d] = arrived[d][X * LIMIT * rank :, :]
     for e in range(X):
         column = lax.rem(x + e, X)
         for d in range(Y):
             for j in range(LIMIT):
-                outs[e][d * LIMIT + j] = arrived[d][column * LIMIT + j]
-
-
-def turn(arrived):
-    vmem = pl.BlockSpec(memory_space=pltpu.VMEM)
-    shape = jax.ShapeDtypeStruct((Y * LIMIT,) + arrived[0].shape[1:], arrived[0].dtype)
+                at = pl.multiple_of((column * LIMIT + j) * rank, rank)
+                outs[e][d * LIMIT + j] = arrived[d][pl.ds(at, rank), :]
+
+
+def turn(rank, arrived):
+    vmem = pl.BlockSpec(memory_space=pltpu.VMEM)
+    shape = jax.ShapeDtypeStruct((Y * LIMIT, rank, arrived[0].shape[-1]), arrived[0].dtype)
     return pl.pallas_call(
         turn_kernel,
-        out_shape=(shape,) * X,
+        out_shape=(shape,) * X
+        + (jax.ShapeDtypeStruct((Y, CODE_ROWS, arrived[0].shape[-1]), arrived[0].dtype),),
         in_specs=[vmem] * Y,
-        out_specs=(vmem,) * X,
+        out_specs=(vmem,) * (X + 1),
         compiler_params=pltpu.CompilerParams(vmem_limit_bytes=6 * MIB),
         cost_estimate=pl.CostEstimate(flops=0, bytes_accessed=4 * Y * arrived[0].size, transcendentals=0),
     )(*arrived)
@@ -188,58 +178,62 @@
     )(code, rows, down.reshape(resident * rank, width))
 
 
-def imported_kernel(resident, rows, down, own, out, rows_held, down_held, sems):
+def imported_kernel(resident, rows, down, own, codes, out, rows_held, down_held, sems):
     rank, count = own.shape
     lanes = out.shape[-1]
     y, _ = spot()
     odd = lax.axis_index("c")
 
-    def reads(g):
-        wanted = pl.ds(g * LIMIT * rank, LIMIT * rank)
+    def group(d):
+        return lax.rem(y - d + Y, Y)
+
+    def reads(d):
+        g = group(d)
         at = g + odd * (Y - 1 - 2 * g)
-        pairs = [(rows.at[at], rows_held.at[g])]
-        pairs += [(down.at[x, wanted], down_held.at[g, pl.ds(x * LIMIT * rank, LIMIT * rank)]) for x in range(X)]
-        return [pltpu.make_async_copy(a, b, sems.at[g, i]) for i, (a, b) in enumerate(pairs)]
-
-    for g in range(Y):
-        for read in reads(g):
+        wanted = pl.ds(pl.multiple_of(g * LIMIT * rank, LIMIT * rank), LIMIT * rank)
+        pairs = [(rows.at[at], rows_held.at[d])]
+        pairs += [(down.at[x, wanted], down_held.at[d, pl.ds(x * LIMIT * rank, LIMIT * rank)]) for x in range(X)]
+        return [pltpu.make_async_copy(a, b, sems.at[d, i]) for i, (a, b) in enumerate(pairs)]
+
+    for d in range(Y):
+        for read in reads(d):
             read.start()
     base = (resident + y * X * LIMIT).astype(jnp.float32)
-    for g in range(Y):
-        for read in reads(g):
+    for d in range(Y):
+        for read in reads(d):
             read.wait()
-        code = rows_held[g, count : count + 1, :count].astype(jnp.float32)
-        total = jnp.where(y == g, own[...], 0.0)
-        product = lax.dot_general(
-            down_held[g], rows_held[g, 0:count, :], NT, preferred_element_type=jnp.float32
-        )
+        tail = codes[d].astype(jnp.float32)
+        code = jnp.concatenate([tail[k : k + 1] for k in range(count // lanes)], axis=1)
+        total = own[...] if d == 0 else jnp.zeros(own.shape, jnp.float32)
+        product = lax.dot_general(down_held[d], rows_held[d], NT, preferred_element_type=jnp.float32)
         for k in range(X * LIMIT):
             total = total + jnp.where(code == base + k, product[k * rank : (k + 1) * rank, :], 0.0)
+        g = group(d)
         for i in range(rank // 8):
             for k in range(count // lanes):
                 out[g, i * (count // lanes) + k] = total[i * 8 : (i + 1) * 8, k * lanes : (k + 1) * lanes]
 
 
-def imported_shrink(resident, rows, down, own):
+def imported_shrink(resident, rows, down, own, codes):
     rank, count = own.shape
-    height, width = rows.shape[1:]
+    width = rows.shape[-1]
     blocks = rank * count // 1024
     vmem = pl.BlockSpec(memory_space=pltpu.VMEM)
     hbm = pl.BlockSpec(memory_space=pl.ANY)
     return pl.pallas_call(
         functools.partial(imported_kernel, resident),
         out_shape=jax.ShapeDtypeStruct((Y, blocks, 8, 128), jnp.float32),
-        in_specs=[hbm, hbm, vmem],
+        in_specs=[hbm, hbm, vmem, vmem],
         out_specs=vmem,
         scratch_shapes=[
-            pltpu.VMEM((Y, height, width), rows.dtype),
+            pltpu.VMEM((Y, count, width), rows.dtype),
             pltpu.VMEM((Y, X * LIMIT * rank, width), rows.dtype),
             pltpu.SemaphoreType.DMA((Y, X + 1)),
         ],
         cost_estimate=pl.CostEstimate(
             flops=2 * down.size * count, bytes_accessed=2 * (down.size + rows.size), transcendentals=0
         ),
-    )(rows, down.reshape(X, -1, width), own)
+    )(rows, down.reshape(X, -1, width), own, codes)
 
 
 def add_kernel(parts, out):
@@ -334,32 +328,31 @@
 
 def shards(inputs, row_adapter_slot, transfer_plan, key_value_weight, adapter_down, adapter_up):
     count = inputs.shape[0]
-    resident = adapter_down.shape[0]
+    resident, rank, _ = adapter_down.shape
     slots = row_adapter_slot.reshape(1, count)
 
-    sent, code = prepare(resident, transfer_plan, slots, inputs)
     rings = [[i * C for i in range(Y)], [i * C + 1 for i in reversed(range(Y))]]
-    rows = lax.all_gather(sent, ("y", "c"), axis_index_groups=rings)
+    rows = lax.all_gather(inputs, ("y", "c"), axis_index_groups=rings)
     down, picked = dispatch(transfer_plan, adapter_down)
     down = lax.all_to_all(down, "x", 0, 0, tiled=True)
 
     late, picked = lax.optimization_barrier((inputs, picked))
     base_part = jnp.dot(late, key_value_weight, preferred_element_type=jnp.float32)
     base = lax.psum_scatter(base_part, ("z", "c"), scatter_dimension=1, tiled=True)
+
+    *ups, code = pick_up(picked, transfer_plan, slots, adapter_up)
     own = local_shrink(code, late, adapter_down)
-
-    ups = pick_up(picked, adapter_up)
     near, far = (1, 7, 2, 6), (3, 5, 4)
     moved = {d: shift(ups[d], "y", Y, d) for d in near}
-    moved, later = lax.optimization_barrier((moved, {d: ups[d] for d in far}))
+    moved, later, own = lax.optimization_barrier((moved, {d: ups[d] for d in far}, own))
     moved |= {d: shift(later[d], "y", Y, d) for d in far}
     moved[0] = ups[0]
     down, moved = lax.optimization_barrier((down, moved))
     ups = [moved[d] for d in range(Y)]
-    ups = turn(ups)
+    *ups, codes = turn(rank, ups)
+    parts = imported_shrink(resident, rows, down, own, codes)
     tables = [ups[0]] + [shift(ups[e], "x", X, e) for e in range(1, X)]
 
-    parts = imported_shrink(resident, rows, down, own)
     parts = lax.all_to_all(parts.reshape(Y * T, 8, 128), ("y", "z", "c"), 0, 0, tiled=True)
     shrink = lax.all_to_all(add_and_spread(parts), ("z", "c"), 0, 0, tiled=True)
     return expand(shrink, code, base, adapter_up, tables)

time: 147 us -> 151 us (1.027); the launches traced: 146 us -> 149 us
  Pallas kernels: 26 us -> 23.4 us
  starting transfers between devices: 66.3 us -> 68.7 us
    pallas_call x3 -> x2, Pallas kernels: 5.18 us -> 2.6 us  [the longest x1 2.52 us: pick_up(): pl.pallas_call(pick_up_kernel, out_shape=(shape,) * Y + (jax.ShapeDtypeSt...]
    ppermute x10, starting transfers between devices: 38.7 us -> 41 us  [shift(): lax.ppermute(array, axis, [(i, (i + by) % size) for i in range(size)])]
    unnamed x20 -> x22, local copies, waits for them, and re-layouts: 2.22 us -> 3.39 us
  transfers between devices with their start and end apart: 15 -> 15, of which waited for: 7 -> 6; matrix products, arithmetic and copies ran while one was open for 1% -> 1% of each run, Pallas kernels for 13% -> 12%
where the time goes in v10:
time: 151 us; the launch traced here: 149 us
  starting transfers between devices  68.7 us (45%)
  waiting for transfers between devices  36.3 us (24%)
  Pallas kernels  23.4 us (15%)
  between operations  15.1 us (10%)
  local copies, waits for them, and re-layouts  3.39 us (2%)
  matrix products  2.07 us (1%)
    ppermute x10, starting transfers between devices, shift(): lax.ppermute(array, axis, [(i, (i + by) % size) for i in range(size)])  41 us
    ppermute x10, waiting for transfers between devices, shift(): lax.ppermute(array, axis, [(i, (i + by) % size) for i in range(size)])  20.5 us
    all_to_all x1, starting transfers between devices, shards(): lax.all_to_all(parts.reshape(Y * T, 8, 128), ('y', 'z', 'c'), 0, 0, tiled...  17.2 us
    all_to_all x1, waiting for transfers between devices, shards(): shrink = lax.all_to_all(add_and_spread(parts), ('z', 'c'), 0, 0, tiled=True)  7.78 us
    all_to_all x1, waiting for transfers between devices, shards(): lax.all_to_all(parts.reshape(Y * T, 8, 128), ('y', 'z', 'c'), 0, 0, tiled...  7.29 us
    pallas_call x1, Pallas kernels, imported_shrink(): pl.pallas_call(functools.partial(imported_kernel, resident), out_shape=ja...  6.9 us
    all_to_all x1, starting transfers between devices, shards(): shrink = lax.all_to_all(add_and_spread(parts), ('z', 'c'), 0, 0, tiled=True)  5.36 us
    pallas_call x1, Pallas kernels, expand(): pl.pallas_call(expand_kernel, out_shape=jax.ShapeDtypeStruct(base.shape,...  5.06 us
  transfers between devices with their start and end apart: 15, of which 6 were waited for; matrix products, arithmetic and copies ran while one was open for 1% of the time, Pallas kernels for 12%

profile of v10, /device:TPU:1, one launch (start us, length us, event | category | flops | bytes accessed | tf_op | source)
XLA Modules:
  0.0 148.9 jit_solution(15337781444002995850)
XLA Ops:
  7.4 0.7 all-gather.3.cloned.1.call-update
  8.1 5.0 %shard_map.64 = (bf16[4,16,64,512]{3,2,1,0:T(8,128)(2,1)}, s32[32,128]{1,0:T(8,128)}) custom-call(s32[32,31]{1,0:T(8,128)} %plan.3, bf16[32,64,512]{2,1,0:T(8,128)(2,1)} %down.1), custom_call_target="tpu_custom_call" | custom-call | bytes 6291456 | tf_op jit(solution)/shard_map/pallas_call | solution.py:66
  13.1 5.0 %all-to-all-start = ((bf16[4,16,64,512]{3,2,1,0:T(8,128)(2,1)}), bf16[4,16,64,512]{3,2,1,0:T(8,128)(2,1)}, u32[]{:S(2)}, u32[]{:S(2)}) async-start(bf16[4,16,64,512]{3,2,1,0:T(8,128)(2,1)} %get-tuple-element.40), calls=%async_computation | async-start | bytes 8388608 | tf_op jit(solution)/shard_map/all_to_all | solution.py:337
  18.2 2.1 %fusion = f32[256,2048]{1,0:T(8,128)} fusion(bf16[256,512]{1,0:T(8,128)(2,1)S(1)} %copy-done.8, bf16[512,2048]{1,0:T(8,128)(2,1)S(1)} %copy-done), kind=kOutput, calls=%fused_computation | convolution fusion | flops 536870912 | bytes 4456448 | tf_op jit(solution)/shard_map/dot_general | solution.py:340
  20.3 2.5 %shard_map.65 = (bf16[528,128]{1,0:T(8,128)(2,1)}, bf16[528,128]{1,0:T(8,128)(2,1)}, bf16[528,128]{1,0:T(8,128)(2,1)}, bf16[528,128]{1,0:T(8,128)(2,1)}, bf16[52...) custom-call(s32[32,128]{1,0:T(8,128)} %get-tuple-element.42.picked, ...), custom_call_target="tpu_custom_call" | custom-call | bytes 1572864 | tf_op jit(solution)/shard_map/pallas_call | solution.py:116
  22.8 4.2 %collective-permute-start = (bf16[528,128]{1,0:T(8,128)(2,1)}, bf16[528,128]{1,0:T(8,128)(2,1)S(1)}, u32[]{:S(2)}, u32[]{:S(2)}) collective-permute-start(bf16[528,128]{1,0:T(8,128)(2,1)} %get-tuple-element.44), channel_id=1, source_target_pairs={{0,64},{64,128},{128,192},{192,256},{256,320},{320,384},{384,448},... | collective-permute-start | bytes 405512 | tf_op jit(solution)/shard_map/ppermute | solution.py:326
  27.0 4.2 %collective-permute-start.1 = (bf16[528,128]{1,0:T(8,128)(2,1)}, bf16[528,128]{1,0:T(8,128)(2,1)S(1)}, u32[]{:S(2)}, u32[]{:S(2)}) collective-permute-start(bf16[528,128]{1,0:T(8,128)(2,1)} %get-tuple-element.45), channel_id=1, source_target_pairs={{0,128},{64,192},{128,256},{192,320},{256,384},{320,448},{384,0},{... | collective-permute-start | bytes 405512 | tf_op jit(solution)/shard_map/ppermute | solution.py:326
  31.2 3.2 %collective-permute-start.2 = (bf16[528,128]{1,0:T(8,128)(2,1)}, bf16[528,128]{1,0:T(8,128)(2,1)S(1)}, u32[]{:S(2)}, u32[]{:S(2)}) collective-permute-start(bf16[528,128]{1,0:T(8,128)(2,1)} %get-tuple-element.46), channel_id=1, source_target_pairs={{0,384},{64,448},{128,0},{192,64},{256,128},{320,192},{384,256},{4... | collective-permute-start | bytes 405512 | tf_op jit(solution)/shard_map/ppermute | solution.py:326
  34.4 2.6 %collective-permute-start.3 = (bf16[528,128]{1,0:T(8,128)(2,1)}, bf16[528,128]{1,0:T(8,128)(2,1)S(1)}, u32[]{:S(2)}, u32[]{:S(2)}) collective-permute-start(bf16[528,128]{1,0:T(8,128)(2,1)} %get-tuple-element.47), channel_id=1, source_target_pairs={{0,448},{64,0},{128,64},{192,128},{256,192},{320,256},{384,320},{4... | collective-permute-start | bytes 405512 | tf_op jit(solution)/shard_map/ppermute | solution.py:326
  37.0 3.1 %shard_map.66.own = f32[64,256]{1,0:T(8,128)} custom-call(s32[1,256]{1,0:T(1,128)} %get-tuple-element.51.code, bf16[256,512]{1,0:T(8,128)(2,1)} %rows, bf16[2048,512]{1,0:T(8,128)(2,1)} %bitcast.7), custom_call_target="tpu_custom_call" | custom-call | flops 536870912 | bytes 2097152 | tf_op jit(solution)/shard_map/pallas_call | solution.py:170
  40.1 3.0 %collective-permute-done.2.refs_6_ = bf16[528,128]{1,0:T(8,128)(2,1)S(1)} collective-permute-done((bf16[528,128]{1,0:T(8,128)(2,1)}, bf16[528,128]{1,0:T(8,128)(2,1)S(1)}, u32[]{:S(2)}, u32[]{:S(2)}) %collective-permute-start.2) | collective-permute-done | bytes 135200 | tf_op jit(solution)/shard_map/ppermute | solution.py:326
  43.1 6.8 %collective-permute-done.3.refs_7_ = bf16[528,128]{1,0:T(8,128)(2,1)S(1)} collective-permute-done((bf16[528,128]{1,0:T(8,128)(2,1)}, bf16[528,128]{1,0:T(8,128)(2,1)S(1)}, u32[]{:S(2)}, u32[]{:S(2)}) %collective-permute-start.3) | collective-permute-done | bytes 135200 | tf_op jit(solution)/shard_map/ppermute | solution.py:326
  49.9 5.8 %collective-permute-start.4 = (bf16[528,128]{1,0:T(8,128)(2,1)}, bf16[528,128]{1,0:T(8,128)(2,1)S(1)}, u32[]{:S(2)}, u32[]{:S(2)}) collective-permute-start(bf16[528,128]{1,0:T(8,128)(2,1)} %get-tuple-element.55), channel_id=1, source_target_pairs={{0,192},{64,256},{128,320},{192,384},{256,448},{320,0},{384,64},{4... | collective-permute-start | bytes 405512 | tf_op jit(solution)/shard_map/ppermute | solution.py:326
  55.7 2.6 %collective-permute-start.5 = (bf16[528,128]{1,0:T(8,128)(2,1)}, bf16[528,128]{1,0:T(8,128)(2,1)S(1)}, u32[]{:S(2)}, u32[]{:S(2)}) collective-permute-start(bf16[528,128]{1,0:T(8,128)(2,1)} %get-tuple-element.56), channel_id=1, source_target_pairs={{0,256},{64,320},{128,384},{192,448},{256,0},{320,64},{384,128},{4... | collective-permute-start | bytes 405512 | tf_op jit(solution)/shard_map/ppermute | solution.py:326
  58.3 6.4 %collective-permute-start.6 = (bf16[528,128]{1,0:T(8,128)(2,1)S(1)}, bf16[528,128]{1,0:T(8,128)(2,1)S(1)}, u32[]{:S(2)}, u32[]{:S(2)}) collective-permute-start(bf16[528,128]{1,0:T(8,128)(2,1)S(1)} %copy-done.10), channel_id=1, source_target_pairs={{0,320},{64,384},{128,448},{192,0},{256,64},{320,128},{384,192},{4... | collective-permute-start | bytes 405512 | tf_op jit(solution)/shard_map/ppermute | solution.py:326
  64.7 1.4 collective-permute-done.4.refs_3_
  66.1 9.2 %collective-permute-done.5.refs_4_ = bf16[528,128]{1,0:T(8,128)(2,1)S(1)} collective-permute-done((bf16[528,128]{1,0:T(8,128)(2,1)}, bf16[528,128]{1,0:T(8,128)(2,1)S(1)}, u32[]{:S(2)}, u32[]{:S(2)}) %collective-permute-start.5) | collective-permute-done | bytes 135200 | tf_op jit(solution)/shard_map/ppermute | solution.py:326
  75.5 0.7 copy-done.1
  76.2 0.6 copy-done.3
  76.8 0.7 copy-done.4
  77.5 0.7 copy-done.6
  78.2 6.9 %shard_map.68 = f32[8,16,8,128]{3,2,1,0:T(8,128)} custom-call(bf16[8,256,512]{2,1,0:T(8,128)(2,1)} %bitcast.8, bf16[4,1024,512]{2,1,0:T(8,128)(2,1)} %bitcast.3.down, f32[64,256]{1,0:T(8,128)} %shard_map.66.own, bf16[8,16,128]{2,1,0:T(8,128)(2,1)} %copy-done.3), custom_call_target="tpu_custom_call" | custom-call | flops 1073741824 | bytes 6291456 | tf_op jit(solution)/shard_map/pallas_call | solution.py:223
  85.1 17.2 %all-to-all-start.1 = ((f32[128,8,128]{2,1,0:T(8,128)}), f32[128,8,128]{2,1,0:T(8,128)S(1)}, u32[]{:S(2)}, u32[]{:S(2)}) async-start(f32[128,8,128]{2,1,0:T(8,128)} %bitcast.9), calls=%async_computation.1 | async-start | bytes 1048576 | tf_op jit(solution)/shard_map/all_to_all | solution.py:356
  102.4 4.8 %collective-permute-start.7 = (bf16[16,64,128]{2,1,0:T(8,128)(2,1)S(1)}, bf16[16,64,128]{2,1,0:T(8,128)(2,1)}, u32[]{:S(2)}, u32[]{:S(2)}) collective-permute-start(bf16[16,64,128]{2,1,0:T(8,128)(2,1)S(1)} %copy-done.7), channel_id=1, source_target_pairs={{0,16},{16,32},{32,48},{48,0},{1,17},{17,33},{33,49},{49,1},{2,18}... | collective-permute-start | bytes 786440 | tf_op jit(solution)/shard_map/ppermute | solution.py:326
  107.2 3.4 %collective-permute-start.8 = (bf16[16,64,128]{2,1,0:T(8,128)(2,1)S(1)}, bf16[16,64,128]{2,1,0:T(8,128)(2,1)}, u32[]{:S(2)}, u32[]{:S(2)}) collective-permute-start(bf16[16,64,128]{2,1,0:T(8,128)(2,1)S(1)} %copy-done.5), channel_id=1, source_target_pairs={{0,32},{16,48},{32,0},{48,16},{1,33},{17,49},{33,1},{49,17},{2,34}... | collective-permute-start | bytes 786440 | tf_op jit(solution)/shard_map/ppermute | solution.py:326
  110.6 3.9 %collective-permute-start.9 = (bf16[16,64,128]{2,1,0:T(8,128)(2,1)S(1)}, bf16[16,64,128]{2,1,0:T(8,128)(2,1)}, u32[]{:S(2)}, u32[]{:S(2)}) collective-permute-start(bf16[16,64,128]{2,1,0:T(8,128)(2,1)S(1)} %get-tuple-element.74), channel_id=1, source_target_pairs={{0,48},{16,0},{32,16},{48,32},{1,49},{17,1},{33,17},{49,33},{2,50}... | collective-permute-start | bytes 786440 | tf_op jit(solution)/shard_map/ppermute | solution.py:326
  114.5 7.3 %all-to-all-done.1.parts = f32[128,8,128]{2,1,0:T(8,128)S(1)} async-done(((f32[128,8,128]{2,1,0:T(8,128)}), f32[128,8,128]{2,1,0:T(8,128)S(1)}, u32[]{:S(2)}, u32[]{:S(2)}) %all-to-all-start.1) | async-done | bytes 524320 | tf_op jit(solution)/shard_map/all_to_all | solution.py:356
  121.8 0.8 shard_map.69
  122.6 5.4 %all-to-all-start.2 = ((f32[16,8,128]{2,1,0:T(8,128)}), f32[16,8,128]{2,1,0:T(8,128)S(1)}, u32[]{:S(2)}, u32[]{:S(2)}) async-start(f32[16,8,128]{2,1,0:T(8,128)} %shard_map.69), calls=%async_computation.2 | async-start | bytes 131072 | tf_op jit(solution)/shard_map/all_to_all | solution.py:357
  128.0 7.8 %all-to-all-done.2.shrink = f32[16,8,128]{2,1,0:T(8,128)S(1)} async-done(((f32[16,8,128]{2,1,0:T(8,128)}), f32[16,8,128]{2,1,0:T(8,128)S(1)}, u32[]{:S(2)}, u32[]{:S(2)}) %all-to-all-start.2) | async-done | bytes 65568 | tf_op jit(solution)/shard_map/all_to_all | solution.py:357
  135.8 0.6 copy-done.9
  136.4 5.1 %shard_map.70 = bf16[256,128]{1,0:T(8,128)(2,1)} custom-call(f32[16,8,128]{2,1,0:T(8,128)} %copy-done.9, s32[1,256]{1,0:T(1,128)} %get-tuple-element.51.code, f32[256,128]{1,0:T(8,128)} %reduce-scatter.2.cloned.1.call-done.base, bf16[32,64,128]{2,1,0:T(8,128)(2,1)} %up.3, bf16[16,64,128]{2,1,0:T(8,128)(2,1)} %copy-done.1, ...), custom_call_target="tpu_custom_call" | custom-call | tf_op jit(solution)/shard_map/pallas_call | solution.py:312
  (30 shorter events, 0.2 us)
Async XLA Ops:
  7.4 10.8 %copy-start = (bf16[512,2048]{1,0:T(8,128)(2,1)S(1)}, bf16[512,2048]{1,0:T(8,128)(2,1)}, u32[]{:S(2)}) copy-start(bf16[512,2048]{1,0:T(8,128)(2,1)} %param.9) | copy-start | bytes 6291460
  7.4 70.8 %all-gather.3.cloned.1.call-start = ((), (), s32[]{:S(2)}) async-start(), calls=%async_computation.5 | async-start | bytes 2359296 | tf_op jit(solution)/shard_map/all_gather | solution.py:335
  13.1 5.1 %copy-start.8 = (bf16[256,512]{1,0:T(8,128)(2,1)S(1)}, bf16[256,512]{1,0:T(8,128)(2,1)}, u32[]{:S(2)}) copy-start(bf16[256,512]{1,0:T(8,128)(2,1)} %rows) | copy-start | bytes 786436
  13.1 62.2 %all-to-all-start = ((bf16[4,16,64,512]{3,2,1,0:T(8,128)(2,1)}), bf16[4,16,64,512]{3,2,1,0:T(8,128)(2,1)}, u32[]{:S(2)}, u32[]{:S(2)}) async-start(bf16[4,16,64,512]{3,2,1,0:T(8,128)(2,1)} %get-tuple-element.40), calls=%async_computation | async-start | bytes 8388608 | tf_op jit(solution)/shard_map/all_to_all | solution.py:337
  18.1 109.9 %reduce-scatter.2.cloned.1.call-start = ((), (), s32[]{:S(2)}) async-start(), calls=%async_computation.4 | async-start | bytes 2228224 | tf_op jit(solution)/shard_map/reduce_scatter | solution.py:341
  22.8 35.5 %copy-start.10 = (bf16[528,128]{1,0:T(8,128)(2,1)S(1)}, bf16[528,128]{1,0:T(8,128)(2,1)}, u32[]{:S(2)}) copy-start(bf16[528,128]{1,0:T(8,128)(2,1)} %get-tuple-element.57) | copy-start | bytes 405508
  22.8 52.5 %copy-start.2 = (bf16[528,128]{1,0:T(8,128)(2,1)S(1)}, bf16[528,128]{1,0:T(8,128)(2,1)}, u32[]{:S(2)}) copy-start(bf16[528,128]{1,0:T(8,128)(2,1)} %get-tuple-element.62.refs_0_) | copy-start | bytes 405508
  22.8 17.3 %collective-permute-start = (bf16[528,128]{1,0:T(8,128)(2,1)}, bf16[528,128]{1,0:T(8,128)(2,1)S(1)}, u32[]{:S(2)}, u32[]{:S(2)}) collective-permute-start(bf16[528,128]{1,0:T(8,128)(2,1)} %get-tuple-element.44), channel_id=1, source_target_pairs={{0,64},{64,128},{128,192},{192,256},{256,320},{320,384},{384,448},... | collective-permute-start | bytes 405512 | tf_op jit(solution)/shard_map/ppermute | solution.py:326
  27.0 13.1 %collective-permute-start.1 = (bf16[528,128]{1,0:T(8,128)(2,1)}, bf16[528,128]{1,0:T(8,128)(2,1)S(1)}, u32[]{:S(2)}, u32[]{:S(2)}) collective-permute-start(bf16[528,128]{1,0:T(8,128)(2,1)} %get-tuple-element.45), channel_id=1, source_target_pairs={{0,128},{64,192},{128,256},{192,320},{256,384},{320,448},{384,0},{... | collective-permute-start | bytes 405512 | tf_op jit(solution)/shard_map/ppermute | solution.py:326
  31.2 11.9 %collective-permute-start.2 = (bf16[528,128]{1,0:T(8,128)(2,1)}, bf16[528,128]{1,0:T(8,128)(2,1)S(1)}, u32[]{:S(2)}, u32[]{:S(2)}) collective-permute-start(bf16[528,128]{1,0:T(8,128)(2,1)} %get-tuple-element.46), channel_id=1, source_target_pairs={{0,384},{64,448},{128,0},{192,64},{256,128},{320,192},{384,256},{4... | collective-permute-start | bytes 405512 | tf_op jit(solution)/shard_map/ppermute | solution.py:326
  34.4 15.5 %collective-permute-start.3 = (bf16[528,128]{1,0:T(8,128)(2,1)}, bf16[528,128]{1,0:T(8,128)(2,1)S(1)}, u32[]{:S(2)}, u32[]{:S(2)}) collective-permute-start(bf16[528,128]{1,0:T(8,128)(2,1)} %get-tuple-element.47), channel_id=1, source_target_pairs={{0,448},{64,0},{128,64},{192,128},{256,192},{320,256},{384,320},{4... | collective-permute-start | bytes 405512 | tf_op jit(solution)/shard_map/ppermute | solution.py:326
  49.9 16.2 %collective-permute-start.4 = (bf16[528,128]{1,0:T(8,128)(2,1)}, bf16[528,128]{1,0:T(8,128)(2,1)S(1)}, u32[]{:S(2)}, u32[]{:S(2)}) collective-permute-start(bf16[528,128]{1,0:T(8,128)(2,1)} %get-tuple-element.55), channel_id=1, source_target_pairs={{0,192},{64,256},{128,320},{192,384},{256,448},{320,0},{384,64},{4... | collective-permute-start | bytes 405512 | tf_op jit(solution)/shard_map/ppermute | solution.py:326
  55.7 19.6 %collective-permute-start.5 = (bf16[528,128]{1,0:T(8,128)(2,1)}, bf16[528,128]{1,0:T(8,128)(2,1)S(1)}, u32[]{:S(2)}, u32[]{:S(2)}) collective-permute-start(bf16[528,128]{1,0:T(8,128)(2,1)} %get-tuple-element.56), channel_id=1, source_target_pairs={{0,256},{64,320},{128,384},{192,448},{256,0},{320,64},{384,128},{4... | collective-permute-start | bytes 405512 | tf_op jit(solution)/shard_map/ppermute | solution.py:326
  58.3 17.0 %collective-permute-start.6 = (bf16[528,128]{1,0:T(8,128)(2,1)S(1)}, bf16[528,128]{1,0:T(8,128)(2,1)S(1)}, u32[]{:S(2)}, u32[]{:S(2)}) collective-permute-start(bf16[528,128]{1,0:T(8,128)(2,1)S(1)} %copy-done.10), channel_id=1, source_target_pairs={{0,320},{64,384},{128,448},{192,0},{256,64},{320,128},{384,192},{4... | collective-permute-start | bytes 405512 | tf_op jit(solution)/shard_map/ppermute | solution.py:326
  75.5 0.7 copy-start.1
  76.2 0.6 copy-start.3
  76.8 0.7 copy-start.4
  77.5 0.7 copy-start.6
  78.2 24.1 %copy-start.7 = (bf16[16,64,128]{2,1,0:T(8,128)(2,1)S(1)}, bf16[16,64,128]{2,1,0:T(8,128)(2,1)}, u32[]{:S(2)}) copy-start(bf16[16,64,128]{2,1,0:T(8,128)(2,1)} %copy-done.6) | copy-start | bytes 786436
  78.2 29.0 %copy-start.5 = (bf16[16,64,128]{2,1,0:T(8,128)(2,1)S(1)}, bf16[16,64,128]{2,1,0:T(8,128)(2,1)}, u32[]{:S(2)}) copy-start(bf16[16,64,128]{2,1,0:T(8,128)(2,1)} %copy-done.4) | copy-start | bytes 786436
  85.1 36.7 %all-to-all-start.1 = ((f32[128,8,128]{2,1,0:T(8,128)}), f32[128,8,128]{2,1,0:T(8,128)S(1)}, u32[]{:S(2)}, u32[]{:S(2)}) async-start(f32[128,8,128]{2,1,0:T(8,128)} %bitcast.9), calls=%async_computation.1 | async-start | bytes 1048576 | tf_op jit(solution)/shard_map/all_to_all | solution.py:356
  102.4 25.6 %collective-permute-start.7 = (bf16[16,64,128]{2,1,0:T(8,128)(2,1)S(1)}, bf16[16,64,128]{2,1,0:T(8,128)(2,1)}, u32[]{:S(2)}, u32[]{:S(2)}) collective-permute-start(bf16[16,64,128]{2,1,0:T(8,128)(2,1)S(1)} %copy-done.7), channel_id=1, source_target_pairs={{0,16},{16,32},{32,48},{48,0},{1,17},{17,33},{33,49},{49,1},{2,18}... | collective-permute-start | bytes 786440 | tf_op jit(solution)/shard_map/ppermute | solution.py:326
  107.2 20.7 %collective-permute-start.8 = (bf16[16,64,128]{2,1,0:T(8,128)(2,1)S(1)}, bf16[16,64,128]{2,1,0:T(8,128)(2,1)}, u32[]{:S(2)}, u32[]{:S(2)}) collective-permute-start(bf16[16,64,128]{2,1,0:T(8,128)(2,1)S(1)} %copy-done.5), channel_id=1, source_target_pairs={{0,32},{16,48},{32,0},{48,16},{1,33},{17,49},{33,1},{49,17},{2,34}... | collective-permute-start | bytes 786440 | tf_op jit(solution)/shard_map/ppermute | solution.py:326
  110.6 17.4 %collective-permute-start.9 = (bf16[16,64,128]{2,1,0:T(8,128)(2,1)S(1)}, bf16[16,64,128]{2,1,0:T(8,128)(2,1)}, u32[]{:S(2)}, u32[]{:S(2)}) collective-permute-start(bf16[16,64,128]{2,1,0:T(8,128)(2,1)S(1)} %get-tuple-element.74), channel_id=1, source_target_pairs={{0,48},{16,0},{32,16},{48,32},{1,49},{17,1},{33,17},{49,33},{2,50}... | collective-permute-start | bytes 786440 | tf_op jit(solution)/shard_map/ppermute | solution.py:326
  122.6 13.2 %all-to-all-start.2 = ((f32[16,8,128]{2,1,0:T(8,128)}), f32[16,8,128]{2,1,0:T(8,128)S(1)}, u32[]{:S(2)}, u32[]{:S(2)}) async-start(f32[16,8,128]{2,1,0:T(8,128)} %shard_map.69), calls=%async_computation.2 | async-start | bytes 131072 | tf_op jit(solution)/shard_map/all_to_all | solution.py:357
  135.8 0.6 copy-start.9
Sparse Core Ops, SparseCore 0:
  10.3 63.9 all-gather.2
Sparse Core Ops, SparseCore 1:
  21.4 67.4 reduce-scatter.1

commit v11 on v9

--- a/solution.py
+++ b/solution.py
@@ -201,13 +201,15 @@
         pairs += [(down.at[x, wanted], down_held.at[g, pl.ds(x * LIMIT * rank, LIMIT * rank)]) for x in range(X)]
         return [pltpu.make_async_copy(a, b, sems.at[g, i]) for i, (a, b) in enumerate(pairs)]
 
-    for g in range(Y):
+    for g in range(3):
         for read in reads(g):
             read.start()
     base = (resident + y * X * LIMIT).astype(jnp.float32)
     for g in range(Y):
         for read in reads(g):
             read.wait()
+        for read in reads(g + 3) if g + 3 < Y else ():
+            read.start()
         code = rows_held[g, count : count + 1, :count].astype(jnp.float32)
         total = jnp.where(y == g, own[...], 0.0)
         product = lax.dot_general(
@@ -248,11 +250,11 @@
         out[t] = total
 
 
-def add_and_spread(parts):
+def add_up(parts, times):
     vmem = pl.BlockSpec(memory_space=pltpu.VMEM)
     return pl.pallas_call(
         add_kernel,
-        out_shape=jax.ShapeDtypeStruct((T,) + parts.shape[1:], jnp.float32),
+        out_shape=jax.ShapeDtypeStruct((times,) + parts.shape[1:], jnp.float32),
         in_specs=[vmem],
         out_specs=vmem,
         compiler_params=pltpu.CompilerParams(vmem_limit_bytes=2 * MIB),
@@ -360,8 +362,9 @@
     tables = [ups[0]] + [shift(ups[e], "x", X, e) for e in range(1, X)]
 
     parts = imported_shrink(resident, rows, down, own)
-    parts = lax.all_to_all(parts.reshape(Y * T, 8, 128), ("y", "z", "c"), 0, 0, tiled=True)
-    shrink = lax.all_to_all(add_and_spread(parts), ("z", "c"), 0, 0, tiled=True)
+    parts = add_up(lax.all_to_all(parts, "y", 0, 0, tiled=True), 1)
+    parts = add_up(lax.all_to_all(parts.reshape(T, 8, 128), ("z", "c"), 0, 0, tiled=True), T)
+    shrink = lax.all_to_all(parts, ("z", "c"), 0, 0, tiled=True)
     return expand(shrink, code, base, adapter_up, tables)
 
 

time: 147 us -> 151 us (1.027)
  blocking collectives: 0 us -> 19.3 us
  starting transfers between devices: 66.3 us -> 54.7 us
  waiting for transfers between devices: 34.8 us -> 31 us
    all_to_all x0 -> x1, blocking collectives: none -> 19.3 us  [shards(): lax.all_to_all(parts.reshape(T, 8, 128), ('z', 'c'), 0, 0, tiled=True)]
    all_to_all x2, starting transfers between devices: 22.5 us -> 10.8 us  [the longest x1 7.38 us: shards(): parts = add_up(lax.all_to_all(parts, 'y', 0, 0, tiled=True), 1)]
    all_to_all x2, waiting for transfers between devices: 14.3 us -> 10.4 us  [the longest x1 7.75 us: shards(): shrink = lax.all_to_all(parts, ('z', 'c'), 0, 0, tiled=True)]
  transfers between devices with their start and end apart: 15 -> 15, of which waited for: 7 -> 7; matrix products, arithmetic and copies ran while one was open for 1% -> 1% of each run, Pallas kernels for 13% -> 12%
where the time goes in v11:
time: 151 us; the launch traced here: 150 us
  starting transfers between devices  54.7 us (36%)
  waiting for transfers between devices  31 us (21%)
  Pallas kernels  25.9 us (17%)
  blocking collectives  19.3 us (13%)
  between operations  15.1 us (10%)
  local copies, waits for them, and re-layouts  2.22 us (1%)
  matrix products  2.09 us (1%)
    ppermute x10, starting transfers between devices, shift(): lax.ppermute(array, axis, [(i, (i + by) % size) for i in range(size)])  38.8 us
    ppermute x10, waiting for transfers between devices, shift(): lax.ppermute(array, axis, [(i, (i + by) % size) for i in range(size)])  20.5 us
    all_to_all x1, blocking collectives, shards(): lax.all_to_all(parts.reshape(T, 8, 128), ('z', 'c'), 0, 0, tiled=True)  19.3 us
    all_to_all x1, waiting for transfers between devices, shards(): shrink = lax.all_to_all(parts, ('z', 'c'), 0, 0, tiled=True)  7.75 us
    all_to_all x1, starting transfers between devices, shards(): parts = add_up(lax.all_to_all(parts, 'y', 0, 0, tiled=True), 1)  7.38 us
    pallas_call x1, Pallas kernels, imported_shrink(): pl.pallas_call(functools.partial(imported_kernel, resident), out_shape=ja...  6.91 us
    pallas_call x1, Pallas kernels, expand(): pl.pallas_call(expand_kernel, out_shape=jax.ShapeDtypeStruct(base.shape,...  5.06 us
    pallas_call x1, Pallas kernels, dispatch(): pl.pallas_call(dispatch_kernel, out_shape=(jax.ShapeDtypeStruct(shape, do...  5.01 us
  transfers between devices with their start and end apart: 15, of which 7 were waited for; matrix products, arithmetic and copies ran while one was open for 1% of the time, Pallas kernels for 12%

profile of v11, /device:TPU:1, one launch (start us, length us, event | category | flops | bytes accessed | tf_op | source)
XLA Modules:
  0.0 150.3 jit_solution(16864878008302960580)
XLA Ops:
  7.4 2.1 %shard_map.64 = (bf16[272,512]{1,0:T(8,128)(2,1)}, s32[1,256]{1,0:T(1,128)}) custom-call(s32[32,31]{1,0:T(8,128)} %plan.3, s32[1,256]{1,0:T(1,128)} %bitcast.10, bf16[256,512]{1,0:T(8,128)(2,1)} %rows.2), custom_call_target="tpu_custom_call" | custom-call | bytes 524288 | tf_op jit(solution)/shard_map/pallas_call | solution.py:107
  9.5 5.0 %shard_map.65 = (bf16[4,16,64,512]{3,2,1,0:T(8,128)(2,1)}, s32[32,128]{1,0:T(8,128)}) custom-call(s32[32,31]{1,0:T(8,128)} %plan.3, bf16[32,64,512]{2,1,0:T(8,128)(2,1)} %down.1), custom_call_target="tpu_custom_call" | custom-call | bytes 6291456 | tf_op jit(solution)/shard_map/pallas_call | solution.py:66
  14.5 5.0 %all-to-all-start = ((bf16[4,16,64,512]{3,2,1,0:T(8,128)(2,1)}), bf16[4,16,64,512]{3,2,1,0:T(8,128)(2,1)}, u32[]{:S(2)}, u32[]{:S(2)}) async-start(bf16[4,16,64,512]{3,2,1,0:T(8,128)(2,1)} %get-tuple-element.40), calls=%async_computation | async-start | bytes 8388608 | tf_op jit(solution)/shard_map/all_to_all | solution.py:346
  19.6 2.1 %fusion = f32[256,2048]{1,0:T(8,128)} fusion(bf16[256,512]{1,0:T(8,128)(2,1)S(1)} %copy-done.5, bf16[512,2048]{1,0:T(8,128)(2,1)S(1)} %copy-done), kind=kOutput, calls=%fused_computation | convolution fusion | flops 536870912 | bytes 4456448 | tf_op jit(solution)/shard_map/dot_general | solution.py:349
  21.7 2.1 %shard_map.66 = (bf16[8,64,128]{2,1,0:T(8,128)(2,1)}, bf16[8,64,128]{2,1,0:T(8,128)(2,1)}, bf16[8,64,128]{2,1,0:T(8,128)(2,1)}, bf16[8,64,128]{2,1,0:T(8,128)(2,...) custom-call(s32[32,128]{1,0:T(8,128)} %get-tuple-element.42.picked, ...), custom_call_target="tpu_custom_call" | custom-call | bytes 1572864 | tf_op jit(solution)/shard_map/pallas_call | solution.py:131
  23.8 4.0 %collective-permute-start = (bf16[8,64,128]{2,1,0:T(8,128)(2,1)}, bf16[8,64,128]{2,1,0:T(8,128)(2,1)S(1)}, u32[]{:S(2)}, u32[]{:S(2)}) collective-permute-start(bf16[8,64,128]{2,1,0:T(8,128)(2,1)} %get-tuple-element.44), channel_id=1, source_target_pairs={{0,64},{64,128},{128,192},{192,256},{256,320},{320,384},{384,448},... | collective-permute-start | bytes 393224 | tf_op jit(solution)/shard_map/ppermute | solution.py:334
  27.9 4.2 %collective-permute-start.1 = (bf16[8,64,128]{2,1,0:T(8,128)(2,1)}, bf16[8,64,128]{2,1,0:T(8,128)(2,1)S(1)}, u32[]{:S(2)}, u32[]{:S(2)}) collective-permute-start(bf16[8,64,128]{2,1,0:T(8,128)(2,1)} %get-tuple-element.45), channel_id=1, source_target_pairs={{0,128},{64,192},{128,256},{192,320},{256,384},{320,448},{384,0},{... | collective-permute-start | bytes 393224 | tf_op jit(solution)/shard_map/ppermute | solution.py:334
  32.1 3.2 %collective-permute-start.2 = (bf16[8,64,128]{2,1,0:T(8,128)(2,1)}, bf16[8,64,128]{2,1,0:T(8,128)(2,1)S(1)}, u32[]{:S(2)}, u32[]{:S(2)}) collective-permute-start(bf16[8,64,128]{2,1,0:T(8,128)(2,1)} %get-tuple-element.46), channel_id=1, source_target_pairs={{0,384},{64,448},{128,0},{192,64},{256,128},{320,192},{384,256},{4... | collective-permute-start | bytes 393224 | tf_op jit(solution)/shard_map/ppermute | solution.py:334
  35.3 2.6 %collective-permute-start.3 = (bf16[8,64,128]{2,1,0:T(8,128)(2,1)}, bf16[8,64,128]{2,1,0:T(8,128)(2,1)S(1)}, u32[]{:S(2)}, u32[]{:S(2)}) collective-permute-start(bf16[8,64,128]{2,1,0:T(8,128)(2,1)} %get-tuple-element.47), channel_id=1, source_target_pairs={{0,448},{64,0},{128,64},{192,128},{256,192},{320,256},{384,320},{4... | collective-permute-start | bytes 393224 | tf_op jit(solution)/shard_map/ppermute | solution.py:334
  37.9 2.7 %collective-permute-done.1.refs_2_ = bf16[8,64,128]{2,1,0:T(8,128)(2,1)S(1)} collective-permute-done((bf16[8,64,128]{2,1,0:T(8,128)(2,1)}, bf16[8,64,128]{2,1,0:T(8,128)(2,1)S(1)}, u32[]{:S(2)}, u32[]{:S(2)}) %collective-permute-start.1) | collective-permute-done | bytes 131104 | tf_op jit(solution)/shard_map/ppermute | solution.py:334
  40.6 0.6 collective-permute-done.2.refs_6_
  41.2 9.5 %collective-permute-done.3.refs_7_ = bf16[8,64,128]{2,1,0:T(8,128)(2,1)S(1)} collective-permute-done((bf16[8,64,128]{2,1,0:T(8,128)(2,1)}, bf16[8,64,128]{2,1,0:T(8,128)(2,1)S(1)}, u32[]{:S(2)}, u32[]{:S(2)}) %collective-permute-start.3) | collective-permute-done | bytes 131104 | tf_op jit(solution)/shard_map/ppermute | solution.py:334
  50.8 5.1 %collective-permute-start.4 = (bf16[8,64,128]{2,1,0:T(8,128)(2,1)}, bf16[8,64,128]{2,1,0:T(8,128)(2,1)S(1)}, u32[]{:S(2)}, u32[]{:S(2)}) collective-permute-start(bf16[8,64,128]{2,1,0:T(8,128)(2,1)} %get-tuple-element.53), channel_id=1, source_target_pairs={{0,192},{64,256},{128,320},{192,384},{256,448},{320,0},{384,64},{4... | collective-permute-start | bytes 393224 | tf_op jit(solution)/shard_map/ppermute | solution.py:334
  55.8 2.9 %collective-permute-start.5 = (bf16[8,64,128]{2,1,0:T(8,128)(2,1)}, bf16[8,64,128]{2,1,0:T(8,128)(2,1)S(1)}, u32[]{:S(2)}, u32[]{:S(2)}) collective-permute-start(bf16[8,64,128]{2,1,0:T(8,128)(2,1)} %get-tuple-element.54), channel_id=1, source_target_pairs={{0,256},{64,320},{128,384},{192,448},{256,0},{320,64},{384,128},{4... | collective-permute-start | bytes 393224 | tf_op jit(solution)/shard_map/ppermute | solution.py:334
  58.7 6.4 %collective-permute-start.6 = (bf16[8,64,128]{2,1,0:T(8,128)(2,1)}, bf16[8,64,128]{2,1,0:T(8,128)(2,1)S(1)}, u32[]{:S(2)}, u32[]{:S(2)}) collective-permute-start(bf16[8,64,128]{2,1,0:T(8,128)(2,1)} %get-tuple-element.55), channel_id=1, source_target_pairs={{0,320},{64,384},{128,448},{192,0},{256,64},{320,128},{384,192},{4... | collective-permute-start | bytes 393224 | tf_op jit(solution)/shard_map/ppermute | solution.py:334
  65.1 3.1 %shard_map.67.own = f32[64,256]{1,0:T(8,128)} custom-call(s32[1,256]{1,0:T(1,128)} %get-tuple-element.59.code, bf16[256,512]{1,0:T(8,128)(2,1)} %rows.2, bf16[2048,512]{1,0:T(8,128)(2,1)} %bitcast.8), custom_call_target="tpu_custom_call" | custom-call | flops 536870912 | bytes 2097152 | tf_op jit(solution)/shard_map/pallas_call | solution.py:180
  68.2 6.9 %collective-permute-done.5.refs_4_ = bf16[8,64,128]{2,1,0:T(8,128)(2,1)S(1)} collective-permute-done((bf16[8,64,128]{2,1,0:T(8,128)(2,1)}, bf16[8,64,128]{2,1,0:T(8,128)(2,1)S(1)}, u32[]{:S(2)}, u32[]{:S(2)}) %collective-permute-start.5) | collective-permute-done | bytes 131104 | tf_op jit(solution)/shard_map/ppermute | solution.py:334
  75.0 0.7 collective-permute-done.6.refs_5_
  75.8 6.9 %shard_map.68 = f32[8,16,8,128]{3,2,1,0:T(8,128)} custom-call(bf16[8,272,512]{2,1,0:T(8,128)(2,1)} %bitcast.9, bf16[4,1024,512]{2,1,0:T(8,128)(2,1)} %bitcast.2.down, f32[64,256]{1,0:T(8,128)} %shard_map.67.own), custom_call_target="tpu_custom_call" | custom-call | flops 1073741824 | bytes 6422528 | tf_op jit(solution)/shard_map/pallas_call | solution.py:231
  82.7 7.4 %all-to-all-start.1 = ((f32[8,16,8,128]{3,2,1,0:T(8,128)}), f32[8,16,8,128]{3,2,1,0:T(8,128)S(1)}, u32[]{:S(2)}, u32[]{:S(2)}) async-start(f32[8,16,8,128]{3,2,1,0:T(8,128)} %shard_map.68), calls=%async_computation.1 | async-start | bytes 1048576 | tf_op jit(solution)/shard_map/all_to_all | solution.py:365
  90.1 0.9 copy-done.4
  91.0 1.0 shard_map.71
  92.0 0.7 copy-done.1
  92.7 2.9 %collective-permute-start.7 = (bf16[16,64,128]{2,1,0:T(8,128)(2,1)}, bf16[16,64,128]{2,1,0:T(8,128)(2,1)S(1)}, u32[]{:S(2)}, u32[]{:S(2)}) collective-permute-start(bf16[16,64,128]{2,1,0:T(8,128)(2,1)} %get-tuple-element.70), channel_id=1, source_target_pairs={{0,16},{16,32},{32,48},{48,0},{1,17},{17,33},{33,49},{49,1},{2,18}... | collective-permute-start | bytes 786440 | tf_op jit(solution)/shard_map/ppermute | solution.py:334
  95.6 4.3 %collective-permute-start.8 = (bf16[16,64,128]{2,1,0:T(8,128)(2,1)}, bf16[16,64,128]{2,1,0:T(8,128)(2,1)S(1)}, u32[]{:S(2)}, u32[]{:S(2)}) collective-permute-start(bf16[16,64,128]{2,1,0:T(8,128)(2,1)} %get-tuple-element.71), channel_id=1, source_target_pairs={{0,32},{16,48},{32,0},{48,16},{1,33},{17,49},{33,1},{49,17},{2,34}... | collective-permute-start | bytes 786440 | tf_op jit(solution)/shard_map/ppermute | solution.py:334
  99.9 3.3 %collective-permute-start.9 = (bf16[16,64,128]{2,1,0:T(8,128)(2,1)}, bf16[16,64,128]{2,1,0:T(8,128)(2,1)S(1)}, u32[]{:S(2)}, u32[]{:S(2)}) collective-permute-start(bf16[16,64,128]{2,1,0:T(8,128)(2,1)} %get-tuple-element.72), channel_id=1, source_target_pairs={{0,48},{16,0},{32,16},{48,32},{1,49},{17,1},{33,17},{49,33},{2,50}... | collective-permute-start | bytes 786440 | tf_op jit(solution)/shard_map/ppermute | solution.py:334
  103.2 2.7 %all-to-all-done.1.parts = f32[8,16,8,128]{3,2,1,0:T(8,128)S(1)} async-done(((f32[8,16,8,128]{3,2,1,0:T(8,128)}), f32[8,16,8,128]{3,2,1,0:T(8,128)S(1)}, u32[]{:S(2)}, u32[]{:S(2)}) %all-to-all-start.1) | async-done | bytes 524320 | tf_op jit(solution)/shard_map/all_to_all | solution.py:365
  105.9 19.3 %all_to_all.20.parts = f32[16,8,128]{2,1,0:T(8,128)S(1)} all-to-all(f32[16,8,128]{2,1,0:T(8,128)S(1)} %bitcast.7), channel_id=1, replica_groups=mesh['y'=8,'x'=4,'z'=8,'c'=2] {'z','c'}, dimensions={0} | all-to-all | bytes 131072 | tf_op jit(solution)/shard_map/all_to_all | solution.py:366
  125.2 0.6 shard_map.70
  125.9 3.5 %all-to-all-start.3 = ((f32[16,8,128]{2,1,0:T(8,128)}), f32[16,8,128]{2,1,0:T(8,128)S(1)}, u32[]{:S(2)}, u32[]{:S(2)}) async-start(f32[16,8,128]{2,1,0:T(8,128)} %shard_map.70), calls=%async_computation.3 | async-start | bytes 131072 | tf_op jit(solution)/shard_map/all_to_all | solution.py:367
  129.4 7.7 %all-to-all-done.3.shrink = f32[16,8,128]{2,1,0:T(8,128)S(1)} async-done(((f32[16,8,128]{2,1,0:T(8,128)}), f32[16,8,128]{2,1,0:T(8,128)S(1)}, u32[]{:S(2)}, u32[]{:S(2)}) %all-to-all-start.3) | async-done | bytes 65568 | tf_op jit(solution)/shard_map/all_to_all | solution.py:367
  137.8 5.1 %shard_map.72 = bf16[256,128]{1,0:T(8,128)(2,1)} custom-call(f32[16,8,128]{2,1,0:T(8,128)} %copy-done.9, s32[1,256]{1,0:T(1,128)} %get-tuple-element.59.code, f32[256,128]{1,0:T(8,128)} %reduce-scatter.2.cloned.1.call-done.base, bf16[32,64,128]{2,1,0:T(8,128)(2,1)} %up.3, bf16[16,64,128]{2,1,0:T(8,128)(2,1)} %copy-done.1, bf16[16,64,128]{2,1,0:T(8,128)(2,1)} %copy-done.6, ...), custom_call_target="tpu_custom_call" | custom-call | tf_op jit(solution)/shard_map/pallas_call | solution.py:320
  (31 shorter events, 0.8 us)
Async XLA Ops:
  7.4 12.2 %copy-start = (bf16[512,2048]{1,0:T(8,128)(2,1)S(1)}, bf16[512,2048]{1,0:T(8,128)(2,1)}, u32[]{:S(2)}) copy-start(bf16[512,2048]{1,0:T(8,128)(2,1)} %param.9) | copy-start | bytes 6291460
  7.4 68.4 %all-gather.3.cloned.1.call-start = ((), (), s32[]{:S(2)}) async-start(), calls=%async_computation.6 | async-start | bytes 2506752 | tf_op jit(solution)/shard_map/all_gather | solution.py:344
  14.5 5.1 %copy-start.5 = (bf16[256,512]{1,0:T(8,128)(2,1)S(1)}, bf16[256,512]{1,0:T(8,128)(2,1)}, u32[]{:S(2)}) copy-start(bf16[256,512]{1,0:T(8,128)(2,1)} %rows.2) | copy-start | bytes 786436
  14.5 61.3 %all-to-all-start = ((bf16[4,16,64,512]{3,2,1,0:T(8,128)(2,1)}), bf16[4,16,64,512]{3,2,1,0:T(8,128)(2,1)}, u32[]{:S(2)}, u32[]{:S(2)}) async-start(bf16[4,16,64,512]{3,2,1,0:T(8,128)(2,1)} %get-tuple-element.40), calls=%async_computation | async-start | bytes 8388608 | tf_op jit(solution)/shard_map/all_to_all | solution.py:346
  19.5 109.9 %reduce-scatter.2.cloned.1.call-start = ((), (), s32[]{:S(2)}) async-start(), calls=%async_computation.5 | async-start | bytes 2228224 | tf_op jit(solution)/shard_map/reduce_scatter | solution.py:350
  23.8 14.0 %collective-permute-start = (bf16[8,64,128]{2,1,0:T(8,128)(2,1)}, bf16[8,64,128]{2,1,0:T(8,128)(2,1)S(1)}, u32[]{:S(2)}, u32[]{:S(2)}) collective-permute-start(bf16[8,64,128]{2,1,0:T(8,128)(2,1)} %get-tuple-element.44), channel_id=1, source_target_pairs={{0,64},{64,128},{128,192},{192,256},{256,320},{320,384},{384,448},... | collective-permute-start | bytes 393224 | tf_op jit(solution)/shard_map/ppermute | solution.py:334
  27.9 12.8 %collective-permute-start.1 = (bf16[8,64,128]{2,1,0:T(8,128)(2,1)}, bf16[8,64,128]{2,1,0:T(8,128)(2,1)S(1)}, u32[]{:S(2)}, u32[]{:S(2)}) collective-permute-start(bf16[8,64,128]{2,1,0:T(8,128)(2,1)} %get-tuple-element.45), channel_id=1, source_target_pairs={{0,128},{64,192},{128,256},{192,320},{256,384},{320,448},{384,0},{... | collective-permute-start | bytes 393224 | tf_op jit(solution)/shard_map/ppermute | solution.py:334
  32.1 9.2 %collective-permute-start.2 = (bf16[8,64,128]{2,1,0:T(8,128)(2,1)}, bf16[8,64,128]{2,1,0:T(8,128)(2,1)S(1)}, u32[]{:S(2)}, u32[]{:S(2)}) collective-permute-start(bf16[8,64,128]{2,1,0:T(8,128)(2,1)} %get-tuple-element.46), channel_id=1, source_target_pairs={{0,384},{64,448},{128,0},{192,64},{256,128},{320,192},{384,256},{4... | collective-permute-start | bytes 393224 | tf_op jit(solution)/shard_map/ppermute | solution.py:334
  35.3 15.5 %collective-permute-start.3 = (bf16[8,64,128]{2,1,0:T(8,128)(2,1)}, bf16[8,64,128]{2,1,0:T(8,128)(2,1)S(1)}, u32[]{:S(2)}, u32[]{:S(2)}) collective-permute-start(bf16[8,64,128]{2,1,0:T(8,128)(2,1)} %get-tuple-element.47), channel_id=1, source_target_pairs={{0,448},{64,0},{128,64},{192,128},{256,192},{320,256},{384,320},{4... | collective-permute-start | bytes 393224 | tf_op jit(solution)/shard_map/ppermute | solution.py:334
  50.8 17.4 %collective-permute-start.4 = (bf16[8,64,128]{2,1,0:T(8,128)(2,1)}, bf16[8,64,128]{2,1,0:T(8,128)(2,1)S(1)}, u32[]{:S(2)}, u32[]{:S(2)}) collective-permute-start(bf16[8,64,128]{2,1,0:T(8,128)(2,1)} %get-tuple-element.53), channel_id=1, source_target_pairs={{0,192},{64,256},{128,320},{192,384},{256,448},{320,0},{384,64},{4... | collective-permute-start | bytes 393224 | tf_op jit(solution)/shard_map/ppermute | solution.py:334
  55.8 19.2 %collective-permute-start.5 = (bf16[8,64,128]{2,1,0:T(8,128)(2,1)}, bf16[8,64,128]{2,1,0:T(8,128)(2,1)S(1)}, u32[]{:S(2)}, u32[]{:S(2)}) collective-permute-start(bf16[8,64,128]{2,1,0:T(8,128)(2,1)} %get-tuple-element.54), channel_id=1, source_target_pairs={{0,256},{64,320},{128,384},{192,448},{256,0},{320,64},{384,128},{4... | collective-permute-start | bytes 393224 | tf_op jit(solution)/shard_map/ppermute | solution.py:334
  58.7 17.1 %collective-permute-start.6 = (bf16[8,64,128]{2,1,0:T(8,128)(2,1)}, bf16[8,64,128]{2,1,0:T(8,128)(2,1)S(1)}, u32[]{:S(2)}, u32[]{:S(2)}) collective-permute-start(bf16[8,64,128]{2,1,0:T(8,128)(2,1)} %get-tuple-element.55), channel_id=1, source_target_pairs={{0,320},{64,384},{128,448},{192,0},{256,64},{320,128},{384,192},{4... | collective-permute-start | bytes 393224 | tf_op jit(solution)/shard_map/ppermute | solution.py:334
  75.8 6.9 %copy-start.3 = (bf16[8,64,128]{2,1,0:T(8,128)(2,1)}, bf16[8,64,128]{2,1,0:T(8,128)(2,1)S(1)}, u32[]{:S(2)}) copy-start(bf16[8,64,128]{2,1,0:T(8,128)(2,1)S(1)} %collective-permute-done.6.refs_5_) | copy-start | bytes 393220
  75.8 14.3 %copy-start.2 = (bf16[8,64,128]{2,1,0:T(8,128)(2,1)S(1)}, bf16[8,64,128]{2,1,0:T(8,128)(2,1)}, u32[]{:S(2)}) copy-start(bf16[8,64,128]{2,1,0:T(8,128)(2,1)} %get-tuple-element.61.refs_0_) | copy-start | bytes 393220
  82.7 23.1 %all-to-all-start.1 = ((f32[8,16,8,128]{3,2,1,0:T(8,128)}), f32[8,16,8,128]{3,2,1,0:T(8,128)S(1)}, u32[]{:S(2)}, u32[]{:S(2)}) async-start(f32[8,16,8,128]{3,2,1,0:T(8,128)} %shard_map.68), calls=%async_computation.1 | async-start | bytes 1048576 | tf_op jit(solution)/shard_map/all_to_all | solution.py:365
  90.1 0.9 copy-start.4
  92.0 0.7 copy-start.1
  92.7 36.7 %collective-permute-start.7 = (bf16[16,64,128]{2,1,0:T(8,128)(2,1)}, bf16[16,64,128]{2,1,0:T(8,128)(2,1)S(1)}, u32[]{:S(2)}, u32[]{:S(2)}) collective-permute-start(bf16[16,64,128]{2,1,0:T(8,128)(2,1)} %get-tuple-element.70), channel_id=1, source_target_pairs={{0,16},{16,32},{32,48},{48,0},{1,17},{17,33},{33,49},{49,1},{2,18}... | collective-permute-start | bytes 786440 | tf_op jit(solution)/shard_map/ppermute | solution.py:334
  95.6 33.7 %collective-permute-start.8 = (bf16[16,64,128]{2,1,0:T(8,128)(2,1)}, bf16[16,64,128]{2,1,0:T(8,128)(2,1)S(1)}, u32[]{:S(2)}, u32[]{:S(2)}) collective-permute-start(bf16[16,64,128]{2,1,0:T(8,128)(2,1)} %get-tuple-element.71), channel_id=1, source_target_pairs={{0,32},{16,48},{32,0},{48,16},{1,33},{17,49},{33,1},{49,17},{2,34}... | collective-permute-start | bytes 786440 | tf_op jit(solution)/shard_map/ppermute | solution.py:334
  99.9 29.4 %collective-permute-start.9 = (bf16[16,64,128]{2,1,0:T(8,128)(2,1)}, bf16[16,64,128]{2,1,0:T(8,128)(2,1)S(1)}, u32[]{:S(2)}, u32[]{:S(2)}) collective-permute-start(bf16[16,64,128]{2,1,0:T(8,128)(2,1)} %get-tuple-element.72), channel_id=1, source_target_pairs={{0,48},{16,0},{32,16},{48,32},{1,49},{17,1},{33,17},{49,33},{2,50}... | collective-permute-start | bytes 786440 | tf_op jit(solution)/shard_map/ppermute | solution.py:334
  125.9 11.3 %all-to-all-start.3 = ((f32[16,8,128]{2,1,0:T(8,128)}), f32[16,8,128]{2,1,0:T(8,128)S(1)}, u32[]{:S(2)}, u32[]{:S(2)}) async-start(f32[16,8,128]{2,1,0:T(8,128)} %shard_map.70), calls=%async_computation.3 | async-start | bytes 131072 | tf_op jit(solution)/shard_map/all_to_all | solution.py:367
  129.3 7.8 %copy-start.6 = (bf16[16,64,128]{2,1,0:T(8,128)(2,1)}, bf16[16,64,128]{2,1,0:T(8,128)(2,1)S(1)}, u32[]{:S(2)}) copy-start(bf16[16,64,128]{2,1,0:T(8,128)(2,1)S(1)} %collective-permute-done.7.refs_1_) | copy-start | bytes 786436
  129.3 7.8 %copy-start.7 = (bf16[16,64,128]{2,1,0:T(8,128)(2,1)}, bf16[16,64,128]{2,1,0:T(8,128)(2,1)S(1)}, u32[]{:S(2)}) copy-start(bf16[16,64,128]{2,1,0:T(8,128)(2,1)S(1)} %collective-permute-done.8.refs_2_) | copy-start | bytes 786436
  129.4 7.8 %copy-start.8 = (bf16[16,64,128]{2,1,0:T(8,128)(2,1)}, bf16[16,64,128]{2,1,0:T(8,128)(2,1)S(1)}, u32[]{:S(2)}) copy-start(bf16[16,64,128]{2,1,0:T(8,128)(2,1)S(1)} %collective-permute-done.9.refs_3_) | copy-start | bytes 786436
  137.2 0.6 copy-start.9
Sparse Core Ops, SparseCore 0:
  10.3 65.1 all-gather.2
Sparse Core Ops, SparseCore 1:
  22.8 67.4 reduce-scatter.1

commit v12 on v9

--- a/solution.py
+++ b/solution.py
@@ -349,12 +349,12 @@
     own = local_shrink(code, late, adapter_down)
 
     ups = pick_up(picked, adapter_up)
-    near, far = (1, 7, 2, 6), (3, 5, 4)
+    near, far, last = (1, 7, 2, 6), (3, 5), Y // 2
     moved = {d: shift(ups[d], "y", Y, d) for d in near}
     moved, later = lax.optimization_barrier((moved, {d: ups[d] for d in far}))
     moved |= {d: shift(later[d], "y", Y, d) for d in far}
-    moved[0] = ups[0]
-    down, moved = lax.optimization_barrier((down, moved))
+    down, moved, later = lax.optimization_barrier((down, moved, ups[last]))
+    moved |= {0: ups[0], last: shift(later, "y", Y, last)}
     ups = [moved[d] for d in range(Y)]
     ups = turn(ups)
     tables = [ups[0]] + [shift(ups[e], "x", X, e) for e in range(1, X)]

time: 147 us -> 159 us (1.082)
  waiting for transfers between devices: 34.8 us -> 42.7 us
  starting transfers between devices: 66.3 us -> 70.8 us
    ppermute x10, waiting for transfers between devices: 20.5 us -> 32.8 us  [shift(): lax.ppermute(array, axis, [(i, (i + by) % size) for i in range(size)])]
    all_to_all x1, waiting for transfers between devices: 6.52 us -> 0.01 us  [shards(): lax.all_to_all(parts.reshape(Y * T, 8, 128), ('y', 'z', 'c'), 0, 0, tiled...]
    all_to_all x1, starting transfers between devices: 5.36 us -> 10.8 us  [shards(): shrink = lax.all_to_all(add_and_spread(parts), ('z', 'c'), 0, 0, tiled=True)]
    all_gather x1, waiting for transfers between devices: 0.01 us -> 2.12 us  [shards(): rows = lax.all_gather(sent, ('y', 'c'), axis_index_groups=rings)]
    all_to_all x1, starting transfers between devices: 17.2 us -> 15.5 us  [shards(): lax.all_to_all(parts.reshape(Y * T, 8, 128), ('y', 'z', 'c'), 0, 0, tiled...]
  transfers between devices with their start and end apart: 15 -> 15, of which waited for: 7 -> 8; matrix products, arithmetic and copies ran while one was open for 1% -> 1% of each run, Pallas kernels for 13% -> 12%
where the time goes in v12:
time: 159 us; the launch traced here: 158 us
  starting transfers between devices  70.8 us (45%)
  waiting for transfers between devices  42.7 us (27%)
  Pallas kernels  26 us (16%)
  between operations  15.1 us (9%)
  matrix products  2.08 us (1%)
    ppermute x10, starting transfers between devices, shift(): lax.ppermute(array, axis, [(i, (i + by) % size) for i in range(size)])  39.4 us
    ppermute x10, waiting for transfers between devices, shift(): lax.ppermute(array, axis, [(i, (i + by) % size) for i in range(size)])  32.8 us
    all_to_all x1, starting transfers between devices, shards(): lax.all_to_all(parts.reshape(Y * T, 8, 128), ('y', 'z', 'c'), 0, 0, tiled...  15.5 us
    all_to_all x1, starting transfers between devices, shards(): shrink = lax.all_to_all(add_and_spread(parts), ('z', 'c'), 0, 0, tiled=True)  10.8 us
    all_to_all x1, waiting for transfers between devices, shards(): shrink = lax.all_to_all(add_and_spread(parts), ('z', 'c'), 0, 0, tiled=True)  7.72 us
    pallas_call x1, Pallas kernels, imported_shrink(): pl.pallas_call(functools.partial(imported_kernel, resident), out_shape=ja...  6.88 us
    pallas_call x1, Pallas kernels, expand(): pl.pallas_call(expand_kernel, out_shape=jax.ShapeDtypeStruct(base.shape,...  5.06 us
    pallas_call x1, Pallas kernels, dispatch(): pl.pallas_call(dispatch_kernel, out_shape=(jax.ShapeDtypeStruct(shape, do...  5 us
  transfers between devices with their start and end apart: 15, of which 8 were waited for; matrix products, arithmetic and copies ran while one was open for 1% of the time, Pallas kernels for 12%

profile of v12, /device:TPU:1, one launch (start us, length us, event | category | flops | bytes accessed | tf_op | source)
XLA Modules:
  0.0 157.9 jit_solution(12348158482408329420)
XLA Ops:
  7.4 2.1 %shard_map.64 = (bf16[272,512]{1,0:T(8,128)(2,1)}, s32[1,256]{1,0:T(1,128)}) custom-call(s32[32,31]{1,0:T(8,128)} %plan.3, s32[1,256]{1,0:T(1,128)} %bitcast.10, bf16[256,512]{1,0:T(8,128)(2,1)} %rows.2), custom_call_target="tpu_custom_call" | custom-call | bytes 524288 | tf_op jit(solution)/shard_map/pallas_call | solution.py:107
  9.5 5.0 %shard_map.65 = (bf16[4,16,64,512]{3,2,1,0:T(8,128)(2,1)}, s32[32,128]{1,0:T(8,128)}) custom-call(s32[32,31]{1,0:T(8,128)} %plan.3, bf16[32,64,512]{2,1,0:T(8,128)(2,1)} %down.1), custom_call_target="tpu_custom_call" | custom-call | bytes 6291456 | tf_op jit(solution)/shard_map/pallas_call | solution.py:66
  14.5 5.0 %all-to-all-start = ((bf16[4,16,64,512]{3,2,1,0:T(8,128)(2,1)}), bf16[4,16,64,512]{3,2,1,0:T(8,128)(2,1)}, u32[]{:S(2)}, u32[]{:S(2)}) async-start(bf16[4,16,64,512]{3,2,1,0:T(8,128)(2,1)} %get-tuple-element.38), calls=%async_computation | async-start | bytes 8388608 | tf_op jit(solution)/shard_map/all_to_all | solution.py:344
  19.6 2.1 %fusion = f32[256,2048]{1,0:T(8,128)} fusion(bf16[256,512]{1,0:T(8,128)(2,1)S(1)} %copy-done.3, bf16[512,2048]{1,0:T(8,128)(2,1)S(1)} %copy-done), kind=kOutput, calls=%fused_computation | convolution fusion | flops 536870912 | bytes 4456448 | tf_op jit(solution)/shard_map/dot_general | solution.py:347
  21.7 2.1 %shard_map.66 = (bf16[8,64,128]{2,1,0:T(8,128)(2,1)}, bf16[8,64,128]{2,1,0:T(8,128)(2,1)}, bf16[8,64,128]{2,1,0:T(8,128)(2,1)}, bf16[8,64,128]{2,1,0:T(8,128)(2,...) custom-call(s32[32,128]{1,0:T(8,128)} %get-tuple-element.40.picked, ...), custom_call_target="tpu_custom_call" | custom-call | bytes 1572864 | tf_op jit(solution)/shard_map/pallas_call | solution.py:131
  23.8 4.0 %collective-permute-start = (bf16[8,64,128]{2,1,0:T(8,128)(2,1)}, bf16[8,64,128]{2,1,0:T(8,128)(2,1)S(1)}, u32[]{:S(2)}, u32[]{:S(2)}) collective-permute-start(bf16[8,64,128]{2,1,0:T(8,128)(2,1)} %get-tuple-element.41), channel_id=1, source_target_pairs={{0,64},{64,128},{128,192},{192,256},{256,320},{320,384},{384,448},... | collective-permute-start | bytes 393224 | tf_op jit(solution)/shard_map/ppermute | solution.py:332
  27.8 4.2 %collective-permute-start.1 = (bf16[8,64,128]{2,1,0:T(8,128)(2,1)}, bf16[8,64,128]{2,1,0:T(8,128)(2,1)S(1)}, u32[]{:S(2)}, u32[]{:S(2)}) collective-permute-start(bf16[8,64,128]{2,1,0:T(8,128)(2,1)} %get-tuple-element.42), channel_id=1, source_target_pairs={{0,128},{64,192},{128,256},{192,320},{256,384},{320,448},{384,0},{... | collective-permute-start | bytes 393224 | tf_op jit(solution)/shard_map/ppermute | solution.py:332
  32.1 3.2 %collective-permute-start.2 = (bf16[8,64,128]{2,1,0:T(8,128)(2,1)}, bf16[8,64,128]{2,1,0:T(8,128)(2,1)S(1)}, u32[]{:S(2)}, u32[]{:S(2)}) collective-permute-start(bf16[8,64,128]{2,1,0:T(8,128)(2,1)} %get-tuple-element.43), channel_id=1, source_target_pairs={{0,384},{64,448},{128,0},{192,64},{256,128},{320,192},{384,256},{4... | collective-permute-start | bytes 393224 | tf_op jit(solution)/shard_map/ppermute | solution.py:332
  35.2 2.6 %collective-permute-start.3 = (bf16[8,64,128]{2,1,0:T(8,128)(2,1)}, bf16[8,64,128]{2,1,0:T(8,128)(2,1)S(1)}, u32[]{:S(2)}, u32[]{:S(2)}) collective-permute-start(bf16[8,64,128]{2,1,0:T(8,128)(2,1)} %get-tuple-element.44), channel_id=1, source_target_pairs={{0,448},{64,0},{128,64},{192,128},{256,192},{320,256},{384,320},{4... | collective-permute-start | bytes 393224 | tf_op jit(solution)/shard_map/ppermute | solution.py:332
  37.9 2.7 %collective-permute-done.1.refs_2_ = bf16[8,64,128]{2,1,0:T(8,128)(2,1)S(1)} collective-permute-done((bf16[8,64,128]{2,1,0:T(8,128)(2,1)}, bf16[8,64,128]{2,1,0:T(8,128)(2,1)S(1)}, u32[]{:S(2)}, u32[]{:S(2)}) %collective-permute-start.1) | collective-permute-done | bytes 131104 | tf_op jit(solution)/shard_map/ppermute | solution.py:332
  40.6 0.7 collective-permute-done.2.refs_6_
  41.3 9.5 %collective-permute-done.3.refs_7_ = bf16[8,64,128]{2,1,0:T(8,128)(2,1)S(1)} collective-permute-done((bf16[8,64,128]{2,1,0:T(8,128)(2,1)}, bf16[8,64,128]{2,1,0:T(8,128)(2,1)S(1)}, u32[]{:S(2)}, u32[]{:S(2)}) %collective-permute-start.3) | collective-permute-done | bytes 131104 | tf_op jit(solution)/shard_map/ppermute | solution.py:332
  50.7 5.2 %collective-permute-start.4 = (bf16[8,64,128]{2,1,0:T(8,128)(2,1)}, bf16[8,64,128]{2,1,0:T(8,128)(2,1)S(1)}, u32[]{:S(2)}, u32[]{:S(2)}) collective-permute-start(bf16[8,64,128]{2,1,0:T(8,128)(2,1)} %get-tuple-element.49), channel_id=1, source_target_pairs={{0,192},{64,256},{128,320},{192,384},{256,448},{320,0},{384,64},{4... | collective-permute-start | bytes 393224 | tf_op jit(solution)/shard_map/ppermute | solution.py:332
  55.9 3.1 %collective-permute-start.5 = (bf16[8,64,128]{2,1,0:T(8,128)(2,1)}, bf16[8,64,128]{2,1,0:T(8,128)(2,1)S(1)}, u32[]{:S(2)}, u32[]{:S(2)}) collective-permute-start(bf16[8,64,128]{2,1,0:T(8,128)(2,1)} %get-tuple-element.50), channel_id=1, source_target_pairs={{0,320},{64,384},{128,448},{192,0},{256,64},{320,128},{384,192},{4... | collective-permute-start | bytes 393224 | tf_op jit(solution)/shard_map/ppermute | solution.py:332
  59.0 3.1 %shard_map.67.own = f32[64,256]{1,0:T(8,128)} custom-call(s32[1,256]{1,0:T(1,128)} %get-tuple-element.55.code, bf16[256,512]{1,0:T(8,128)(2,1)} %rows.2, bf16[2048,512]{1,0:T(8,128)(2,1)} %bitcast.7), custom_call_target="tpu_custom_call" | custom-call | flops 536870912 | bytes 2097152 | tf_op jit(solution)/shard_map/pallas_call | solution.py:180
  62.1 5.1 %collective-permute-done.4.refs_3_ = bf16[8,64,128]{2,1,0:T(8,128)(2,1)S(1)} collective-permute-done((bf16[8,64,128]{2,1,0:T(8,128)(2,1)}, bf16[8,64,128]{2,1,0:T(8,128)(2,1)S(1)}, u32[]{:S(2)}, u32[]{:S(2)}) %collective-permute-start.4) | collective-permute-done | bytes 131104 | tf_op jit(solution)/shard_map/ppermute | solution.py:332
  67.2 2.2 %collective-permute-done.5.refs_5_ = bf16[8,64,128]{2,1,0:T(8,128)(2,1)S(1)} collective-permute-done((bf16[8,64,128]{2,1,0:T(8,128)(2,1)}, bf16[8,64,128]{2,1,0:T(8,128)(2,1)S(1)}, u32[]{:S(2)}, u32[]{:S(2)}) %collective-permute-start.5) | collective-permute-done | bytes 131104 | tf_op jit(solution)/shard_map/ppermute | solution.py:332
  69.4 2.1 %all-gather.3.cloned.1.call-done = bf16[2176,512]{1,0:T(8,128)(2,1)} async-done(((bf16[272,512]{1,0:T(8,128)(2,1)}), bf16[2176,512]{1,0:T(8,128)(2,1)}) %all-gather.3.cloned.1.call-update) | async-done | bytes 2228240 | tf_op jit(solution)/shard_map/all_gather | solution.py:342
  71.5 6.9 %shard_map.68 = f32[8,16,8,128]{3,2,1,0:T(8,128)} custom-call(bf16[8,272,512]{2,1,0:T(8,128)(2,1)} %bitcast.8, bf16[4,1024,512]{2,1,0:T(8,128)(2,1)} %bitcast.2.down, f32[64,256]{1,0:T(8,128)} %shard_map.67.own), custom_call_target="tpu_custom_call" | custom-call | flops 1073741824 | bytes 6422528 | tf_op jit(solution)/shard_map/pallas_call | solution.py:229
  78.4 15.5 %all-to-all-start.1 = ((f32[128,8,128]{2,1,0:T(8,128)}), f32[128,8,128]{2,1,0:T(8,128)S(1)}, u32[]{:S(2)}, u32[]{:S(2)}) async-start(f32[128,8,128]{2,1,0:T(8,128)} %bitcast.9), calls=%async_computation.1 | async-start | bytes 1048576 | tf_op jit(solution)/shard_map/all_to_all | solution.py:363
  94.0 7.5 %collective-permute-start.6 = (bf16[8,64,128]{2,1,0:T(8,128)(2,1)}, bf16[8,64,128]{2,1,0:T(8,128)(2,1)S(1)}, u32[]{:S(2)}, u32[]{:S(2)}) collective-permute-start(bf16[8,64,128]{2,1,0:T(8,128)(2,1)} %get-tuple-element.61), channel_id=1, source_target_pairs={{0,256},{64,320},{128,384},{192,448},{256,0},{320,64},{384,128},{4... | collective-permute-start | bytes 393224 | tf_op jit(solution)/shard_map/ppermute | solution.py:332
  101.5 12.6 %collective-permute-done.6.refs_4_ = bf16[8,64,128]{2,1,0:T(8,128)(2,1)S(1)} collective-permute-done((bf16[8,64,128]{2,1,0:T(8,128)(2,1)}, bf16[8,64,128]{2,1,0:T(8,128)(2,1)S(1)}, u32[]{:S(2)}, u32[]{:S(2)}) %collective-permute-start.6) | collective-permute-done | bytes 131104 | tf_op jit(solution)/shard_map/ppermute | solution.py:332
  114.1 1.0 shard_map.70
  115.0 0.7 copy-done.1
  115.7 2.2 %collective-permute-start.7 = (bf16[16,64,128]{2,1,0:T(8,128)(2,1)}, bf16[16,64,128]{2,1,0:T(8,128)(2,1)S(1)}, u32[]{:S(2)}, u32[]{:S(2)}) collective-permute-start(bf16[16,64,128]{2,1,0:T(8,128)(2,1)} %get-tuple-element.66), channel_id=1, source_target_pairs={{0,16},{16,32},{32,48},{48,0},{1,17},{17,33},{33,49},{49,1},{2,18}... | collective-permute-start | bytes 786440 | tf_op jit(solution)/shard_map/ppermute | solution.py:332
  117.9 4.3 %collective-permute-start.8 = (bf16[16,64,128]{2,1,0:T(8,128)(2,1)}, bf16[16,64,128]{2,1,0:T(8,128)(2,1)S(1)}, u32[]{:S(2)}, u32[]{:S(2)}) collective-permute-start(bf16[16,64,128]{2,1,0:T(8,128)(2,1)} %get-tuple-element.67), channel_id=1, source_target_pairs={{0,32},{16,48},{32,0},{48,16},{1,33},{17,49},{33,1},{49,17},{2,34}... | collective-permute-start | bytes 786440 | tf_op jit(solution)/shard_map/ppermute | solution.py:332
  122.2 3.1 %collective-permute-start.9 = (bf16[16,64,128]{2,1,0:T(8,128)(2,1)}, bf16[16,64,128]{2,1,0:T(8,128)(2,1)S(1)}, u32[]{:S(2)}, u32[]{:S(2)}) collective-permute-start(bf16[16,64,128]{2,1,0:T(8,128)(2,1)} %get-tuple-element.68), channel_id=1, source_target_pairs={{0,48},{16,0},{32,16},{48,32},{1,49},{17,1},{33,17},{49,33},{2,50}... | collective-permute-start | bytes 786440 | tf_op jit(solution)/shard_map/ppermute | solution.py:332
  125.3 0.8 shard_map.69
  126.1 10.8 %all-to-all-start.2 = ((f32[16,8,128]{2,1,0:T(8,128)}), f32[16,8,128]{2,1,0:T(8,128)S(1)}, u32[]{:S(2)}, u32[]{:S(2)}) async-start(f32[16,8,128]{2,1,0:T(8,128)} %shard_map.69), calls=%async_computation.2 | async-start | bytes 131072 | tf_op jit(solution)/shard_map/all_to_all | solution.py:364
  137.0 7.7 %all-to-all-done.2.shrink = f32[16,8,128]{2,1,0:T(8,128)S(1)} async-done(((f32[16,8,128]{2,1,0:T(8,128)}), f32[16,8,128]{2,1,0:T(8,128)S(1)}, u32[]{:S(2)}, u32[]{:S(2)}) %all-to-all-start.2) | async-done | bytes 65568 | tf_op jit(solution)/shard_map/all_to_all | solution.py:364
  144.7 0.6 copy-done.7
  145.4 5.1 %shard_map.71 = bf16[256,128]{1,0:T(8,128)(2,1)} custom-call(f32[16,8,128]{2,1,0:T(8,128)} %copy-done.7, s32[1,256]{1,0:T(1,128)} %get-tuple-element.55.code, f32[256,128]{1,0:T(8,128)} %reduce-scatter.2.cloned.1.call-done.base, bf16[32,64,128]{2,1,0:T(8,128)(2,1)} %up.3, bf16[16,64,128]{2,1,0:T(8,128)(2,1)} %copy-done.1, bf16[16,64,128]{2,1,0:T(8,128)(2,1)} %copy-done.4, ...), custom_call_target="tpu_custom_call" | custom-call | tf_op jit(solution)/shard_map/pallas_call | solution.py:318
  (25 shorter events, 0.2 us)
Async XLA Ops:
  7.4 12.2 %copy-start = (bf16[512,2048]{1,0:T(8,128)(2,1)S(1)}, bf16[512,2048]{1,0:T(8,128)(2,1)}, u32[]{:S(2)}) copy-start(bf16[512,2048]{1,0:T(8,128)(2,1)} %param.9) | copy-start | bytes 6291460
  7.4 64.2 %all-gather.3.cloned.1.call-start = ((), (), s32[]{:S(2)}) async-start(), calls=%async_computation.5 | async-start | bytes 2506752 | tf_op jit(solution)/shard_map/all_gather | solution.py:342
  14.5 5.1 %copy-start.3 = (bf16[256,512]{1,0:T(8,128)(2,1)S(1)}, bf16[256,512]{1,0:T(8,128)(2,1)}, u32[]{:S(2)}) copy-start(bf16[256,512]{1,0:T(8,128)(2,1)} %rows.2) | copy-start | bytes 786436
  14.5 54.9 %all-to-all-start = ((bf16[4,16,64,512]{3,2,1,0:T(8,128)(2,1)}), bf16[4,16,64,512]{3,2,1,0:T(8,128)(2,1)}, u32[]{:S(2)}, u32[]{:S(2)}) async-start(bf16[4,16,64,512]{3,2,1,0:T(8,128)(2,1)} %get-tuple-element.38), calls=%async_computation | async-start | bytes 8388608 | tf_op jit(solution)/shard_map/all_to_all | solution.py:344
  19.5 117.5 %reduce-scatter.2.cloned.1.call-start = ((), (), s32[]{:S(2)}) async-start(), calls=%async_computation.4 | async-start | bytes 2228224 | tf_op jit(solution)/shard_map/reduce_scatter | solution.py:348
  23.8 14.0 %collective-permute-start = (bf16[8,64,128]{2,1,0:T(8,128)(2,1)}, bf16[8,64,128]{2,1,0:T(8,128)(2,1)S(1)}, u32[]{:S(2)}, u32[]{:S(2)}) collective-permute-start(bf16[8,64,128]{2,1,0:T(8,128)(2,1)} %get-tuple-element.41), channel_id=1, source_target_pairs={{0,64},{64,128},{128,192},{192,256},{256,320},{320,384},{384,448},... | collective-permute-start | bytes 393224 | tf_op jit(solution)/shard_map/ppermute | solution.py:332
  27.8 12.7 %collective-permute-start.1 = (bf16[8,64,128]{2,1,0:T(8,128)(2,1)}, bf16[8,64,128]{2,1,0:T(8,128)(2,1)S(1)}, u32[]{:S(2)}, u32[]{:S(2)}) collective-permute-start(bf16[8,64,128]{2,1,0:T(8,128)(2,1)} %get-tuple-element.42), channel_id=1, source_target_pairs={{0,128},{64,192},{128,256},{192,320},{256,384},{320,448},{384,0},{... | collective-permute-start | bytes 393224 | tf_op jit(solution)/shard_map/ppermute | solution.py:332
  32.1 9.2 %collective-permute-start.2 = (bf16[8,64,128]{2,1,0:T(8,128)(2,1)}, bf16[8,64,128]{2,1,0:T(8,128)(2,1)S(1)}, u32[]{:S(2)}, u32[]{:S(2)}) collective-permute-start(bf16[8,64,128]{2,1,0:T(8,128)(2,1)} %get-tuple-element.43), channel_id=1, source_target_pairs={{0,384},{64,448},{128,0},{192,64},{256,128},{320,192},{384,256},{4... | collective-permute-start | bytes 393224 | tf_op jit(solution)/shard_map/ppermute | solution.py:332
  35.2 15.5 %collective-permute-start.3 = (bf16[8,64,128]{2,1,0:T(8,128)(2,1)}, bf16[8,64,128]{2,1,0:T(8,128)(2,1)S(1)}, u32[]{:S(2)}, u32[]{:S(2)}) collective-permute-start(bf16[8,64,128]{2,1,0:T(8,128)(2,1)} %get-tuple-element.44), channel_id=1, source_target_pairs={{0,448},{64,0},{128,64},{192,128},{256,192},{320,256},{384,320},{4... | collective-permute-start | bytes 393224 | tf_op jit(solution)/shard_map/ppermute | solution.py:332
  50.7 16.5 %collective-permute-start.4 = (bf16[8,64,128]{2,1,0:T(8,128)(2,1)}, bf16[8,64,128]{2,1,0:T(8,128)(2,1)S(1)}, u32[]{:S(2)}, u32[]{:S(2)}) collective-permute-start(bf16[8,64,128]{2,1,0:T(8,128)(2,1)} %get-tuple-element.49), channel_id=1, source_target_pairs={{0,192},{64,256},{128,320},{192,384},{256,448},{320,0},{384,64},{4... | collective-permute-start | bytes 393224 | tf_op jit(solution)/shard_map/ppermute | solution.py:332
  55.9 13.5 %collective-permute-start.5 = (bf16[8,64,128]{2,1,0:T(8,128)(2,1)}, bf16[8,64,128]{2,1,0:T(8,128)(2,1)S(1)}, u32[]{:S(2)}, u32[]{:S(2)}) collective-permute-start(bf16[8,64,128]{2,1,0:T(8,128)(2,1)} %get-tuple-element.50), channel_id=1, source_target_pairs={{0,320},{64,384},{128,448},{192,0},{256,64},{320,128},{384,192},{4... | collective-permute-start | bytes 393224 | tf_op jit(solution)/shard_map/ppermute | solution.py:332
  71.5 42.5 %copy-start.2 = (bf16[8,64,128]{2,1,0:T(8,128)(2,1)S(1)}, bf16[8,64,128]{2,1,0:T(8,128)(2,1)}, u32[]{:S(2)}) copy-start(bf16[8,64,128]{2,1,0:T(8,128)(2,1)} %get-tuple-element.57.refs_0_) | copy-start | bytes 393220
  78.4 46.9 %all-to-all-start.1 = ((f32[128,8,128]{2,1,0:T(8,128)}), f32[128,8,128]{2,1,0:T(8,128)S(1)}, u32[]{:S(2)}, u32[]{:S(2)}) async-start(f32[128,8,128]{2,1,0:T(8,128)} %bitcast.9), calls=%async_computation.1 | async-start | bytes 1048576 | tf_op jit(solution)/shard_map/all_to_all | solution.py:363
  94.0 20.1 %collective-permute-start.6 = (bf16[8,64,128]{2,1,0:T(8,128)(2,1)}, bf16[8,64,128]{2,1,0:T(8,128)(2,1)S(1)}, u32[]{:S(2)}, u32[]{:S(2)}) collective-permute-start(bf16[8,64,128]{2,1,0:T(8,128)(2,1)} %get-tuple-element.61), channel_id=1, source_target_pairs={{0,256},{64,320},{128,384},{192,448},{256,0},{320,64},{384,128},{4... | collective-permute-start | bytes 393224 | tf_op jit(solution)/shard_map/ppermute | solution.py:332
  115.0 0.7 copy-start.1
  115.7 21.2 %collective-permute-start.7 = (bf16[16,64,128]{2,1,0:T(8,128)(2,1)}, bf16[16,64,128]{2,1,0:T(8,128)(2,1)S(1)}, u32[]{:S(2)}, u32[]{:S(2)}) collective-permute-start(bf16[16,64,128]{2,1,0:T(8,128)(2,1)} %get-tuple-element.66), channel_id=1, source_target_pairs={{0,16},{16,32},{32,48},{48,0},{1,17},{17,33},{33,49},{49,1},{2,18}... | collective-permute-start | bytes 786440 | tf_op jit(solution)/shard_map/ppermute | solution.py:332
  117.9 19.0 %collective-permute-start.8 = (bf16[16,64,128]{2,1,0:T(8,128)(2,1)}, bf16[16,64,128]{2,1,0:T(8,128)(2,1)S(1)}, u32[]{:S(2)}, u32[]{:S(2)}) collective-permute-start(bf16[16,64,128]{2,1,0:T(8,128)(2,1)} %get-tuple-element.67), channel_id=1, source_target_pairs={{0,32},{16,48},{32,0},{48,16},{1,33},{17,49},{33,1},{49,17},{2,34}... | collective-permute-start | bytes 786440 | tf_op jit(solution)/shard_map/ppermute | solution.py:332
  122.2 14.7 %collective-permute-start.9 = (bf16[16,64,128]{2,1,0:T(8,128)(2,1)}, bf16[16,64,128]{2,1,0:T(8,128)(2,1)S(1)}, u32[]{:S(2)}, u32[]{:S(2)}) collective-permute-start(bf16[16,64,128]{2,1,0:T(8,128)(2,1)} %get-tuple-element.68), channel_id=1, source_target_pairs={{0,48},{16,0},{32,16},{48,32},{1,49},{17,1},{33,17},{49,33},{2,50}... | collective-permute-start | bytes 786440 | tf_op jit(solution)/shard_map/ppermute | solution.py:332
  126.1 18.6 %all-to-all-start.2 = ((f32[16,8,128]{2,1,0:T(8,128)}), f32[16,8,128]{2,1,0:T(8,128)S(1)}, u32[]{:S(2)}, u32[]{:S(2)}) async-start(f32[16,8,128]{2,1,0:T(8,128)} %shard_map.69), calls=%async_computation.2 | async-start | bytes 131072 | tf_op jit(solution)/shard_map/all_to_all | solution.py:364
  136.9 7.8 %copy-start.4 = (bf16[16,64,128]{2,1,0:T(8,128)(2,1)}, bf16[16,64,128]{2,1,0:T(8,128)(2,1)S(1)}, u32[]{:S(2)}) copy-start(bf16[16,64,128]{2,1,0:T(8,128)(2,1)S(1)} %collective-permute-done.7.refs_1_) | copy-start | bytes 786436
  137.0 7.8 %copy-start.5 = (bf16[16,64,128]{2,1,0:T(8,128)(2,1)}, bf16[16,64,128]{2,1,0:T(8,128)(2,1)S(1)}, u32[]{:S(2)}) copy-start(bf16[16,64,128]{2,1,0:T(8,128)(2,1)S(1)} %collective-permute-done.8.refs_2_) | copy-start | bytes 786436
  137.0 7.8 %copy-start.6 = (bf16[16,64,128]{2,1,0:T(8,128)(2,1)}, bf16[16,64,128]{2,1,0:T(8,128)(2,1)S(1)}, u32[]{:S(2)}) copy-start(bf16[16,64,128]{2,1,0:T(8,128)(2,1)S(1)} %collective-permute-done.9.refs_3_) | copy-start | bytes 786436
  144.7 0.6 copy-start.7
Sparse Core Ops, SparseCore 0:
  10.3 61.2 all-gather.2
Sparse Core Ops, SparseCore 1:
  22.8 67.2 reduce-scatter.1

commit v13 on v7

--- a/solution.py
+++ b/solution.py
@@ -349,12 +349,17 @@
     own = local_shrink(code, late, adapter_down)
 
     ups = pick_up(picked, adapter_up)
-    ups = [ups[0]] + [shift(ups[d], "y", Y, d) for d in range(1, Y)]
-    down, ups = lax.optimization_barrier((down, ups))
-    ups = turn(ups)
+    near, far = (1, 7, 2, 6), (4, 3, 5)
+    moved = [shift(ups[d], "y", Y, d) for d in near]
+    moved, later = lax.optimization_barrier((moved, [ups[d] for d in far]))
+    moved_far = [shift(ups_d, "y", Y, d) for ups_d, d in zip(later, far)]
+    down, moved = lax.optimization_barrier((down, moved))
+    parts = imported_shrink(resident, rows, down, own)
+    parts, moved_far = lax.optimization_barrier((parts, moved_far))
+    moved = dict(zip(near + far, moved + moved_far)) | {0: ups[0]}
+    ups = turn([moved[d] for d in range(Y)])
     tables = [ups[0]] + [shift(ups[e], "x", X, e) for e in range(1, X)]
 
-    parts = imported_shrink(resident, rows, down, own)
     parts = lax.all_to_all(parts.reshape(Y * T, 8, 128), ("y", "z", "c"), 0, 0, tiled=True)
     shrink = lax.all_to_all(add_and_spread(parts), ("z", "c"), 0, 0, tiled=True)
     return expand(shrink, code, base, adapter_up, tables)

time: 149 us -> 144 us (0.966)
  waiting for transfers between devices: 39.6 us -> 34.4 us
    ppermute x10, waiting for transfers between devices: 17.8 us -> 10.4 us  [shift(): lax.ppermute(array, axis, [(i, (i + by) % size) for i in range(size)])]
    all_gather x1, waiting for transfers between devices: 7.41 us -> 9.59 us  [shards(): rows = lax.all_gather(sent, ('y', 'c'), axis_index_groups=rings)]
    ppermute x10, starting transfers between devices: 39.6 us -> 37.7 us  [shift(): lax.ppermute(array, axis, [(i, (i + by) % size) for i in range(size)])]
  transfers between devices with their start and end apart: 15 -> 15, of which waited for: 7 -> 5; matrix products, arithmetic and copies ran while one was open for 1% -> 1% of each run, Pallas kernels for 13% -> 13%
where the time goes in v13:
time: 144 us; the launch traced here: 143 us
  starting transfers between devices  62.7 us (44%)
  waiting for transfers between devices  34.4 us (24%)
  Pallas kernels  26 us (18%)
  between operations  15.1 us (10%)
  local copies, waits for them, and re-layouts  2.86 us (2%)
  matrix products  2.09 us (1%)
    ppermute x10, starting transfers between devices, shift(): lax.ppermute(array, axis, [(i, (i + by) % size) for i in range(size)])  37.7 us
    all_to_all x1, starting transfers between devices, shards(): lax.all_to_all(parts.reshape(Y * T, 8, 128), ('y', 'z', 'c'), 0, 0, tiled...  14.6 us
    ppermute x10, waiting for transfers between devices, shift(): lax.ppermute(array, axis, [(i, (i + by) % size) for i in range(size)])  10.4 us
    all_gather x1, waiting for transfers between devices, shards(): rows = lax.all_gather(sent, ('y', 'c'), axis_index_groups=rings)  9.59 us
    all_to_all x1, waiting for transfers between devices, shards(): shrink = lax.all_to_all(add_and_spread(parts), ('z', 'c'), 0, 0, tiled=True)  7.75 us
    pallas_call x1, Pallas kernels, imported_shrink(): pl.pallas_call(functools.partial(imported_kernel, resident), out_shape=ja...  6.88 us
    all_to_all x1, waiting for transfers between devices, shards(): lax.all_to_all(parts.reshape(Y * T, 8, 128), ('y', 'z', 'c'), 0, 0, tiled...  6.68 us
    all_to_all x1, starting transfers between devices, shards(): shrink = lax.all_to_all(add_and_spread(parts), ('z', 'c'), 0, 0, tiled=True)  5.36 us
  transfers between devices with their start and end apart: 15, of which 5 were waited for; matrix products, arithmetic and copies ran while one was open for 1% of the time, Pallas kernels for 13%

profile of v13, /device:TPU:1, one launch (start us, length us, event | category | flops | bytes accessed | tf_op | source)
XLA Modules:
  0.0 143.2 jit_solution(15661718211210946104)
XLA Ops:
  7.4 2.1 %shard_map.64 = (bf16[272,512]{1,0:T(8,128)(2,1)}, s32[1,256]{1,0:T(1,128)}) custom-call(s32[32,31]{1,0:T(8,128)} %plan.3, s32[1,256]{1,0:T(1,128)} %bitcast.10, bf16[256,512]{1,0:T(8,128)(2,1)} %rows.2), custom_call_target="tpu_custom_call" | custom-call | bytes 524288 | tf_op jit(solution)/shard_map/pallas_call | solution.py:107
  9.5 5.0 %shard_map.65 = (bf16[4,16,64,512]{3,2,1,0:T(8,128)(2,1)}, s32[32,128]{1,0:T(8,128)}) custom-call(s32[32,31]{1,0:T(8,128)} %plan.3, bf16[32,64,512]{2,1,0:T(8,128)(2,1)} %down.1), custom_call_target="tpu_custom_call" | custom-call | bytes 6291456 | tf_op jit(solution)/shard_map/pallas_call | solution.py:66
  14.5 5.0 %all-to-all-start = ((bf16[4,16,64,512]{3,2,1,0:T(8,128)(2,1)}), bf16[4,16,64,512]{3,2,1,0:T(8,128)(2,1)}, u32[]{:S(2)}, u32[]{:S(2)}) async-start(bf16[4,16,64,512]{3,2,1,0:T(8,128)(2,1)} %get-tuple-element.40), calls=%async_computation | async-start | bytes 8388608 | tf_op jit(solution)/shard_map/all_to_all | solution.py:344
  19.5 0.0 reduce-scatter.2.cloned.1.call-start
  19.6 2.1 %fusion = f32[256,2048]{1,0:T(8,128)} fusion(bf16[256,512]{1,0:T(8,128)(2,1)S(1)} %copy-done.5, bf16[512,2048]{1,0:T(8,128)(2,1)S(1)} %copy-done), kind=kOutput, calls=%fused_computation | convolution fusion | flops 536870912 | bytes 4456448 | tf_op jit(solution)/shard_map/dot_general | solution.py:347
  21.7 2.1 %shard_map.66 = (bf16[8,64,128]{2,1,0:T(8,128)(2,1)}, bf16[8,64,128]{2,1,0:T(8,128)(2,1)}, bf16[8,64,128]{2,1,0:T(8,128)(2,1)}, bf16[8,64,128]{2,1,0:T(8,128)(2,...) custom-call(s32[32,128]{1,0:T(8,128)} %get-tuple-element.42.picked, ...), custom_call_target="tpu_custom_call" | custom-call | bytes 1572864 | tf_op jit(solution)/shard_map/pallas_call | solution.py:131
  23.8 4.0 %collective-permute-start = (bf16[8,64,128]{2,1,0:T(8,128)(2,1)}, bf16[8,64,128]{2,1,0:T(8,128)(2,1)S(1)}, u32[]{:S(2)}, u32[]{:S(2)}) collective-permute-start(bf16[8,64,128]{2,1,0:T(8,128)(2,1)} %get-tuple-element.43), channel_id=1, source_target_pairs={{0,64},{64,128},{128,192},{192,256},{256,320},{320,384},{384,448},... | collective-permute-start | bytes 393224 | tf_op jit(solution)/shard_map/ppermute | solution.py:332
  27.9 3.8 %collective-permute-start.1 = (bf16[8,64,128]{2,1,0:T(8,128)(2,1)}, bf16[8,64,128]{2,1,0:T(8,128)(2,1)S(1)}, u32[]{:S(2)}, u32[]{:S(2)}) collective-permute-start(bf16[8,64,128]{2,1,0:T(8,128)(2,1)} %get-tuple-element.44), channel_id=1, source_target_pairs={{0,448},{64,0},{128,64},{192,128},{256,192},{320,256},{384,320},{4... | collective-permute-start | bytes 393224 | tf_op jit(solution)/shard_map/ppermute | solution.py:332
  31.7 2.5 %collective-permute-start.2 = (bf16[8,64,128]{2,1,0:T(8,128)(2,1)}, bf16[8,64,128]{2,1,0:T(8,128)(2,1)S(1)}, u32[]{:S(2)}, u32[]{:S(2)}) collective-permute-start(bf16[8,64,128]{2,1,0:T(8,128)(2,1)} %get-tuple-element.45), channel_id=1, source_target_pairs={{0,128},{64,192},{128,256},{192,320},{256,384},{320,448},{384,0},{... | collective-permute-start | bytes 393224 | tf_op jit(solution)/shard_map/ppermute | solution.py:332
  34.2 4.9 %collective-permute-start.3 = (bf16[8,64,128]{2,1,0:T(8,128)(2,1)}, bf16[8,64,128]{2,1,0:T(8,128)(2,1)S(1)}, u32[]{:S(2)}, u32[]{:S(2)}) collective-permute-start(bf16[8,64,128]{2,1,0:T(8,128)(2,1)} %get-tuple-element.46), channel_id=1, source_target_pairs={{0,384},{64,448},{128,0},{192,64},{256,128},{320,192},{384,256},{4... | collective-permute-start | bytes 393224 | tf_op jit(solution)/shard_map/ppermute | solution.py:332
  39.1 5.0 %collective-permute-done.2.refs_2_ = bf16[8,64,128]{2,1,0:T(8,128)(2,1)S(1)} collective-permute-done((bf16[8,64,128]{2,1,0:T(8,128)(2,1)}, bf16[8,64,128]{2,1,0:T(8,128)(2,1)S(1)}, u32[]{:S(2)}, u32[]{:S(2)}) %collective-permute-start.2) | collective-permute-done | bytes 131104 | tf_op jit(solution)/shard_map/ppermute | solution.py:332
  44.1 5.4 %collective-permute-done.3.refs_6_ = bf16[8,64,128]{2,1,0:T(8,128)(2,1)S(1)} collective-permute-done((bf16[8,64,128]{2,1,0:T(8,128)(2,1)}, bf16[8,64,128]{2,1,0:T(8,128)(2,1)S(1)}, u32[]{:S(2)}, u32[]{:S(2)}) %collective-permute-start.3) | collective-permute-done | bytes 131104 | tf_op jit(solution)/shard_map/ppermute | solution.py:332
  49.5 4.0 %collective-permute-start.4 = (bf16[8,64,128]{2,1,0:T(8,128)(2,1)}, bf16[8,64,128]{2,1,0:T(8,128)(2,1)S(1)}, u32[]{:S(2)}, u32[]{:S(2)}) collective-permute-start(bf16[8,64,128]{2,1,0:T(8,128)(2,1)} %get-tuple-element.57), channel_id=1, source_target_pairs={{0,256},{64,320},{128,384},{192,448},{256,0},{320,64},{384,128},{4... | collective-permute-start | bytes 393224 | tf_op jit(solution)/shard_map/ppermute | solution.py:332
  53.4 2.2 %collective-permute-start.5 = (bf16[8,64,128]{2,1,0:T(8,128)(2,1)}, bf16[8,64,128]{2,1,0:T(8,128)(2,1)S(1)}, u32[]{:S(2)}, u32[]{:S(2)}) collective-permute-start(bf16[8,64,128]{2,1,0:T(8,128)(2,1)} %get-tuple-element.58), channel_id=1, source_target_pairs={{0,192},{64,256},{128,320},{192,384},{256,448},{320,0},{384,64},{4... | collective-permute-start | bytes 393224 | tf_op jit(solution)/shard_map/ppermute | solution.py:332
  55.6 6.1 %collective-permute-start.6 = (bf16[8,64,128]{2,1,0:T(8,128)(2,1)}, bf16[8,64,128]{2,1,0:T(8,128)(2,1)S(1)}, u32[]{:S(2)}, u32[]{:S(2)}) collective-permute-start(bf16[8,64,128]{2,1,0:T(8,128)(2,1)} %get-tuple-element.59), channel_id=1, source_target_pairs={{0,320},{64,384},{128,448},{192,0},{256,64},{320,128},{384,192},{4... | collective-permute-start | bytes 393224 | tf_op jit(solution)/shard_map/ppermute | solution.py:332
  61.7 3.1 %shard_map.67.own = f32[64,256]{1,0:T(8,128)} custom-call(s32[1,256]{1,0:T(1,128)} %get-tuple-element.55.code, bf16[256,512]{1,0:T(8,128)(2,1)} %rows.2, bf16[2048,512]{1,0:T(8,128)(2,1)} %bitcast.7), custom_call_target="tpu_custom_call" | custom-call | flops 536870912 | bytes 2097152 | tf_op jit(solution)/shard_map/pallas_call | solution.py:180
  64.8 9.6 %all-gather.3.cloned.1.call-done = bf16[2176,512]{1,0:T(8,128)(2,1)} async-done(((bf16[272,512]{1,0:T(8,128)(2,1)}), bf16[2176,512]{1,0:T(8,128)(2,1)}) %all-gather.3.cloned.1.call-update) | async-done | bytes 2228240 | tf_op jit(solution)/shard_map/all_gather | solution.py:342
  74.4 6.9 %shard_map.68 = f32[8,16,8,128]{3,2,1,0:T(8,128)} custom-call(bf16[8,272,512]{2,1,0:T(8,128)(2,1)} %bitcast.8, bf16[4,1024,512]{2,1,0:T(8,128)(2,1)} %bitcast.2.down, f32[64,256]{1,0:T(8,128)} %shard_map.67.own), custom_call_target="tpu_custom_call" | custom-call | flops 1073741824 | bytes 6422528 | tf_op jit(solution)/shard_map/pallas_call | solution.py:229
  81.4 0.6 copy-done.3
  82.0 14.6 %all-to-all-start.1 = ((f32[128,8,128]{2,1,0:T(8,128)}), f32[128,8,128]{2,1,0:T(8,128)S(1)}, u32[]{:S(2)}, u32[]{:S(2)}) async-start(f32[128,8,128]{2,1,0:T(8,128)} %bitcast.9), calls=%async_computation.1 | async-start | bytes 1048576 | tf_op jit(solution)/shard_map/all_to_all | solution.py:363
  96.7 0.9 copy-done.4
  97.5 1.0 shard_map.70
  98.5 0.7 copy-done.1
  99.2 2.8 %collective-permute-start.7 = (bf16[16,64,128]{2,1,0:T(8,128)(2,1)}, bf16[16,64,128]{2,1,0:T(8,128)(2,1)S(1)}, u32[]{:S(2)}, u32[]{:S(2)}) collective-permute-start(bf16[16,64,128]{2,1,0:T(8,128)(2,1)} %get-tuple-element.70), channel_id=1, source_target_pairs={{0,16},{16,32},{32,48},{48,0},{1,17},{17,33},{33,49},{49,1},{2,18}... | collective-permute-start | bytes 786440 | tf_op jit(solution)/shard_map/ppermute | solution.py:332
  102.0 4.4 %collective-permute-start.8 = (bf16[16,64,128]{2,1,0:T(8,128)(2,1)}, bf16[16,64,128]{2,1,0:T(8,128)(2,1)S(1)}, u32[]{:S(2)}, u32[]{:S(2)}) collective-permute-start(bf16[16,64,128]{2,1,0:T(8,128)(2,1)} %get-tuple-element.71), channel_id=1, source_target_pairs={{0,32},{16,48},{32,0},{48,16},{1,33},{17,49},{33,1},{49,17},{2,34}... | collective-permute-start | bytes 786440 | tf_op jit(solution)/shard_map/ppermute | solution.py:332
  106.3 3.1 %collective-permute-start.9 = (bf16[16,64,128]{2,1,0:T(8,128)(2,1)}, bf16[16,64,128]{2,1,0:T(8,128)(2,1)S(1)}, u32[]{:S(2)}, u32[]{:S(2)}) collective-permute-start(bf16[16,64,128]{2,1,0:T(8,128)(2,1)} %get-tuple-element.72), channel_id=1, source_target_pairs={{0,48},{16,0},{32,16},{48,32},{1,49},{17,1},{33,17},{49,33},{2,50}... | collective-permute-start | bytes 786440 | tf_op jit(solution)/shard_map/ppermute | solution.py:332
  109.4 6.7 %all-to-all-done.1.parts = f32[128,8,128]{2,1,0:T(8,128)S(1)} async-done(((f32[128,8,128]{2,1,0:T(8,128)}), f32[128,8,128]{2,1,0:T(8,128)S(1)}, u32[]{:S(2)}, u32[]{:S(2)}) %all-to-all-start.1) | async-done | bytes 524320 | tf_op jit(solution)/shard_map/all_to_all | solution.py:363
  116.1 0.8 shard_map.69
  116.9 5.4 %all-to-all-start.2 = ((f32[16,8,128]{2,1,0:T(8,128)}), f32[16,8,128]{2,1,0:T(8,128)S(1)}, u32[]{:S(2)}, u32[]{:S(2)}) async-start(f32[16,8,128]{2,1,0:T(8,128)} %shard_map.69), calls=%async_computation.2 | async-start | bytes 131072 | tf_op jit(solution)/shard_map/all_to_all | solution.py:364
  122.3 7.7 %all-to-all-done.2.shrink = f32[16,8,128]{2,1,0:T(8,128)S(1)} async-done(((f32[16,8,128]{2,1,0:T(8,128)}), f32[16,8,128]{2,1,0:T(8,128)S(1)}, u32[]{:S(2)}, u32[]{:S(2)}) %all-to-all-start.2) | async-done | bytes 65568 | tf_op jit(solution)/shard_map/all_to_all | solution.py:364
  130.1 0.6 copy-done.9
  130.7 5.1 %shard_map.71 = bf16[256,128]{1,0:T(8,128)(2,1)} custom-call(f32[16,8,128]{2,1,0:T(8,128)} %copy-done.9, s32[1,256]{1,0:T(1,128)} %get-tuple-element.55.code, f32[256,128]{1,0:T(8,128)} %reduce-scatter.2.cloned.1.call-done.base, bf16[32,64,128]{2,1,0:T(8,128)(2,1)} %up.3, bf16[16,64,128]{2,1,0:T(8,128)(2,1)} %copy-done.1, bf16[16,64,128]{2,1,0:T(8,128)(2,1)} %copy-done.6, ...), custom_call_target="tpu_custom_call" | custom-call | tf_op jit(solution)/shard_map/pallas_call | solution.py:318
  (29 shorter events, 0.1 us)
Async XLA Ops:
  7.4 12.2 %copy-start = (bf16[512,2048]{1,0:T(8,128)(2,1)S(1)}, bf16[512,2048]{1,0:T(8,128)(2,1)}, u32[]{:S(2)}) copy-start(bf16[512,2048]{1,0:T(8,128)(2,1)} %param.9) | copy-start | bytes 6291460
  7.4 67.1 %all-gather.3.cloned.1.call-start = ((), (), s32[]{:S(2)}) async-start(), calls=%async_computation.5 | async-start | bytes 2506752 | tf_op jit(solution)/shard_map/all_gather | solution.py:342
  14.5 5.1 %copy-start.5 = (bf16[256,512]{1,0:T(8,128)(2,1)S(1)}, bf16[256,512]{1,0:T(8,128)(2,1)}, u32[]{:S(2)}) copy-start(bf16[256,512]{1,0:T(8,128)(2,1)} %rows.2) | copy-start | bytes 786436
  14.5 50.3 %all-to-all-start = ((bf16[4,16,64,512]{3,2,1,0:T(8,128)(2,1)}), bf16[4,16,64,512]{3,2,1,0:T(8,128)(2,1)}, u32[]{:S(2)}, u32[]{:S(2)}) async-start(bf16[4,16,64,512]{3,2,1,0:T(8,128)(2,1)} %get-tuple-element.40), calls=%async_computation | async-start | bytes 8388608 | tf_op jit(solution)/shard_map/all_to_all | solution.py:344
  19.5 102.8 %reduce-scatter.2.cloned.1.call-start = ((), (), s32[]{:S(2)}) async-start(), calls=%async_computation.4 | async-start | bytes 2228224 | tf_op jit(solution)/shard_map/reduce_scatter | solution.py:348
  23.8 15.3 %collective-permute-start = (bf16[8,64,128]{2,1,0:T(8,128)(2,1)}, bf16[8,64,128]{2,1,0:T(8,128)(2,1)S(1)}, u32[]{:S(2)}, u32[]{:S(2)}) collective-permute-start(bf16[8,64,128]{2,1,0:T(8,128)(2,1)} %get-tuple-element.43), channel_id=1, source_target_pairs={{0,64},{64,128},{128,192},{192,256},{256,320},{320,384},{384,448},... | collective-permute-start | bytes 393224 | tf_op jit(solution)/shard_map/ppermute | solution.py:332
  27.9 11.2 %collective-permute-start.1 = (bf16[8,64,128]{2,1,0:T(8,128)(2,1)}, bf16[8,64,128]{2,1,0:T(8,128)(2,1)S(1)}, u32[]{:S(2)}, u32[]{:S(2)}) collective-permute-start(bf16[8,64,128]{2,1,0:T(8,128)(2,1)} %get-tuple-element.44), channel_id=1, source_target_pairs={{0,448},{64,0},{128,64},{192,128},{256,192},{320,256},{384,320},{4... | collective-permute-start | bytes 393224 | tf_op jit(solution)/shard_map/ppermute | solution.py:332
  31.7 12.4 %collective-permute-start.2 = (bf16[8,64,128]{2,1,0:T(8,128)(2,1)}, bf16[8,64,128]{2,1,0:T(8,128)(2,1)S(1)}, u32[]{:S(2)}, u32[]{:S(2)}) collective-permute-start(bf16[8,64,128]{2,1,0:T(8,128)(2,1)} %get-tuple-element.45), channel_id=1, source_target_pairs={{0,128},{64,192},{128,256},{192,320},{256,384},{320,448},{384,0},{... | collective-permute-start | bytes 393224 | tf_op jit(solution)/shard_map/ppermute | solution.py:332
  34.2 15.3 %collective-permute-start.3 = (bf16[8,64,128]{2,1,0:T(8,128)(2,1)}, bf16[8,64,128]{2,1,0:T(8,128)(2,1)S(1)}, u32[]{:S(2)}, u32[]{:S(2)}) collective-permute-start(bf16[8,64,128]{2,1,0:T(8,128)(2,1)} %get-tuple-element.46), channel_id=1, source_target_pairs={{0,384},{64,448},{128,0},{192,64},{256,128},{320,192},{384,256},{4... | collective-permute-start | bytes 393224 | tf_op jit(solution)/shard_map/ppermute | solution.py:332
  49.5 31.9 %collective-permute-start.4 = (bf16[8,64,128]{2,1,0:T(8,128)(2,1)}, bf16[8,64,128]{2,1,0:T(8,128)(2,1)S(1)}, u32[]{:S(2)}, u32[]{:S(2)}) collective-permute-start(bf16[8,64,128]{2,1,0:T(8,128)(2,1)} %get-tuple-element.57), channel_id=1, source_target_pairs={{0,256},{64,320},{128,384},{192,448},{256,0},{320,64},{384,128},{4... | collective-permute-start | bytes 393224 | tf_op jit(solution)/shard_map/ppermute | solution.py:332
  53.4 27.9 %collective-permute-start.5 = (bf16[8,64,128]{2,1,0:T(8,128)(2,1)}, bf16[8,64,128]{2,1,0:T(8,128)(2,1)S(1)}, u32[]{:S(2)}, u32[]{:S(2)}) collective-permute-start(bf16[8,64,128]{2,1,0:T(8,128)(2,1)} %get-tuple-element.58), channel_id=1, source_target_pairs={{0,192},{64,256},{128,320},{192,384},{256,448},{320,0},{384,64},{4... | collective-permute-start | bytes 393224 | tf_op jit(solution)/shard_map/ppermute | solution.py:332
  55.6 25.7 %collective-permute-start.6 = (bf16[8,64,128]{2,1,0:T(8,128)(2,1)}, bf16[8,64,128]{2,1,0:T(8,128)(2,1)S(1)}, u32[]{:S(2)}, u32[]{:S(2)}) collective-permute-start(bf16[8,64,128]{2,1,0:T(8,128)(2,1)} %get-tuple-element.59), channel_id=1, source_target_pairs={{0,320},{64,384},{128,448},{192,0},{256,64},{320,128},{384,192},{4... | collective-permute-start | bytes 393224 | tf_op jit(solution)/shard_map/ppermute | solution.py:332
  74.4 22.2 %copy-start.2 = (bf16[8,64,128]{2,1,0:T(8,128)(2,1)S(1)}, bf16[8,64,128]{2,1,0:T(8,128)(2,1)}, u32[]{:S(2)}) copy-start(bf16[8,64,128]{2,1,0:T(8,128)(2,1)} %get-tuple-element.61.refs_0_) | copy-start | bytes 393220
  81.4 0.7 copy-start.3
  82.0 34.1 %all-to-all-start.1 = ((f32[128,8,128]{2,1,0:T(8,128)}), f32[128,8,128]{2,1,0:T(8,128)S(1)}, u32[]{:S(2)}, u32[]{:S(2)}) async-start(f32[128,8,128]{2,1,0:T(8,128)} %bitcast.9), calls=%async_computation.1 | async-start | bytes 1048576 | tf_op jit(solution)/shard_map/all_to_all | solution.py:363
  96.6 0.9 copy-start.4
  98.5 0.7 copy-start.1
  99.2 23.0 %collective-permute-start.7 = (bf16[16,64,128]{2,1,0:T(8,128)(2,1)}, bf16[16,64,128]{2,1,0:T(8,128)(2,1)S(1)}, u32[]{:S(2)}, u32[]{:S(2)}) collective-permute-start(bf16[16,64,128]{2,1,0:T(8,128)(2,1)} %get-tuple-element.70), channel_id=1, source_target_pairs={{0,16},{16,32},{32,48},{48,0},{1,17},{17,33},{33,49},{49,1},{2,18}... | collective-permute-start | bytes 786440 | tf_op jit(solution)/shard_map/ppermute | solution.py:332
  102.0 20.3 %collective-permute-start.8 = (bf16[16,64,128]{2,1,0:T(8,128)(2,1)}, bf16[16,64,128]{2,1,0:T(8,128)(2,1)S(1)}, u32[]{:S(2)}, u32[]{:S(2)}) collective-permute-start(bf16[16,64,128]{2,1,0:T(8,128)(2,1)} %get-tuple-element.71), channel_id=1, source_target_pairs={{0,32},{16,48},{32,0},{48,16},{1,33},{17,49},{33,1},{49,17},{2,34}... | collective-permute-start | bytes 786440 | tf_op jit(solution)/shard_map/ppermute | solution.py:332
  106.3 15.9 %collective-permute-start.9 = (bf16[16,64,128]{2,1,0:T(8,128)(2,1)}, bf16[16,64,128]{2,1,0:T(8,128)(2,1)S(1)}, u32[]{:S(2)}, u32[]{:S(2)}) collective-permute-start(bf16[16,64,128]{2,1,0:T(8,128)(2,1)} %get-tuple-element.72), channel_id=1, source_target_pairs={{0,48},{16,0},{32,16},{48,32},{1,49},{17,1},{33,17},{49,33},{2,50}... | collective-permute-start | bytes 786440 | tf_op jit(solution)/shard_map/ppermute | solution.py:332
  116.9 13.2 %all-to-all-start.2 = ((f32[16,8,128]{2,1,0:T(8,128)}), f32[16,8,128]{2,1,0:T(8,128)S(1)}, u32[]{:S(2)}, u32[]{:S(2)}) async-start(f32[16,8,128]{2,1,0:T(8,128)} %shard_map.69), calls=%async_computation.2 | async-start | bytes 131072 | tf_op jit(solution)/shard_map/all_to_all | solution.py:364
  122.2 7.8 %copy-start.6 = (bf16[16,64,128]{2,1,0:T(8,128)(2,1)}, bf16[16,64,128]{2,1,0:T(8,128)(2,1)S(1)}, u32[]{:S(2)}) copy-start(bf16[16,64,128]{2,1,0:T(8,128)(2,1)S(1)} %collective-permute-done.7.refs_1_) | copy-start | bytes 786436
  122.2 7.8 %copy-start.7 = (bf16[16,64,128]{2,1,0:T(8,128)(2,1)}, bf16[16,64,128]{2,1,0:T(8,128)(2,1)S(1)}, u32[]{:S(2)}) copy-start(bf16[16,64,128]{2,1,0:T(8,128)(2,1)S(1)} %collective-permute-done.8.refs_2_) | copy-start | bytes 786436
  122.3 7.8 %copy-start.8 = (bf16[16,64,128]{2,1,0:T(8,128)(2,1)}, bf16[16,64,128]{2,1,0:T(8,128)(2,1)S(1)}, u32[]{:S(2)}) copy-start(bf16[16,64,128]{2,1,0:T(8,128)(2,1)S(1)} %collective-permute-done.9.refs_3_) | copy-start | bytes 786436
  130.1 0.6 copy-start.9
Sparse Core Ops, SparseCore 0:
  10.3 64.1 all-gather.2
Sparse Core Ops, SparseCore 1:
  22.8 67.4 reduce-scatter.1

commit v14 on v13

--- a/solution.py
+++ b/solution.py
@@ -284,12 +284,11 @@
     at = jnp.where(imported < 0, code[...], resident + (e * Y + d) * LIMIT + imported % LIMIT)
     column = jnp.transpose(jnp.broadcast_to(at, (8, count)).astype(jnp.float32))[:, :1]
     pair = jnp.concatenate([rows, rows], axis=1)
-    high = pair.astype(jnp.bfloat16).astype(jnp.float32)
-    low = pair - high
+    high = pair.astype(jnp.bfloat16)
+    low = (pair - high.astype(jnp.float32)).astype(jnp.bfloat16)
     half = lax.broadcasted_iota(jnp.int32, pair.shape, 1) // rank
-    wanted = jnp.broadcast_to(column, pair.shape) - half.astype(jnp.float32)
-    both = jnp.concatenate([high, low], axis=0)
-    wanted = jnp.concatenate([wanted, wanted], axis=0)
+    wanted = (jnp.broadcast_to(column, pair.shape) - half.astype(jnp.float32)).astype(jnp.bfloat16)
+    nothing = jnp.zeros(pair.shape, jnp.bfloat16)
     total = jnp.zeros((2 * count, out.shape[1]), jnp.float32)
     step = 4
     bounds = [resident + e * imported_each for e in range(X + 1)]
@@ -298,12 +297,13 @@
             copies[0].wait()
         if 2 * first in bounds:
             copies[1 + bounds.index(2 * first)].wait()
+        hits = [wanted == jnp.bfloat16(2 * p) for p in range(first, first + step)]
         placed = jnp.concatenate(
             [
-                jnp.where(wanted == float(2 * p), both, 0.0).astype(jnp.bfloat16)
-                for p in range(first, first + step)
+                jnp.concatenate([jnp.where(hit, part, nothing) for hit in hits], axis=1)
+                for part in (high, low)
             ],
-            axis=1,
+            axis=0,
         )
         maps = held[2 * first : 2 * (first + step)].reshape(2 * step * rank, out.shape[1])
         total = total + jnp.dot(placed, maps, preferred_element_type=jnp.float32)
@@ -351,7 +351,7 @@
     ups = pick_up(picked, adapter_up)
     near, far = (1, 7, 2, 6), (4, 3, 5)
     moved = [shift(ups[d], "y", Y, d) for d in near]
-    moved, later = lax.optimization_barrier((moved, [ups[d] for d in far]))
+    moved, later, own = lax.optimization_barrier((moved, [ups[d] for d in far], own))
     moved_far = [shift(ups_d, "y", Y, d) for ups_d, d in zip(later, far)]
     down, moved = lax.optimization_barrier((down, moved))
     parts = imported_shrink(resident, rows, down, own)

time: 144 us -> 144 us (level)
    ppermute x10, waiting for transfers between devices: 10.4 us -> 7.68 us  [shift(): lax.ppermute(array, axis, [(i, (i + by) % size) for i in range(size)])]
    all_gather x1, waiting for transfers between devices: 9.59 us -> 12.2 us  [shards(): rows = lax.all_gather(sent, ('y', 'c'), axis_index_groups=rings)]
  transfers between devices with their start and end apart: 15 -> 15, of which waited for: 5 -> 6; matrix products, arithmetic and copies ran while one was open for 1% -> 1% of each run, Pallas kernels for 13% -> 13%
where the time goes in v14:
time: 144 us; the launch traced here: 143 us
  starting transfers between devices  62.1 us (43%)
  waiting for transfers between devices  34.8 us (24%)
  Pallas kernels  26 us (18%)
  between operations  15.1 us (10%)
  local copies, waits for them, and re-layouts  2.88 us (2%)
  matrix products  2.09 us (1%)
    ppermute x10, starting transfers between devices, shift(): lax.ppermute(array, axis, [(i, (i + by) % size) for i in range(size)])  37.8 us
    all_to_all x1, starting transfers between devices, shards(): lax.all_to_all(parts.reshape(Y * T, 8, 128), ('y', 'z', 'c'), 0, 0, tiled...  13.9 us
    all_gather x1, waiting for transfers between devices, shards(): rows = lax.all_gather(sent, ('y', 'c'), axis_index_groups=rings)  12.2 us
    all_to_all x1, waiting for transfers between devices, shards(): shrink = lax.all_to_all(add_and_spread(parts), ('z', 'c'), 0, 0, tiled=True)  7.75 us
    ppermute x10, waiting for transfers between devices, shift(): lax.ppermute(array, axis, [(i, (i + by) % size) for i in range(size)])  7.68 us
    pallas_call x1, Pallas kernels, imported_shrink(): pl.pallas_call(functools.partial(imported_kernel, resident), out_shape=ja...  6.88 us
    all_to_all x1, waiting for transfers between devices, shards(): lax.all_to_all(parts.reshape(Y * T, 8, 128), ('y', 'z', 'c'), 0, 0, tiled...  6.13 us
    all_to_all x1, starting transfers between devices, shards(): shrink = lax.all_to_all(add_and_spread(parts), ('z', 'c'), 0, 0, tiled=True)  5.36 us
  transfers between devices with their start and end apart: 15, of which 6 were waited for; matrix products, arithmetic and copies ran while one was open for 1% of the time, Pallas kernels for 13%

profile of v14, /device:TPU:1, one launch (start us, length us, event | category | flops | bytes accessed | tf_op | source)
XLA Modules:
  0.0 143.0 jit_solution(448885972593852579)
XLA Ops:
  7.4 2.1 %shard_map.64 = (bf16[272,512]{1,0:T(8,128)(2,1)}, s32[1,256]{1,0:T(1,128)}) custom-call(s32[32,31]{1,0:T(8,128)} %plan.3, s32[1,256]{1,0:T(1,128)} %bitcast.10, bf16[256,512]{1,0:T(8,128)(2,1)} %rows.2), custom_call_target="tpu_custom_call" | custom-call | bytes 524288 | tf_op jit(solution)/shard_map/pallas_call | solution.py:107
  9.5 5.0 %shard_map.65 = (bf16[4,16,64,512]{3,2,1,0:T(8,128)(2,1)}, s32[32,128]{1,0:T(8,128)}) custom-call(s32[32,31]{1,0:T(8,128)} %plan.3, bf16[32,64,512]{2,1,0:T(8,128)(2,1)} %down.1), custom_call_target="tpu_custom_call" | custom-call | bytes 6291456 | tf_op jit(solution)/shard_map/pallas_call | solution.py:66
  14.5 5.0 %all-to-all-start = ((bf16[4,16,64,512]{3,2,1,0:T(8,128)(2,1)}), bf16[4,16,64,512]{3,2,1,0:T(8,128)(2,1)}, u32[]{:S(2)}, u32[]{:S(2)}) async-start(bf16[4,16,64,512]{3,2,1,0:T(8,128)(2,1)} %get-tuple-element.41), calls=%async_computation | async-start | bytes 8388608 | tf_op jit(solution)/shard_map/all_to_all | solution.py:344
  19.6 2.1 %fusion = f32[256,2048]{1,0:T(8,128)} fusion(bf16[256,512]{1,0:T(8,128)(2,1)S(1)} %copy-done.5, bf16[512,2048]{1,0:T(8,128)(2,1)S(1)} %copy-done), kind=kOutput, calls=%fused_computation | convolution fusion | flops 536870912 | bytes 4456448 | tf_op jit(solution)/shard_map/dot_general | solution.py:347
  21.7 2.1 %shard_map.66 = (bf16[8,64,128]{2,1,0:T(8,128)(2,1)}, bf16[8,64,128]{2,1,0:T(8,128)(2,1)}, bf16[8,64,128]{2,1,0:T(8,128)(2,1)}, bf16[8,64,128]{2,1,0:T(8,128)(2,...) custom-call(s32[32,128]{1,0:T(8,128)} %get-tuple-element.43.picked, ...), custom_call_target="tpu_custom_call" | custom-call | bytes 1572864 | tf_op jit(solution)/shard_map/pallas_call | solution.py:131
  23.8 4.2 %collective-permute-start = (bf16[8,64,128]{2,1,0:T(8,128)(2,1)}, bf16[8,64,128]{2,1,0:T(8,128)(2,1)S(1)}, u32[]{:S(2)}, u32[]{:S(2)}) collective-permute-start(bf16[8,64,128]{2,1,0:T(8,128)(2,1)} %get-tuple-element.44), channel_id=1, source_target_pairs={{0,64},{64,128},{128,192},{192,256},{256,320},{320,384},{384,448},... | collective-permute-start | bytes 393224 | tf_op jit(solution)/shard_map/ppermute | solution.py:332
  28.0 3.8 %collective-permute-start.1 = (bf16[8,64,128]{2,1,0:T(8,128)(2,1)}, bf16[8,64,128]{2,1,0:T(8,128)(2,1)S(1)}, u32[]{:S(2)}, u32[]{:S(2)}) collective-permute-start(bf16[8,64,128]{2,1,0:T(8,128)(2,1)} %get-tuple-element.45), channel_id=1, source_target_pairs={{0,448},{64,0},{128,64},{192,128},{256,192},{320,256},{384,320},{4... | collective-permute-start | bytes 393224 | tf_op jit(solution)/shard_map/ppermute | solution.py:332
  31.8 2.5 %collective-permute-start.2 = (bf16[8,64,128]{2,1,0:T(8,128)(2,1)}, bf16[8,64,128]{2,1,0:T(8,128)(2,1)S(1)}, u32[]{:S(2)}, u32[]{:S(2)}) collective-permute-start(bf16[8,64,128]{2,1,0:T(8,128)(2,1)} %get-tuple-element.46), channel_id=1, source_target_pairs={{0,128},{64,192},{128,256},{192,320},{256,384},{320,448},{384,0},{... | collective-permute-start | bytes 393224 | tf_op jit(solution)/shard_map/ppermute | solution.py:332
  34.3 4.9 %collective-permute-start.3 = (bf16[8,64,128]{2,1,0:T(8,128)(2,1)}, bf16[8,64,128]{2,1,0:T(8,128)(2,1)S(1)}, u32[]{:S(2)}, u32[]{:S(2)}) collective-permute-start(bf16[8,64,128]{2,1,0:T(8,128)(2,1)} %get-tuple-element.47), channel_id=1, source_target_pairs={{0,384},{64,448},{128,0},{192,64},{256,128},{320,192},{384,256},{4... | collective-permute-start | bytes 393224 | tf_op jit(solution)/shard_map/ppermute | solution.py:332
  39.2 3.1 %shard_map.67.own = f32[64,256]{1,0:T(8,128)} custom-call(s32[1,256]{1,0:T(1,128)} %get-tuple-element.51.code, bf16[256,512]{1,0:T(8,128)(2,1)} %rows.2, bf16[2048,512]{1,0:T(8,128)(2,1)} %bitcast.7), custom_call_target="tpu_custom_call" | custom-call | flops 536870912 | bytes 2097152 | tf_op jit(solution)/shard_map/pallas_call | solution.py:180
  42.3 1.9 %collective-permute-done.2.refs_2_ = bf16[8,64,128]{2,1,0:T(8,128)(2,1)S(1)} collective-permute-done((bf16[8,64,128]{2,1,0:T(8,128)(2,1)}, bf16[8,64,128]{2,1,0:T(8,128)(2,1)S(1)}, u32[]{:S(2)}, u32[]{:S(2)}) %collective-permute-start.2) | collective-permute-done | bytes 131104 | tf_op jit(solution)/shard_map/ppermute | solution.py:332
  44.2 5.8 %collective-permute-done.3.refs_6_ = bf16[8,64,128]{2,1,0:T(8,128)(2,1)S(1)} collective-permute-done((bf16[8,64,128]{2,1,0:T(8,128)(2,1)}, bf16[8,64,128]{2,1,0:T(8,128)(2,1)S(1)}, u32[]{:S(2)}, u32[]{:S(2)}) %collective-permute-start.3) | collective-permute-done | bytes 131104 | tf_op jit(solution)/shard_map/ppermute | solution.py:332
  50.0 3.4 %collective-permute-start.4 = (bf16[8,64,128]{2,1,0:T(8,128)(2,1)S(1)}, bf16[8,64,128]{2,1,0:T(8,128)(2,1)S(1)}, u32[]{:S(2)}, u32[]{:S(2)}) collective-permute-start(bf16[8,64,128]{2,1,0:T(8,128)(2,1)S(1)} %copy-done.12), channel_id=1, source_target_pairs={{0,256},{64,320},{128,384},{192,448},{256,0},{320,64},{384,128},{4... | collective-permute-start | bytes 393224 | tf_op jit(solution)/shard_map/ppermute | solution.py:332
  53.4 2.4 %collective-permute-start.5 = (bf16[8,64,128]{2,1,0:T(8,128)(2,1)S(1)}, bf16[8,64,128]{2,1,0:T(8,128)(2,1)S(1)}, u32[]{:S(2)}, u32[]{:S(2)}) collective-permute-start(bf16[8,64,128]{2,1,0:T(8,128)(2,1)S(1)} %copy-done.11), channel_id=1, source_target_pairs={{0,192},{64,256},{128,320},{192,384},{256,448},{320,0},{384,64},{4... | collective-permute-start | bytes 393224 | tf_op jit(solution)/shard_map/ppermute | solution.py:332
  55.8 5.9 %collective-permute-start.6 = (bf16[8,64,128]{2,1,0:T(8,128)(2,1)S(1)}, bf16[8,64,128]{2,1,0:T(8,128)(2,1)S(1)}, u32[]{:S(2)}, u32[]{:S(2)}) collective-permute-start(bf16[8,64,128]{2,1,0:T(8,128)(2,1)S(1)} %copy-done.10), channel_id=1, source_target_pairs={{0,320},{64,384},{128,448},{192,0},{256,64},{320,128},{384,192},{4... | collective-permute-start | bytes 393224 | tf_op jit(solution)/shard_map/ppermute | solution.py:332
  61.7 1.0 all-to-all-done
  62.8 12.2 %all-gather.3.cloned.1.call-done = bf16[2176,512]{1,0:T(8,128)(2,1)} async-done(((bf16[272,512]{1,0:T(8,128)(2,1)}), bf16[2176,512]{1,0:T(8,128)(2,1)}) %all-gather.3.cloned.1.call-update) | async-done | bytes 2228240 | tf_op jit(solution)/shard_map/all_gather | solution.py:342
  74.9 6.9 %shard_map.68 = f32[8,16,8,128]{3,2,1,0:T(8,128)} custom-call(bf16[8,272,512]{2,1,0:T(8,128)(2,1)} %bitcast.8, bf16[4,1024,512]{2,1,0:T(8,128)(2,1)} %bitcast.3.down, f32[64,256]{1,0:T(8,128)} %shard_map.67.own), custom_call_target="tpu_custom_call" | custom-call | flops 1073741824 | bytes 6422528 | tf_op jit(solution)/shard_map/pallas_call | solution.py:229
  81.9 0.6 copy-done.3
  82.5 13.9 %all-to-all-start.1 = ((f32[128,8,128]{2,1,0:T(8,128)}), f32[128,8,128]{2,1,0:T(8,128)S(1)}, u32[]{:S(2)}, u32[]{:S(2)}) async-start(f32[128,8,128]{2,1,0:T(8,128)} %bitcast.9), calls=%async_computation.1 | async-start | bytes 1048576 | tf_op jit(solution)/shard_map/all_to_all | solution.py:363
  96.4 0.9 copy-done.4
  97.3 1.0 shard_map.70
  98.3 0.7 copy-done.1
  99.0 3.3 %collective-permute-start.7 = (bf16[16,64,128]{2,1,0:T(8,128)(2,1)}, bf16[16,64,128]{2,1,0:T(8,128)(2,1)S(1)}, u32[]{:S(2)}, u32[]{:S(2)}) collective-permute-start(bf16[16,64,128]{2,1,0:T(8,128)(2,1)} %get-tuple-element.72), channel_id=1, source_target_pairs={{0,16},{16,32},{32,48},{48,0},{1,17},{17,33},{33,49},{49,1},{2,18}... | collective-permute-start | bytes 786440 | tf_op jit(solution)/shard_map/ppermute | solution.py:332
  102.3 4.3 %collective-permute-start.8 = (bf16[16,64,128]{2,1,0:T(8,128)(2,1)}, bf16[16,64,128]{2,1,0:T(8,128)(2,1)S(1)}, u32[]{:S(2)}, u32[]{:S(2)}) collective-permute-start(bf16[16,64,128]{2,1,0:T(8,128)(2,1)} %get-tuple-element.73), channel_id=1, source_target_pairs={{0,32},{16,48},{32,0},{48,16},{1,33},{17,49},{33,1},{49,17},{2,34}... | collective-permute-start | bytes 786440 | tf_op jit(solution)/shard_map/ppermute | solution.py:332
  106.6 3.1 %collective-permute-start.9 = (bf16[16,64,128]{2,1,0:T(8,128)(2,1)}, bf16[16,64,128]{2,1,0:T(8,128)(2,1)S(1)}, u32[]{:S(2)}, u32[]{:S(2)}) collective-permute-start(bf16[16,64,128]{2,1,0:T(8,128)(2,1)} %get-tuple-element.74), channel_id=1, source_target_pairs={{0,48},{16,0},{32,16},{48,32},{1,49},{17,1},{33,17},{49,33},{2,50}... | collective-permute-start | bytes 786440 | tf_op jit(solution)/shard_map/ppermute | solution.py:332
  109.8 6.1 %all-to-all-done.1.parts = f32[128,8,128]{2,1,0:T(8,128)S(1)} async-done(((f32[128,8,128]{2,1,0:T(8,128)}), f32[128,8,128]{2,1,0:T(8,128)S(1)}, u32[]{:S(2)}, u32[]{:S(2)}) %all-to-all-start.1) | async-done | bytes 524320 | tf_op jit(solution)/shard_map/all_to_all | solution.py:363
  115.9 0.8 shard_map.69
  116.7 5.4 %all-to-all-start.2 = ((f32[16,8,128]{2,1,0:T(8,128)}), f32[16,8,128]{2,1,0:T(8,128)S(1)}, u32[]{:S(2)}, u32[]{:S(2)}) async-start(f32[16,8,128]{2,1,0:T(8,128)} %shard_map.69), calls=%async_computation.2 | async-start | bytes 131072 | tf_op jit(solution)/shard_map/all_to_all | solution.py:364
  122.1 7.7 %all-to-all-done.2.shrink = f32[16,8,128]{2,1,0:T(8,128)S(1)} async-done(((f32[16,8,128]{2,1,0:T(8,128)}), f32[16,8,128]{2,1,0:T(8,128)S(1)}, u32[]{:S(2)}, u32[]{:S(2)}) %all-to-all-start.2) | async-done | bytes 65568 | tf_op jit(solution)/shard_map/all_to_all | solution.py:364
  129.9 0.6 copy-done.9
  130.5 5.1 %shard_map.71 = bf16[256,128]{1,0:T(8,128)(2,1)} custom-call(f32[16,8,128]{2,1,0:T(8,128)} %copy-done.9, s32[1,256]{1,0:T(1,128)} %get-tuple-element.51.code, f32[256,128]{1,0:T(8,128)} %reduce-scatter.2.cloned.1.call-done.base, bf16[32,64,128]{2,1,0:T(8,128)(2,1)} %up.3, bf16[16,64,128]{2,1,0:T(8,128)(2,1)} %copy-done.1, bf16[16,64,128]{2,1,0:T(8,128)(2,1)} %copy-done.6, ...), custom_call_target="tpu_custom_call" | custom-call | tf_op jit(solution)/shard_map/pallas_call | solution.py:318
  (35 shorter events, 0.2 us)
Async XLA Ops:
  7.4 12.2 %copy-start = (bf16[512,2048]{1,0:T(8,128)(2,1)S(1)}, bf16[512,2048]{1,0:T(8,128)(2,1)}, u32[]{:S(2)}) copy-start(bf16[512,2048]{1,0:T(8,128)(2,1)} %param.9) | copy-start | bytes 6291460
  7.4 67.6 %all-gather.3.cloned.1.call-start = ((), (), s32[]{:S(2)}) async-start(), calls=%async_computation.5 | async-start | bytes 2506752 | tf_op jit(solution)/shard_map/all_gather | solution.py:342
  14.5 5.1 %copy-start.5 = (bf16[256,512]{1,0:T(8,128)(2,1)S(1)}, bf16[256,512]{1,0:T(8,128)(2,1)}, u32[]{:S(2)}) copy-start(bf16[256,512]{1,0:T(8,128)(2,1)} %rows.2) | copy-start | bytes 786436
  14.5 48.2 %all-to-all-start = ((bf16[4,16,64,512]{3,2,1,0:T(8,128)(2,1)}), bf16[4,16,64,512]{3,2,1,0:T(8,128)(2,1)}, u32[]{:S(2)}, u32[]{:S(2)}) async-start(bf16[4,16,64,512]{3,2,1,0:T(8,128)(2,1)} %get-tuple-element.41), calls=%async_computation | async-start | bytes 8388608 | tf_op jit(solution)/shard_map/all_to_all | solution.py:344
  19.5 102.6 %reduce-scatter.2.cloned.1.call-start = ((), (), s32[]{:S(2)}) async-start(), calls=%async_computation.4 | async-start | bytes 2228224 | tf_op jit(solution)/shard_map/reduce_scatter | solution.py:348
  23.8 26.2 %copy-start.12 = (bf16[8,64,128]{2,1,0:T(8,128)(2,1)S(1)}, bf16[8,64,128]{2,1,0:T(8,128)(2,1)}, u32[]{:S(2)}) copy-start(bf16[8,64,128]{2,1,0:T(8,128)(2,1)} %get-tuple-element.59) | copy-start | bytes 393220
  23.8 29.6 %copy-start.11 = (bf16[8,64,128]{2,1,0:T(8,128)(2,1)S(1)}, bf16[8,64,128]{2,1,0:T(8,128)(2,1)}, u32[]{:S(2)}) copy-start(bf16[8,64,128]{2,1,0:T(8,128)(2,1)} %get-tuple-element.60) | copy-start | bytes 393220
  23.8 32.0 %copy-start.10 = (bf16[8,64,128]{2,1,0:T(8,128)(2,1)S(1)}, bf16[8,64,128]{2,1,0:T(8,128)(2,1)}, u32[]{:S(2)}) copy-start(bf16[8,64,128]{2,1,0:T(8,128)(2,1)} %get-tuple-element.61) | copy-start | bytes 393220
  23.8 18.5 %collective-permute-start = (bf16[8,64,128]{2,1,0:T(8,128)(2,1)}, bf16[8,64,128]{2,1,0:T(8,128)(2,1)S(1)}, u32[]{:S(2)}, u32[]{:S(2)}) collective-permute-start(bf16[8,64,128]{2,1,0:T(8,128)(2,1)} %get-tuple-element.44), channel_id=1, source_target_pairs={{0,64},{64,128},{128,192},{192,256},{256,320},{320,384},{384,448},... | collective-permute-start | bytes 393224 | tf_op jit(solution)/shard_map/ppermute | solution.py:332
  28.0 14.3 %collective-permute-start.1 = (bf16[8,64,128]{2,1,0:T(8,128)(2,1)}, bf16[8,64,128]{2,1,0:T(8,128)(2,1)S(1)}, u32[]{:S(2)}, u32[]{:S(2)}) collective-permute-start(bf16[8,64,128]{2,1,0:T(8,128)(2,1)} %get-tuple-element.45), channel_id=1, source_target_pairs={{0,448},{64,0},{128,64},{192,128},{256,192},{320,256},{384,320},{4... | collective-permute-start | bytes 393224 | tf_op jit(solution)/shard_map/ppermute | solution.py:332
  31.8 12.4 %collective-permute-start.2 = (bf16[8,64,128]{2,1,0:T(8,128)(2,1)}, bf16[8,64,128]{2,1,0:T(8,128)(2,1)S(1)}, u32[]{:S(2)}, u32[]{:S(2)}) collective-permute-start(bf16[8,64,128]{2,1,0:T(8,128)(2,1)} %get-tuple-element.46), channel_id=1, source_target_pairs={{0,128},{64,192},{128,256},{192,320},{256,384},{320,448},{384,0},{... | collective-permute-start | bytes 393224 | tf_op jit(solution)/shard_map/ppermute | solution.py:332
  34.3 15.7 %collective-permute-start.3 = (bf16[8,64,128]{2,1,0:T(8,128)(2,1)}, bf16[8,64,128]{2,1,0:T(8,128)(2,1)S(1)}, u32[]{:S(2)}, u32[]{:S(2)}) collective-permute-start(bf16[8,64,128]{2,1,0:T(8,128)(2,1)} %get-tuple-element.47), channel_id=1, source_target_pairs={{0,384},{64,448},{128,0},{192,64},{256,128},{320,192},{384,256},{4... | collective-permute-start | bytes 393224 | tf_op jit(solution)/shard_map/ppermute | solution.py:332
  50.0 31.8 %collective-permute-start.4 = (bf16[8,64,128]{2,1,0:T(8,128)(2,1)S(1)}, bf16[8,64,128]{2,1,0:T(8,128)(2,1)S(1)}, u32[]{:S(2)}, u32[]{:S(2)}) collective-permute-start(bf16[8,64,128]{2,1,0:T(8,128)(2,1)S(1)} %copy-done.12), channel_id=1, source_target_pairs={{0,256},{64,320},{128,384},{192,448},{256,0},{320,64},{384,128},{4... | collective-permute-start | bytes 393224 | tf_op jit(solution)/shard_map/ppermute | solution.py:332
  53.4 28.4 %collective-permute-start.5 = (bf16[8,64,128]{2,1,0:T(8,128)(2,1)S(1)}, bf16[8,64,128]{2,1,0:T(8,128)(2,1)S(1)}, u32[]{:S(2)}, u32[]{:S(2)}) collective-permute-start(bf16[8,64,128]{2,1,0:T(8,128)(2,1)S(1)} %copy-done.11), channel_id=1, source_target_pairs={{0,192},{64,256},{128,320},{192,384},{256,448},{320,0},{384,64},{4... | collective-permute-start | bytes 393224 | tf_op jit(solution)/shard_map/ppermute | solution.py:332
  55.8 26.0 %collective-permute-start.6 = (bf16[8,64,128]{2,1,0:T(8,128)(2,1)S(1)}, bf16[8,64,128]{2,1,0:T(8,128)(2,1)S(1)}, u32[]{:S(2)}, u32[]{:S(2)}) collective-permute-start(bf16[8,64,128]{2,1,0:T(8,128)(2,1)S(1)} %copy-done.10), channel_id=1, source_target_pairs={{0,320},{64,384},{128,448},{192,0},{256,64},{320,128},{384,192},{4... | collective-permute-start | bytes 393224 | tf_op jit(solution)/shard_map/ppermute | solution.py:332
  74.9 21.5 %copy-start.2 = (bf16[8,64,128]{2,1,0:T(8,128)(2,1)S(1)}, bf16[8,64,128]{2,1,0:T(8,128)(2,1)}, u32[]{:S(2)}) copy-start(bf16[8,64,128]{2,1,0:T(8,128)(2,1)} %get-tuple-element.63.refs_0_) | copy-start | bytes 393220
  81.8 0.7 copy-start.3
  82.5 33.4 %all-to-all-start.1 = ((f32[128,8,128]{2,1,0:T(8,128)}), f32[128,8,128]{2,1,0:T(8,128)S(1)}, u32[]{:S(2)}, u32[]{:S(2)}) async-start(f32[128,8,128]{2,1,0:T(8,128)} %bitcast.9), calls=%async_computation.1 | async-start | bytes 1048576 | tf_op jit(solution)/shard_map/all_to_all | solution.py:363
  96.4 0.9 copy-start.4
  98.3 0.7 copy-start.1
  99.0 23.0 %collective-permute-start.7 = (bf16[16,64,128]{2,1,0:T(8,128)(2,1)}, bf16[16,64,128]{2,1,0:T(8,128)(2,1)S(1)}, u32[]{:S(2)}, u32[]{:S(2)}) collective-permute-start(bf16[16,64,128]{2,1,0:T(8,128)(2,1)} %get-tuple-element.72), channel_id=1, source_target_pairs={{0,16},{16,32},{32,48},{48,0},{1,17},{17,33},{33,49},{49,1},{2,18}... | collective-permute-start | bytes 786440 | tf_op jit(solution)/shard_map/ppermute | solution.py:332
  102.3 19.7 %collective-permute-start.8 = (bf16[16,64,128]{2,1,0:T(8,128)(2,1)}, bf16[16,64,128]{2,1,0:T(8,128)(2,1)S(1)}, u32[]{:S(2)}, u32[]{:S(2)}) collective-permute-start(bf16[16,64,128]{2,1,0:T(8,128)(2,1)} %get-tuple-element.73), channel_id=1, source_target_pairs={{0,32},{16,48},{32,0},{48,16},{1,33},{17,49},{33,1},{49,17},{2,34}... | collective-permute-start | bytes 786440 | tf_op jit(solution)/shard_map/ppermute | solution.py:332
  106.6 15.4 %collective-permute-start.9 = (bf16[16,64,128]{2,1,0:T(8,128)(2,1)}, bf16[16,64,128]{2,1,0:T(8,128)(2,1)S(1)}, u32[]{:S(2)}, u32[]{:S(2)}) collective-permute-start(bf16[16,64,128]{2,1,0:T(8,128)(2,1)} %get-tuple-element.74), channel_id=1, source_target_pairs={{0,48},{16,0},{32,16},{48,32},{1,49},{17,1},{33,17},{49,33},{2,50}... | collective-permute-start | bytes 786440 | tf_op jit(solution)/shard_map/ppermute | solution.py:332
  116.7 13.2 %all-to-all-start.2 = ((f32[16,8,128]{2,1,0:T(8,128)}), f32[16,8,128]{2,1,0:T(8,128)S(1)}, u32[]{:S(2)}, u32[]{:S(2)}) async-start(f32[16,8,128]{2,1,0:T(8,128)} %shard_map.69), calls=%async_computation.2 | async-start | bytes 131072 | tf_op jit(solution)/shard_map/all_to_all | solution.py:364
  122.0 7.8 %copy-start.6 = (bf16[16,64,128]{2,1,0:T(8,128)(2,1)}, bf16[16,64,128]{2,1,0:T(8,128)(2,1)S(1)}, u32[]{:S(2)}) copy-start(bf16[16,64,128]{2,1,0:T(8,128)(2,1)S(1)} %collective-permute-done.7.refs_1_) | copy-start | bytes 786436
  122.0 7.8 %copy-start.7 = (bf16[16,64,128]{2,1,0:T(8,128)(2,1)}, bf16[16,64,128]{2,1,0:T(8,128)(2,1)S(1)}, u32[]{:S(2)}) copy-start(bf16[16,64,128]{2,1,0:T(8,128)(2,1)S(1)} %collective-permute-done.8.refs_2_) | copy-start | bytes 786436
  122.1 7.8 %copy-start.8 = (bf16[16,64,128]{2,1,0:T(8,128)(2,1)}, bf16[16,64,128]{2,1,0:T(8,128)(2,1)S(1)}, u32[]{:S(2)}) copy-start(bf16[16,64,128]{2,1,0:T(8,128)(2,1)S(1)} %collective-permute-done.9.refs_3_) | copy-start | bytes 786436
  129.8 0.6 copy-start.9
Sparse Core Ops, SparseCore 0:
  10.3 64.6 all-gather.2
Sparse Core Ops, SparseCore 1:
  22.8 67.4 reduce-scatter.1

commit v15 on v14

--- a/solution.py
+++ b/solution.py
@@ -290,7 +290,7 @@
     wanted = (jnp.broadcast_to(column, pair.shape) - half.astype(jnp.float32)).astype(jnp.bfloat16)
     nothing = jnp.zeros(pair.shape, jnp.bfloat16)
     total = jnp.zeros((2 * count, out.shape[1]), jnp.float32)
-    step = 4
+    step = 8
     bounds = [resident + e * imported_each for e in range(X + 1)]
     for first in range(0, held.shape[0] // 2, step):
         if first == 0:
@@ -349,14 +349,15 @@
     own = local_shrink(code, late, adapter_down)
 
     ups = pick_up(picked, adapter_up)
-    near, far = (1, 7, 2, 6), (4, 3, 5)
+    near, far, last = (1, 7, 2, 6), 4, (3, 5)
     moved = [shift(ups[d], "y", Y, d) for d in near]
-    moved, later, own = lax.optimization_barrier((moved, [ups[d] for d in far], own))
-    moved_far = [shift(ups_d, "y", Y, d) for ups_d, d in zip(later, far)]
-    down, moved = lax.optimization_barrier((down, moved))
+    moved, later, own = lax.optimization_barrier((moved, ups[far], own))
+    moved.append(shift(later, "y", Y, far))
+    moved, later = lax.optimization_barrier((moved, [ups[d] for d in last]))
+    moved_far = [shift(ups_d, "y", Y, d) for ups_d, d in zip(later, last)]
     parts = imported_shrink(resident, rows, down, own)
     parts, moved_far = lax.optimization_barrier((parts, moved_far))
-    moved = dict(zip(near + far, moved + moved_far)) | {0: ups[0]}
+    moved = dict(zip(near + (far,) + last, moved + moved_far)) | {0: ups[0]}
     ups = turn([moved[d] for d in range(Y)])
     tables = [ups[0]] + [shift(ups[e], "x", X, e) for e in range(1, X)]
 

time: 144 us -> 148 us (1.028)
  starting transfers between devices: 62.1 us -> 68.2 us
  waiting for transfers between devices: 34.8 us -> 32.5 us
    all_gather x1, waiting for transfers between devices: 12.2 us -> 0.02 us  [shards(): rows = lax.all_gather(sent, ('y', 'c'), axis_index_groups=rings)]
    ppermute x10, waiting for transfers between devices: 7.68 us -> 18.4 us  [shift(): lax.ppermute(array, axis, [(i, (i + by) % size) for i in range(size)])]
    all_to_all x1, starting transfers between devices: 13.9 us -> 20.2 us  [shards(): lax.all_to_all(parts.reshape(Y * T, 8, 128), ('y', 'z', 'c'), 0, 0, tiled...]
  transfers between devices with their start and end apart: 15 -> 15, of which waited for: 6 -> 5; matrix products, arithmetic and copies ran while one was open for 1% -> 1% of each run, Pallas kernels for 13% -> 13%
where the time goes in v15:
time: 148 us; the launch traced here: 147 us
  starting transfers between devices  68.2 us (46%)
  waiting for transfers between devices  32.5 us (22%)
  Pallas kernels  26 us (18%)
  between operations  15.1 us (10%)
  local copies, waits for them, and re-layouts  2.88 us (2%)
  matrix products  2.09 us (1%)
    ppermute x10, starting transfers between devices, shift(): lax.ppermute(array, axis, [(i, (i + by) % size) for i in range(size)])  37.6 us
    all_to_all x1, starting transfers between devices, shards(): lax.all_to_all(parts.reshape(Y * T, 8, 128), ('y', 'z', 'c'), 0, 0, tiled...  20.2 us
    ppermute x10, waiting for transfers between devices, shift(): lax.ppermute(array, axis, [(i, (i + by) % size) for i in range(size)])  18.4 us
    all_to_all x1, waiting for transfers between devices, shards(): shrink = lax.all_to_all(add_and_spread(parts), ('z', 'c'), 0, 0, tiled=True)  7.75 us
    pallas_call x1, Pallas kernels, imported_shrink(): pl.pallas_call(functools.partial(imported_kernel, resident), out_shape=ja...  6.88 us
    all_to_all x1, waiting for transfers between devices, shards(): lax.all_to_all(parts.reshape(Y * T, 8, 128), ('y', 'z', 'c'), 0, 0, tiled...  6.34 us
    all_to_all x1, starting transfers between devices, shards(): shrink = lax.all_to_all(add_and_spread(parts), ('z', 'c'), 0, 0, tiled=True)  5.36 us
    pallas_call x1, Pallas kernels, expand(): pl.pallas_call(expand_kernel, out_shape=jax.ShapeDtypeStruct(base.shape,...  5.06 us
  transfers between devices with their start and end apart: 15, of which 5 were waited for; matrix products, arithmetic and copies ran while one was open for 1% of the time, Pallas kernels for 13%

profile of v15, /device:TPU:1, one launch (start us, length us, event | category | flops | bytes accessed | tf_op | source)
XLA Modules:
  0.0 146.8 jit_solution(119197660492336914)
XLA Ops:
  7.4 2.1 %shard_map.64 = (bf16[272,512]{1,0:T(8,128)(2,1)}, s32[1,256]{1,0:T(1,128)}) custom-call(s32[32,31]{1,0:T(8,128)} %plan.3, s32[1,256]{1,0:T(1,128)} %bitcast.10, bf16[256,512]{1,0:T(8,128)(2,1)} %rows.2), custom_call_target="tpu_custom_call" | custom-call | bytes 524288 | tf_op jit(solution)/shard_map/pallas_call | solution.py:107
  9.5 5.0 %shard_map.65 = (bf16[4,16,64,512]{3,2,1,0:T(8,128)(2,1)}, s32[32,128]{1,0:T(8,128)}) custom-call(s32[32,31]{1,0:T(8,128)} %plan.3, bf16[32,64,512]{2,1,0:T(8,128)(2,1)} %down.1), custom_call_target="tpu_custom_call" | custom-call | bytes 6291456 | tf_op jit(solution)/shard_map/pallas_call | solution.py:66
  14.5 5.0 %all-to-all-start = ((bf16[4,16,64,512]{3,2,1,0:T(8,128)(2,1)}), bf16[4,16,64,512]{3,2,1,0:T(8,128)(2,1)}, u32[]{:S(2)}, u32[]{:S(2)}) async-start(bf16[4,16,64,512]{3,2,1,0:T(8,128)(2,1)} %get-tuple-element.40), calls=%async_computation | async-start | bytes 8388608 | tf_op jit(solution)/shard_map/all_to_all | solution.py:344
  19.5 0.0 reduce-scatter.2.cloned.1.call-start
  19.6 2.1 %fusion = f32[256,2048]{1,0:T(8,128)} fusion(bf16[256,512]{1,0:T(8,128)(2,1)S(1)} %copy-done.5, bf16[512,2048]{1,0:T(8,128)(2,1)S(1)} %copy-done), kind=kOutput, calls=%fused_computation | convolution fusion | flops 536870912 | bytes 4456448 | tf_op jit(solution)/shard_map/dot_general | solution.py:347
  21.7 2.1 %shard_map.66 = (bf16[8,64,128]{2,1,0:T(8,128)(2,1)}, bf16[8,64,128]{2,1,0:T(8,128)(2,1)}, bf16[8,64,128]{2,1,0:T(8,128)(2,1)}, bf16[8,64,128]{2,1,0:T(8,128)(2,...) custom-call(s32[32,128]{1,0:T(8,128)} %get-tuple-element.42.picked, ...), custom_call_target="tpu_custom_call" | custom-call | bytes 1572864 | tf_op jit(solution)/shard_map/pallas_call | solution.py:131
  23.8 4.2 %collective-permute-start = (bf16[8,64,128]{2,1,0:T(8,128)(2,1)}, bf16[8,64,128]{2,1,0:T(8,128)(2,1)S(1)}, u32[]{:S(2)}, u32[]{:S(2)}) collective-permute-start(bf16[8,64,128]{2,1,0:T(8,128)(2,1)} %get-tuple-element.43), channel_id=1, source_target_pairs={{0,64},{64,128},{128,192},{192,256},{256,320},{320,384},{384,448},... | collective-permute-start | bytes 393224 | tf_op jit(solution)/shard_map/ppermute | solution.py:332
  28.0 3.8 %collective-permute-start.1 = (bf16[8,64,128]{2,1,0:T(8,128)(2,1)}, bf16[8,64,128]{2,1,0:T(8,128)(2,1)S(1)}, u32[]{:S(2)}, u32[]{:S(2)}) collective-permute-start(bf16[8,64,128]{2,1,0:T(8,128)(2,1)} %get-tuple-element.44), channel_id=1, source_target_pairs={{0,448},{64,0},{128,64},{192,128},{256,192},{320,256},{384,320},{4... | collective-permute-start | bytes 393224 | tf_op jit(solution)/shard_map/ppermute | solution.py:332
  31.8 2.5 %collective-permute-start.2 = (bf16[8,64,128]{2,1,0:T(8,128)(2,1)}, bf16[8,64,128]{2,1,0:T(8,128)(2,1)S(1)}, u32[]{:S(2)}, u32[]{:S(2)}) collective-permute-start(bf16[8,64,128]{2,1,0:T(8,128)(2,1)} %get-tuple-element.45), channel_id=1, source_target_pairs={{0,128},{64,192},{128,256},{192,320},{256,384},{320,448},{384,0},{... | collective-permute-start | bytes 393224 | tf_op jit(solution)/shard_map/ppermute | solution.py:332
  34.3 4.9 %collective-permute-start.3 = (bf16[8,64,128]{2,1,0:T(8,128)(2,1)}, bf16[8,64,128]{2,1,0:T(8,128)(2,1)S(1)}, u32[]{:S(2)}, u32[]{:S(2)}) collective-permute-start(bf16[8,64,128]{2,1,0:T(8,128)(2,1)} %get-tuple-element.46), channel_id=1, source_target_pairs={{0,384},{64,448},{128,0},{192,64},{256,128},{320,192},{384,256},{4... | collective-permute-start | bytes 393224 | tf_op jit(solution)/shard_map/ppermute | solution.py:332
  39.2 3.1 %shard_map.67.own = f32[64,256]{1,0:T(8,128)} custom-call(s32[1,256]{1,0:T(1,128)} %get-tuple-element.48.code, bf16[256,512]{1,0:T(8,128)(2,1)} %rows.2, bf16[2048,512]{1,0:T(8,128)(2,1)} %bitcast.7), custom_call_target="tpu_custom_call" | custom-call | flops 536870912 | bytes 2097152 | tf_op jit(solution)/shard_map/pallas_call | solution.py:180
  42.3 1.9 %collective-permute-done.2.refs_2_ = bf16[8,64,128]{2,1,0:T(8,128)(2,1)S(1)} collective-permute-done((bf16[8,64,128]{2,1,0:T(8,128)(2,1)}, bf16[8,64,128]{2,1,0:T(8,128)(2,1)S(1)}, u32[]{:S(2)}, u32[]{:S(2)}) %collective-permute-start.2) | collective-permute-done | bytes 131104 | tf_op jit(solution)/shard_map/ppermute | solution.py:332
  44.2 5.8 %collective-permute-done.3.refs_6_ = bf16[8,64,128]{2,1,0:T(8,128)(2,1)S(1)} collective-permute-done((bf16[8,64,128]{2,1,0:T(8,128)(2,1)}, bf16[8,64,128]{2,1,0:T(8,128)(2,1)S(1)}, u32[]{:S(2)}, u32[]{:S(2)}) %collective-permute-start.3) | collective-permute-done | bytes 131104 | tf_op jit(solution)/shard_map/ppermute | solution.py:332
  50.0 3.4 %collective-permute-start.4 = (bf16[8,64,128]{2,1,0:T(8,128)(2,1)S(1)}, bf16[8,64,128]{2,1,0:T(8,128)(2,1)S(1)}, u32[]{:S(2)}, u32[]{:S(2)}) collective-permute-start(bf16[8,64,128]{2,1,0:T(8,128)(2,1)S(1)} %copy-done.12), channel_id=1, source_target_pairs={{0,256},{64,320},{128,384},{192,448},{256,0},{320,64},{384,128},{4... | collective-permute-start | bytes 393224 | tf_op jit(solution)/shard_map/ppermute | solution.py:332
  53.4 10.7 %collective-permute-done.4.refs_4_ = bf16[8,64,128]{2,1,0:T(8,128)(2,1)S(1)} collective-permute-done((bf16[8,64,128]{2,1,0:T(8,128)(2,1)S(1)}, bf16[8,64,128]{2,1,0:T(8,128)(2,1)S(1)}, u32[]{:S(2)}, u32[]{:S(2)}) %collective-permute-start.4) | collective-permute-done | bytes 131104 | tf_op jit(solution)/shard_map/ppermute | solution.py:332
  64.1 4.4 %collective-permute-start.5 = (bf16[8,64,128]{2,1,0:T(8,128)(2,1)S(1)}, bf16[8,64,128]{2,1,0:T(8,128)(2,1)S(1)}, u32[]{:S(2)}, u32[]{:S(2)}) collective-permute-start(bf16[8,64,128]{2,1,0:T(8,128)(2,1)S(1)} %copy-done.11), channel_id=1, source_target_pairs={{0,192},{64,256},{128,320},{192,384},{256,448},{320,0},{384,64},{4... | collective-permute-start | bytes 393224 | tf_op jit(solution)/shard_map/ppermute | solution.py:332
  68.5 3.9 %collective-permute-start.6 = (bf16[8,64,128]{2,1,0:T(8,128)(2,1)S(1)}, bf16[8,64,128]{2,1,0:T(8,128)(2,1)S(1)}, u32[]{:S(2)}, u32[]{:S(2)}) collective-permute-start(bf16[8,64,128]{2,1,0:T(8,128)(2,1)S(1)} %copy-done.10), channel_id=1, source_target_pairs={{0,320},{64,384},{128,448},{192,0},{256,64},{320,128},{384,192},{4... | collective-permute-start | bytes 393224 | tf_op jit(solution)/shard_map/ppermute | solution.py:332
  72.5 6.9 %shard_map.68 = f32[8,16,8,128]{3,2,1,0:T(8,128)} custom-call(bf16[8,272,512]{2,1,0:T(8,128)(2,1)} %bitcast.8, bf16[4,1024,512]{2,1,0:T(8,128)(2,1)} %bitcast.2.down, f32[64,256]{1,0:T(8,128)} %shard_map.67.own), custom_call_target="tpu_custom_call" | custom-call | flops 1073741824 | bytes 6422528 | tf_op jit(solution)/shard_map/pallas_call | solution.py:229
  79.4 0.6 copy-done.3
  80.0 20.2 %all-to-all-start.1 = ((f32[128,8,128]{2,1,0:T(8,128)}), f32[128,8,128]{2,1,0:T(8,128)S(1)}, u32[]{:S(2)}, u32[]{:S(2)}) async-start(f32[128,8,128]{2,1,0:T(8,128)} %bitcast.9), calls=%async_computation.1 | async-start | bytes 1048576 | tf_op jit(solution)/shard_map/all_to_all | solution.py:364
  100.3 0.9 copy-done.4
  101.2 1.0 shard_map.70
  102.1 0.7 copy-done.1
  102.8 3.1 %collective-permute-start.7 = (bf16[16,64,128]{2,1,0:T(8,128)(2,1)}, bf16[16,64,128]{2,1,0:T(8,128)(2,1)S(1)}, u32[]{:S(2)}, u32[]{:S(2)}) collective-permute-start(bf16[16,64,128]{2,1,0:T(8,128)(2,1)} %get-tuple-element.70), channel_id=1, source_target_pairs={{0,16},{16,32},{32,48},{48,0},{1,17},{17,33},{33,49},{49,1},{2,18}... | collective-permute-start | bytes 786440 | tf_op jit(solution)/shard_map/ppermute | solution.py:332
  105.9 4.4 %collective-permute-start.8 = (bf16[16,64,128]{2,1,0:T(8,128)(2,1)}, bf16[16,64,128]{2,1,0:T(8,128)(2,1)S(1)}, u32[]{:S(2)}, u32[]{:S(2)}) collective-permute-start(bf16[16,64,128]{2,1,0:T(8,128)(2,1)} %get-tuple-element.71), channel_id=1, source_target_pairs={{0,32},{16,48},{32,0},{48,16},{1,33},{17,49},{33,1},{49,17},{2,34}... | collective-permute-start | bytes 786440 | tf_op jit(solution)/shard_map/ppermute | solution.py:332
  110.3 3.0 %collective-permute-start.9 = (bf16[16,64,128]{2,1,0:T(8,128)(2,1)}, bf16[16,64,128]{2,1,0:T(8,128)(2,1)S(1)}, u32[]{:S(2)}, u32[]{:S(2)}) collective-permute-start(bf16[16,64,128]{2,1,0:T(8,128)(2,1)} %get-tuple-element.72), channel_id=1, source_target_pairs={{0,48},{16,0},{32,16},{48,32},{1,49},{17,1},{33,17},{49,33},{2,50}... | collective-permute-start | bytes 786440 | tf_op jit(solution)/shard_map/ppermute | solution.py:332
  113.4 6.3 %all-to-all-done.1.parts = f32[128,8,128]{2,1,0:T(8,128)S(1)} async-done(((f32[128,8,128]{2,1,0:T(8,128)}), f32[128,8,128]{2,1,0:T(8,128)S(1)}, u32[]{:S(2)}, u32[]{:S(2)}) %all-to-all-start.1) | async-done | bytes 524320 | tf_op jit(solution)/shard_map/all_to_all | solution.py:364
  119.7 0.8 shard_map.69
  120.5 5.4 %all-to-all-start.2 = ((f32[16,8,128]{2,1,0:T(8,128)}), f32[16,8,128]{2,1,0:T(8,128)S(1)}, u32[]{:S(2)}, u32[]{:S(2)}) async-start(f32[16,8,128]{2,1,0:T(8,128)} %shard_map.69), calls=%async_computation.2 | async-start | bytes 131072 | tf_op jit(solution)/shard_map/all_to_all | solution.py:365
  125.9 7.7 %all-to-all-done.2.shrink = f32[16,8,128]{2,1,0:T(8,128)S(1)} async-done(((f32[16,8,128]{2,1,0:T(8,128)}), f32[16,8,128]{2,1,0:T(8,128)S(1)}, u32[]{:S(2)}, u32[]{:S(2)}) %all-to-all-start.2) | async-done | bytes 65568 | tf_op jit(solution)/shard_map/all_to_all | solution.py:365
  133.7 0.6 copy-done.9
  134.3 5.1 %shard_map.71 = bf16[256,128]{1,0:T(8,128)(2,1)} custom-call(f32[16,8,128]{2,1,0:T(8,128)} %copy-done.9, s32[1,256]{1,0:T(1,128)} %get-tuple-element.48.code, f32[256,128]{1,0:T(8,128)} %reduce-scatter.2.cloned.1.call-done.base, bf16[32,64,128]{2,1,0:T(8,128)(2,1)} %up.3, bf16[16,64,128]{2,1,0:T(8,128)(2,1)} %copy-done.1, bf16[16,64,128]{2,1,0:T(8,128)(2,1)} %copy-done.6, ...), custom_call_target="tpu_custom_call" | custom-call | tf_op jit(solution)/shard_map/pallas_call | solution.py:318
  (35 shorter events, 0.1 us)
Async XLA Ops:
  7.4 12.2 %copy-start = (bf16[512,2048]{1,0:T(8,128)(2,1)S(1)}, bf16[512,2048]{1,0:T(8,128)(2,1)}, u32[]{:S(2)}) copy-start(bf16[512,2048]{1,0:T(8,128)(2,1)} %param.9) | copy-start | bytes 6291460
  7.4 65.1 %all-gather.3.cloned.1.call-start = ((), (), s32[]{:S(2)}) async-start(), calls=%async_computation.5 | async-start | bytes 2506752 | tf_op jit(solution)/shard_map/all_gather | solution.py:342
  14.5 5.1 %copy-start.5 = (bf16[256,512]{1,0:T(8,128)(2,1)S(1)}, bf16[256,512]{1,0:T(8,128)(2,1)}, u32[]{:S(2)}) copy-start(bf16[256,512]{1,0:T(8,128)(2,1)} %rows.2) | copy-start | bytes 786436
  14.5 57.9 %all-to-all-start = ((bf16[4,16,64,512]{3,2,1,0:T(8,128)(2,1)}), bf16[4,16,64,512]{3,2,1,0:T(8,128)(2,1)}, u32[]{:S(2)}, u32[]{:S(2)}) async-start(bf16[4,16,64,512]{3,2,1,0:T(8,128)(2,1)} %get-tuple-element.40), calls=%async_computation | async-start | bytes 8388608 | tf_op jit(solution)/shard_map/all_to_all | solution.py:344
  19.5 106.4 %reduce-scatter.2.cloned.1.call-start = ((), (), s32[]{:S(2)}) async-start(), calls=%async_computation.4 | async-start | bytes 2228224 | tf_op jit(solution)/shard_map/reduce_scatter | solution.py:348
  23.8 26.2 %copy-start.12 = (bf16[8,64,128]{2,1,0:T(8,128)(2,1)S(1)}, bf16[8,64,128]{2,1,0:T(8,128)(2,1)}, u32[]{:S(2)}) copy-start(bf16[8,64,128]{2,1,0:T(8,128)(2,1)} %get-tuple-element.55) | copy-start | bytes 393220
  23.8 40.3 %copy-start.11 = (bf16[8,64,128]{2,1,0:T(8,128)(2,1)S(1)}, bf16[8,64,128]{2,1,0:T(8,128)(2,1)}, u32[]{:S(2)}) copy-start(bf16[8,64,128]{2,1,0:T(8,128)(2,1)} %get-tuple-element.58) | copy-start | bytes 393220
  23.8 44.6 %copy-start.10 = (bf16[8,64,128]{2,1,0:T(8,128)(2,1)S(1)}, bf16[8,64,128]{2,1,0:T(8,128)(2,1)}, u32[]{:S(2)}) copy-start(bf16[8,64,128]{2,1,0:T(8,128)(2,1)} %get-tuple-element.59) | copy-start | bytes 393220
  23.8 18.5 %collective-permute-start = (bf16[8,64,128]{2,1,0:T(8,128)(2,1)}, bf16[8,64,128]{2,1,0:T(8,128)(2,1)S(1)}, u32[]{:S(2)}, u32[]{:S(2)}) collective-permute-start(bf16[8,64,128]{2,1,0:T(8,128)(2,1)} %get-tuple-element.43), channel_id=1, source_target_pairs={{0,64},{64,128},{128,192},{192,256},{256,320},{320,384},{384,448},... | collective-permute-start | bytes 393224 | tf_op jit(solution)/shard_map/ppermute | solution.py:332
  28.0 14.3 %collective-permute-start.1 = (bf16[8,64,128]{2,1,0:T(8,128)(2,1)}, bf16[8,64,128]{2,1,0:T(8,128)(2,1)S(1)}, u32[]{:S(2)}, u32[]{:S(2)}) collective-permute-start(bf16[8,64,128]{2,1,0:T(8,128)(2,1)} %get-tuple-element.44), channel_id=1, source_target_pairs={{0,448},{64,0},{128,64},{192,128},{256,192},{320,256},{384,320},{4... | collective-permute-start | bytes 393224 | tf_op jit(solution)/shard_map/ppermute | solution.py:332
  31.8 12.4 %collective-permute-start.2 = (bf16[8,64,128]{2,1,0:T(8,128)(2,1)}, bf16[8,64,128]{2,1,0:T(8,128)(2,1)S(1)}, u32[]{:S(2)}, u32[]{:S(2)}) collective-permute-start(bf16[8,64,128]{2,1,0:T(8,128)(2,1)} %get-tuple-element.45), channel_id=1, source_target_pairs={{0,128},{64,192},{128,256},{192,320},{256,384},{320,448},{384,0},{... | collective-permute-start | bytes 393224 | tf_op jit(solution)/shard_map/ppermute | solution.py:332
  34.3 15.7 %collective-permute-start.3 = (bf16[8,64,128]{2,1,0:T(8,128)(2,1)}, bf16[8,64,128]{2,1,0:T(8,128)(2,1)S(1)}, u32[]{:S(2)}, u32[]{:S(2)}) collective-permute-start(bf16[8,64,128]{2,1,0:T(8,128)(2,1)} %get-tuple-element.46), channel_id=1, source_target_pairs={{0,384},{64,448},{128,0},{192,64},{256,128},{320,192},{384,256},{4... | collective-permute-start | bytes 393224 | tf_op jit(solution)/shard_map/ppermute | solution.py:332
  50.0 14.1 %collective-permute-start.4 = (bf16[8,64,128]{2,1,0:T(8,128)(2,1)S(1)}, bf16[8,64,128]{2,1,0:T(8,128)(2,1)S(1)}, u32[]{:S(2)}, u32[]{:S(2)}) collective-permute-start(bf16[8,64,128]{2,1,0:T(8,128)(2,1)S(1)} %copy-done.12), channel_id=1, source_target_pairs={{0,256},{64,320},{128,384},{192,448},{256,0},{320,64},{384,128},{4... | collective-permute-start | bytes 393224 | tf_op jit(solution)/shard_map/ppermute | solution.py:332
  64.1 15.2 %collective-permute-start.5 = (bf16[8,64,128]{2,1,0:T(8,128)(2,1)S(1)}, bf16[8,64,128]{2,1,0:T(8,128)(2,1)S(1)}, u32[]{:S(2)}, u32[]{:S(2)}) collective-permute-start(bf16[8,64,128]{2,1,0:T(8,128)(2,1)S(1)} %copy-done.11), channel_id=1, source_target_pairs={{0,192},{64,256},{128,320},{192,384},{256,448},{320,0},{384,64},{4... | collective-permute-start | bytes 393224 | tf_op jit(solution)/shard_map/ppermute | solution.py:332
  68.5 10.9 %collective-permute-start.6 = (bf16[8,64,128]{2,1,0:T(8,128)(2,1)S(1)}, bf16[8,64,128]{2,1,0:T(8,128)(2,1)S(1)}, u32[]{:S(2)}, u32[]{:S(2)}) collective-permute-start(bf16[8,64,128]{2,1,0:T(8,128)(2,1)S(1)} %copy-done.10), channel_id=1, source_target_pairs={{0,320},{64,384},{128,448},{192,0},{256,64},{320,128},{384,192},{4... | collective-permute-start | bytes 393224 | tf_op jit(solution)/shard_map/ppermute | solution.py:332
  72.4 27.8 %copy-start.2 = (bf16[8,64,128]{2,1,0:T(8,128)(2,1)S(1)}, bf16[8,64,128]{2,1,0:T(8,128)(2,1)}, u32[]{:S(2)}) copy-start(bf16[8,64,128]{2,1,0:T(8,128)(2,1)} %get-tuple-element.61.refs_0_) | copy-start | bytes 393220
  79.4 0.7 copy-start.3
  80.0 39.7 %all-to-all-start.1 = ((f32[128,8,128]{2,1,0:T(8,128)}), f32[128,8,128]{2,1,0:T(8,128)S(1)}, u32[]{:S(2)}, u32[]{:S(2)}) async-start(f32[128,8,128]{2,1,0:T(8,128)} %bitcast.9), calls=%async_computation.1 | async-start | bytes 1048576 | tf_op jit(solution)/shard_map/all_to_all | solution.py:364
  100.3 0.9 copy-start.4
  102.1 0.7 copy-start.1
  102.8 23.0 %collective-permute-start.7 = (bf16[16,64,128]{2,1,0:T(8,128)(2,1)}, bf16[16,64,128]{2,1,0:T(8,128)(2,1)S(1)}, u32[]{:S(2)}, u32[]{:S(2)}) collective-permute-start(bf16[16,64,128]{2,1,0:T(8,128)(2,1)} %get-tuple-element.70), channel_id=1, source_target_pairs={{0,16},{16,32},{32,48},{48,0},{1,17},{17,33},{33,49},{49,1},{2,18}... | collective-permute-start | bytes 786440 | tf_op jit(solution)/shard_map/ppermute | solution.py:332
  105.9 19.9 %collective-permute-start.8 = (bf16[16,64,128]{2,1,0:T(8,128)(2,1)}, bf16[16,64,128]{2,1,0:T(8,128)(2,1)S(1)}, u32[]{:S(2)}, u32[]{:S(2)}) collective-permute-start(bf16[16,64,128]{2,1,0:T(8,128)(2,1)} %get-tuple-element.71), channel_id=1, source_target_pairs={{0,32},{16,48},{32,0},{48,16},{1,33},{17,49},{33,1},{49,17},{2,34}... | collective-permute-start | bytes 786440 | tf_op jit(solution)/shard_map/ppermute | solution.py:332
  110.3 15.5 %collective-permute-start.9 = (bf16[16,64,128]{2,1,0:T(8,128)(2,1)}, bf16[16,64,128]{2,1,0:T(8,128)(2,1)S(1)}, u32[]{:S(2)}, u32[]{:S(2)}) collective-permute-start(bf16[16,64,128]{2,1,0:T(8,128)(2,1)} %get-tuple-element.72), channel_id=1, source_target_pairs={{0,48},{16,0},{32,16},{48,32},{1,49},{17,1},{33,17},{49,33},{2,50}... | collective-permute-start | bytes 786440 | tf_op jit(solution)/shard_map/ppermute | solution.py:332
  120.5 13.2 %all-to-all-start.2 = ((f32[16,8,128]{2,1,0:T(8,128)}), f32[16,8,128]{2,1,0:T(8,128)S(1)}, u32[]{:S(2)}, u32[]{:S(2)}) async-start(f32[16,8,128]{2,1,0:T(8,128)} %shard_map.69), calls=%async_computation.2 | async-start | bytes 131072 | tf_op jit(solution)/shard_map/all_to_all | solution.py:365
  125.8 7.8 %copy-start.6 = (bf16[16,64,128]{2,1,0:T(8,128)(2,1)}, bf16[16,64,128]{2,1,0:T(8,128)(2,1)S(1)}, u32[]{:S(2)}) copy-start(bf16[16,64,128]{2,1,0:T(8,128)(2,1)S(1)} %collective-permute-done.7.refs_1_) | copy-start | bytes 786436
  125.9 7.8 %copy-start.7 = (bf16[16,64,128]{2,1,0:T(8,128)(2,1)}, bf16[16,64,128]{2,1,0:T(8,128)(2,1)S(1)}, u32[]{:S(2)}) copy-start(bf16[16,64,128]{2,1,0:T(8,128)(2,1)S(1)} %collective-permute-done.8.refs_2_) | copy-start | bytes 786436
  125.9 7.8 %copy-start.8 = (bf16[16,64,128]{2,1,0:T(8,128)(2,1)}, bf16[16,64,128]{2,1,0:T(8,128)(2,1)S(1)}, u32[]{:S(2)}) copy-start(bf16[16,64,128]{2,1,0:T(8,128)(2,1)S(1)} %collective-permute-done.9.refs_3_) | copy-start | bytes 786436
  133.7 0.6 copy-start.9
Sparse Core Ops, SparseCore 0:
  10.3 58.8 all-gather.2
Sparse Core Ops, SparseCore 1:
  22.8 67.4 reduce-scatter.1
